TPU v7x, 32 devices: a whole 2x2x4 slice. The times are simulated.
32 devices in a mesh: dp: 4 (over y, x), fsdp: 8 (over z, core).
Axes of the slice: x: 2, y: 2, z: 4, core: 2. Of those that a mesh axis runs over, the one named last changes fastest.
Arguments:
- images: bfloat16 [1280, 16, 256], P(('dp', 'fsdp'))
- partner: int32 [1280], P(('dp', 'fsdp')), may hold values from 0 to 39
- mix_pair: int32 [1280, 2], P(('dp', 'fsdp')), may hold values from 1 to 8
- labels: int32 [1280], P(('dp', 'fsdp')), may hold values from 0 to 999
- step: int32 [1], replicated, may hold values from 2 to 20
- layer_mats: float32 [3, 512, 1536], P(None, 'fsdp')
- layer_side: float32 [3, 142, 1536], P(None, None, 'fsdp')
- layer_vecs: float32 [3, 576], P(None, 'fsdp')
- head_mat: float32 [1280, 1258], P('fsdp')
- fc_bias: float32 [1000], replicated, may hold values from -3 to 3
- mats_first: float32 [3, 512, 1536], P(None, 'fsdp')
- mats_second: float32 [3, 512, 1536], P(None, 'fsdp'), as said below
- side_first: float32 [3, 142, 1536], P(None, None, 'fsdp')
- side_second: float32 [3, 142, 1536], P(None, None, 'fsdp'), as said below
- vecs_first: float32 [3, 576], P(None, 'fsdp')
- vecs_second: float32 [3, 576], P(None, 'fsdp'), as said below
- head_first: float32 [1280, 1258], P('fsdp')
- head_second: float32 [1280, 1258], P('fsdp'), as said below
- bias_first: float32 [1000], replicated
- bias_second: float32 [1000], replicated, as said below
Outputs:
- loss: float32 [], replicated
- mats_new: float32 [3, 512, 1536], P(None, 'fsdp')
- mats_moment: float32 [3, 512, 1536], P(None, 'fsdp')
- mats_square: float32 [3, 512, 1536], P(None, 'fsdp')
- side_new: float32 [3, 142, 1536], P(None, None, 'fsdp')
- side_moment: float32 [3, 142, 1536], P(None, None, 'fsdp')
- side_square: float32 [3, 142, 1536], P(None, None, 'fsdp')
- vecs_new: float32 [3, 576], P(None, 'fsdp')
- vecs_moment: float32 [3, 576], P(None, 'fsdp')
- vecs_square: float32 [3, 576], P(None, 'fsdp')
- head_new: float32 [1280, 1258], P('fsdp')
- head_moment: float32 [1280, 1258], P('fsdp')
- head_square: float32 [1280, 1258], P('fsdp')
- bias_new: float32 [1000], replicated
- bias_moment: float32 [1000], replicated
- bias_square: float32 [1000], replicated
- norms: float32 [2, 17], replicated
Inputs may be any that keep to these rules, and one draw needn't show every extreme that they name: partner[i] indexes an image within the block of 40 consecutive images that holds image i. `mats_second`: entries are positive. `side_second`: entries are positive. `vecs_second`: entries are positive. `head_second`: entries are positive. `bias_second`: entries are positive.
All inputs are finite; a program needn't handle non-finite values.
Results may differ from a plain program's by a relative error of at most 0.01.
Values may be sent and summed in bfloat16 or wider, within the bound.
No kernel may reach another device: no remote copies, remote signals or barrier semaphores. Data moves between devices by JAX's collectives and lax.ppermute only.
A program may use at most 256 MiB of HBM per device.

v0:
```python
import jax
import jax.numpy as jnp
from jax import lax
from jax.sharding import PartitionSpec as P

WIDTH = 256
SQUEEZE = 64
CLASSES = 1000
EDGE = 4
LAYERS = 3
MAP = 16
SIDE = 142
HEADCOLS = 1258


EPS_BN = 0.001
BETA_ONE = 0.9
BETA_TWO = 0.999
EPS_ADAM = 1e-06
DECAY_RATE = 0.01
RATE_MATRIX = 0.5
RATE_VECTOR = 0.25
HIGHEST = lax.Precision.HIGHEST
ROWS_DIMS = (((0,), (0,)), ((), ()))
COLS_DIMS = (((1,), (1,)), ((), ()))


def in_blocks(array, dim, peers):
    before, after = (array.shape[:dim], array.shape[dim + 1 :])
    return jnp.moveaxis(array.reshape(*before, peers, -1, *after), dim, 0)


def sum_at_owner(array, axis, dim):
    peers = lax.axis_size(axis)
    tiles = lax.all_to_all(in_blocks(array, dim, peers), axis, 0, 0, tiled=True)
    return jnp.sum(tiles.astype(jnp.float32), axis=0)


def silu_slope(values):
    sigmoid = jax.nn.sigmoid(values)
    return sigmoid * (1.0 + values * (1.0 - sigmoid))


def batch_normalize(hidden, row_count):
    totals, squares = lax.psum(
        (jnp.sum(hidden, axis=0), jnp.sum(hidden * hidden, axis=0)), ("dp", "fsdp")
    )
    center = totals / row_count
    inverse = lax.rsqrt(squares / row_count - center * center + EPS_BN)
    return ((hidden - center) * inverse, inverse)


def normalize_back(grad_out, normed, inverse, norm_gain, row_count):
    local_bias = jnp.sum(grad_out, axis=0)
    local_gain = jnp.sum(grad_out * normed, axis=0)
    sum_bias, sum_gain = lax.psum((local_bias, local_gain), ("dp", "fsdp"))
    grad_in = (
        inverse * norm_gain * (grad_out - sum_bias / row_count - normed * (sum_gain / row_count))
    )
    return (grad_in, local_gain, local_bias)


def pad_map(values):
    return jnp.pad(values, ((0, 0), (1, 1), (1, 1), (0, 0)))


def depthwise(values, kernel):
    padded = pad_map(values)
    edge_len = values.shape[1]
    output = jnp.zeros_like(values)
    for row_shift in range(3):
        for col_shift in range(3):
            output = (
                output
                + padded[:, row_shift : row_shift + edge_len, col_shift : col_shift + edge_len, :]
                * kernel[3 * row_shift + col_shift]
            )
    return output


def depthwise_back(grad_out, values, kernel):
    padded = pad_map(values)
    padded_grad = pad_map(grad_out)
    edge_len = values.shape[1]
    grad_in = jnp.zeros_like(values)
    kernel_grads = []
    for row_shift in range(3):
        for col_shift in range(3):
            grad_in = (
                grad_in
                + padded_grad[
                    :,
                    2 - row_shift : 2 - row_shift + edge_len,
                    2 - col_shift : 2 - col_shift + edge_len,
                    :,
                ]
                * kernel[3 * row_shift + col_shift]
            )
            kernel_grads.append(
                jnp.sum(
                    padded[:, row_shift : row_shift + edge_len, col_shift : col_shift + edge_len, :]
                    * grad_out,
                    axis=(0, 1, 2),
                )
            )
    return (grad_in, jnp.stack(kernel_grads))


def layer_forward(stream, matrices, side_params, vectors, row_count):
    model_width = stream.shape[1]
    squeeze = vectors.shape[0] - 2 * model_width
    bias_row = 9 + 2 * squeeze
    side_full = side_params.astype(jnp.float32)
    vector_full = vectors.astype(jnp.float32)
    local_images = stream.shape[0] // MAP
    hidden_one = jnp.dot(
        stream.astype(jnp.bfloat16), matrices[:model_width], preferred_element_type=jnp.float32
    )
    normed_one, inverse_one = batch_normalize(hidden_one, row_count)
    active_one = jax.nn.silu(normed_one * side_full[bias_row + 1] + side_full[bias_row + 2])
    spatial = depthwise(active_one.reshape(local_images, EDGE, EDGE, -1), side_full[:9]).reshape(
        hidden_one.shape
    )
    normed_two, inverse_two = batch_normalize(spatial, row_count)
    active_two = jax.nn.silu(
        normed_two * side_full[bias_row + 3] + side_full[bias_row + 4]
    ).reshape(local_images, MAP, -1)
    pooled = jnp.mean(active_two, axis=1)
    squeeze_pre = (
        jnp.dot(pooled, side_full[9 : 9 + squeeze].T, precision=HIGHEST) + vector_full[:squeeze]
    )
    squeezed = jax.nn.silu(squeeze_pre)
    excite = jax.nn.sigmoid(
        jnp.dot(squeezed, side_full[9 + squeeze : bias_row], precision=HIGHEST)
        + side_full[bias_row]
    )
    scaled = (active_two * excite[:, None, :]).reshape(hidden_one.shape).astype(jnp.bfloat16)
    projected = lax.dot_general(
        scaled, matrices[model_width:], COLS_DIMS, preferred_element_type=jnp.float32
    )
    normed_three, inverse_three = batch_normalize(projected, row_count)
    output = stream + (
        normed_three * vector_full[squeeze : squeeze + model_width]
        + vector_full[squeeze + model_width :]
    )
    saved_layer = (
        stream,
        normed_one,
        inverse_one,
        normed_two,
        inverse_two,
        pooled,
        squeeze_pre,
        squeezed,
        excite,
        scaled,
        normed_three,
        inverse_three,
    )
    return (output, saved_layer)


def layer_backward(grad_stream, saved_layer, matrices, side_params, vectors, row_count, is_first):
    (
        stream,
        normed_one,
        inverse_one,
        normed_two,
        inverse_two,
        pooled,
        squeeze_pre,
        squeezed,
        excite,
        scaled,
        normed_three,
        inverse_three,
    ) = saved_layer
    model_width = stream.shape[1]
    squeeze = vectors.shape[0] - 2 * model_width
    bias_row = 9 + 2 * squeeze
    side_full = side_params.astype(jnp.float32)
    vector_full = vectors.astype(jnp.float32)
    local_images = stream.shape[0] // MAP
    grad_proj, gain_three, bias_three = normalize_back(
        grad_stream,
        normed_three,
        inverse_three,
        vector_full[squeeze : squeeze + model_width],
        row_count,
    )
    grad_proj = grad_proj.astype(jnp.bfloat16)
    grad_out_weight = lax.dot_general(
        grad_proj, scaled, ROWS_DIMS, preferred_element_type=jnp.float32
    )
    grad_scaled = jnp.dot(
        grad_proj, matrices[model_width:], preferred_element_type=jnp.float32
    ).reshape(local_images, MAP, -1)
    pre_two = normed_two * side_full[bias_row + 3] + side_full[bias_row + 4]
    active_two = jax.nn.silu(pre_two).reshape(local_images, MAP, -1)
    grad_active = grad_scaled * excite[:, None, :]
    grad_excite = jnp.sum(grad_scaled * active_two, axis=1)
    grad_gate = grad_excite * excite * (1.0 - excite)
    grad_excite_weight = jnp.dot(squeezed.T, grad_gate, precision=HIGHEST)
    grad_squeezed = jnp.dot(grad_gate, side_full[9 + squeeze : bias_row].T, precision=HIGHEST)
    grad_pre = grad_squeezed * silu_slope(squeeze_pre)
    grad_reduce_weight = jnp.dot(grad_pre.T, pooled, precision=HIGHEST)
    grad_pooled = jnp.dot(grad_pre, side_full[9 : 9 + squeeze], precision=HIGHEST)
    grad_active = grad_active + grad_pooled[:, None, :] / MAP
    grad_two = grad_active.reshape(normed_two.shape) * silu_slope(pre_two)
    grad_spatial, gain_two, bias_two = normalize_back(
        grad_two, normed_two, inverse_two, side_full[bias_row + 3], row_count
    )
    pre_one = normed_one * side_full[bias_row + 1] + side_full[bias_row + 2]
    active_one = jax.nn.silu(pre_one).reshape(local_images, EDGE, EDGE, -1)
    grad_active_one, kernel_grad = depthwise_back(
        grad_spatial.reshape(active_one.shape), active_one, side_full[:9]
    )
    grad_one = grad_active_one.reshape(normed_one.shape) * silu_slope(pre_one)
    grad_hidden, gain_one, bias_one = normalize_back(
        grad_one, normed_one, inverse_one, side_full[bias_row + 1], row_count
    )
    grad_hidden = grad_hidden.astype(jnp.bfloat16)
    grad_in_weight = lax.dot_general(
        stream.astype(jnp.bfloat16), grad_hidden, ROWS_DIMS, preferred_element_type=jnp.float32
    )
    grad_matrices = jnp.concatenate([grad_in_weight, grad_out_weight], axis=0)
    grad_side = jnp.concatenate(
        [
            kernel_grad,
            grad_reduce_weight,
            grad_excite_weight,
            jnp.sum(grad_gate, axis=0)[None],
            gain_one[None],
            bias_one[None],
            gain_two[None],
            bias_two[None],
        ],
        axis=0,
    )
    grad_vectors = jnp.concatenate([jnp.sum(grad_pre, axis=0), gain_three, bias_three])
    grad_below = None
    if not is_first:
        grad_below = grad_stream + lax.dot_general(
            grad_hidden, matrices[:model_width], COLS_DIMS, preferred_element_type=jnp.float32
        )
    return (grad_below, grad_matrices, grad_side, grad_vectors)


def lamb_moments(weight, moment_one, moment_two, gradient, decay_mask, step_float):
    first_new = BETA_ONE * moment_one + (1.0 - BETA_ONE) * gradient
    second_new = BETA_TWO * moment_two + (1.0 - BETA_TWO) * gradient * gradient
    corrected = (
        first_new
        / (1.0 - BETA_ONE**step_float)
        / (jnp.sqrt(second_new / (1.0 - BETA_TWO**step_float)) + EPS_ADAM)
    )
    return (first_new, second_new, corrected + DECAY_RATE * decay_mask * weight)


def group_sums(mats_rows, side_rows, head_cols):
    per_layer = jnp.stack(
        [
            jnp.sum(mats_rows[:, :WIDTH], axis=1),
            jnp.sum(mats_rows[:, WIDTH:], axis=1),
            jnp.sum(side_rows[:, :9], axis=1),
            jnp.sum(side_rows[:, 9 : 9 + SQUEEZE], axis=1),
            jnp.sum(side_rows[:, 9 + SQUEEZE : 9 + 2 * SQUEEZE], axis=1),
        ],
        axis=1,
    )
    tail = jnp.stack([jnp.sum(head_cols[:WIDTH]), jnp.sum(head_cols[WIDTH : WIDTH + CLASSES])])
    return jnp.concatenate([per_layer.reshape(-1), tail])


def rate_maps(trust_ratio):
    groups = trust_ratio[: 5 * LAYERS].reshape(LAYERS, 5)
    row_ids = jnp.arange(2 * WIDTH)[None, :]
    mats_rate = RATE_MATRIX * jnp.where(row_ids < WIDTH, groups[:, 0:1], groups[:, 1:2])
    side_ids = jnp.arange(SIDE)[None, :]
    side_rate = jnp.where(
        side_ids < 9,
        RATE_MATRIX * groups[:, 2:3],
        jnp.where(
            side_ids < 9 + SQUEEZE,
            RATE_MATRIX * groups[:, 3:4],
            jnp.where(side_ids < 9 + 2 * SQUEEZE, RATE_MATRIX * groups[:, 4:5], RATE_VECTOR),
        ),
    )
    col_ids = jnp.arange(HEADCOLS)
    head_rate = jnp.where(
        col_ids < WIDTH,
        RATE_MATRIX * trust_ratio[5 * LAYERS],
        jnp.where(
            col_ids < WIDTH + CLASSES, RATE_MATRIX * trust_ratio[5 * LAYERS + 1], RATE_VECTOR
        ),
    )
    return (mats_rate, side_rate, head_rate)


def body(
    images,
    partner,
    mix_pair,
    labels,
    step,
    layer_mats,
    layer_side,
    layer_vecs,
    head_mat,
    fc_bias,
    mats_first,
    mats_second,
    side_first,
    side_second,
    vecs_first,
    vecs_second,
    head_first,
    head_second,
    bias_first,
    bias_second,
):
    local_images = images.shape[0]
    replicas = lax.axis_size("dp") * lax.axis_size("fsdp")
    image_count = float(local_images * replicas)
    row_count = float(local_images * MAP * replicas)
    pair_float = mix_pair.astype(jnp.float32)
    mixing = pair_float[:, 0] / (pair_float[:, 0] + pair_float[:, 1])
    pixels = images.astype(jnp.float32)
    mixed = mixing[:, None, None] * pixels + (1.0 - mixing)[:, None, None] * pixels[partner]
    partner_label = labels[partner]
    stream = mixed.reshape(local_images * MAP, WIDTH)
    saved_all = []
    weights_all = []
    for layer_index in range(LAYERS):
        gathered = (
            lax.all_gather(
                layer_mats[layer_index].astype(jnp.bfloat16), "fsdp", axis=0, tiled=True
            ),
            lax.all_gather(
                layer_side[layer_index].astype(jnp.bfloat16), "fsdp", axis=1, tiled=True
            ),
            lax.all_gather(
                layer_vecs[layer_index].astype(jnp.bfloat16), "fsdp", axis=0, tiled=True
            ),
        )
        stream, saved_layer = layer_forward(
            stream, gathered[0], gathered[1], gathered[2], row_count
        )
        saved_all.append(saved_layer)
        weights_all.append(gathered)
    head_full = lax.all_gather(head_mat.astype(jnp.bfloat16), "fsdp", axis=0, tiled=True)
    classes = fc_bias.shape[0]
    head_gain = head_full[:, WIDTH + classes].astype(jnp.float32)
    head_shift = head_full[:, WIDTH + classes + 1].astype(jnp.float32)
    stream_low = stream.astype(jnp.bfloat16)
    head_hidden = lax.dot_general(
        stream_low, head_full[:, :WIDTH], COLS_DIMS, preferred_element_type=jnp.float32
    )
    head_normed, head_inverse = batch_normalize(head_hidden, row_count)
    head_pre = head_normed * head_gain + head_shift
    features = jnp.mean(jax.nn.silu(head_pre).reshape(local_images, MAP, -1), axis=1)
    classifier = head_full[:, WIDTH : WIDTH + classes]
    features_low = features.astype(jnp.bfloat16)
    logits = jnp.dot(features_low, classifier, preferred_element_type=jnp.float32) + fc_bias
    row_max = jnp.max(logits, axis=1, keepdims=True)
    log_total = row_max[:, 0] + jnp.log(jnp.sum(jnp.exp(logits - row_max), axis=1))
    class_ids = jnp.arange(classes, dtype=jnp.int32)[None, :]
    own_hot = (labels[:, None] == class_ids).astype(jnp.float32)
    other_hot = (partner_label[:, None] == class_ids).astype(jnp.float32)
    own_logit = jnp.sum(own_hot * logits, axis=1)
    other_logit = jnp.sum(other_hot * logits, axis=1)
    loss_local = jnp.sum(
        mixing * (log_total - own_logit) + (1.0 - mixing) * (log_total - other_logit)
    )
    softmax_rows = jnp.exp(logits - log_total[:, None])
    grad_logits = (
        softmax_rows - mixing[:, None] * own_hot - (1.0 - mixing)[:, None] * other_hot
    ) / image_count
    loss_sum, grad_bias = lax.psum((loss_local, jnp.sum(grad_logits, axis=0)), ("dp", "fsdp"))
    loss_value = loss_sum / image_count
    grad_low = grad_logits.astype(jnp.bfloat16)
    grad_classifier = lax.dot_general(
        features_low, grad_low, ROWS_DIMS, preferred_element_type=jnp.float32
    )
    grad_features = lax.dot_general(
        grad_low, classifier, COLS_DIMS, preferred_element_type=jnp.float32
    )
    grad_spread = jnp.broadcast_to(
        grad_features[:, None, :] / MAP, (local_images, MAP, grad_features.shape[1])
    ).reshape(head_pre.shape)
    grad_head_pre = grad_spread * silu_slope(head_pre)
    grad_head_hidden, head_gain_grad, head_shift_grad = normalize_back(
        grad_head_pre, head_normed, head_inverse, head_gain, row_count
    )
    grad_head_hidden = grad_head_hidden.astype(jnp.bfloat16)
    grad_head_weight = lax.dot_general(
        grad_head_hidden, stream_low, ROWS_DIMS, preferred_element_type=jnp.float32
    )
    grad_stream = jnp.dot(
        grad_head_hidden, head_full[:, :WIDTH], preferred_element_type=jnp.float32
    )
    head_local = jnp.concatenate(
        [grad_head_weight, grad_classifier, head_gain_grad[:, None], head_shift_grad[:, None]],
        axis=1,
    )
    mats_list = [None] * LAYERS
    side_list = [None] * LAYERS
    vecs_list = [None] * LAYERS
    for layer_index in reversed(range(LAYERS)):
        gathered = weights_all[layer_index]
        grad_stream, grad_matrices, grad_side, grad_vectors = layer_backward(
            grad_stream,
            saved_all[layer_index],
            gathered[0],
            gathered[1],
            gathered[2],
            row_count,
            layer_index == 0,
        )
        grad_matrices, grad_side, grad_vectors = (
            sum_at_owner(grad_matrices.astype(jnp.bfloat16), "fsdp", 0),
            sum_at_owner(grad_side.astype(jnp.bfloat16), "fsdp", 1),
            sum_at_owner(grad_vectors.astype(jnp.bfloat16), "fsdp", 0),
        )
        mats_list[layer_index] = grad_matrices
        side_list[layer_index] = grad_side
        vecs_list[layer_index] = grad_vectors
    shard_mats = jnp.stack(mats_list)
    shard_side = jnp.stack(side_list)
    shard_vecs = jnp.stack(vecs_list)
    shard_head = lax.psum_scatter(head_local, "fsdp", scatter_dimension=0, tiled=True)
    shard_mats, shard_side, shard_vecs, shard_head = (
        lax.psum(shard_mats.astype(jnp.bfloat16), "dp").astype(jnp.float32),
        lax.psum(shard_side.astype(jnp.bfloat16), "dp").astype(jnp.float32),
        lax.psum(shard_vecs.astype(jnp.bfloat16), "dp").astype(jnp.float32),
        lax.psum(shard_head.astype(jnp.bfloat16), "dp").astype(jnp.float32),
    )
    step_float = step[0].astype(jnp.float32)
    side_decay = (jnp.arange(SIDE) < 9 + 2 * SQUEEZE).astype(jnp.float32)[None, :, None]
    head_decay = (jnp.arange(HEADCOLS) < WIDTH + CLASSES).astype(jnp.float32)[None, :]
    mats_moment, mats_square, mats_dir = lamb_moments(
        layer_mats, mats_first, mats_second, shard_mats, 1.0, step_float
    )
    side_moment, side_square, side_dir = lamb_moments(
        layer_side, side_first, side_second, shard_side, side_decay, step_float
    )
    vecs_moment, vecs_square, vecs_dir = lamb_moments(
        layer_vecs, vecs_first, vecs_second, shard_vecs, 0.0, step_float
    )
    head_moment, head_square, head_dir = lamb_moments(
        head_mat, head_first, head_second, shard_head, head_decay, step_float
    )
    bias_moment, bias_square, bias_dir = lamb_moments(
        fc_bias, bias_first, bias_second, grad_bias, 0.0, step_float
    )
    rows_dev = layer_mats.shape[1]
    row_start = lax.axis_index("fsdp") * rows_dev

    def place_rows(row_sums):
        return lax.dynamic_update_slice_in_dim(
            jnp.zeros((LAYERS, 2 * WIDTH), jnp.float32), row_sums, row_start, axis=1
        )

    weight_squares = group_sums(
        place_rows(jnp.sum(layer_mats * layer_mats, axis=2)),
        jnp.sum(layer_side * layer_side, axis=2),
        jnp.sum(head_mat * head_mat, axis=0),
    )
    update_squares = group_sums(
        place_rows(jnp.sum(mats_dir * mats_dir, axis=2)),
        jnp.sum(side_dir * side_dir, axis=2),
        jnp.sum(head_dir * head_dir, axis=0),
    )
    weight_squares, update_squares = lax.psum((weight_squares, update_squares), "fsdp")
    weight_norm = jnp.sqrt(weight_squares)
    update_norm = jnp.sqrt(update_squares)
    mats_rate, side_rate, head_rate = rate_maps(weight_norm / update_norm)
    mats_rate = lax.dynamic_slice_in_dim(mats_rate, row_start, rows_dev, axis=1)
    mats_new = layer_mats - mats_rate[:, :, None] * mats_dir
    side_new = layer_side - side_rate[:, :, None] * side_dir
    vecs_new = layer_vecs - RATE_VECTOR * vecs_dir
    head_new = head_mat - head_rate[None, :] * head_dir
    bias_new = fc_bias - RATE_VECTOR * bias_dir
    norms = jnp.stack([weight_norm, update_norm])
    return (
        loss_value,
        mats_new,
        mats_moment,
        mats_square,
        side_new,
        side_moment,
        side_square,
        vecs_new,
        vecs_moment,
        vecs_square,
        head_new,
        head_moment,
        head_square,
        bias_new,
        bias_moment,
        bias_square,
        norms,
    )


def solution(mesh):
    return jax.shard_map(
        body,
        mesh=mesh,
        in_specs=(
            P(("dp", "fsdp"), None, None),
            P(("dp", "fsdp")),
            P(("dp", "fsdp"), None),
            P(("dp", "fsdp")),
            P(),
            P(None, "fsdp", None),
            P(None, None, "fsdp"),
            P(None, "fsdp"),
            P("fsdp", None),
            P(),
            P(None, "fsdp", None),
            P(None, "fsdp", None),
            P(None, None, "fsdp"),
            P(None, None, "fsdp"),
            P(None, "fsdp"),
            P(None, "fsdp"),
            P("fsdp", None),
            P("fsdp", None),
            P(),
            P(),
        ),
        out_specs=(
            P(),
            P(None, "fsdp", None),
            P(None, "fsdp", None),
            P(None, "fsdp", None),
            P(None, None, "fsdp"),
            P(None, None, "fsdp"),
            P(None, None, "fsdp"),
            P(None, "fsdp"),
            P(None, "fsdp"),
            P(None, "fsdp"),
            P("fsdp", None),
            P("fsdp", None),
            P("fsdp", None),
            P(),
            P(),
            P(),
            P(),
        ),
        check_vma=False,
    )
```

profile of v0, /device:TPU:0, one launch (start us, length us, event | category | flops | bytes accessed | tf_op | source)
XLA Modules:
  0.0 1956.9 jit_solution(3172190164409934256)
XLA Ops:
  134.3 82.7 %slice_reduce_fusion.30 = (f32[1536]{0:T(1024)S(1)}, f32[1536]{0:T(1024)S(1)}, f32[1536]{0:T(1024)S(1)}, f32[1536]{0:T(1024)S(1)}, f32[1536]{0:T(1024)S(1)}, /*i...) fusion(f32[1,142,1536]{1,0,2:T(1,128)S(1)} %copy-done.1), kind=kLoop, calls=%fused_computation.305 | loop fusion | bytes 172032 | tf_op jit(solution)/shard_map/slice | solution.py:126
  222.6 82.7 %slice_reduce_fusion.16 = (f32[1536]{0:T(1024)}, f32[1536]{0:T(1024)}, f32[1536]{0:T(1024)}, f32[1536]{0:T(1024)}, f32[1536]{0:T(1024)}, /*index=5*/f32[1536]{0:...) fusion(f32[1,142,1536]{1,0,2:T(1,128)S(1)} %convert_element_typ, ...), kind=kLoop, calls=%fused_computation.289 | loop fusion | bytes 172032 | tf_op jit(solution)/shard_map/slice | solution.py:126
  310.9 82.9 %slice_reduce_fusion.2 = (f32[1536]{0:T(1024)}, f32[1536]{0:T(1024)}, f32[1536]{0:T(1024)}, f32[1536]{0:T(1024)}, f32[1536]{0:T(1024)}, /*index=5*/f32[1536]{0:T...) fusion(f32[1,142,1536]{1,0,2:T(1,128)S(1)} %convert_element_typ, ...), kind=kLoop, calls=%fused_computation.273 | loop fusion | bytes 172032 | tf_op jit(solution)/shard_map/slice | solution.py:126
  400.5 39.8 %all-reduce.28 = (f32[1536]{0:T(1024)S(1)}, f32[1536]{0:T(1024)S(1)}) all-reduce(f32[1536]{0:T(1024)S(1)} %get-tuple-element.149, f32[1536]{0:T(1024)S(1)} %get-tuple-element.148), channel_id=1, replica_groups=mesh['dp'=4,'fsdp'=8] {'dp','fsdp'}, use_global_device_ids=true, to_apply=%region_3.0 | all-reduce | flops 3072 | bytes 24576 | tf_op jit(solution)/shard_map/psum | solution.py:45
  474.4 40.7 %all-reduce.27 = (f32[1536]{0:T(1024)S(1)}, f32[1536]{0:T(1024)S(1)}) all-reduce(f32[1536]{0:T(1024)S(1)} %get-tuple-element.147, f32[1536]{0:T(1024)S(1)} %get-tuple-element.146), channel_id=1, replica_groups=mesh['dp'=4,'fsdp'=8] {'dp','fsdp'}, use_global_device_ids=true, to_apply=%region_7.8 | all-reduce | flops 3072 | bytes 24576 | tf_op jit(solution)/shard_map/psum | solution.py:45
  526.4 39.8 %all-reduce.26 = (f32[256]{0:T(256)S(1)}, f32[256]{0:T(256)S(1)}) all-reduce(f32[256]{0:T(256)S(1)} %get-tuple-element.209, f32[256]{0:T(256)S(1)} %get-tuple-element.208), channel_id=1, replica_groups=mesh['dp'=4,'fsdp'=8] {'dp','fsdp'}, use_global_device_ids=true, to_apply=%region_12.13 | all-reduce | flops 512 | bytes 4096 | tf_op jit(solution)/shard_map/psum | solution.py:45
  570.9 40.7 %all-reduce.25 = (f32[1536]{0:T(1024)S(1)}, f32[1536]{0:T(1024)S(1)}) all-reduce(f32[1536]{0:T(1024)S(1)} %get-tuple-element.145, f32[1536]{0:T(1024)S(1)} %get-tuple-element.144), channel_id=1, replica_groups=mesh['dp'=4,'fsdp'=8] {'dp','fsdp'}, use_global_device_ids=true, to_apply=%region_16.17 | all-reduce | flops 3072 | bytes 24576 | tf_op jit(solution)/shard_map/psum | solution.py:45
  646.6 39.8 %all-reduce.24 = (f32[1536]{0:T(1024)S(1)}, f32[1536]{0:T(1024)S(1)}) all-reduce(f32[1536]{0:T(1024)S(1)} %get-tuple-element.143, f32[1536]{0:T(1024)S(1)} %get-tuple-element.142), channel_id=1, replica_groups=mesh['dp'=4,'fsdp'=8] {'dp','fsdp'}, use_global_device_ids=true, to_apply=%region_20.21 | all-reduce | flops 3072 | bytes 24576 | tf_op jit(solution)/shard_map/psum | solution.py:45
  696.8 40.8 %all-reduce.23 = (f32[256]{0:T(256)S(1)}, f32[256]{0:T(256)S(1)}) all-reduce(f32[256]{0:T(256)S(1)} %get-tuple-element.207, f32[256]{0:T(256)S(1)} %get-tuple-element.206), channel_id=1, replica_groups=mesh['dp'=4,'fsdp'=8] {'dp','fsdp'}, use_global_device_ids=true, to_apply=%region_25.26 | all-reduce | flops 512 | bytes 4096 | tf_op jit(solution)/shard_map/psum | solution.py:45
  752.8 39.9 %all-reduce.22 = (f32[1536]{0:T(1024)S(1)}, f32[1536]{0:T(1024)S(1)}) all-reduce(f32[1536]{0:T(1024)S(1)} %get-tuple-element.141, f32[1536]{0:T(1024)S(1)} %get-tuple-element.140), channel_id=1, replica_groups=mesh['dp'=4,'fsdp'=8] {'dp','fsdp'}, use_global_device_ids=true, to_apply=%region_29.30 | all-reduce | flops 3072 | bytes 24576 | tf_op jit(solution)/shard_map/psum | solution.py:45
  832.8 41.2 %all-reduce.21 = (f32[1536]{0:T(1024)S(1)}, f32[1536]{0:T(1024)S(1)}) all-reduce(f32[1536]{0:T(1024)S(1)} %get-tuple-element.139, f32[1536]{0:T(1024)S(1)} %get-tuple-element.138), channel_id=1, replica_groups=mesh['dp'=4,'fsdp'=8] {'dp','fsdp'}, use_global_device_ids=true, to_apply=%region_33.34 | all-reduce | flops 3072 | bytes 24576 | tf_op jit(solution)/shard_map/psum | solution.py:45
  884.3 39.4 %all-reduce.20 = (f32[256]{0:T(256)S(1)}, f32[256]{0:T(256)S(1)}) all-reduce(f32[256]{0:T(256)S(1)} %get-tuple-element.205, f32[256]{0:T(256)S(1)} %get-tuple-element.204), channel_id=1, replica_groups=mesh['dp'=4,'fsdp'=8] {'dp','fsdp'}, use_global_device_ids=true, to_apply=%region_38.39 | all-reduce | flops 512 | bytes 4096 | tf_op jit(solution)/shard_map/psum | solution.py:45
  927.6 41.0 %all-reduce.19 = (f32[1280]{0:T(1024)}, f32[1280]{0:T(1024)}) all-reduce(f32[1280]{0:T(1024)} %get-tuple-element.153, f32[1280]{0:T(1024)} %get-tuple-element.152), channel_id=1, replica_groups=mesh['dp'=4,'fsdp'=8] {'dp','fsdp'}, use_global_device_ids=true, to_apply=%region_42.43 | all-reduce | flops 2560 | bytes 20480 | tf_op jit(solution)/shard_map/psum | solution.py:45
  987.5 40.5 %all-reduce.18 = (f32[1280]{0:T(1024)}, f32[1280]{0:T(1024)}) all-reduce(f32[1280]{0:T(1024)} %copy-done.148, f32[1280]{0:T(1024)} %copy-done.147), channel_id=1, replica_groups=mesh['dp'=4,'fsdp'=8] {'dp','fsdp'}, use_global_device_ids=true, to_apply=%region_64.65 | all-reduce | flops 2560 | bytes 20480 | tf_op jit(solution)/shard_map/psum | solution.py:56
  1034.6 41.2 %all-reduce.17 = (f32[256]{0:T(256)S(1)}, f32[256]{0:T(256)S(1)}) all-reduce(f32[256]{0:T(256)S(1)} %get-tuple-element.203, f32[256]{0:T(256)S(1)} %get-tuple-element.202), channel_id=1, replica_groups=mesh['dp'=4,'fsdp'=8] {'dp','fsdp'}, use_global_device_ids=true, to_apply=%region_68.69 | all-reduce | flops 512 | bytes 4096 | tf_op jit(solution)/shard_map/psum | solution.py:56
  1088.5 39.8 %all-reduce.16 = (f32[1536]{0:T(1024)S(1)}, f32[1536]{0:T(1024)S(1)}) all-reduce(f32[1536]{0:T(1024)S(1)} %get-tuple-element.137, f32[1536]{0:T(1024)S(1)} %get-tuple-element.136), channel_id=1, replica_groups=mesh['dp'=4,'fsdp'=8] {'dp','fsdp'}, use_global_device_ids=true, to_apply=%region_73.74 | all-reduce | flops 3072 | bytes 24576 | tf_op jit(solution)/shard_map/psum | solution.py:56
  1184.2 40.8 %all-reduce.15 = (f32[1536]{0:T(1024)S(1)}, f32[1536]{0:T(1024)S(1)}) all-reduce(f32[1536]{0:T(1024)S(1)} %get-tuple-element.135, f32[1536]{0:T(1024)S(1)} %get-tuple-element.134), channel_id=1, replica_groups=mesh['dp'=4,'fsdp'=8] {'dp','fsdp'}, use_global_device_ids=true, to_apply=%region_77.78 | all-reduce | flops 3072 | bytes 24576 | tf_op jit(solution)/shard_map/psum | solution.py:56
  1232.5 39.9 %all-reduce.14 = (f32[256]{0:T(256)S(1)}, f32[256]{0:T(256)S(1)}) all-reduce(f32[256]{0:T(256)S(1)} %get-tuple-element.201, f32[256]{0:T(256)S(1)} %get-tuple-element.200), channel_id=1, replica_groups=mesh['dp'=4,'fsdp'=8] {'dp','fsdp'}, use_global_device_ids=true, to_apply=%region_81.82 | all-reduce | flops 512 | bytes 4096 | tf_op jit(solution)/shard_map/psum | solution.py:56
  1285.6 41.0 %all-reduce.13 = (f32[1536]{0:T(1024)S(1)}, f32[1536]{0:T(1024)S(1)}) all-reduce(f32[1536]{0:T(1024)S(1)} %get-tuple-element.133, f32[1536]{0:T(1024)S(1)} %get-tuple-element.132), channel_id=1, replica_groups=mesh['dp'=4,'fsdp'=8] {'dp','fsdp'}, use_global_device_ids=true, to_apply=%region_86.87 | all-reduce | flops 3072 | bytes 24576 | tf_op jit(solution)/shard_map/psum | solution.py:56
  1382.5 39.6 %all-reduce.12 = (f32[1536]{0:T(1024)S(1)}, f32[1536]{0:T(1024)S(1)}) all-reduce(f32[1536]{0:T(1024)S(1)} %get-tuple-element.131, f32[1536]{0:T(1024)S(1)} %get-tuple-element.130), channel_id=1, replica_groups=mesh['dp'=4,'fsdp'=8] {'dp','fsdp'}, use_global_device_ids=true, to_apply=%region_90.91 | all-reduce | flops 3072 | bytes 24576 | tf_op jit(solution)/shard_map/psum | solution.py:56
  1429.6 41.0 %all-reduce.11 = (f32[256]{0:T(256)S(1)}, f32[256]{0:T(256)S(1)}) all-reduce(f32[256]{0:T(256)S(1)} %get-tuple-element.199, f32[256]{0:T(256)S(1)} %get-tuple-element.198), channel_id=1, replica_groups=mesh['dp'=4,'fsdp'=8] {'dp','fsdp'}, use_global_device_ids=true, to_apply=%region_94.95 | all-reduce | flops 512 | bytes 4096 | tf_op jit(solution)/shard_map/psum | solution.py:56
  1482.0 39.5 %all-reduce.10 = (f32[1536]{0:T(1024)}, f32[1536]{0:T(1024)}) all-reduce(f32[1536]{0:T(1024)S(1)} %get-tuple-element.129, f32[1536]{0:T(1024)S(1)} %get-tuple-element.128), channel_id=1, replica_groups=mesh['dp'=4,'fsdp'=8] {'dp','fsdp'}, use_global_device_ids=true, to_apply=%region_99.100 | all-reduce | flops 3072 | bytes 24576 | tf_op jit(solution)/shard_map/psum | solution.py:56
  1703.0 34.2 %all-to-all-done.2 = bf16[8,64,1536]{2,1,0:T(8,128)(2,1)} async-done(((bf16[8,64,1536]{2,1,0:T(8,128)(2,1)}), bf16[8,64,1536]{2,1,0:T(8,128)(2,1)}, u32[]{:S(2)}, u32[]{:S(2)}) %all-to-all-start.2) | async-done | bytes 1572896 | tf_op jit(solution)/shard_map/all_to_all | solution.py:35
  1743.3 55.8 %all-reduce.9 = (f32[]{:T(128)}, f32[1536]{0:T(1024)}, f32[1536]{0:T(1024)}, f32[1000]{0:T(1024)}) all-reduce(f32[]{:T(128)} %add_reduce_fusion, f32[1536]{0:T(1024)} %get-tuple-element.127, f32[1536]{0:T(1024)} %copy-done.203, f32[1000]{0:T(1024)S(1)} %get-tuple-element.210), channel_id=1, replica_groups=mesh['dp'=4,'fsdp'=8] {'dp','fsdp'}, use_global_device_ids=true, to_apply=%region_49.50 | all-reduce | flops 4073 | bytes 32584 | tf_op jit(solution)/shard_map/psum | solution.py:379
  (949 shorter events, 829.8 us)
Async XLA Ops:
  7.2 389.6 %all-gather.16.cloned.1.call-start = ((), (), s32[]{:S(2)}) async-start(), calls=%async_computation.11 | async-start | bytes 1769472 | tf_op jit(solution)/shard_map/all_gather | solution.py:336
  10.6 556.3 %all-gather.18.cloned.1.call-start = ((), (), s32[]{:S(2)}) async-start(), calls=%async_computation.12 | async-start | bytes 1769472 | tf_op jit(solution)/shard_map/all_gather | solution.py:336
  11.4 727.0 %all-gather.20.cloned.1.call-start = ((), (), s32[]{:S(2)}) async-start(), calls=%async_computation.13 | async-start | bytes 1769472 | tf_op jit(solution)/shard_map/all_gather | solution.py:336
  12.1 913.0 %all-gather.14.cloned.1.call-start = ((), (), s32[]{:S(2)}) async-start(), calls=%async_computation.10 | async-start | bytes 3686400 | tf_op jit(solution)/shard_map/all_gather | solution.py:351
  134.3 262.5 %copy-start.39 = (bf16[640,256]{1,0:T(8,128)(2,1)}, bf16[640,256]{1,0:T(8,128)(2,1)S(1)}, u32[]{:S(2)}) copy-start(bf16[640,256]{1,0:T(8,128)(2,1)S(1)} %bitcast_convert_fusion) | copy-start | bytes 983044
  217.0 223.9 %copy-start.109 = (f32[1536]{0:T(1024)}, f32[1536]{0:T(1024)S(1)}, u32[]{:S(2)}) copy-start(f32[1536]{0:T(1024)S(1)} %get-tuple-element.196) | copy-start | bytes 18436
  217.0 223.9 %copy-start.140 = (f32[1536]{0:T(1024)}, f32[1536]{0:T(1024)S(1)}, u32[]{:S(2)}) copy-start(f32[1536]{0:T(1024)S(1)} %get-tuple-element.195) | copy-start | bytes 18436
  217.0 234.3 %copy-start.149 = (f32[1536]{0:T(1024)}, f32[1536]{0:T(1024)S(1)}, u32[]{:S(2)}) copy-start(f32[1536]{0:T(1024)S(1)} %get-tuple-element.186) | copy-start | bytes 18436
  217.0 234.3 %copy-start.151 = (f32[1536]{0:T(1024)}, f32[1536]{0:T(1024)S(1)}, u32[]{:S(2)}) copy-start(f32[1536]{0:T(1024)S(1)} %get-tuple-element.187) | copy-start | bytes 18436
  217.0 234.3 %copy-start.153 = (f32[1536]{0:T(1024)}, f32[1536]{0:T(1024)S(1)}, u32[]{:S(2)}) copy-start(f32[1536]{0:T(1024)S(1)} %get-tuple-element.188) | copy-start | bytes 18436
  217.1 298.7 %copy-start.98 = (f32[1536]{0:T(1024)}, f32[1536]{0:T(1024)S(1)}, u32[]{:S(2)}) copy-start(f32[1536]{0:T(1024)S(1)} %get-tuple-element.185) | copy-start | bytes 18436
  217.1 305.1 %copy-start.90 = (f32[1536]{0:T(1024)}, f32[1536]{0:T(1024)S(1)}, u32[]{:S(2)}) copy-start(f32[1536]{0:T(1024)S(1)} %get-tuple-element.184) | copy-start | bytes 18436
  738.3 186.0 %copy-start.12 = (f32[640,256]{1,0:T(8,128)}, f32[640,256]{1,0:T(8,128)S(1)}, u32[]{:S(2)}) copy-start(f32[640,256]{1,0:T(8,128)S(1)} %add_add_fusion) | copy-start | bytes 1966084
  1539.5 104.8 %all-to-all-start.5 = ((bf16[8,142,192]{2,1,0:T(8,128)(2,1)}), bf16[8,142,192]{2,1,0:T(8,128)(2,1)S(1)}, u32[]{:S(2)}, u32[]{:S(2)}) async-start(bf16[8,142,192]{2,1,0:T(8,128)(2,1)} %bitcast.230), calls=%async_computation.5 | async-start | bytes 1179648 | tf_op jit(solution)/shard_map/all_to_all | solution.py:35
  1543.1 309.8 %reduce-scatter.4.cloned.1.call-start = ((), (), s32[]{:S(2)}) async-start(), calls=%async_computation.14 | async-start | bytes 7372800 | tf_op jit(solution)/shard_map/reduce_scatter | solution.py:431
  1645.2 28.8 %all-to-all-start.4 = ((bf16[8,142,192]{2,1,0:T(8,128)(2,1)}), bf16[8,142,192]{2,1,0:T(8,128)(2,1)}, u32[]{:S(2)}, u32[]{:S(2)}) async-start(bf16[8,142,192]{2,1,0:T(8,128)(2,1)} %bitcast.60), calls=%async_computation.4 | async-start | bytes 1179648 | tf_op jit(solution)/shard_map/all_to_all | solution.py:35
  1673.9 21.0 %all-to-all-start.3 = ((bf16[8,142,192]{2,1,0:T(8,128)(2,1)}), bf16[8,142,192]{2,1,0:T(8,128)(2,1)}, u32[]{:S(2)}, u32[]{:S(2)}) async-start(bf16[8,142,192]{2,1,0:T(8,128)(2,1)} %bitcast.231), calls=%async_computation.3 | async-start | bytes 1179648 | tf_op jit(solution)/shard_map/all_to_all | solution.py:35
  1694.9 42.3 %all-to-all-start.2 = ((bf16[8,64,1536]{2,1,0:T(8,128)(2,1)}), bf16[8,64,1536]{2,1,0:T(8,128)(2,1)}, u32[]{:S(2)}, u32[]{:S(2)}) async-start(bf16[8,64,1536]{2,1,0:T(8,128)(2,1)} %bitcast.229), calls=%async_computation.2 | async-start | bytes 3145728 | tf_op jit(solution)/shard_map/all_to_all | solution.py:35
  1737.2 71.0 %all-to-all-start.1 = ((bf16[8,64,1536]{2,1,0:T(8,128)(2,1)}), bf16[8,64,1536]{2,1,0:T(8,128)(2,1)S(1)}, u32[]{:S(2)}, u32[]{:S(2)}) async-start(bf16[8,64,1536]{2,1,0:T(8,128)(2,1)} %bitcast.228), calls=%async_computation.1 | async-start | bytes 3145728 | tf_op jit(solution)/shard_map/all_to_all | solution.py:35
  1808.2 42.1 %all-to-all-start = ((bf16[8,64,1536]{2,1,0:T(8,128)(2,1)}), bf16[8,64,1536]{2,1,0:T(8,128)(2,1)}, u32[]{:S(2)}, u32[]{:S(2)}) async-start(bf16[8,64,1536]{2,1,0:T(8,128)(2,1)} %bitcast.48), calls=%async_computation | async-start | bytes 3145728 | tf_op jit(solution)/shard_map/all_to_all | solution.py:35
  1812.5 97.2 %all-reduce.34.cloned.1.call-start = ((), (), s32[]{:S(2)}) async-start(), calls=%async_computation.15 | async-start | bytes 2441216 | tf_op jit(solution)/shard_map/psum | solution.py:433
  1856.8 8.7 all-to-all-start.8
  1865.6 8.7 all-to-all-start.7
  1874.3 8.7 all-to-all-start.6
  (284 other events, 6629.1 us)
Sparse Core Ops, SparseCore 0:
  10.8 28.1 all-gather.15
  40.6 28.0 all-gather.17
  71.0 29.3 all-gather.19
  102.4 42.6 all-gather.13
  1588.5 80.0 reduce-scatter.3
  1855.0 54.7 all-reduce.33
where the time goes:
time: 1970 us; the launch traced here: 1960 us
  blocking collectives  941 us (48%)
  local copies, waits for them, and re-layouts  455 us (23%)
  other arithmetic  334 us (17%)
  waiting for transfers between devices  114 us (6%)
  matrix products  55 us (3%)
  starting transfers between devices  35.4 us (2%)
  between operations  22.2 us (1%)
    psum x10, blocking collectives, batch_normalize(): lax.psum((jnp.sum(hidden, axis=0), jnp.sum(hidden * hidden, axis=0)), ('d...  403 us
    psum x9, blocking collectives, normalize_back(): sum_bias, sum_gain = lax.psum((local_bias, local_gain), ('dp', 'fsdp'))  363 us
    slice x3, local copies, waits for them, and re-layouts, layer_forward(): side_full[bias_row + 3]  248 us
    reduce_sum x6, other arithmetic, depthwise_back(): jnp.sum(padded[:, row_shift:row_shift + edge_len, col_shift:col_shift + e...  114 us
    all_to_all x9, waiting for transfers between devices, sum_at_owner(): tiles = lax.all_to_all(in_blocks(array, dim, peers), axis, 0, 0, tiled=True)  96.4 us
    all_gather x3, blocking collectives, body(): lax.all_gather(layer_side[layer_index].astype(jnp.bfloat16), 'fsdp', axis...  72.9 us
    psum x1, blocking collectives, body(): lax.psum((loss_local, jnp.sum(grad_logits, axis=0)), ('dp', 'fsdp'))  55.8 us
    reduce_sum x3, other arithmetic, batch_normalize(): jnp.sum(hidden, axis=0)  54.4 us
  transfers between devices with their start and end apart: 15, of which 8 were waited for; matrix products, arithmetic and copies ran while one was open for 31% of the time, Pallas kernels for 0%

commit v1 on v0

v1 whole, which is shorter than its diff:
```python
import functools

import jax
import jax.numpy as jnp
from jax import lax
from jax.experimental import pallas as pl
from jax.experimental.pallas import tpu as pltpu
from jax.sharding import PartitionSpec as P

WIDTH = 256
EXPAND = 1536
SQUEEZE = 64
HEAD = 1280
CLASSES = 1000
LOGITS = 1024
EDGE = 4
LAYERS = 3
MAP = 16
SIDE = 142
SIDE_PAD = 144
VECS = 576
HEADCOLS = 1258
HEADPAD = 1280

EPS_BN = 0.001
BETA_ONE = 0.9
BETA_TWO = 0.999
EPS_ADAM = 1e-06
DECAY_RATE = 0.01
RATE_MATRIX = 0.5
RATE_VECTOR = 0.25

BOTH = ("dp", "fsdp")
F32 = jnp.float32
BF16 = jnp.bfloat16
HIGHEST = lax.Precision.HIGHEST
LANE = 128
TILE = 8
ROWS = MAP * TILE
CHUNK = 256
VMEM_BYTES = 44 * 1024 * 1024

NT = (((1,), (1,)), ((), ()))
TN = (((0,), (0,)), ((), ()))


def call(kernel, outs, ins, scratch=()):
    return pl.pallas_call(
        kernel,
        out_shape=outs,
        in_specs=[pl.BlockSpec(memory_space=pltpu.VMEM)] * len(ins),
        out_specs=[pl.BlockSpec(memory_space=pltpu.VMEM)] * len(outs),
        scratch_shapes=list(scratch),
        compiler_params=pltpu.CompilerParams(vmem_limit_bytes=VMEM_BYTES),
    )(*ins)


def shape(dims, dtype=F32):
    return jax.ShapeDtypeStruct(dims, dtype)


def dot(left, right):
    return jnp.dot(left, right, preferred_element_type=F32)


def dot_nt(left, right):
    return lax.dot_general(left, right, NT, preferred_element_type=F32)


def dot_tn(left, right):
    return lax.dot_general(left, right, TN, preferred_element_type=F32)


def halves(value):
    high = value.astype(BF16)
    return high, (value - high.astype(F32)).astype(BF16)


def sigmoid(value):
    return 0.5 * jnp.tanh(0.5 * value) + 0.5


def chunk_at(index, size=CHUNK):
    return pl.ds(pl.multiple_of(index * size, size), size)


def spread(rows, first, count):
    return jnp.concatenate([rows[first + k : first + k + 1, :] for k in range(count)], axis=1)


def fold(vectors, rows):
    pieces = [
        vector[:, k * LANE : (k + 1) * LANE]
        for vector in vectors
        for k in range(vector.shape[1] // LANE)
    ]
    if rows > len(pieces):
        pieces.append(jnp.zeros((rows - len(pieces), LANE), F32))
    return jnp.concatenate(pieces, axis=0)


def padded(rows):
    return -(-rows // 8) * 8


def moment_rows(columns):
    return padded(3 * columns // LANE)


def pack_moments(total, squares, count):
    mean = total / count
    spread_sum = jnp.maximum(squares - total * mean, 0.0)
    high = mean.astype(BF16).astype(F32)
    return fold([high, mean - high, spread_sum], moment_rows(total.shape[1])).astype(BF16)


def read_moments(recv_ref, columns, count):
    groups = columns // LANE
    devices = recv_ref.shape[0]
    parts = recv_ref[...].astype(F32)
    means = parts[:, :groups] + parts[:, groups : 2 * groups]
    mean = jnp.sum(means, axis=0) / devices
    apart = means - mean[None]
    spread_sum = jnp.sum(parts[:, 2 * groups : 3 * groups], axis=0) / count
    variance = (spread_sum + jnp.sum(apart * apart, axis=0)) / devices
    return spread(mean, 0, groups), lax.rsqrt(spread(variance, 0, groups) + EPS_BN)


def read_sums(recv_ref):
    return jnp.sum(recv_ref[...].astype(F32), axis=0)


def share(payload):
    devices = lax.axis_size("dp") * lax.axis_size("fsdp")
    copies = jnp.broadcast_to(payload[None], (devices, *payload.shape))
    return lax.all_to_all(copies, BOTH, 0, 0)


def as_tile(block):
    return block.reshape(MAP, TILE, LANE)


def sum_columns(x_ref, w_ref, transposed, h_scr, stat_scr):
    columns = stat_scr.shape[1]

    def step(index, carry):
        at = chunk_at(index)
        if transposed:
            h_scr[...] = dot_nt(x_ref[...], w_ref[at, :WIDTH])
        else:
            h_scr[...] = dot(x_ref[...], w_ref[:WIDTH, at])
        hidden = h_scr[...]
        stat_scr[0:1, at] = jnp.sum(hidden, axis=0, keepdims=True)
        stat_scr[1:2, at] = jnp.sum(hidden * hidden, axis=0, keepdims=True)
        return carry

    lax.fori_loop(0, columns // CHUNK, step, 0)


def enter_kernel(images_ref, partner_ref, mix_ref, mats_ref, x_ref, pay_ref, xb_scr, h_scr, stat_scr):
    count = images_ref.shape[0]
    pixels = images_ref[...]
    row = lax.broadcasted_iota(jnp.int32, (ROWS, count), 0)
    column = lax.broadcasted_iota(jnp.int32, (ROWS, count), 1)
    place = lax.shift_right_logical(row, 3)
    inside = jnp.bitwise_and(row, 7)
    pair = mix_ref[...].astype(F32)
    mixing = pair[:, 0:1] / (pair[:, 0:1] + pair[:, 1:2])
    for tile in range(count // ROWS):
        near = slice(tile * TILE, (tile + 1) * TILE)
        other = jnp.concatenate([partner_ref[near, :]] * MAP, axis=0)
        weight = jnp.concatenate([mixing[near, :]] * MAP, axis=0)
        own_hot = jnp.where(column == (tile * TILE + inside) * MAP + place, 1.0, 0.0).astype(BF16)
        other_hot = jnp.where(column == other * MAP + place, 1.0, 0.0).astype(BF16)
        mixed = weight * dot(own_hot, pixels) + (1.0 - weight) * dot(other_hot, pixels)
        x_ref[tile * ROWS : (tile + 1) * ROWS, :] = mixed
    xb_scr[...] = x_ref[...].astype(BF16)
    sum_columns(xb_scr, mats_ref, False, h_scr, stat_scr)
    pay_ref[...] = pack_moments(stat_scr[0:1, :], stat_scr[1:2, :], count)


def enter(images, partner, mix_pair, mats):
    count = images.shape[0]
    return call(
        enter_kernel,
        [shape((count, WIDTH)), shape((moment_rows(EXPAND), LANE), BF16)],
        [images, partner, mix_pair, mats],
        [pltpu.VMEM((count, WIDTH), BF16), pltpu.VMEM((count, CHUNK), F32), pltpu.VMEM((8, EXPAND), F32)],
    )


def tap_terms():
    for row in range(EDGE):
        for col in range(EDGE):
            for row_shift in range(3):
                for col_shift in range(3):
                    from_row, from_col = row + row_shift - 1, col + col_shift - 1
                    if 0 <= from_row < EDGE and 0 <= from_col < EDGE:
                        yield EDGE * row + col, 3 * row_shift + col_shift, EDGE * from_row + from_col


TERMS = list(tap_terms())


def spatial_kernel(x_ref, mats_ref, side_ref, recv_ref, d_ref, pay_ref, norm_ref, xb_scr, h_scr, row_scr, stat_scr):
    count = x_ref.shape[0]
    xb_scr[...] = x_ref[...].astype(BF16)
    rows = side_ref[2 * SQUEEZE : SIDE_PAD, :].astype(F32)
    mean, inverse = read_moments(recv_ref, EXPAND, count)
    norm_ref[0:1, :] = mean
    norm_ref[1:2, :] = inverse
    scale = inverse * rows[10:11, :]
    row_scr[0:9, :] = rows[0:9, :]
    row_scr[9:10, :] = scale
    row_scr[10:11, :] = rows[11:12, :] - mean * scale

    def step(index, carry):
        h_scr[...] = dot(xb_scr[...], mats_ref[:WIDTH, chunk_at(index)])
        for part in range(CHUNK // LANE):
            lanes = chunk_at(index * (CHUNK // LANE) + part, LANE)
            taps = [jnp.broadcast_to(row_scr[k : k + 1, lanes], (TILE, LANE)) for k in range(9)]
            scale_row = row_scr[9:10, lanes]
            shift_row = row_scr[10:11, lanes]

            def tile_step(tile, sums):
                at = chunk_at(tile, ROWS)
                pre = h_scr[at, part * LANE : (part + 1) * LANE] * scale_row + shift_row
                active = as_tile(pre * sigmoid(pre))
                result = [None] * MAP
                for target, tap, source in TERMS:
                    term = active[source] * taps[tap]
                    result[target] = term if result[target] is None else result[target] + term
                total, squares = sums
                for value in result:
                    total = total + value
                    squares = squares + value * value
                d_ref[at, lanes] = jnp.concatenate(result, axis=0).astype(BF16)
                return total, squares

            zero = jnp.zeros((TILE, LANE), F32)
            total, squares = lax.fori_loop(0, count // ROWS, tile_step, (zero, zero))
            stat_scr[0:1, lanes] = jnp.sum(total, axis=0, keepdims=True)
            stat_scr[1:2, lanes] = jnp.sum(squares, axis=0, keepdims=True)
        return carry

    lax.fori_loop(0, EXPAND // CHUNK, step, 0)
    pay_ref[...] = pack_moments(stat_scr[0:1, :], stat_scr[1:2, :], count)


def spatial(x, mats, side, recv):
    count = x.shape[0]
    return call(
        spatial_kernel,
        [shape((count, EXPAND), BF16), shape((moment_rows(EXPAND), LANE), BF16), shape((8, EXPAND))],
        [x, mats, side, recv],
        [
            pltpu.VMEM((count, WIDTH), BF16),
            pltpu.VMEM((count, CHUNK), F32),
            pltpu.VMEM((16, EXPAND), F32),
            pltpu.VMEM((8, EXPAND), F32),
        ],
    )


def project_kernel(
    d_ref, mats_ref, side_ref, vec_ref, recv_ref,
    p_ref, pay_ref, norm_ref, pooled_ref, excite_ref, squeeze_ref,
    a_scr, y_scr, row_scr,
):
    count = d_ref.shape[0]
    tiles = count // ROWS
    rows = side_ref[2 * SQUEEZE : SIDE_PAD, :].astype(F32)
    mean, inverse = read_moments(recv_ref, EXPAND, count)
    norm_ref[0:1, :] = mean
    norm_ref[1:2, :] = inverse
    scale = inverse * rows[12:13, :]
    row_scr[0:1, :] = scale
    row_scr[1:2, :] = rows[13:14, :] - mean * scale

    def activate(index, carry):
        lanes = chunk_at(index, LANE)
        scale_row = row_scr[0:1, lanes]
        shift_row = row_scr[1:2, lanes]
        for tile in range(tiles):
            at = slice(tile * ROWS, (tile + 1) * ROWS)
            pre = d_ref[at, lanes].astype(F32) * scale_row + shift_row
            active = pre * sigmoid(pre)
            a_scr[at, lanes] = active
            pooled_ref[tile * TILE : (tile + 1) * TILE, lanes] = jnp.sum(as_tile(active), axis=0) / MAP
        return carry

    lax.fori_loop(0, EXPAND // LANE, activate, 0)
    reduce_mat = side_ref[0:SQUEEZE, :]
    excite_mat = side_ref[SQUEEZE : 2 * SQUEEZE, :]
    high, low = halves(pooled_ref[...])
    before = dot_nt(high, reduce_mat) + dot_nt(low, reduce_mat) + vec_ref[2:3, :SQUEEZE]
    squeeze_ref[...] = before
    high, low = halves(before * sigmoid(before))
    excite_ref[...] = sigmoid(dot(high, excite_mat) + dot(low, excite_mat) + rows[9:10, :])

    def gate(index, carry):
        lanes = chunk_at(index, LANE)
        for tile in range(tiles):
            at = slice(tile * ROWS, (tile + 1) * ROWS)
            factor = excite_ref[tile * TILE : (tile + 1) * TILE, lanes]
            scaled = as_tile(a_scr[at, lanes]) * factor[None]
            y_scr[at, lanes] = scaled.reshape(ROWS, LANE).astype(BF16)
        return carry

    lax.fori_loop(0, EXPAND // LANE, gate, 0)
    projected = dot_nt(y_scr[...], mats_ref[WIDTH:, :])
    p_ref[...] = projected
    total = jnp.sum(projected, axis=0, keepdims=True)
    squares = jnp.sum(projected * projected, axis=0, keepdims=True)
    pay_ref[...] = pack_moments(total, squares, count)


def project(d, mats, side, vec, recv):
    count = d.shape[0]
    images = count // MAP
    return call(
        project_kernel,
        [
            shape((count, WIDTH)),
            shape((moment_rows(WIDTH), LANE), BF16),
            shape((8, EXPAND)),
            shape((images, EXPAND)),
            shape((images, EXPAND)),
            shape((images, SQUEEZE)),
        ],
        [d, mats, side, vec, recv],
        [
            pltpu.VMEM((count, EXPAND), F32),
            pltpu.VMEM((count, EXPAND), BF16),
            pltpu.VMEM((8, EXPAND), F32),
        ],
    )


def residual_kernel(transposed, x_ref, p_ref, vec_ref, recv_ref, w_ref, out_ref, pay_ref, norm_ref, cross_ref, xb_scr, h_scr, stat_scr):
    count = x_ref.shape[0]
    mean, inverse = read_moments(recv_ref, WIDTH, count)
    norm_ref[0:1, :] = mean
    norm_ref[1:2, :] = inverse
    normed = (p_ref[...] - mean) * inverse
    result = x_ref[...] + (normed * vec_ref[0:1, :] + vec_ref[1:2, :])
    out_ref[...] = result
    xb_scr[...] = result.astype(BF16)
    high, low = halves(normed)
    cross_ref[...] = dot_tn(high, xb_scr[...]) + dot_tn(low, xb_scr[...])
    sum_columns(xb_scr, w_ref, transposed, h_scr, stat_scr)
    pay_ref[...] = pack_moments(stat_scr[0:1, :], stat_scr[1:2, :], count)


def residual(x, p, vec, recv, weights, transposed):
    count = x.shape[0]
    columns = HEAD if transposed else EXPAND
    return call(
        functools.partial(residual_kernel, transposed),
        [
            shape((count, WIDTH)),
            shape((moment_rows(columns), LANE), BF16),
            shape((8, WIDTH)),
            shape((WIDTH, WIDTH)),
        ],
        [x, p, vec, recv, weights],
        [pltpu.VMEM((count, WIDTH), BF16), pltpu.VMEM((count, CHUNK), F32), pltpu.VMEM((8, columns), F32)],
    )


def head_rows(head_ref):
    pick_row = lax.broadcasted_iota(jnp.int32, (TILE, LANE), 0)
    pick_col = lax.broadcasted_iota(jnp.int32, (TILE, LANE), 1)
    first = WIDTH + CLASSES - (HEADPAD - LANE)
    pick = jnp.where((pick_col == pick_row + first) & (pick_row < 2), 1.0, 0.0).astype(BF16)
    return dot_nt(pick, head_ref[:, HEADPAD - LANE :])


def head_kernel(
    image_count, x_ref, head_ref, bias_ref, label_col_ref, label_row_ref, partner_ref, mix_ref,
    p_ref, norm3_ref, recv_ref,
    dz_ref, pay_ref, norm_ref, grad_fc_ref,
    xb_scr, h_scr, f_scr, g_scr, q_scr, row_scr, stat_scr,
):
    count = x_ref.shape[0]
    tiles = count // ROWS
    images = count // MAP
    xb_scr[...] = x_ref[...].astype(BF16)
    mean, inverse = read_moments(recv_ref, HEAD, count)
    gain_bias = head_rows(head_ref)
    norm_ref[0:1, :] = mean
    norm_ref[1:2, :] = inverse
    scale = inverse * gain_bias[0:1, :]
    norm_ref[2:3, :] = gain_bias[0:1, :]
    row_scr[0:1, :] = scale
    row_scr[1:2, :] = gain_bias[1:2, :] - mean * scale
    row_scr[2:3, :] = mean

    def features(index, carry):
        at_chunk = chunk_at(index)
        h_scr[:, at_chunk] = dot_nt(xb_scr[...], head_ref[at_chunk, :WIDTH])
        for part in range(CHUNK // LANE):
            lanes = chunk_at(index * (CHUNK // LANE) + part, LANE)
            scale_row = row_scr[0:1, lanes]
            shift_row = row_scr[1:2, lanes]
            for tile in range(tiles):
                pre = h_scr[tile * ROWS : (tile + 1) * ROWS, lanes] * scale_row + shift_row
                active = as_tile(pre * sigmoid(pre))
                f_scr[tile * TILE : (tile + 1) * TILE, lanes] = jnp.sum(active, axis=0) / MAP
        return carry

    lax.fori_loop(0, HEAD // CHUNK, features, 0)
    features_low = f_scr[...].astype(BF16)
    classifier = head_ref[:, WIDTH:]
    ids = lax.broadcasted_iota(jnp.int32, (images, LOGITS), 1)
    logits = dot(features_low, classifier) + bias_ref[...]
    logits = jnp.where(ids < CLASSES, logits, -1e30)
    row_max = jnp.max(logits, axis=1, keepdims=True)
    log_total = row_max + jnp.log(jnp.sum(jnp.exp(logits - row_max), axis=1, keepdims=True))
    pair = mix_ref[...].astype(F32)
    mixing = pair[:, 0:1] / (pair[:, 0:1] + pair[:, 1:2])
    people = lax.broadcasted_iota(jnp.int32, (images, images), 1)
    label_row = jnp.broadcast_to(label_row_ref[...].astype(F32), (images, images))
    partner_label = jnp.sum(
        jnp.where(people == partner_ref[...], label_row, 0.0), axis=1, keepdims=True
    ).astype(jnp.int32)
    own_hot = jnp.where(ids == label_col_ref[...], 1.0, 0.0)
    other_hot = jnp.where(ids == partner_label, 1.0, 0.0)
    own_logit = jnp.sum(own_hot * logits, axis=1, keepdims=True)
    other_logit = jnp.sum(other_hot * logits, axis=1, keepdims=True)
    loss = mixing * (log_total - own_logit) + (1.0 - mixing) * (log_total - other_logit)
    loss = jnp.sum(loss, axis=0, keepdims=True)
    grad_logits = (
        jnp.exp(logits - log_total) - mixing * own_hot - (1.0 - mixing) * other_hot
    ) / image_count
    grad_low = grad_logits.astype(BF16)
    grad_fc_ref[...] = dot_tn(features_low, grad_low).astype(BF16)
    g_scr[...] = dot_nt(grad_low, classifier) / MAP
    bias_sum = jnp.sum(grad_logits, axis=0, keepdims=True)
    bias_ids = lax.broadcasted_iota(jnp.int32, (1, LOGITS), 1)
    loss_high = loss.astype(BF16).astype(F32)
    bias_sum = jnp.where(bias_ids == CLASSES, loss_high, bias_sum)
    bias_sum = jnp.where(bias_ids == CLASSES + 1, loss - loss_high, bias_sum)

    def back(index, carry):
        lanes = chunk_at(index, LANE)
        scale_row = row_scr[0:1, lanes]
        shift_row = row_scr[1:2, lanes]
        mean_row = row_scr[2:3, lanes]
        total = jnp.zeros((TILE, LANE), F32)
        weighted = jnp.zeros((TILE, LANE), F32)
        for tile in range(tiles):
            at = slice(tile * ROWS, (tile + 1) * ROWS)
            hidden = h_scr[at, lanes]
            pre = hidden * scale_row + shift_row
            gate = sigmoid(pre)
            slope = as_tile(gate * (1.0 + pre * (1.0 - gate)))
            grad = slope * g_scr[tile * TILE : (tile + 1) * TILE, lanes][None]
            total = total + jnp.sum(grad, axis=0)
            weighted = weighted + jnp.sum(grad * as_tile(hidden - mean_row), axis=0)
            flat = grad.reshape(ROWS, LANE)
            dz_ref[at, lanes] = flat.astype(BF16)
            q_scr[at, lanes] = (flat * scale_row).astype(BF16)
        stat_scr[0:1, lanes] = jnp.sum(total, axis=0, keepdims=True)
        stat_scr[1:2, lanes] = jnp.sum(weighted, axis=0, keepdims=True)
        return carry

    lax.fori_loop(0, HEAD // LANE, back, 0)
    below = dot(q_scr[...], head_ref[:, :WIDTH])
    normed = (p_ref[...] - norm3_ref[0:1, :]) * norm3_ref[1:2, :]
    below_sum = jnp.sum(below, axis=0, keepdims=True)
    below_gain = jnp.sum(below * normed, axis=0, keepdims=True)
    pay_ref[...] = fold(
        [stat_scr[0:1, :], stat_scr[1:2, :] * inverse, below_sum, below_gain, bias_sum], 32
    ).astype(BF16)


def head(x, head_full, bias, label_col, label_row, partner, mix_pair, p, norm3, recv, image_count):
    count = x.shape[0]
    images = count // MAP
    return call(
        functools.partial(head_kernel, image_count),
        [
            shape((count, HEAD), BF16),
            shape((32, LANE), BF16),
            shape((8, HEAD)),
            shape((HEAD, LOGITS), BF16),
        ],
        [x, head_full, bias, label_col, label_row, partner, mix_pair, p, norm3, recv],
        [
            pltpu.VMEM((count, WIDTH), BF16),
            pltpu.VMEM((count, HEAD), F32),
            pltpu.VMEM((images, HEAD), F32),
            pltpu.VMEM((images, HEAD), F32),
            pltpu.VMEM((count, HEAD), BF16),
            pltpu.VMEM((8, HEAD), F32),
            pltpu.VMEM((8, HEAD), F32),
        ],
    )


def upper_back(
    is_head, row_count, x_ref, w_ref, dz_ref, norm_ref, gain, sums, columns,
    xb_scr, xt_scr, h_scr, row_scr, dh_scr, grad_w_ref, glob_ref,
):
    groups = columns // LANE
    sum_bias = spread(sums, 0, groups)
    sum_gain = spread(sums, groups, groups)
    glob_ref[0:1, :] = sum_gain
    glob_ref[1:2, :] = sum_bias
    mean = norm_ref[0:1, :]
    inverse = norm_ref[1:2, :]
    scale = inverse * gain
    slant = scale * inverse * (sum_gain / row_count)
    row_scr[0:1, :columns] = scale
    row_scr[1:2, :columns] = slant
    row_scr[2:3, :columns] = mean * slant - scale * (sum_bias / row_count)
    xb_scr[...] = x_ref[...].astype(BF16)
    xt_scr[...] = xb_scr[...].T

    def step(index, carry):
        at = chunk_at(index)
        if is_head:
            h_scr[...] = dot_nt(xb_scr[...], w_ref[at, :WIDTH])
        else:
            h_scr[...] = dot(xb_scr[...], w_ref[:WIDTH, at])
        grad = (
            dz_ref[:, at].astype(F32) * row_scr[0:1, at]
            - h_scr[...] * row_scr[1:2, at]
            + row_scr[2:3, at]
        )
        low = grad.astype(BF16)
        dh_scr[:, at] = low
        if is_head:
            grad_w_ref[at, :] = dot_tn(low, xb_scr[...]).astype(BF16)
        else:
            grad_w_ref[:, at] = dot(xt_scr[...], low).astype(BF16)
        return carry

    lax.fori_loop(0, columns // CHUNK, step, 0)
    return scale * sum_bias, slant * row_count


def gate_kernel(
    is_head, row_count,
    recv_ref, x_ref, w_ref, dz_ref, norm_ref, upside_ref, cross_ref, stream_ref,
    p_ref, norm3_ref, vec_ref, mats_ref, d_ref, norm2_ref, side_ref, pooled_ref, excite_ref, squeeze_ref,
    dz2_ref, pay_ref, stream_out_ref, grad_w_ref, grad_p_ref, grad_side_ref, grad_sb_ref, glob_ref, glob3_ref,
    xb_scr, xt_scr, h_scr, row_scr, dh_scr, u_scr, slope_scr, y_scr, gp_scr, gt_scr, ge_scr, pool_scr, stat_scr,
):
    columns = HEAD if is_head else EXPAND
    groups = columns // LANE
    count = x_ref.shape[0]
    tiles = count // ROWS
    sums = read_sums(recv_ref)
    if is_head:
        gain = norm_ref[2:3, :]
    else:
        gain = upside_ref[2 * SQUEEZE : SIDE_PAD, :].astype(F32)[10:11, :]
    bias_pull, slant = upper_back(
        is_head, row_count, x_ref, w_ref, dz_ref, norm_ref, gain, sums, columns,
        xb_scr, xt_scr, h_scr, row_scr, dh_scr, grad_w_ref, glob_ref,
    )
    if is_head:
        weights_t = w_ref[:, :WIDTH]
        slanted = weights_t.astype(F32) * jnp.broadcast_to(slant, (TILE, columns)).T[:, 0:1]
        high, low = halves(slanted)
        spread_mat = dot_tn(high, weights_t) + dot_tn(low, weights_t)
        pull = jnp.dot(jnp.broadcast_to(bias_pull, (TILE, columns)), weights_t.astype(F32),
                       preferred_element_type=F32, precision=HIGHEST)[0:1, :]
        stream = dot(dh_scr[:, :columns], weights_t)
    else:
        weights = w_ref[:WIDTH, :]
        high, low = halves(weights.astype(F32) * slant)
        spread_mat = dot_nt(high, weights) + dot_nt(low, weights)
        pull = lax.dot_general(jnp.broadcast_to(bias_pull, (TILE, columns)), weights.astype(F32), NT,
                               preferred_element_type=F32, precision=HIGHEST)[0:1, :]
        stream = stream_ref[...] + dot_nt(dh_scr[:, :columns], weights)
    stream_out_ref[...] = stream
    sum_bias = spread(sums, 2 * groups, WIDTH // LANE) - pull
    corrected = jnp.sum(cross_ref[...].T * spread_mat, axis=0, keepdims=True) / row_count
    sum_gain = spread(sums, 2 * groups + WIDTH // LANE, WIDTH // LANE) - corrected
    glob3_ref[0:1, :] = sum_gain
    glob3_ref[1:2, :] = sum_bias
    if is_head:
        glob3_ref[2:6, :] = jnp.concatenate(
            [spread(sums, 2 * groups + 4 + 2 * k, 2) for k in range(LOGITS // WIDTH)], axis=0
        )
    inverse3 = norm3_ref[1:2, :]
    normed = (p_ref[...] - norm3_ref[0:1, :]) * inverse3
    grad_p = (inverse3 * vec_ref[0:1, :]) * (
        stream - sum_bias / row_count - normed * (sum_gain / row_count)
    )
    gp_scr[...] = grad_p.astype(BF16)
    gt_scr[...] = gp_scr[...].T

    rows = side_ref[2 * SQUEEZE : SIDE_PAD, :].astype(F32)
    mean2 = norm2_ref[0:1, :]
    scale2 = norm2_ref[1:2, :] * rows[12:13, :]
    row_scr[0:1, :EXPAND] = scale2
    row_scr[1:2, :EXPAND] = rows[13:14, :] - mean2 * scale2
    row_scr[2:3, :EXPAND] = mean2

    def first(index, carry):
        at_chunk = chunk_at(index)
        h_scr[...] = dot(gp_scr[...], mats_ref[WIDTH:, at_chunk])
        for part in range(CHUNK // LANE):
            lanes = chunk_at(index * (CHUNK // LANE) + part, LANE)
            scale_row = row_scr[0:1, lanes]
            shift_row = row_scr[1:2, lanes]
            for tile in range(tiles):
                at = slice(tile * ROWS, (tile + 1) * ROWS)
                near = slice(tile * TILE, (tile + 1) * TILE)
                pre = d_ref[at, lanes].astype(F32) * scale_row + shift_row
                gate = sigmoid(pre)
                active = pre * gate
                slope = gate + active - active * gate
                grad = h_scr[at, part * LANE : (part + 1) * LANE]
                factor = excite_ref[near, lanes]
                ge_scr[near, lanes] = jnp.sum(as_tile(grad * active), axis=0)
                y_scr[at, lanes] = (as_tile(active) * factor[None]).reshape(ROWS, LANE).astype(BF16)
                slope_scr[at, lanes] = slope
                u_scr[at, lanes] = (as_tile(grad * slope) * factor[None]).reshape(ROWS, LANE)
        grad_p_ref[:, at_chunk] = dot(gt_scr[...], y_scr[:, at_chunk]).astype(BF16)
        return carry

    lax.fori_loop(0, EXPAND // CHUNK, first, 0)
    excite = excite_ref[...]
    grad_gate = ge_scr[...] * excite * (1.0 - excite)
    before = squeeze_ref[...]
    opened = sigmoid(before)
    squeezed = before * opened
    reduce_mat = side_ref[0:SQUEEZE, :]
    excite_mat = side_ref[SQUEEZE : 2 * SQUEEZE, :]
    high, low = halves(grad_gate)
    grad_squeezed = dot_nt(high, excite_mat) + dot_nt(low, excite_mat)
    grad_pre = grad_squeezed * (opened * (1.0 + before * (1.0 - opened)))
    squeezed_high, squeezed_low = halves(squeezed)
    grad_excite = dot_tn(squeezed_high, high) + dot_tn(squeezed_low, high) + dot_tn(squeezed_high, low)
    pre_high, pre_low = halves(grad_pre)
    pooled_high, pooled_low = halves(pooled_ref[...])
    grad_reduce = (
        dot_tn(pre_high, pooled_high) + dot_tn(pre_low, pooled_high) + dot_tn(pre_high, pooled_low)
    )
    grad_side_ref[0:SQUEEZE, :] = grad_reduce.astype(BF16)
    grad_side_ref[SQUEEZE : 2 * SQUEEZE, :] = grad_excite.astype(BF16)
    grad_sb_ref[0:1, :] = jnp.sum(grad_gate, axis=0, keepdims=True)
    grad_sb_ref[1:2, :SQUEEZE] = jnp.sum(grad_pre, axis=0, keepdims=True)
    grad_sb_ref[1:2, SQUEEZE:] = jnp.zeros((1, EXPAND - SQUEEZE), F32)
    pool_scr[...] = (dot(pre_high, reduce_mat) + dot(pre_low, reduce_mat)) / MAP

    def second(index, carry):
        lanes = chunk_at(index, LANE)
        mean_row = row_scr[2:3, lanes]
        total = jnp.zeros((TILE, LANE), F32)
        weighted = jnp.zeros((TILE, LANE), F32)
        for tile in range(tiles):
            at = slice(tile * ROWS, (tile + 1) * ROWS)
            pool = pool_scr[tile * TILE : (tile + 1) * TILE, lanes]
            grad = as_tile(u_scr[at, lanes]) + as_tile(slope_scr[at, lanes]) * pool[None]
            total = total + jnp.sum(grad, axis=0)
            weighted = weighted + jnp.sum(
                grad * as_tile(d_ref[at, lanes].astype(F32) - mean_row), axis=0
            )
            dz2_ref[at, lanes] = grad.reshape(ROWS, LANE).astype(BF16)
        stat_scr[0:1, lanes] = jnp.sum(total, axis=0, keepdims=True)
        stat_scr[1:2, lanes] = jnp.sum(weighted, axis=0, keepdims=True)
        return carry

    lax.fori_loop(0, EXPAND // LANE, second, 0)
    pay_ref[...] = fold(
        [stat_scr[0:1, :], stat_scr[1:2, :] * norm2_ref[1:2, :]], 24
    ).astype(BF16)


def gate_back(is_head, row_count, recv, upper, cross, stream, lower):
    count = upper["x"].shape[0]
    images = count // MAP
    columns = HEAD if is_head else EXPAND
    grad_w = (HEAD, WIDTH) if is_head else (WIDTH, EXPAND)
    return call(
        functools.partial(gate_kernel, is_head, row_count),
        [
            shape((count, EXPAND), BF16),
            shape((24, LANE), BF16),
            shape((count, WIDTH)),
            shape(grad_w, BF16),
            shape((WIDTH, EXPAND), BF16),
            shape((2 * SQUEEZE, EXPAND), BF16),
            shape((8, EXPAND)),
            shape((8, columns)),
            shape((8, WIDTH)),
        ],
        [
            recv, upper["x"], upper["weights"], upper["dz"], upper["norm"], upper["side"], cross, stream,
            lower["p"], lower["norm3"], lower["vec"], lower["mats"], lower["d"], lower["norm2"],
            lower["side"], lower["pooled"], lower["excite"], lower["squeeze"],
        ],
        [
            pltpu.VMEM((count, WIDTH), BF16),
            pltpu.VMEM((WIDTH, count), BF16),
            pltpu.VMEM((count, CHUNK), F32),
            pltpu.VMEM((8, EXPAND), F32),
            pltpu.VMEM((count, EXPAND), BF16),
            pltpu.VMEM((count, EXPAND), F32),
            pltpu.VMEM((count, EXPAND), F32),
            pltpu.VMEM((count, EXPAND), BF16),
            pltpu.VMEM((count, WIDTH), BF16),
            pltpu.VMEM((WIDTH, count), BF16),
            pltpu.VMEM((images, EXPAND), F32),
            pltpu.VMEM((images, EXPAND), F32),
            pltpu.VMEM((8, EXPAND), F32),
        ],
    )


def tap_kernel(
    is_first, row_count,
    recv_ref, dz2_ref, d_ref, norm2_ref, x_ref, mats_ref, norm1_ref, side_ref, stream_ref, p_ref, norm3_ref,
    dz_ref, pay_ref, taps_ref, glob_ref,
    xb_scr, h_scr, row_scr, q_scr, stat_scr,
):
    count = x_ref.shape[0]
    groups = EXPAND // LANE
    sums = read_sums(recv_ref)
    sum_bias = spread(sums, 0, groups)
    sum_gain = spread(sums, groups, groups)
    glob_ref[0:1, :] = sum_gain
    glob_ref[1:2, :] = sum_bias
    rows = side_ref[2 * SQUEEZE : SIDE_PAD, :].astype(F32)
    mean2 = norm2_ref[0:1, :]
    inverse2 = norm2_ref[1:2, :]
    scale2 = inverse2 * rows[12:13, :]
    slant2 = scale2 * inverse2 * (sum_gain / row_count)
    mean1 = norm1_ref[0:1, :]
    scale1 = norm1_ref[1:2, :] * rows[10:11, :]
    row_scr[0:9, :] = rows[0:9, :]
    row_scr[9:10, :] = scale2
    row_scr[10:11, :] = slant2
    row_scr[11:12, :] = mean2 * slant2 - scale2 * (sum_bias / row_count)
    row_scr[12:13, :] = scale1
    row_scr[13:14, :] = rows[11:12, :] - mean1 * scale1
    row_scr[14:15, :] = mean1
    xb_scr[...] = x_ref[...].astype(BF16)

    def step(index, carry):
        h_scr[...] = dot(xb_scr[...], mats_ref[:WIDTH, chunk_at(index)])
        for part in range(CHUNK // LANE):
            lanes = chunk_at(index * (CHUNK // LANE) + part, LANE)
            near = slice(part * LANE, (part + 1) * LANE)
            taps = [jnp.broadcast_to(row_scr[k : k + 1, lanes], (TILE, LANE)) for k in range(9)]

            def tile_step(tile, sums_in):
                at = chunk_at(tile, ROWS)
                grad_d = as_tile(
                    dz2_ref[at, lanes].astype(F32) * row_scr[9:10, lanes]
                    - d_ref[at, lanes].astype(F32) * row_scr[10:11, lanes]
                    + row_scr[11:12, lanes]
                )
                hidden = h_scr[at, near]
                pre = hidden * row_scr[12:13, lanes] + row_scr[13:14, lanes]
                gate = sigmoid(pre)
                flat = pre * gate
                active = as_tile(flat)
                slope = as_tile(gate + flat - flat * gate)
                apart = as_tile(hidden - row_scr[14:15, lanes])
                grad_a = [None] * MAP
                tap_sums = [None] * 9
                for target, tap, source in TERMS:
                    term = grad_d[target] * taps[tap]
                    grad_a[source] = term if grad_a[source] is None else grad_a[source] + term
                    term = grad_d[target] * active[source]
                    tap_sums[tap] = term if tap_sums[tap] is None else tap_sums[tap] + term
                total, weighted = sums_in[9], sums_in[10]
                grads = []
                for place in range(MAP):
                    grad = grad_a[place] * slope[place]
                    total = total + grad
                    weighted = weighted + grad * apart[place]
                    grads.append(grad)
                grad = jnp.concatenate(grads, axis=0)
                dz_ref[at, lanes] = grad.astype(BF16)
                if not is_first:
                    q_scr[at, lanes] = (grad * row_scr[12:13, lanes]).astype(BF16)
                return (*[sums_in[k] + tap_sums[k] for k in range(9)], total, weighted)

            zero = jnp.zeros((TILE, LANE), F32)
            result = lax.fori_loop(0, count // ROWS, tile_step, (zero,) * 11)
            for k in range(9):
                taps_ref[k : k + 1, lanes] = jnp.sum(result[k], axis=0, keepdims=True)
            stat_scr[0:1, lanes] = jnp.sum(result[9], axis=0, keepdims=True)
            stat_scr[1:2, lanes] = jnp.sum(result[10], axis=0, keepdims=True)
        return carry

    lax.fori_loop(0, EXPAND // CHUNK, step, 0)
    vectors = [stat_scr[0:1, :], stat_scr[1:2, :] * norm1_ref[1:2, :]]
    if not is_first:
        below = stream_ref[...] + dot_nt(q_scr[...], mats_ref[:WIDTH, :])
        normed = (p_ref[...] - norm3_ref[0:1, :]) * norm3_ref[1:2, :]
        vectors.append(jnp.sum(below, axis=0, keepdims=True))
        vectors.append(jnp.sum(below * normed, axis=0, keepdims=True))
    pay_ref[...] = fold(vectors, pay_ref.shape[0]).astype(BF16)


def tap_back(is_first, row_count, recv, dz2, layer, stream, below):
    count = dz2.shape[0]
    return call(
        functools.partial(tap_kernel, is_first, row_count),
        [
            shape((count, EXPAND), BF16),
            shape((24 if is_first else 32, LANE), BF16),
            shape((16, EXPAND)),
            shape((8, EXPAND)),
        ],
        [
            recv, dz2, layer["d"], layer["norm2"], layer["x"], layer["mats"], layer["norm1"], layer["side"],
            stream, below["p"], below["norm3"],
        ],
        [
            pltpu.VMEM((count, WIDTH), BF16),
            pltpu.VMEM((count, CHUNK), F32),
            pltpu.VMEM((16, EXPAND), F32),
            pltpu.VMEM((count, EXPAND), BF16),
            pltpu.VMEM((8, EXPAND), F32),
        ],
    )


def last_kernel(
    row_count, recv_ref, x_ref, w_ref, dz_ref, norm_ref, side_ref,
    grad_w_ref, glob_ref, xb_scr, xt_scr, h_scr, row_scr, dh_scr,
):
    gain = side_ref[2 * SQUEEZE : SIDE_PAD, :].astype(F32)[10:11, :]
    upper_back(
        False, row_count, x_ref, w_ref, dz_ref, norm_ref, gain, read_sums(recv_ref), EXPAND,
        xb_scr, xt_scr, h_scr, row_scr, dh_scr, grad_w_ref, glob_ref,
    )


def last_back(row_count, recv, layer, dz):
    count = dz.shape[0]
    return call(
        functools.partial(last_kernel, row_count),
        [shape((WIDTH, EXPAND), BF16), shape((8, EXPAND))],
        [recv, layer["x"], layer["mats"], dz, layer["norm1"], layer["side"]],
        [
            pltpu.VMEM((count, WIDTH), BF16),
            pltpu.VMEM((WIDTH, count), BF16),
            pltpu.VMEM((count, CHUNK), F32),
            pltpu.VMEM((8, EXPAND), F32),
            pltpu.VMEM((count, EXPAND), BF16),
        ],
    )


def lamb_moments(weight, moment_one, moment_two, gradient, decay_mask, step_float):
    first_new = BETA_ONE * moment_one + (1.0 - BETA_ONE) * gradient
    second_new = BETA_TWO * moment_two + (1.0 - BETA_TWO) * gradient * gradient
    corrected = (
        first_new
        / (1.0 - BETA_ONE**step_float)
        / (jnp.sqrt(second_new / (1.0 - BETA_TWO**step_float)) + EPS_ADAM)
    )
    return (first_new, second_new, corrected + DECAY_RATE * decay_mask * weight)


def group_sums(mats, side, head, row_ids):
    rows = jnp.sum(mats * mats, axis=2)
    is_expand = (row_ids < WIDTH)[None, :]
    side_rows = jnp.sum(side * side, axis=2)
    head_cols = jnp.sum(head * head, axis=0)
    per_layer = jnp.stack(
        [
            jnp.sum(jnp.where(is_expand, rows, 0.0), axis=1),
            jnp.sum(jnp.where(is_expand, 0.0, rows), axis=1),
            jnp.sum(side_rows[:, :9], axis=1),
            jnp.sum(side_rows[:, 9 : 9 + SQUEEZE], axis=1),
            jnp.sum(side_rows[:, 9 + SQUEEZE : 9 + 2 * SQUEEZE], axis=1),
        ],
        axis=1,
    )
    tail = jnp.stack([jnp.sum(head_cols[:WIDTH]), jnp.sum(head_cols[WIDTH : WIDTH + CLASSES])])
    return jnp.concatenate([per_layer.reshape(-1), tail])


def rate_maps(trust_ratio, row_ids):
    groups = trust_ratio[: 5 * LAYERS].reshape(LAYERS, 5)
    mats_rate = RATE_MATRIX * jnp.where(row_ids[None, :] < WIDTH, groups[:, 0:1], groups[:, 1:2])
    side_ids = jnp.arange(SIDE)[None, :]
    side_rate = jnp.where(
        side_ids < 9,
        RATE_MATRIX * groups[:, 2:3],
        jnp.where(
            side_ids < 9 + SQUEEZE,
            RATE_MATRIX * groups[:, 3:4],
            jnp.where(side_ids < 9 + 2 * SQUEEZE, RATE_MATRIX * groups[:, 4:5], RATE_VECTOR),
        ),
    )
    col_ids = jnp.arange(HEADCOLS)
    head_rate = jnp.where(
        col_ids < WIDTH,
        RATE_MATRIX * trust_ratio[5 * LAYERS],
        jnp.where(
            col_ids < WIDTH + CLASSES, RATE_MATRIX * trust_ratio[5 * LAYERS + 1], RATE_VECTOR
        ),
    )
    return (mats_rate, side_rate, head_rate)


def body(
    images, partner, mix_pair, labels, step,
    layer_mats, layer_side, layer_vecs, head_mat, fc_bias,
    mats_first, mats_second, side_first, side_second, vecs_first, vecs_second,
    head_first, head_second, bias_first, bias_second,
):
    local_images = images.shape[0]
    owners = lax.axis_size("fsdp")
    replicas = lax.axis_size("dp") * owners
    image_count = float(local_images * replicas)
    count = local_images * MAP
    row_count = float(count * replicas)
    mine = lax.axis_index("fsdp")
    side_width = layer_side.shape[2]
    vec_width = layer_vecs.shape[1]
    rows_dev = layer_mats.shape[1]

    side_low = jnp.concatenate(
        [
            layer_side[:, 9 : 9 + 2 * SQUEEZE],
            layer_side[:, :9],
            layer_side[:, 9 + 2 * SQUEEZE :],
            jnp.pad(layer_vecs, ((0, 0), (0, side_width - vec_width)))[:, None, :],
            jnp.zeros((LAYERS, 1, side_width), F32),
        ],
        axis=1,
    ).astype(BF16)
    mats_all = [
        lax.all_gather(layer_mats[k].astype(BF16), "fsdp", axis=0, tiled=True) for k in range(LAYERS)
    ]
    side_all = lax.all_gather(side_low, "fsdp", axis=2, tiled=True)
    head_full = lax.all_gather(
        jnp.pad(head_mat, ((0, 0), (0, HEADPAD - HEADCOLS))).astype(BF16), "fsdp", axis=0, tiled=True
    )
    vecs_all = side_all[:, SIDE, :].reshape(LAYERS, owners, side_width)[:, :, :vec_width]
    vecs_all = vecs_all.reshape(LAYERS, VECS).astype(F32)
    vecs_all = jnp.stack(
        [
            vecs_all[:, SQUEEZE : SQUEEZE + WIDTH],
            vecs_all[:, SQUEEZE + WIDTH :],
            jnp.pad(vecs_all[:, :SQUEEZE], ((0, 0), (0, WIDTH - SQUEEZE))),
        ],
        axis=1,
    )
    vecs_all = jnp.pad(vecs_all, ((0, 0), (0, 5), (0, 0)))

    partner_col = partner[:, None]
    layers = []
    crosses = []
    x, pay = enter(images.reshape(count, WIDTH), partner_col, mix_pair, mats_all[0])
    for k in range(LAYERS):
        mats, side, vec = mats_all[k], side_all[k], vecs_all[k]
        d, pay, norm1 = spatial(x, mats, side, share(pay))
        p, pay, norm2, pooled, excite, squeeze = project(d, mats, side, vec, share(pay))
        last = k == LAYERS - 1
        above, pay, norm3, cross = residual(
            x, p, vec, share(pay), head_full if last else mats_all[k + 1], last
        )
        crosses.append(lax.psum(cross, BOTH))
        layers.append(
            dict(
                x=x, d=d, norm1=norm1, p=p, norm2=norm2, pooled=pooled, excite=excite, squeeze=squeeze,
                norm3=norm3, mats=mats, weights=mats, side=side, vec=vec,
            )
        )
        x = above
    top = layers[-1]
    dz, pay, head_norm, grad_fc = head(
        x, head_full, jnp.pad(fc_bias, (0, LOGITS - CLASSES))[None], labels[:, None], labels[None, :],
        partner_col, mix_pair, top["p"], top["norm3"], share(pay), image_count,
    )
    upper = dict(x=x, weights=head_full, dz=dz, norm=head_norm, side=top["side"])
    stream = x
    mats_grads = [None] * LAYERS
    side_grads = [None] * LAYERS
    globs = [None] * LAYERS
    for k in reversed(range(LAYERS)):
        layer = layers[k]
        is_head = k == LAYERS - 1
        dz2, pay, stream, grad_w, grad_p, grad_side, grad_sb, glob, glob3 = gate_back(
            is_head, row_count, share(pay), upper, crosses[k], stream, layer
        )
        if is_head:
            head_glob, head_glob3, grad_head = glob, glob3, grad_w
        else:
            globs[k + 1]["one"] = glob
            mats_grads[k + 1] = (grad_w, mats_grads[k + 1])
        mats_grads[k] = grad_p
        dz, pay, taps, glob2 = tap_back(
            k == 0, row_count, share(pay), dz2, layer, stream, layers[max(k - 1, 0)]
        )
        globs[k] = dict(two=glob2, three=glob3)
        sb_row = jnp.pad(
            jnp.pad(grad_sb[1, :SQUEEZE], (0, VECS - SQUEEZE)).reshape(owners, vec_width),
            ((0, 0), (0, side_width - vec_width)),
        ).reshape(1, EXPAND)
        side_grads[k] = jnp.concatenate(
            [taps[:9].astype(BF16), grad_side, grad_sb[0:1].astype(BF16), sb_row.astype(BF16)], axis=0
        )
        upper = dict(x=layer["x"], weights=layer["mats"], dz=dz, norm=layer["norm1"], side=layer["side"])
    grad_w, globs[0]["one"] = last_back(row_count, share(pay), layers[0], dz)
    mats_grads[0] = (grad_w, mats_grads[0])

    def to_owner(array, dim):
        return lax.psum_scatter(array, "fsdp", scatter_dimension=dim, tiled=True)

    shard_mats = jnp.stack([to_owner(jnp.concatenate(pair, axis=0), 0) for pair in mats_grads])
    shard_side = jnp.stack([to_owner(array, 1) for array in side_grads])
    shard_head = to_owner(jnp.concatenate([grad_head, grad_fc], axis=1), 0)
    shard_mats, shard_side, shard_head = lax.psum((shard_mats, shard_side, shard_head), "dp")
    shard_mats = shard_mats.astype(F32)
    shard_side = shard_side.astype(F32)
    shard_head = shard_head.astype(F32)

    def own_columns(vector, width):
        return lax.dynamic_slice_in_dim(vector, mine * width, width, axis=-1)

    side_tail = jnp.stack(
        [
            own_columns(jnp.concatenate([g["one"][0:2], g["two"][0:2]], axis=0), side_width)
            for g in globs
        ]
    )
    vec_tail = jnp.stack(
        [
            own_columns(
                jnp.concatenate([jnp.zeros((SQUEEZE,), F32), g["three"][0], g["three"][1]]), vec_width
            )
            for g in globs
        ]
    )
    vec_ids = mine * vec_width + jnp.arange(vec_width)
    grad_vecs = jnp.where(
        vec_ids[None, :] < SQUEEZE, shard_side[:, SIDE - 4, :vec_width], vec_tail
    )
    grad_side = jnp.concatenate([shard_side[:, : SIDE - 4], side_tail], axis=1)
    head_tail = own_columns(head_glob[0:2], head_mat.shape[0]).T
    grad_head = jnp.concatenate([shard_head[:, : WIDTH + CLASSES], head_tail], axis=1)
    bias_loss = head_glob3[2:6].reshape(LOGITS)
    grad_bias = bias_loss[:CLASSES]
    loss_value = (bias_loss[CLASSES] + bias_loss[CLASSES + 1]) / image_count

    step_float = step[0].astype(F32)
    side_decay = (jnp.arange(SIDE) < 9 + 2 * SQUEEZE).astype(F32)[None, :, None]
    head_decay = (jnp.arange(HEADCOLS) < WIDTH + CLASSES).astype(F32)[None, :]
    mats_moment, mats_square, mats_dir = lamb_moments(
        layer_mats, mats_first, mats_second, shard_mats, 1.0, step_float
    )
    side_moment, side_square, side_dir = lamb_moments(
        layer_side, side_first, side_second, grad_side, side_decay, step_float
    )
    vecs_moment, vecs_square, vecs_dir = lamb_moments(
        layer_vecs, vecs_first, vecs_second, grad_vecs, 0.0, step_float
    )
    head_moment, head_square, head_dir = lamb_moments(
        head_mat, head_first, head_second, grad_head, head_decay, step_float
    )
    bias_moment, bias_square, bias_dir = lamb_moments(
        fc_bias, bias_first, bias_second, grad_bias, 0.0, step_float
    )
    row_ids = mine * rows_dev + jnp.arange(rows_dev)
    squares = jnp.stack(
        [
            group_sums(layer_mats, layer_side, head_mat, row_ids),
            group_sums(mats_dir, side_dir, head_dir, row_ids),
        ]
    )
    squares = jnp.broadcast_to(squares[None], (owners, *squares.shape))
    norms = jnp.sqrt(jnp.sum(lax.all_to_all(squares, "fsdp", 0, 0), axis=0))
    mats_rate, side_rate, head_rate = rate_maps(norms[0] / norms[1], row_ids)
    mats_new = layer_mats - mats_rate[:, :, None] * mats_dir
    side_new = layer_side - side_rate[:, :, None] * side_dir
    vecs_new = layer_vecs - RATE_VECTOR * vecs_dir
    head_new = head_mat - head_rate[None, :] * head_dir
    bias_new = fc_bias - RATE_VECTOR * bias_dir
    return (
        loss_value,
        mats_new, mats_moment, mats_square,
        side_new, side_moment, side_square,
        vecs_new, vecs_moment, vecs_square,
        head_new, head_moment, head_square,
        bias_new, bias_moment, bias_square,
        norms,
    )


def solution(mesh):
    rows, columns = P(None, "fsdp", None), P(None, None, "fsdp")
    vecs, heads = P(None, "fsdp"), P("fsdp", None)
    return jax.shard_map(
        body,
        mesh=mesh,
        in_specs=(
            P(BOTH, None, None), P(BOTH), P(BOTH, None), P(BOTH), P(),
            rows, columns, vecs, heads, P(),
            rows, rows, columns, columns, vecs, vecs, heads, heads, P(), P(),
        ),
        out_specs=(
            P(),
            rows, rows, rows,
            columns, columns, columns,
            vecs, vecs, vecs,
            heads, heads, heads,
            P(), P(), P(), P(),
        ),
        check_vma=False,
    )
```

time: 1970 us -> 958 us (0.49)
  blocking collectives: 941 us -> 54.3 us
  waiting for transfers between devices: 114 us -> 478 us
  other arithmetic: 334 us -> 37.9 us
  local copies, waits for them, and re-layouts: 455 us -> 186 us
  Pallas kernels: 0 us -> 120 us
  matrix products: 55 us -> 0 us
    psum x22 -> x0, blocking collectives: 849 us -> none  [the longest x10 403 us: batch_normalize(): lax.psum((jnp.sum(hidden, axis=0), jnp.sum(hidden * hidden, axis=0)), ('d...]
    reduce_sum x45 -> x7, other arithmetic: 247 us -> 8.8 us  [the longest x2 4.73 us: group_sums(): rows = jnp.sum(mats * mats, axis=2)]
    slice x14 -> x27, local copies, waits for them, and re-layouts: 262 us -> 25.1 us  [the longest x1 9.54 us: body(): mats, side, vec = (mats_all[k], side_all[k], vecs_all[k])]
    psum x1 -> x2, waiting for transfers between devices: 15.7 us -> 191 us  [the longest x1 137 us: body(): crosses.append(lax.psum(cross, BOTH))]
    reduce_scatter x1 -> x4, waiting for transfers between devices: 0.01 us -> 138 us  [to_owner(): return lax.psum_scatter(array, 'fsdp', scatter_dimension=dim, tiled=True)]
    pallas_call x0 -> x18, Pallas kernels: none -> 120 us  [call(): pl.pallas_call(kernel, out_shape=outs, in_specs=[pl.BlockSpec(memory_spac...]
    unnamed x602 -> x399, local copies, waits for them, and re-layouts: 39.7 us -> 136 us
    reshape x15 -> x3, local copies, waits for them, and re-layouts: 78.9 us -> 1.52 us  [body(): jnp.pad(grad_sb[1, :SQUEEZE], (0, VECS - SQUEEZE))]
  transfers between devices with their start and end apart: 15 -> 28, of which waited for: 8 -> 19; matrix products, arithmetic and copies ran while one was open for 31% -> 9% of each run, Pallas kernels for 0% -> 9%
where the time goes in v1:
time: 958 us; the launch traced here: 944 us
  waiting for transfers between devices  478 us (50%)
  local copies, waits for them, and re-layouts  186 us (19%)
  Pallas kernels  120 us (13%)
  blocking collectives  54.3 us (6%)
  starting transfers between devices  48.7 us (5%)
  other arithmetic  37.9 us (4%)
  between operations  20.3 us (2%)
    reduce_scatter x4, waiting for transfers between devices, to_owner(): return lax.psum_scatter(array, 'fsdp', scatter_dimension=dim, tiled=True)  138 us
    psum x1, waiting for transfers between devices, body(): crosses.append(lax.psum(cross, BOTH))  137 us
    unnamed x399, local copies, waits for them, and re-layouts  136 us
    pallas_call x18, Pallas kernels, call(): pl.pallas_call(kernel, out_shape=outs, in_specs=[pl.BlockSpec(memory_spac...  120 us
    all_to_all x13, waiting for transfers between devices, share(): return lax.all_to_all(copies, BOTH, 0, 0)  82.3 us
    all_to_all x4, blocking collectives, share(): return lax.all_to_all(copies, BOTH, 0, 0)  54.3 us
    psum x1, waiting for transfers between devices, body(): lax.psum((shard_mats, shard_side, shard_head), 'dp')  54 us
    all_to_all x13, starting transfers between devices, share(): return lax.all_to_all(copies, BOTH, 0, 0)  43.3 us
  transfers between devices with their start and end apart: 28, of which 19 were waited for; matrix products, arithmetic and copies ran while one was open for 9% of the time, Pallas kernels for 9%

profile of v1, /device:TPU:0, one launch (start us, length us, event | category | flops | bytes accessed | tf_op | source)
XLA Modules:
  0.0 943.9 jit_solution(15203645376524869337)
XLA Ops:
  16.7 21.7 %all-gather.13.cloned.1.call-done = bf16[1,512,1536]{2,1,0:T(8,128)(2,1)} async-done(((bf16[1,64,1536]{2,1,0:T(8,128)(2,1)}), bf16[1,512,1536]{2,1,0:T(8,128)(2,1)}) %all-gather.13.cloned.1.call-update) | async-done | bytes 1572880 | tf_op jit(solution)/shard_map/all_gather | solution.py:938
  48.2 37.3 %all-gather.9.cloned.1.call-done = bf16[3,144,1536]{1,0,2:T(4,128)(2,1)} async-done(((bf16[3,144,192]{1,0,2:T(4,128)(2,1)}), bf16[3,144,1536]{1,0,2:T(4,128)(2,1)}) %all-gather.9.cloned.1.call-update) | async-done | bytes 1327120 | tf_op jit(solution)/shard_map/all_gather | solution.py:940
  85.5 9.5 %fusion.22 = (bf16[1,144,1536]{1,0,2:T(2,128)(2,1)}, bf16[1,144,1536]{1,0,2:T(2,128)(2,1)}, bf16[1,144,1536]{1,0,2:T(2,128)(2,1)S(1)}) fusion(bf16[3,144,1536]{1,0,2:T(4,128)(2,1)} %all-gather.9.cloned.1.call-done), kind=kLoop, calls=%fused_computation.119 | loop fusion | bytes 2654208 | tf_op jit(solution)/shard_map/slice | solution.py:961
  116.9 10.2 %all-to-all-done.1.recv_ref = bf16[32,40,128]{2,1,0:T(8,128)(2,1)} async-done(((bf16[32,40,128]{2,1,0:T(8,128)(2,1)}), bf16[32,40,128]{2,1,0:T(8,128)(2,1)}, u32[]{:S(2)}, u32[]{:S(2)}) %all-to-all-start.1) | async-done | bytes 327712 | tf_op jit(solution)/shard_map/all_to_all | solution.py:136
  163.1 16.9 %all-to-all-done.3.recv_ref = bf16[32,40,128]{2,1,0:T(8,128)(2,1)S(1)} async-done(((bf16[32,40,128]{2,1,0:T(8,128)(2,1)}), bf16[32,40,128]{2,1,0:T(8,128)(2,1)S(1)}, u32[]{:S(2)}, u32[]{:S(2)}) %all-to-all-start.3) | async-done | bytes 327712 | tf_op jit(solution)/shard_map/all_to_all | solution.py:136
  185.1 14.9 %all_to_all.90.recv_ref = bf16[32,40,128]{2,1,0:T(8,128)(2,1)S(1)} all-to-all(bf16[32,40,128]{2,1,0:T(8,128)(2,1)S(1)} %broadcast_in_dim.260), channel_id=1, replica_groups=mesh['dp'=4,'fsdp'=8] {'dp','fsdp'}, dimensions={0} | all-to-all | bytes 655360 | tf_op jit(solution)/shard_map/all_to_all | solution.py:136
  231.3 7.6 all-to-all-done.6.recv_ref
  246.8 14.0 %all_to_all.91.recv_ref = bf16[32,40,128]{2,1,0:T(8,128)(2,1)S(1)} all-to-all(bf16[32,40,128]{2,1,0:T(8,128)(2,1)S(1)} %broadcast_in_dim.263), channel_id=1, replica_groups=mesh['dp'=4,'fsdp'=8] {'dp','fsdp'}, dimensions={0} | all-to-all | bytes 655360 | tf_op jit(solution)/shard_map/all_to_all | solution.py:136
  291.3 8.4 all-to-all-done.9.recv_ref
  305.9 8.0 shard_map.333
  321.2 137.4 %all-reduce.15.cloned.1.call-done = (f32[256,256]{1,0:T(8,128)}, f32[256,256]{1,0:T(8,128)}, f32[256,256]{1,0:T(8,128)}) async-done(((f32[256,256]{1,0:T(8,128)}, f32[256,256]{1,0:T(8,128)}, f32[256,256]{1,0:T(8,128)}), (f32[256,256]{1,0:T(8,128)}, f32[256,256]{1,0:T(8,128)}, f32[256,256]{1,0:T(8,128)})) %all-reduce.15.cloned.1.call-update) | async-done | bytes 786448 | tf_op jit(solution)/shard_map/psum | solution.py:968
  469.0 15.3 %shard_map.334 = (bf16[640,1536]{1,0:T(8,128)(2,1)}, bf16[24,128]{1,0:T(8,128)(2,1)S(1)}, f32[640,256]{1,0:T(8,128)S(1)}, bf16[1280,256]{1,0:T(8,128)(2,1)S(1)},...) custom-call(bf16[32,32,128]{2,1,0:T(8,128)(2,1)S(1)} %all-to-all-don, ...), custom_call_target="tpu_custom_call" | custom-call | tf_op jit(solution)/shard_map/pallas_call | solution.py:48
  485.2 12.2 %all_to_all.92.recv_ref = bf16[32,24,128]{2,1,0:T(8,128)(2,1)S(1)} all-to-all(bf16[32,24,128]{2,1,0:T(8,128)(2,1)S(1)} %broadcast_in_dim.272), channel_id=1, replica_groups=mesh['dp'=4,'fsdp'=8] {'dp','fsdp'}, dimensions={0} | all-to-all | bytes 393216 | tf_op jit(solution)/shard_map/all_to_all | solution.py:136
  499.0 9.0 shard_map.335
  535.7 15.5 %shard_map.336 = (bf16[640,1536]{1,0:T(8,128)(2,1)}, bf16[24,128]{1,0:T(8,128)(2,1)S(1)}, f32[640,256]{1,0:T(8,128)S(1)}, bf16[256,1536]{1,0:T(8,128)(2,1)S(1)},...) custom-call(bf16[32,32,128]{2,1,0:T(8,128)(2,1)S(1)} %all-to-all-don, ...), custom_call_target="tpu_custom_call" | custom-call | tf_op jit(solution)/shard_map/pallas_call | solution.py:48
  579.8 9.1 shard_map.337
  615.6 15.6 %shard_map.338 = (bf16[640,1536]{1,0:T(8,128)(2,1)}, bf16[24,128]{1,0:T(8,128)(2,1)S(1)}, f32[640,256]{1,0:T(8,128)S(1)}, bf16[256,1536]{1,0:T(8,128)(2,1)S(1)},...) custom-call(bf16[32,32,128]{2,1,0:T(8,128)(2,1)S(1)} %all-to-all-don, ...), custom_call_target="tpu_custom_call" | custom-call | tf_op jit(solution)/shard_map/pallas_call | solution.py:48
  657.4 8.2 shard_map.339
  674.1 13.2 %all_to_all.93.recv_ref = bf16[32,24,128]{2,1,0:T(8,128)(2,1)S(1)} all-to-all(bf16[32,24,128]{2,1,0:T(8,128)(2,1)S(1)} %broadcast_in_dim.277), channel_id=1, replica_groups=mesh['dp'=4,'fsdp'=8] {'dp','fsdp'}, dimensions={0} | all-to-all | bytes 393216 | tf_op jit(solution)/shard_map/all_to_all | solution.py:136
  706.4 28.9 %reduce-scatter.18.cloned.1.call-done = bf16[64,1536]{1,0:T(8,128)(2,1)} async-done(((bf16[512,1536]{1,0:T(8,128)(2,1)}), bf16[64,1536]{1,0:T(8,128)(2,1)}) %reduce-scatter.18.cloned.1.call-update) | async-done | bytes 196624 | tf_op jit(solution)/shard_map/reduce_scatter | solution.py:1014
  735.3 34.7 %reduce-scatter.16.cloned.1.call-done = bf16[64,1536]{1,0:T(8,128)(2,1)} async-done(((bf16[512,1536]{1,0:T(8,128)(2,1)}), bf16[64,1536]{1,0:T(8,128)(2,1)}) %reduce-scatter.16.cloned.1.call-update) | async-done | bytes 196624 | tf_op jit(solution)/shard_map/reduce_scatter | solution.py:1014
  770.0 34.5 %reduce-scatter.14.cloned.1.call-done = bf16[64,1536]{1,0:T(8,128)(2,1)} async-done(((bf16[512,1536]{1,0:T(8,128)(2,1)}), bf16[64,1536]{1,0:T(8,128)(2,1)}) %reduce-scatter.14.cloned.1.call-update) | async-done | bytes 196624 | tf_op jit(solution)/shard_map/reduce_scatter | solution.py:1014
  806.6 39.8 %reduce-scatter.20.cloned.1.call-done = bf16[160,1280]{1,0:T(8,128)(2,1)} async-done(((bf16[1280,1280]{1,0:T(8,128)(2,1)}), bf16[160,1280]{1,0:T(8,128)(2,1)}) %reduce-scatter.20.cloned.1.call-update) | async-done | bytes 409616 | tf_op jit(solution)/shard_map/reduce_scatter | solution.py:1014
  851.6 54.0 %all-reduce.17.cloned.1.call-done = (bf16[3,139,192]{2,1,0:T(8,128)(2,1)}, bf16[3,64,1536]{2,1,0:T(8,128)(2,1)}, bf16[160,1280]{1,0:T(8,128)(2,1)}) async-done(((bf16[3,139,192]{2,1,0:T(8,128)(2,1)}, bf16[3,64,1536]{2,1,0:T(8,128)(2,1)}, bf16[160,1280]{1,0:T(8,128)(2,1)}), (bf16[3,139,192]{2,1,0:T(8,128)(2,1)}, bf16[3,64,1536]{2,1,0:T(8,128)(2,1)}, ...) | async-done | bytes 1159568 | tf_op jit(solution)/shard_map/psum | solution.py:1019
  (609 shorter events, 347.9 us)
Async XLA Ops:
  7.2 31.2 %all-gather.13.cloned.1.call-start = ((), (), s32[]{:S(2)}) async-start(), calls=%async_computation.31 | async-start | bytes 1769472 | tf_op jit(solution)/shard_map/all_gather | solution.py:938
  10.5 75.0 %all-gather.9.cloned.1.call-start = ((), (), s32[]{:S(2)}) async-start(), calls=%async_computation.25 | async-start | bytes 3538944 | tf_op jit(solution)/shard_map/all_gather | solution.py:940
  13.6 127.6 %all-gather.15.cloned.1.call-start = ((), (), s32[]{:S(2)}) async-start(), calls=%async_computation.32 | async-start | bytes 1769472 | tf_op jit(solution)/shard_map/all_gather | solution.py:938
  14.4 194.7 %all-gather.17.cloned.1.call-start = ((), (), s32[]{:S(2)}) async-start(), calls=%async_computation.33 | async-start | bytes 1769472 | tf_op jit(solution)/shard_map/all_gather | solution.py:938
  14.9 255.2 %all-gather.11.cloned.1.call-start = ((), (), s32[]{:S(2)}) async-start(), calls=%async_computation.26 | async-start | bytes 3686400 | tf_op jit(solution)/shard_map/all_gather | solution.py:941
  44.0 56.7 %all-to-all-start = ((bf16[32,40,128]{2,1,0:T(8,128)(2,1)}), bf16[32,40,128]{2,1,0:T(8,128)(2,1)S(1)}, u32[]{:S(2)}, u32[]{:S(2)}) async-start(bf16[32,40,128]{2,1,0:T(8,128)(2,1)} %broadcast_in_dim.256), calls=%async_computation | async-start | bytes 655360 | tf_op jit(solution)/shard_map/all_to_all | solution.py:136
  111.2 15.9 %all-to-all-start.1 = ((bf16[32,40,128]{2,1,0:T(8,128)(2,1)}), bf16[32,40,128]{2,1,0:T(8,128)(2,1)}, u32[]{:S(2)}, u32[]{:S(2)}) async-start(bf16[32,40,128]{2,1,0:T(8,128)(2,1)} %broadcast_in_dim.257), calls=%async_computation.1 | async-start | bytes 655360 | tf_op jit(solution)/shard_map/all_to_all | solution.py:136
  136.4 12.2 %all-to-all-start.2 = ((bf16[32,8,128]{2,1,0:T(8,128)(2,1)}), bf16[32,8,128]{2,1,0:T(8,128)(2,1)S(1)}, u32[]{:S(2)}, u32[]{:S(2)}) async-start(bf16[32,8,128]{2,1,0:T(8,128)(2,1)} %broadcast_in_dim.258), calls=%async_computation.2 | async-start | bytes 131072 | tf_op jit(solution)/shard_map/all_to_all | solution.py:136
  156.9 23.1 %all-to-all-start.3 = ((bf16[32,40,128]{2,1,0:T(8,128)(2,1)}), bf16[32,40,128]{2,1,0:T(8,128)(2,1)S(1)}, u32[]{:S(2)}, u32[]{:S(2)}) async-start(bf16[32,40,128]{2,1,0:T(8,128)(2,1)} %broadcast_in_dim.259), calls=%async_computation.3 | async-start | bytes 655360 | tf_op jit(solution)/shard_map/all_to_all | solution.py:136
  224.0 14.9 %all-to-all-start.6 = ((bf16[32,40,128]{2,1,0:T(8,128)(2,1)}), bf16[32,40,128]{2,1,0:T(8,128)(2,1)S(1)}, u32[]{:S(2)}, u32[]{:S(2)}) async-start(bf16[32,40,128]{2,1,0:T(8,128)(2,1)} %broadcast_in_dim.262), calls=%async_computation.6 | async-start | bytes 655360 | tf_op jit(solution)/shard_map/all_to_all | solution.py:136
  286.7 13.0 %all-to-all-start.9 = ((bf16[32,32,128]{2,1,0:T(8,128)(2,1)}), bf16[32,32,128]{2,1,0:T(8,128)(2,1)S(1)}, u32[]{:S(2)}, u32[]{:S(2)}) async-start(bf16[32,32,128]{2,1,0:T(8,128)(2,1)} %broadcast_in_dim.268), calls=%async_computation.9 | async-start | bytes 524288 | tf_op jit(solution)/shard_map/all_to_all | solution.py:136
  318.0 140.6 %all-to-all-start.10 = ((bf16[32,32,128]{2,1,0:T(8,128)(2,1)}), bf16[32,32,128]{2,1,0:T(8,128)(2,1)S(1)}, u32[]{:S(2)}, u32[]{:S(2)}) async-start(bf16[32,32,128]{2,1,0:T(8,128)(2,1)} %broadcast_in_dim.269), calls=%async_computation.10 | async-start | bytes 524288 | tf_op jit(solution)/shard_map/all_to_all | solution.py:136
  320.6 138.0 %all-reduce.15.cloned.1.call-start = ((), (), s32[]{:S(2)}) async-start(), calls=%async_computation.37 | async-start | bytes 1572864 | tf_op jit(solution)/shard_map/psum | solution.py:968
  511.4 14.0 %all-to-all-start.12 = ((bf16[32,32,128]{2,1,0:T(8,128)(2,1)}), bf16[32,32,128]{2,1,0:T(8,128)(2,1)S(1)}, u32[]{:S(2)}, u32[]{:S(2)}) async-start(bf16[32,32,128]{2,1,0:T(8,128)(2,1)} %broadcast_in_dim.273), calls=%async_computation.12 | async-start | bytes 524288 | tf_op jit(solution)/shard_map/all_to_all | solution.py:136
  514.4 188.3 %reduce-scatter.26.cloned.1.call-start = ((), (), s32[]{:S(2)}) async-start(), calls=%async_computation.36 | async-start | bytes 884736
  557.1 14.7 %all-to-all-start.13 = ((bf16[32,24,128]{2,1,0:T(8,128)(2,1)}), bf16[32,24,128]{2,1,0:T(8,128)(2,1)S(1)}, u32[]{:S(2)}, u32[]{:S(2)}) async-start(bf16[32,24,128]{2,1,0:T(8,128)(2,1)} %broadcast_in_dim.274), calls=%async_computation.13 | async-start | bytes 393216 | tf_op jit(solution)/shard_map/all_to_all | solution.py:136
  592.2 13.1 %all-to-all-start.14 = ((bf16[32,32,128]{2,1,0:T(8,128)(2,1)}), bf16[32,32,128]{2,1,0:T(8,128)(2,1)S(1)}, u32[]{:S(2)}, u32[]{:S(2)}) async-start(bf16[32,32,128]{2,1,0:T(8,128)(2,1)} %broadcast_in_dim.275), calls=%async_computation.14 | async-start | bytes 524288 | tf_op jit(solution)/shard_map/all_to_all | solution.py:136
  595.0 108.7 %reduce-scatter.24.cloned.1.call-start = ((), (), s32[]{:S(2)}) async-start(), calls=%async_computation.35 | async-start | bytes 884736
  640.6 64.1 %reduce-scatter.22.cloned.1.call-start = ((), (), s32[]{:S(2)}) async-start(), calls=%async_computation.34 | async-start | bytes 884736
  670.0 65.3 %reduce-scatter.18.cloned.1.call-start = ((), (), s32[]{:S(2)}) async-start(), calls=%async_computation.29 | async-start | bytes 1769472 | tf_op jit(solution)/shard_map/reduce_scatter | solution.py:1014
  671.4 98.6 %reduce-scatter.16.cloned.1.call-start = ((), (), s32[]{:S(2)}) async-start(), calls=%async_computation.28 | async-start | bytes 1769472 | tf_op jit(solution)/shard_map/reduce_scatter | solution.py:1014
  674.0 130.5 %reduce-scatter.14.cloned.1.call-start = ((), (), s32[]{:S(2)}) async-start(), calls=%async_computation.27 | async-start | bytes 1769472 | tf_op jit(solution)/shard_map/reduce_scatter | solution.py:1014
  693.7 152.7 %reduce-scatter.20.cloned.1.call-start = ((), (), s32[]{:S(2)}) async-start(), calls=%async_computation.30 | async-start | bytes 3686400 | tf_op jit(solution)/shard_map/reduce_scatter | solution.py:1014
  697.0 208.6 %all-reduce.17.cloned.1.call-start = ((), (), s32[]{:S(2)}) async-start(), calls=%async_computation.38 | async-start | bytes 2441216 | tf_op jit(solution)/shard_map/psum | solution.py:1019
  (196 other events, 1496.4 us)
Sparse Core Ops, SparseCore 0:
  10.6 27.7 all-gather.12
  40.6 44.8 all-gather.8
  87.7 23.8 all-gather.14
  113.7 25.5 all-gather.16
  141.4 46.1 all-gather.10
  327.2 131.3 all-reduce.14
  525.5 33.1 reduce-scatter.25
  603.1 32.7 reduce-scatter.23
  670.1 30.7 reduce-scatter.21
  703.1 32.1 reduce-scatter.17
  737.6 32.3 reduce-scatter.15
  772.2 32.2 reduce-scatter.13
  806.8 39.5 reduce-scatter.19
  851.2 54.4 all-reduce.16

commit v2 on v1

v2 whole, which is shorter than its diff:
```python
import functools

import jax
import jax.numpy as jnp
from jax import lax
from jax.experimental import pallas as pl
from jax.experimental.pallas import tpu as pltpu
from jax.sharding import PartitionSpec as P

WIDTH = 256
EXPAND = 1536
SQUEEZE = 64
HEAD = 1280
CLASSES = 1000
LOGITS = 1024
EDGE = 4
LAYERS = 3
MAP = 16
SIDE = 142
SIDE_PAD = 144
VECS = 576
HEADCOLS = 1258
HEADPAD = 1280

EPS_BN = 0.001
BETA_ONE = 0.9
BETA_TWO = 0.999
EPS_ADAM = 1e-06
DECAY_RATE = 0.01
RATE_MATRIX = 0.5
RATE_VECTOR = 0.25

BOTH = ("dp", "fsdp")
F32 = jnp.float32
BF16 = jnp.bfloat16
LANE = 128
TILE = 8
ROWS = MAP * TILE
CHUNK = 256
PARTS = CHUNK // LANE
VMEM_BYTES = 48 * 1024 * 1024

NT = (((1,), (1,)), ((), ()))
TN = (((0,), (0,)), ((), ()))


class Refs:
    def __init__(self, names, refs, loads, stores):
        for name, ref in zip(names, refs):
            setattr(self, name, ref)
        self.loads = loads
        self.stores = stores
        self.pending = {}

    def start(self):
        for index, (name, where) in enumerate(self.loads):
            source = getattr(self, name + "_far")
            if where is not None:
                source = source.at[where]
            copy = pltpu.make_async_copy(source, getattr(self, name), self.load_sem.at[index])
            copy.start()
            self.pending[name] = copy

    def wait(self, *names):
        for name in names:
            self.pending.pop(name).wait()

    def send(self, *names):
        for name in names:
            copy = pltpu.make_async_copy(
                getattr(self, name), getattr(self, name + "_far"), self.store_sem.at[self.stores.index(name)]
            )
            copy.start()
            self.pending["out " + name] = copy

    def finish(self):
        for name in list(self.pending):
            self.pending.pop(name).wait()


def shape(dims, dtype=F32):
    return jax.ShapeDtypeStruct(dims, dtype)


def call(kernel, ins, outs, scratch):
    near, far = pl.BlockSpec(memory_space=pltpu.VMEM), pl.BlockSpec(memory_space=pltpu.HBM)
    names, arrays, in_specs, loads, stores, extra = [], [], [], [], [], {}
    for name, (array, place) in ins.items():
        arrays.append(array)
        if isinstance(place, str) and place == "near":
            names.append(name)
            in_specs.append(near)
            continue
        names.append(name + "_far")
        in_specs.append(far)
        where = None if isinstance(place, str) else place
        dims = array.shape
        if where is not None:
            dims = tuple(
                len(range(*part.indices(size))) for part, size in zip(where, array.shape)
            )
            where = tuple(
                pl.ds(part.indices(size)[0], dim) for part, size, dim in zip(where, array.shape, dims)
            )
        loads.append((name, where))
        extra[name] = pltpu.VMEM(dims, array.dtype)
    out_shapes, out_specs, out_names = [], [], []
    for name, (struct, place) in outs.items():
        if place in ("near", "both"):
            names.append(name)
            out_names.append(name)
            out_shapes.append(struct)
            out_specs.append(near)
        if place in ("far", "both"):
            names.append(name + "_far")
            out_names.append(name + "_far" if place == "both" else name)
            out_shapes.append(struct)
            out_specs.append(far)
            stores.append(name)
            if place == "far":
                extra[name] = pltpu.VMEM(struct.shape, struct.dtype)
    extra.update(scratch)
    extra["load_sem"] = pltpu.SemaphoreType.DMA((max(len(loads), 1),))
    extra["store_sem"] = pltpu.SemaphoreType.DMA((max(len(stores), 1),))

    def flat(*refs):
        kernel(Refs(names + list(extra), refs, loads, stores))

    results = pl.pallas_call(
        flat,
        out_shape=out_shapes,
        in_specs=in_specs,
        out_specs=out_specs,
        scratch_shapes=list(extra.values()),
        compiler_params=pltpu.CompilerParams(vmem_limit_bytes=VMEM_BYTES),
    )(*arrays)
    return dict(zip(out_names, results))


def dot(left, right):
    return jnp.dot(left, right, preferred_element_type=F32)


def dot_nt(left, right):
    return lax.dot_general(left, right, NT, preferred_element_type=F32)


def dot_tn(left, right):
    return lax.dot_general(left, right, TN, preferred_element_type=F32)


def halves(value):
    high = value.astype(BF16)
    return high, (value - high.astype(F32)).astype(BF16)


def stacked(value):
    return jnp.concatenate(halves(value), axis=0)


def folded(value):
    count = value.shape[0] // 2
    return value[:count] + value[count:]


def sigmoid(value):
    return 0.5 * jnp.tanh(0.5 * value) + 0.5


def chunk_at(index, size=CHUNK):
    return pl.ds(pl.multiple_of(index * size, size), size)


def tile_rows(tile):
    return slice(tile * ROWS, (tile + 1) * ROWS)


def tile_images(tile):
    return slice(tile * TILE, (tile + 1) * TILE)


def as_tile(block):
    return block.reshape(MAP, TILE, LANE)


def spread(rows, first, count):
    return jnp.concatenate([rows[first + k : first + k + 1, :] for k in range(count)], axis=1)


def fold(vectors, rows):
    pieces = [
        vector[:, k * LANE : (k + 1) * LANE]
        for vector in vectors
        for k in range(vector.shape[1] // LANE)
    ]
    if rows > len(pieces):
        pieces.append(jnp.zeros((rows - len(pieces), LANE), F32))
    return jnp.concatenate(pieces, axis=0)


def column_sum(value):
    return jnp.sum(value, axis=0, keepdims=True)


def slice_rows(devices):
    return max(1, WIDTH // devices)


def write_alike(pay_ref, rows):
    pay_ref[...] = jnp.broadcast_to(rows.astype(BF16)[None], pay_ref.shape)


def write_with_slices(pay_ref, rows, matrix):
    devices = pay_ref.shape[0]
    part = slice_rows(devices)
    first = rows.shape[0]
    low = rows.astype(BF16)
    for device in range(devices):
        own = matrix[device * part : (device + 1) * part, :]
        block = jnp.concatenate([own[:, :LANE], own[:, LANE:]], axis=0)
        if 2 * part < 16:
            block = jnp.concatenate([block, jnp.zeros((16 - 2 * part, LANE), F32)], axis=0)
        pay_ref[device, 0:first, :] = low
        pay_ref[device, first : first + 16, :] = block.astype(BF16)


def read_matrix(recv_ref, first):
    devices, rows = recv_ref.shape[:2]
    part = slice_rows(devices)
    if part == TILE:
        values = recv_ref[...].astype(F32)
        left = values[:, first : first + part].reshape(WIDTH, LANE)
        right = values[:, first + part : first + 2 * part].reshape(WIDTH, LANE)
        return jnp.concatenate([left, right], axis=1)
    flat = recv_ref[...].reshape(devices * rows, LANE)
    row = lax.broadcasted_iota(jnp.int32, (WIDTH, devices * rows), 0)
    column = lax.broadcasted_iota(jnp.int32, (WIDTH, devices * rows), 1)
    source = row // part * rows + first + row % part
    left = dot(jnp.where(column == source, 1.0, 0.0).astype(BF16), flat)
    right = dot(jnp.where(column == source + part, 1.0, 0.0).astype(BF16), flat)
    return jnp.concatenate([left, right], axis=1)


def moment_rows(columns):
    return -(-3 * columns // LANE // 8) * 8


def centred(total, squares, count):
    return jnp.maximum(squares - total * total / count, 0.0)


def pack_moments(total, squares, count):
    mean = total / count
    high = mean.astype(BF16).astype(F32)
    return fold([high, mean - high, centred(total, squares, count)], moment_rows(total.shape[1]))


def read_moments(recv_ref, columns, count):
    groups = columns // LANE
    devices = recv_ref.shape[0]
    parts = recv_ref[...].astype(F32)
    means = parts[:, :groups] + parts[:, groups : 2 * groups]
    mean = jnp.sum(means, axis=0) / devices
    apart = means - mean[None]
    spread_sum = jnp.sum(parts[:, 2 * groups : 3 * groups], axis=0) / count
    variance = (spread_sum + jnp.sum(apart * apart, axis=0)) / devices
    return spread(mean, 0, groups), lax.rsqrt(spread(variance, 0, groups) + EPS_BN)


def pack_product_moments(x_ref, total, squares, count):
    sums = column_sum(x_ref[...].astype(F32))
    high = sums.astype(BF16).astype(F32)
    return fold([high, sums - high, centred(total, squares, count)], 16)


def read_product_moments(recv_ref, weights, transposed, columns, count):
    devices, rows = recv_ref.shape[:2]
    values = recv_ref[...]
    flat = values.reshape(devices * rows, LANE)
    row = lax.broadcasted_iota(jnp.int32, (devices, devices * rows), 0)
    column = lax.broadcasted_iota(jnp.int32, (devices, devices * rows), 1) - row * rows
    left = dot(jnp.where((column == 0) | (column == 2), 1.0, 0.0).astype(BF16), flat)
    right = dot(jnp.where((column == 1) | (column == 3), 1.0, 0.0).astype(BF16), flat)
    sums = stacked(jnp.concatenate([left, right], axis=1) / count)
    means = folded(dot_nt(sums, weights) if transposed else dot(sums, weights))
    mean = column_sum(means) / devices
    apart = means - mean
    squares = jnp.sum(values.astype(F32), axis=0)
    variance = (spread(squares, 4, columns // LANE) / count + column_sum(apart * apart)) / devices
    return mean, lax.rsqrt(variance + EPS_BN)


def read_sums(recv_ref):
    return jnp.sum(recv_ref[...].astype(F32), axis=0)


def keep_norm(norm_ref, mean, inverse, gain, bias):
    scale = inverse * gain
    norm_ref[0:1, :] = mean
    norm_ref[1:2, :] = inverse
    norm_ref[2:3, :] = scale
    norm_ref[3:4, :] = bias - mean * scale
    norm_ref[4:8, :] = jnp.zeros((4, norm_ref.shape[1]), F32)


def product_sums(x_ref, w_ref, transposed, h_ref, stat_ref):
    def step(index, carry):
        at = chunk_at(index)
        if transposed:
            h_ref[...] = dot_nt(x_ref[...], w_ref[at, :])
        else:
            h_ref[...] = dot(x_ref[...], w_ref[:, at])
        hidden = h_ref[...]
        stat_ref[0:1, at] = column_sum(hidden)
        stat_ref[1:2, at] = column_sum(hidden * hidden)
        return carry

    lax.fori_loop(0, stat_ref.shape[1] // CHUNK, step, 0)


def mix_kernel(r):
    count = r.images.shape[0]
    pixels = r.images[...]
    row = lax.broadcasted_iota(jnp.int32, (ROWS, count), 0)
    column = lax.broadcasted_iota(jnp.int32, (ROWS, count), 1)
    place = lax.shift_right_logical(row, 3)
    inside = jnp.bitwise_and(row, 7)
    pair = r.mix[...].astype(F32)
    mixing = pair[:, 0:1] / (pair[:, 0:1] + pair[:, 1:2])
    for tile in range(count // ROWS):
        near = tile_images(tile)
        other = jnp.concatenate([r.partner[near, :]] * MAP, axis=0)
        weight = jnp.concatenate([mixing[near, :]] * MAP, axis=0)
        own_hot = jnp.where(column == (tile * TILE + inside) * MAP + place, 1.0, 0.0).astype(BF16)
        other_hot = jnp.where(column == other * MAP + place, 1.0, 0.0).astype(BF16)
        mixed = weight * dot(own_hot, pixels) + (1.0 - weight) * dot(other_hot, pixels)
        r.x[tile_rows(tile), :] = mixed
    r.xb[...] = r.x[...].astype(BF16)
    r.send("x", "xb")
    r.finish()


def mix(images, partner, mix_pair):
    dims = images.shape
    return call(
        mix_kernel,
        dict(images=(images, "near"), partner=(partner, "near"), mix=(mix_pair, "near")),
        dict(x=(shape(dims), "far"), xb=(shape(dims, BF16), "both")),
        {},
    )


def first_kernel(r):
    count = r.xb.shape[0]
    r.start()
    r.wait("w")
    product_sums(r.xb, r.w, False, r.h, r.stat)
    write_alike(r.pay, pack_product_moments(r.xb, r.stat[0:1, :], r.stat[1:2, :], count))


def first(xb, mats, devices):
    count = xb.shape[0]
    return call(
        first_kernel,
        dict(xb=(xb, "near"), w=(mats, (slice(0, WIDTH), slice(None)))),
        dict(pay=(shape((devices, 16, LANE), BF16), "near")),
        dict(h=pltpu.VMEM((count, CHUNK), F32), stat=pltpu.VMEM((8, EXPAND), F32)),
    )


def tap_terms():
    for row in range(EDGE):
        for col in range(EDGE):
            for row_shift in range(3):
                for col_shift in range(3):
                    from_row, from_col = row + row_shift - 1, col + col_shift - 1
                    if 0 <= from_row < EDGE and 0 <= from_col < EDGE:
                        yield EDGE * row + col, 3 * row_shift + col_shift, EDGE * from_row + from_col


TERMS = list(tap_terms())


def spatial_kernel(r):
    count = r.xb.shape[0]
    r.start()
    r.wait("side", "w")
    rows = r.side[...].astype(F32)
    r.taps[0:9, :] = rows[0:9, :]
    mean, inverse = read_product_moments(r.recv, r.w[...], False, EXPAND, count)
    keep_norm(r.norm, mean, inverse, rows[10:11, :], rows[11:12, :])
    r.send("norm")
    if r.recv.shape[1] > 16:
        r.cross[...] = jnp.sum(r.recv[...].astype(F32)[:, 16:32], axis=0)

    def step(index, carry):
        at_chunk = chunk_at(index)
        r.h[...] = dot(r.xb[...], r.w[:, at_chunk])
        for part in range(PARTS):
            lanes = chunk_at(index * PARTS + part, LANE)
            taps = [jnp.broadcast_to(r.taps[k : k + 1, lanes], (TILE, LANE)) for k in range(9)]
            scale_row = r.norm[2:3, lanes]
            shift_row = r.norm[3:4, lanes]

            def tile_step(tile, sums):
                at = chunk_at(tile, ROWS)
                pre = r.h[at, part * LANE : (part + 1) * LANE] * scale_row + shift_row
                active = as_tile(pre * sigmoid(pre))
                result = [None] * MAP
                for target, tap, source in TERMS:
                    term = active[source] * taps[tap]
                    result[target] = term if result[target] is None else result[target] + term
                total, squares = sums
                for value in result:
                    total = total + value
                    squares = squares + value * value
                r.d[at, lanes] = jnp.concatenate(result, axis=0).astype(BF16)
                return total, squares

            zero = jnp.zeros((TILE, LANE), F32)
            total, squares = lax.fori_loop(0, count // ROWS, tile_step, (zero, zero))
            r.stat[0:1, lanes] = column_sum(total)
            r.stat[1:2, lanes] = column_sum(squares)
        pltpu.make_async_copy(r.d.at[:, at_chunk], r.d_far.at[:, at_chunk], r.part_sem.at[index]).start()
        return carry

    lax.fori_loop(0, EXPAND // CHUNK, step, 0)
    write_alike(r.pay, pack_moments(r.stat[0:1, :], r.stat[1:2, :], count))
    for index in range(EXPAND // CHUNK):
        at_chunk = pl.ds(index * CHUNK, CHUNK)
        pltpu.make_async_copy(r.d.at[:, at_chunk], r.d_far.at[:, at_chunk], r.part_sem.at[index]).wait()
    r.finish()


def spatial(xb, mats, side, recv):
    count = xb.shape[0]
    devices = recv.shape[0]
    outs = dict(
        d=(shape((count, EXPAND), BF16), "both"),
        pay=(shape((devices, moment_rows(EXPAND), LANE), BF16), "near"),
        norm=(shape((8, EXPAND)), "far"),
    )
    if recv.shape[1] > 16:
        outs["cross"] = (shape((16, LANE)), "near")
    return call(
        spatial_kernel,
        dict(
            recv=(recv, "near"),
            xb=(xb, "near"),
            side=(side, (slice(2 * SQUEEZE, SIDE_PAD), slice(None))),
            w=(mats, (slice(0, WIDTH), slice(None))),
        ),
        outs,
        dict(
            h=pltpu.VMEM((count, CHUNK), F32),
            taps=pltpu.VMEM((16, EXPAND), F32),
            stat=pltpu.VMEM((8, EXPAND), F32),
            part_sem=pltpu.SemaphoreType.DMA((EXPAND // CHUNK,)),
        ),
    )


def project_kernel(with_cross, r):
    count = r.d.shape[0]
    tiles = count // ROWS
    r.start()
    mean, inverse = read_moments(r.recv, EXPAND, count)
    r.wait("side")
    rows = r.side[2 * SQUEEZE : SIDE_PAD, :].astype(F32)
    keep_norm(r.norm, mean, inverse, rows[12:13, :], rows[13:14, :])
    r.send("norm")

    def activate(index, carry):
        lanes = chunk_at(index, LANE)
        scale_row = r.norm[2:3, lanes]
        shift_row = r.norm[3:4, lanes]
        for tile in range(tiles):
            at = tile_rows(tile)
            pre = r.d[at, lanes].astype(F32) * scale_row + shift_row
            active = pre * sigmoid(pre)
            r.a[at, lanes] = active
            r.pooled[tile_images(tile), lanes] = jnp.sum(as_tile(active), axis=0) / MAP
        return carry

    lax.fori_loop(0, EXPAND // LANE, activate, 0)
    r.send("pooled")
    before = folded(dot_nt(stacked(r.pooled[...]), r.side[0:SQUEEZE, :])) + r.vec[2:3, :SQUEEZE]
    r.squeeze[...] = before
    r.send("squeeze")
    opened = folded(dot(stacked(before * sigmoid(before)), r.side[SQUEEZE : 2 * SQUEEZE, :]))
    r.excite[...] = sigmoid(opened + rows[9:10, :])
    r.send("excite")

    def gate(index, carry):
        lanes = chunk_at(index, LANE)
        for tile in range(tiles):
            at = tile_rows(tile)
            scaled = as_tile(r.a[at, lanes]) * r.excite[tile_images(tile), lanes][None]
            r.y[at, lanes] = scaled.reshape(ROWS, LANE).astype(BF16)
        return carry

    lax.fori_loop(0, EXPAND // LANE, gate, 0)
    r.wait("w")
    projected = dot_nt(r.y[...], r.w[...])
    r.p[...] = projected
    moments = pack_moments(column_sum(projected), column_sum(projected * projected), count)
    if with_cross:
        moments = jnp.concatenate([moments, r.cross[...]], axis=0)
    write_alike(r.pay, moments)
    r.finish()


def project(d, mats, side, vec, recv, cross):
    count = d.shape[0]
    images = count // MAP
    devices = recv.shape[0]
    ins = dict(
        recv=(recv, "near"),
        d=(d, "near"),
        vec=(vec, "near"),
        side=(side, "far"),
        w=(mats, (slice(WIDTH, 2 * WIDTH), slice(None))),
    )
    rows = moment_rows(WIDTH)
    if cross is not None:
        ins["cross"] = (cross, "near")
        rows += 16
    return call(
        functools.partial(project_kernel, cross is not None),
        ins,
        dict(
            p=(shape((count, WIDTH)), "near"),
            pay=(shape((devices, rows, LANE), BF16), "near"),
            norm=(shape((8, EXPAND)), "far"),
            pooled=(shape((images, EXPAND)), "far"),
            excite=(shape((images, EXPAND)), "far"),
            squeeze=(shape((images, SQUEEZE)), "far"),
        ),
        dict(a=pltpu.VMEM((count, EXPAND), F32), y=pltpu.VMEM((count, EXPAND), BF16)),
    )


def residual_kernel(transposed, with_cross, r):
    count = r.p.shape[0]
    r.start()
    mean, inverse = read_moments(r.recv, WIDTH, count)
    keep_norm(r.norm, mean, inverse, r.vec[0:1, :], r.vec[1:2, :])
    if with_cross:
        r.cross[...] = read_matrix(r.recv, moment_rows(WIDTH))
        r.send("cross")
    normed = (r.p[...] - mean) * inverse
    r.normed[...] = normed
    r.wait("before")
    result = r.before[...] + (normed * r.vec[0:1, :] + r.vec[1:2, :])
    r.x[...] = result
    r.xb[...] = result.astype(BF16)
    r.send("norm", "normed", "x", "xb")
    cross = dot_tn(normed.astype(BF16), r.xb[...])
    r.wait("w")
    product_sums(r.xb, r.w, transposed, r.h, r.stat)
    moments = pack_product_moments(r.xb, r.stat[0:1, :], r.stat[1:2, :], count)
    write_with_slices(r.pay, moments, cross)
    r.finish()


def residual(x, p, vec, recv, weights, transposed):
    count = x.shape[0]
    devices = recv.shape[0]
    with_cross = recv.shape[1] > moment_rows(WIDTH)
    columns = HEAD if transposed else EXPAND
    where = (slice(0, HEAD), slice(0, WIDTH)) if transposed else (slice(0, WIDTH), slice(None))
    outs = dict(
        x=(shape((count, WIDTH)), "far"),
        xb=(shape((count, WIDTH), BF16), "both"),
        normed=(shape((count, WIDTH)), "far"),
        pay=(shape((devices, 32, LANE), BF16), "near"),
        norm=(shape((8, WIDTH)), "far"),
    )
    if with_cross:
        outs["cross"] = (shape((WIDTH, WIDTH)), "far")
    return call(
        functools.partial(residual_kernel, transposed, with_cross),
        dict(
            recv=(recv, "near"), p=(p, "near"), vec=(vec, "near"), before=(x, "far"), w=(weights, where)
        ),
        outs,
        dict(h=pltpu.VMEM((count, CHUNK), F32), stat=pltpu.VMEM((8, columns), F32)),
    )


def head_rows(last_columns):
    pick_row = lax.broadcasted_iota(jnp.int32, (TILE, LANE), 0)
    pick_col = lax.broadcasted_iota(jnp.int32, (TILE, LANE), 1)
    first_col = WIDTH + CLASSES - (HEADPAD - LANE)
    pick = jnp.where((pick_col == pick_row + first_col) & (pick_row < 2), 1.0, 0.0).astype(BF16)
    return dot_nt(pick, last_columns)


def head_kernel(image_count, r):
    count = r.xb.shape[0]
    tiles = count // ROWS
    images = count // MAP
    r.start()
    r.wait("w")
    mean, inverse = read_product_moments(r.recv, r.w[...], True, HEAD, count)
    cross = jnp.sum(r.recv[...].astype(F32)[:, 16:32], axis=0)
    r.wait("classifier")
    gain_bias = head_rows(r.classifier[:, LOGITS - LANE :])
    keep_norm(r.norm, mean, inverse, gain_bias[0:1, :], gain_bias[1:2, :])
    r.send("norm")

    def features(index, carry):
        at_chunk = chunk_at(index)
        r.h[:, at_chunk] = dot_nt(r.xb[...], r.w[at_chunk, :])
        for part in range(PARTS):
            lanes = chunk_at(index * PARTS + part, LANE)
            scale_row = r.norm[2:3, lanes]
            shift_row = r.norm[3:4, lanes]
            for tile in range(tiles):
                pre = r.h[tile_rows(tile), lanes] * scale_row + shift_row
                active = as_tile(pre * sigmoid(pre))
                r.f[tile_images(tile), lanes] = jnp.sum(active, axis=0) / MAP
        return carry

    lax.fori_loop(0, HEAD // CHUNK, features, 0)
    features_low = r.f[...].astype(BF16)
    classifier = r.classifier[...]
    ids = lax.broadcasted_iota(jnp.int32, (images, LOGITS), 1)
    logits = dot(features_low, classifier) + r.bias[...]
    logits = jnp.where(ids < CLASSES, logits, -1e30)
    row_max = jnp.max(logits, axis=1, keepdims=True)
    log_total = row_max + jnp.log(jnp.sum(jnp.exp(logits - row_max), axis=1, keepdims=True))
    pair = r.mix[...].astype(F32)
    mixing = pair[:, 0:1] / (pair[:, 0:1] + pair[:, 1:2])
    people = lax.broadcasted_iota(jnp.int32, (images, images), 1)
    label_row = jnp.broadcast_to(r.label_row[...].astype(F32), (images, images))
    partner_label = jnp.sum(
        jnp.where(people == r.partner[...], label_row, 0.0), axis=1, keepdims=True
    ).astype(jnp.int32)
    own_hot = jnp.where(ids == r.label_col[...], 1.0, 0.0)
    other_hot = jnp.where(ids == partner_label, 1.0, 0.0)
    own_logit = jnp.sum(own_hot * logits, axis=1, keepdims=True)
    other_logit = jnp.sum(other_hot * logits, axis=1, keepdims=True)
    loss = column_sum(mixing * (log_total - own_logit) + (1.0 - mixing) * (log_total - other_logit))
    grad_logits = (
        jnp.exp(logits - log_total) - mixing * own_hot - (1.0 - mixing) * other_hot
    ) / image_count
    grad_low = grad_logits.astype(BF16)
    r.grad_fc[...] = dot_tn(features_low, grad_low).astype(BF16)
    r.send("grad_fc")
    r.f[...] = dot_nt(grad_low, classifier) / MAP
    bias_sum = column_sum(grad_logits)
    bias_ids = lax.broadcasted_iota(jnp.int32, (1, LOGITS), 1)
    loss_high = loss.astype(BF16).astype(F32)
    bias_sum = jnp.where(bias_ids == CLASSES, loss_high, bias_sum)
    bias_sum = jnp.where(bias_ids == CLASSES + 1, loss - loss_high, bias_sum)

    def back(index, carry):
        lanes = chunk_at(index, LANE)
        scale_row = r.norm[2:3, lanes]
        shift_row = r.norm[3:4, lanes]
        mean_row = r.norm[0:1, lanes]
        total = jnp.zeros((TILE, LANE), F32)
        weighted = jnp.zeros((TILE, LANE), F32)
        for tile in range(tiles):
            at = tile_rows(tile)
            hidden = r.h[at, lanes]
            pre = hidden * scale_row + shift_row
            gate = sigmoid(pre)
            slope = as_tile(gate * (1.0 + pre * (1.0 - gate)))
            grad = slope * r.f[tile_images(tile), lanes][None]
            total = total + jnp.sum(grad, axis=0)
            weighted = weighted + jnp.sum(grad * as_tile(hidden - mean_row), axis=0)
            flat = grad.reshape(ROWS, LANE)
            r.dz[at, lanes] = flat.astype(BF16)
            r.q[at, lanes] = (flat * scale_row).astype(BF16)
        r.stat[0:1, lanes] = column_sum(total)
        r.stat[1:2, lanes] = column_sum(weighted)
        return carry

    lax.fori_loop(0, HEAD // LANE, back, 0)
    below = dot(r.q[...], r.w[...])
    r.wait("normed")
    rows = fold(
        [
            r.stat[0:1, :], r.stat[1:2, :] * inverse,
            column_sum(below), column_sum(below * r.normed[...]), bias_sum,
        ],
        32,
    )
    write_alike(r.pay, jnp.concatenate([rows, cross], axis=0))
    r.finish()


def head(xb, head_full, bias, label_col, label_row, partner, mix_pair, normed, recv, image_count):
    count = xb.shape[0]
    images = count // MAP
    devices = recv.shape[0]
    return call(
        functools.partial(head_kernel, image_count),
        dict(
            recv=(recv, "near"),
            xb=(xb, "near"),
            bias=(bias, "near"),
            label_col=(label_col, "near"),
            label_row=(label_row, "near"),
            partner=(partner, "near"),
            mix=(mix_pair, "near"),
            w=(head_full, (slice(0, HEAD), slice(0, WIDTH))),
            classifier=(head_full, (slice(0, HEAD), slice(WIDTH, HEADPAD))),
            normed=(normed, "far"),
        ),
        dict(
            dz=(shape((count, HEAD), BF16), "near"),
            pay=(shape((devices, 48, LANE), BF16), "near"),
            norm=(shape((8, HEAD)), "far"),
            grad_fc=(shape((HEAD, LOGITS), BF16), "far"),
        ),
        dict(
            h=pltpu.VMEM((count, HEAD), F32),
            f=pltpu.VMEM((images, HEAD), F32),
            q=pltpu.VMEM((count, HEAD), BF16),
            stat=pltpu.VMEM((8, HEAD), F32),
        ),
    )


def product_back(is_head, row_count, sums, columns, r):
    groups = columns // LANE
    sum_bias = spread(sums, 0, groups)
    sum_gain = spread(sums, groups, groups)
    r.glob[0:1, :] = sum_gain
    r.glob[1:2, :] = sum_bias
    r.glob[2:8, :] = jnp.zeros((6, columns), F32)
    r.send("glob")
    r.wait("unorm", "xb", "w")
    mean = r.unorm[0:1, :]
    scale = r.unorm[2:3, :]
    slant = scale * r.unorm[1:2, :] * (sum_gain / row_count)
    r.coef[0:1, :columns] = slant
    r.coef[1:2, :columns] = mean * slant - scale * (sum_bias / row_count)
    r.xt[...] = r.xb[...].T
    count = r.xb.shape[0]

    def step(index, carry):
        at = chunk_at(index)
        if is_head:
            r.h[...] = dot_nt(r.xb[...], r.w[at, :])
        else:
            r.h[...] = dot(r.xb[...], r.w[:, at])
        grad = r.dz[:, at].astype(F32) * r.unorm[2:3, at] - r.h[...] * r.coef[0:1, at] + r.coef[1:2, at]
        low = grad.astype(BF16)
        r.dh[0:count, at] = low
        if is_head:
            r.grad_w[at, :] = dot_tn(low, r.xb[...]).astype(r.grad_w.dtype)
        else:
            r.grad_w[:, at] = dot(r.xt[...], low).astype(r.grad_w.dtype)
        return carry

    lax.fori_loop(0, columns // CHUNK, step, 0)
    return scale * sum_bias, slant


def owner_blocks(r, owners, row_of_owner, taps):
    rows_dev = 2 * WIDTH // owners
    width = EXPAND // owners
    vec_width = VECS // owners
    chunks = EXPAND // CHUNK
    squeeze_sums = jnp.concatenate([r.squeeze_sum[...], jnp.zeros((1, VECS - LANE), F32)], axis=1)
    for owner in range(owners):
        at = slice(owner * width, (owner + 1) * width)
        squeeze_row = squeeze_sums[:, owner * vec_width : (owner + 1) * vec_width]
        squeeze_row = jnp.concatenate([squeeze_row, jnp.zeros((1, width - vec_width), F32)], axis=1)
        pieces = [r.excite_sum[:, at], squeeze_row]
        pieces.append(taps[0:9, at] if taps is not None else jnp.zeros((9, width), F32))
        pieces.append(jnp.zeros((5, width), F32))
        first_row = chunks * rows_dev
        r.grads[owner, first_row : first_row + 2 * SQUEEZE, 0:width] = r.rx[:, at].astype(BF16)
        last_row = first_row + 2 * SQUEEZE
        r.grads[owner, last_row : last_row + 16, 0:width] = jnp.concatenate(pieces, axis=0).astype(BF16)


def gate_kernel(is_head, row_count, owners, r):
    columns = HEAD if is_head else EXPAND
    groups = columns // LANE
    count = r.xb.shape[0]
    tiles = count // ROWS
    rows_dev = 2 * WIDTH // owners
    r.start()
    sums = read_sums(r.recv)
    bias_pull, slant = product_back(is_head, row_count, sums, columns, r)
    if is_head:
        r.send("grad_w")
        weights = r.w[...].astype(F32)
        column = lax.broadcasted_iota(jnp.int32, (1, WIDTH), 1)
        high, low = halves(jnp.broadcast_to(bias_pull, (TILE, columns)))
        pull = column_sum(dot(high, r.w[...]) + dot(low, r.w[...])) / TILE
        turned = jnp.broadcast_to(slant, (LANE, columns)).T
        slanted = (weights * jnp.concatenate([turned, turned], axis=1)).astype(BF16)
        square = dot_tn(slanted, r.w[...])
        stream = dot(r.dh[0:count, :columns], r.w[...])
        cross = read_matrix(r.recv, 32)
    else:
        r.dh[count : count + WIDTH, :] = (r.w[...].astype(F32) * slant).astype(BF16)
        high, low = halves(bias_pull)
        r.dh[count + WIDTH :, :] = jnp.concatenate(
            [high.astype(F32), low.astype(F32), jnp.zeros((14, columns), F32)], axis=0
        ).astype(BF16)
        product = dot_nt(r.dh[...], r.w[...])
        square = product[count : count + WIDTH]
        pull = column_sum(product[count + WIDTH : count + WIDTH + 2])
        stream = r.stream_in[...] + product[0:count]
        r.wait("cross")
        cross = r.cross[...]
    r.stream[...] = stream
    sum_bias = spread(sums, 2 * groups, WIDTH // LANE) - pull
    corrected = column_sum(cross.T * square)
    sum_gain = spread(sums, 2 * groups + WIDTH // LANE, WIDTH // LANE) - corrected
    r.glob3[0:1, :] = sum_gain
    r.glob3[1:2, :] = sum_bias
    if is_head:
        first_row = 2 * groups + 2 * WIDTH // LANE
        r.glob3[2:6, :] = jnp.concatenate(
            [spread(sums, first_row + PARTS * k, PARTS) for k in range(LOGITS // WIDTH)], axis=0
        )
    else:
        r.glob3[2:6, :] = jnp.zeros((4, WIDTH), F32)
    r.glob3[6:8, :] = jnp.zeros((2, WIDTH), F32)
    r.send("glob3")
    r.wait("norm3", "normed")
    grad_p = r.norm3[2:3, :] * (
        stream - sum_bias / row_count - r.normed[...] * (sum_gain / row_count)
    )
    r.gp[...] = grad_p.astype(BF16)
    r.gt[...] = r.gp[...].T
    r.wait("wp", "d", "norm2", "excite")
    half = owners // 2

    def first(index, carry):
        at_chunk = chunk_at(index)
        r.h[...] = dot(r.gp[...], r.wp[:, at_chunk])
        for part in range(PARTS):
            lanes = chunk_at(index * PARTS + part, LANE)
            scale_row = r.norm2[2:3, lanes]
            shift_row = r.norm2[3:4, lanes]
            for tile in range(tiles):
                at = tile_rows(tile)
                near = tile_images(tile)
                pre = r.d[at, lanes].astype(F32) * scale_row + shift_row
                gate = sigmoid(pre)
                active = pre * gate
                slope = gate + active - active * gate
                grad = r.h[at, part * LANE : (part + 1) * LANE]
                factor = r.excite[near, lanes]
                r.ge[near, lanes] = jnp.sum(as_tile(grad * active), axis=0)
                r.y[at, lanes] = (as_tile(active) * factor[None]).reshape(ROWS, LANE).astype(BF16)
                r.slope[at, lanes] = slope
                r.u[at, lanes] = (as_tile(grad * slope) * factor[None]).reshape(ROWS, LANE)
        grad_p_chunk = dot(r.gt[...], r.y[:, at_chunk])
        place = pl.ds(pl.multiple_of(index * rows_dev, rows_dev), rows_dev)
        for owner in range(half):
            cut = slice(owner * rows_dev, (owner + 1) * rows_dev)
            r.grads[half + owner, place, :] = grad_p_chunk[cut, :].astype(BF16)
            if is_head:
                r.grads[owner, place, :] = jnp.zeros((rows_dev, CHUNK), BF16)
            else:
                r.grads[owner, place, :] = r.grad_w[cut, at_chunk]
        return carry

    lax.fori_loop(0, EXPAND // CHUNK, first, 0)
    r.wait("pooled", "squeeze", "side")
    excite = r.excite[...]
    grad_gate = r.ge[...] * excite * (1.0 - excite)
    before = r.squeeze[...]
    opened = sigmoid(before)
    squeezed = before * opened
    reduce_mat = r.side[0:SQUEEZE, :]
    excite_mat = r.side[SQUEEZE:, :]
    gate_high, gate_low = halves(grad_gate)
    grad_squeezed = folded(dot_nt(jnp.concatenate([gate_high, gate_low], axis=0), excite_mat))
    grad_pre = grad_squeezed * (opened * (1.0 + before * (1.0 - opened)))
    r.pool[...] = folded(dot(stacked(grad_pre), reduce_mat)) / MAP

    def second(index, carry):
        lanes = chunk_at(index, LANE)
        mean_row = r.norm2[0:1, lanes]
        total = jnp.zeros((TILE, LANE), F32)
        weighted = jnp.zeros((TILE, LANE), F32)
        for tile in range(tiles):
            at = tile_rows(tile)
            pool = r.pool[tile_images(tile), lanes]
            grad = as_tile(r.u[at, lanes]) + as_tile(r.slope[at, lanes]) * pool[None]
            total = total + jnp.sum(grad, axis=0)
            weighted = weighted + jnp.sum(
                grad * as_tile(r.d[at, lanes].astype(F32) - mean_row), axis=0
            )
            r.dz2[at, lanes] = grad.reshape(ROWS, LANE).astype(BF16)
        r.stat[0:1, lanes] = column_sum(total)
        r.stat[1:2, lanes] = column_sum(weighted)
        return carry

    lax.fori_loop(0, EXPAND // LANE, second, 0)
    write_alike(r.pay, fold([r.stat[0:1, :], r.stat[1:2, :] * r.norm2[1:2, :]], 24))
    squeezed_high, squeezed_low = halves(squeezed)
    pre_high, pre_low = halves(grad_pre)
    pooled_high, pooled_low = halves(r.pooled[...])
    r.rx[SQUEEZE:, :] = dot_tn(
        jnp.concatenate([squeezed_high, squeezed_low, squeezed_high], axis=0),
        jnp.concatenate([gate_high, gate_high, gate_low], axis=0),
    )
    r.rx[0:SQUEEZE, :] = dot_tn(
        jnp.concatenate([pre_high, pre_low, pre_high], axis=0),
        jnp.concatenate([pooled_high, pooled_high, pooled_low], axis=0),
    )
    r.excite_sum[...] = column_sum(grad_gate)
    r.squeeze_sum[...] = jnp.concatenate(
        [column_sum(grad_pre), jnp.zeros((1, LANE - SQUEEZE), F32)], axis=1
    )
    taps = None
    if not is_head:
        r.wait("taps")
        taps = r.taps[...]
    owner_blocks(r, owners, half, taps)
    r.send("grads")
    r.finish()


def gate_back(is_head, row_count, owners, recv, upper, cross, stream, lower):
    count = upper["xb_far"].shape[0]
    images = count // MAP
    devices = recv.shape[0]
    columns = HEAD if is_head else EXPAND
    block = EXPAND // CHUNK * (2 * WIDTH // owners) + 2 * SQUEEZE + 16
    where = (slice(0, HEAD), slice(0, WIDTH)) if is_head else (slice(0, WIDTH), slice(None))
    ins = dict(
        recv=(recv, "near"),
        dz=(upper["dz"], "near"),
        unorm=(upper["norm"], "far"),
        xb=(upper["xb_far"], "far"),
        w=(upper["weights"], where),
        norm3=(lower["norm3"], "far"),
        normed=(lower["normed"], "far"),
        norm2=(lower["norm2"], "far"),
        wp=(lower["mats"], (slice(WIDTH, 2 * WIDTH), slice(None))),
        d=(lower["d_far"], "far"),
        excite=(lower["excite"], "far"),
        pooled=(lower["pooled"], "far"),
        squeeze=(lower["squeeze"], "far"),
        side=(lower["side"], (slice(0, 2 * SQUEEZE), slice(None))),
    )
    outs = dict(
        dz2=(shape((count, EXPAND), BF16), "near"),
        pay=(shape((devices, 24, LANE), BF16), "near"),
        stream=(shape((count, WIDTH)), "near"),
        grads=(shape((owners, block, CHUNK), BF16), "far"),
        glob=(shape((8, columns)), "far"),
        glob3=(shape((8, WIDTH)), "far"),
    )
    scratch = dict(
        xt=pltpu.VMEM((WIDTH, count), BF16),
        h=pltpu.VMEM((count, CHUNK), F32),
        coef=pltpu.VMEM((8, EXPAND), F32),
        dh=pltpu.VMEM((count + WIDTH + 16, columns), BF16),
        u=pltpu.VMEM((count, EXPAND), F32),
        slope=pltpu.VMEM((count, EXPAND), F32),
        y=pltpu.VMEM((count, EXPAND), BF16),
        gp=pltpu.VMEM((count, WIDTH), BF16),
        gt=pltpu.VMEM((WIDTH, count), BF16),
        ge=pltpu.VMEM((images, EXPAND), F32),
        pool=pltpu.VMEM((images, EXPAND), F32),
        rx=pltpu.VMEM((2 * SQUEEZE, EXPAND), F32),
        excite_sum=pltpu.VMEM((1, EXPAND), F32),
        squeeze_sum=pltpu.VMEM((1, LANE), F32),
        stat=pltpu.VMEM((8, EXPAND), F32),
    )
    if is_head:
        outs["grad_w"] = (shape((HEAD, WIDTH), BF16), "far")
    else:
        ins["cross"] = (cross, "far")
        ins["stream_in"] = (stream, "near")
        ins["taps"] = (upper["taps"], "far")
        scratch["grad_w"] = pltpu.VMEM((WIDTH, EXPAND), BF16)
    return call(functools.partial(gate_kernel, is_head, row_count, owners), ins, outs, scratch)


def tap_kernel(is_first, row_count, r):
    count = r.dz2.shape[0]
    groups = EXPAND // LANE
    r.start()
    sums = read_sums(r.recv)
    sum_bias = spread(sums, 0, groups)
    sum_gain = spread(sums, groups, groups)
    r.glob[0:1, :] = sum_gain
    r.glob[1:2, :] = sum_bias
    r.glob[2:8, :] = jnp.zeros((6, EXPAND), F32)
    r.send("glob")
    r.wait("side", "norm2")
    scale2 = r.norm2[2:3, :]
    slant2 = scale2 * r.norm2[1:2, :] * (sum_gain / row_count)
    r.coef[0:9, :] = r.side[...].astype(F32)[0:9, :]
    r.coef[9:10, :] = slant2
    r.coef[10:11, :] = r.norm2[0:1, :] * slant2 - scale2 * (sum_bias / row_count)
    r.wait("norm1", "xb", "w", "d")

    def step(index, carry):
        at_chunk = chunk_at(index)
        r.h[...] = dot(r.xb[...], r.w[:, at_chunk])
        for part in range(PARTS):
            lanes = chunk_at(index * PARTS + part, LANE)
            near = slice(part * LANE, (part + 1) * LANE)
            taps = [jnp.broadcast_to(r.coef[k : k + 1, lanes], (TILE, LANE)) for k in range(9)]

            def tile_step(tile, sums_in):
                at = chunk_at(tile, ROWS)
                grad_d = as_tile(
                    r.dz2[at, lanes].astype(F32) * r.norm2[2:3, lanes]
                    - r.d[at, lanes].astype(F32) * r.coef[9:10, lanes]
                    + r.coef[10:11, lanes]
                )
                hidden = r.h[at, near]
                pre = hidden * r.norm1[2:3, lanes] + r.norm1[3:4, lanes]
                gate = sigmoid(pre)
                flat = pre * gate
                active = as_tile(flat)
                slope = as_tile(gate + flat - flat * gate)
                apart = as_tile(hidden - r.norm1[0:1, lanes])
                grad_a = [None] * MAP
                tap_sums = [None] * 9
                for target, tap, source in TERMS:
                    term = grad_d[target] * taps[tap]
                    grad_a[source] = term if grad_a[source] is None else grad_a[source] + term
                    term = grad_d[target] * active[source]
                    tap_sums[tap] = term if tap_sums[tap] is None else tap_sums[tap] + term
                total, weighted = sums_in[9], sums_in[10]
                grads = []
                for place in range(MAP):
                    grad = grad_a[place] * slope[place]
                    total = total + grad
                    weighted = weighted + grad * apart[place]
                    grads.append(grad)
                grad = jnp.concatenate(grads, axis=0)
                r.dz[at, lanes] = grad.astype(BF16)
                if not is_first:
                    r.q[at, lanes] = (grad * r.norm1[2:3, lanes]).astype(BF16)
                return (*[sums_in[k] + tap_sums[k] for k in range(9)], total, weighted)

            zero = jnp.zeros((TILE, LANE), F32)
            result = lax.fori_loop(0, count // ROWS, tile_step, (zero,) * 11)
            for k in range(9):
                r.taps[k : k + 1, lanes] = column_sum(result[k])
            r.stat[0:1, lanes] = column_sum(result[9])
            r.stat[1:2, lanes] = column_sum(result[10])
        return carry

    lax.fori_loop(0, EXPAND // CHUNK, step, 0)
    r.taps[9:16, :] = jnp.zeros((7, EXPAND), F32)
    r.send("taps")
    vectors = [r.stat[0:1, :], r.stat[1:2, :] * r.norm1[1:2, :]]
    if not is_first:
        below = r.stream[...] + dot_nt(r.q[...], r.w[...])
        r.wait("normed")
        vectors.append(column_sum(below))
        vectors.append(column_sum(below * r.normed[...]))
    write_alike(r.pay, fold(vectors, r.pay.shape[1]))
    r.finish()


def tap_back(is_first, row_count, recv, dz2, layer, stream, below):
    count = dz2.shape[0]
    devices = recv.shape[0]
    ins = dict(
        recv=(recv, "near"),
        dz2=(dz2, "near"),
        side=(layer["side"], (slice(2 * SQUEEZE, SIDE_PAD), slice(None))),
        norm2=(layer["norm2"], "far"),
        norm1=(layer["norm1"], "far"),
        xb=(layer["xb_far"], "far"),
        w=(layer["mats"], (slice(0, WIDTH), slice(None))),
        d=(layer["d_far"], "far"),
    )
    scratch = dict(
        h=pltpu.VMEM((count, CHUNK), F32),
        coef=pltpu.VMEM((16, EXPAND), F32),
        stat=pltpu.VMEM((8, EXPAND), F32),
    )
    if not is_first:
        ins["stream"] = (stream, "near")
        ins["normed"] = (below["normed"], "far")
        scratch["q"] = pltpu.VMEM((count, EXPAND), BF16)
    return call(
        functools.partial(tap_kernel, is_first, row_count),
        ins,
        dict(
            dz=(shape((count, EXPAND), BF16), "near"),
            pay=(shape((devices, 24 if is_first else 32, LANE), BF16), "near"),
            taps=(shape((16, EXPAND)), "far"),
            glob=(shape((8, EXPAND)), "far"),
        ),
        scratch,
    )


def last_kernel(row_count, replicas, owners, r):
    r.start()
    product_back(False, row_count, read_sums(r.recv), EXPAND, r)
    half = owners // 2
    part = slice_rows(replicas * owners)
    rows_dev = 2 * WIDTH // owners
    chunks = EXPAND // CHUNK
    pad = r.grads.shape[1] - chunks * part
    for replica in range(replicas):
        for owner in range(owners):
            first_row = rows_dev * (owner % half) + (2 * replica + owner // half) * part
            own = r.grad_w[first_row : first_row + part, :]
            block = jnp.concatenate(
                [own[:, k * CHUNK : (k + 1) * CHUNK] for k in range(chunks)]
                + ([jnp.zeros((pad, CHUNK), F32)] if pad else []),
                axis=0,
            )
            r.grads[replica * owners + owner, :, :] = block.astype(BF16)
    r.finish()


def last_back(row_count, replicas, owners, recv, layer, dz):
    count = dz.shape[0]
    devices = recv.shape[0]
    block = -(-EXPAND // CHUNK * slice_rows(devices) // 16) * 16
    return call(
        functools.partial(last_kernel, row_count, replicas, owners),
        dict(
            recv=(recv, "near"),
            dz=(dz, "near"),
            unorm=(layer["norm1"], "far"),
            xb=(layer["xb_far"], "far"),
            w=(layer["mats"], (slice(0, WIDTH), slice(None))),
        ),
        dict(
            grads=(shape((devices, block, CHUNK), BF16), "near"),
            glob=(shape((8, EXPAND)), "far"),
        ),
        dict(
            xt=pltpu.VMEM((WIDTH, count), BF16),
            h=pltpu.VMEM((count, CHUNK), F32),
            coef=pltpu.VMEM((8, EXPAND), F32),
            dh=pltpu.VMEM((count, EXPAND), BF16),
            grad_w=pltpu.VMEM((WIDTH, EXPAND), F32),
        ),
    )


def lamb_moments(weight, moment_one, moment_two, gradient, decay_mask, step_float):
    first_new = BETA_ONE * moment_one + (1.0 - BETA_ONE) * gradient
    second_new = BETA_TWO * moment_two + (1.0 - BETA_TWO) * gradient * gradient
    corrected = (
        first_new
        / (1.0 - BETA_ONE**step_float)
        / (jnp.sqrt(second_new / (1.0 - BETA_TWO**step_float)) + EPS_ADAM)
    )
    return (first_new, second_new, corrected + DECAY_RATE * decay_mask * weight)


def group_sums(mats, side, head_shard, row_ids):
    rows = jnp.sum(mats * mats, axis=2)
    is_expand = (row_ids < WIDTH)[None, :]
    side_rows = jnp.sum(side * side, axis=2)
    head_cols = jnp.sum(head_shard * head_shard, axis=0)
    per_layer = jnp.stack(
        [
            jnp.sum(jnp.where(is_expand, rows, 0.0), axis=1),
            jnp.sum(jnp.where(is_expand, 0.0, rows), axis=1),
            jnp.sum(side_rows[:, :9], axis=1),
            jnp.sum(side_rows[:, 9 : 9 + SQUEEZE], axis=1),
            jnp.sum(side_rows[:, 9 + SQUEEZE : 9 + 2 * SQUEEZE], axis=1),
        ],
        axis=1,
    )
    tail = jnp.stack([jnp.sum(head_cols[:WIDTH]), jnp.sum(head_cols[WIDTH : WIDTH + CLASSES])])
    return jnp.concatenate([per_layer.reshape(-1), tail])


def rate_maps(trust_ratio, row_ids):
    groups = trust_ratio[: 5 * LAYERS].reshape(LAYERS, 5)
    mats_rate = RATE_MATRIX * jnp.where(row_ids[None, :] < WIDTH, groups[:, 0:1], groups[:, 1:2])
    side_ids = jnp.arange(SIDE)[None, :]
    side_rate = jnp.where(
        side_ids < 9,
        RATE_MATRIX * groups[:, 2:3],
        jnp.where(
            side_ids < 9 + SQUEEZE,
            RATE_MATRIX * groups[:, 3:4],
            jnp.where(side_ids < 9 + 2 * SQUEEZE, RATE_MATRIX * groups[:, 4:5], RATE_VECTOR),
        ),
    )
    col_ids = jnp.arange(HEADCOLS)
    head_rate = jnp.where(
        col_ids < WIDTH,
        RATE_MATRIX * trust_ratio[5 * LAYERS],
        jnp.where(
            col_ids < WIDTH + CLASSES, RATE_MATRIX * trust_ratio[5 * LAYERS + 1], RATE_VECTOR
        ),
    )
    return (mats_rate, side_rate, head_rate)


def exchange(payload):
    return lax.all_to_all(payload, BOTH, 0, 0)


def spread_over(array, axis):
    copies = jnp.broadcast_to(array[None], (lax.axis_size(axis), *array.shape))
    return lax.all_to_all(copies, axis, 0, 0)


def replica_sum(array):
    return jnp.sum(spread_over(array, "dp").astype(F32), axis=0)


def body(
    images, partner, mix_pair, labels, step,
    layer_mats, layer_side, layer_vecs, head_mat, fc_bias,
    mats_first, mats_second, side_first, side_second, vecs_first, vecs_second,
    head_first, head_second, bias_first, bias_second,
):
    local_images = images.shape[0]
    owners = lax.axis_size("fsdp")
    replicas = lax.axis_size("dp")
    devices = owners * replicas
    image_count = float(local_images * devices)
    count = local_images * MAP
    row_count = float(count * devices)
    mine = lax.axis_index("fsdp")
    side_width = layer_side.shape[2]
    vec_width = layer_vecs.shape[1]
    rows_dev = layer_mats.shape[1]
    half = owners // 2

    side_low = jnp.concatenate(
        [
            layer_side[:, 9 : 9 + 2 * SQUEEZE],
            layer_side[:, :9],
            layer_side[:, 9 + 2 * SQUEEZE :],
            jnp.pad(layer_vecs, ((0, 0), (0, side_width - vec_width)))[:, None, :],
            jnp.zeros((LAYERS, 1, side_width), F32),
        ],
        axis=1,
    ).astype(BF16)
    mats_all = [
        lax.all_gather(layer_mats[k].astype(BF16), "fsdp", axis=0, tiled=True) for k in range(LAYERS)
    ]
    side_zero = lax.all_gather(side_low[0], "fsdp", axis=1, tiled=True)
    side_room = -(-side_width // CHUNK) * CHUNK
    side_rest = lax.all_gather(
        jnp.pad(side_low[1:], ((0, 0), (0, 0), (0, side_room - side_width))), "fsdp", axis=0
    )
    side_rest = jnp.moveaxis(side_rest[..., :side_width], 0, 2).reshape(LAYERS - 1, SIDE_PAD, EXPAND)
    side_all = [side_zero, side_rest[0], side_rest[1]]
    head_full = lax.all_gather(
        jnp.pad(head_mat, ((0, 0), (0, HEADPAD - HEADCOLS))).astype(BF16), "fsdp", axis=0, tiled=True
    )

    def vec_rows(side):
        vec = side[SIDE].reshape(owners, side_width)[:, :vec_width].reshape(VECS).astype(F32)
        squeeze_bias = jnp.pad(vec[:SQUEEZE], (0, WIDTH - SQUEEZE))
        rows = jnp.stack([vec[SQUEEZE : SQUEEZE + WIDTH], vec[SQUEEZE + WIDTH :], squeeze_bias])
        return jnp.pad(rows, ((0, 5), (0, 0)))

    vecs_all = [vec_rows(side) for side in side_all]

    partner_col = partner[:, None]
    layers = []
    crosses = []
    entry = mix(images.reshape(count, WIDTH), partner_col, mix_pair)
    x, xb, xb_far = entry["x"], entry["xb"], entry["xb_far"]
    pay = first(xb, mats_all[0], devices)["pay"]
    for k in range(LAYERS):
        mats, side, vec = mats_all[k], side_all[k], vecs_all[k]
        one = spatial(xb, mats, side, exchange(pay))
        two = project(one["d"], mats, side, vec, exchange(one["pay"]), one.get("cross"))
        last = k == LAYERS - 1
        three = residual(
            x, two["p"], vec, exchange(two["pay"]), head_full if last else mats_all[k + 1], last
        )
        if "cross" in three:
            crosses.append(three["cross"])
        layers.append(
            dict(
                xb_far=xb_far, d_far=one["d_far"], norm1=one["norm"], norm2=two["norm"],
                pooled=two["pooled"], excite=two["excite"], squeeze=two["squeeze"],
                norm3=three["norm"], normed=three["normed"], mats=mats, weights=mats, side=side,
            )
        )
        x, xb, xb_far, pay = three["x"], three["xb"], three["xb_far"], three["pay"]
    top = head(
        xb, head_full, jnp.pad(fc_bias, (0, LOGITS - CLASSES))[None], labels[:, None], labels[None, :],
        partner_col, mix_pair, layers[-1]["normed"], exchange(pay), image_count,
    )

    def to_owner(blocks):
        rows = blocks.shape[0] * blocks.shape[1]
        return lax.psum_scatter(
            blocks.reshape(rows, blocks.shape[2]), "fsdp", scatter_dimension=0, tiled=True
        )

    upper = dict(xb_far=xb_far, weights=head_full, dz=top["dz"], norm=top["norm"])
    pay = top["pay"]
    stream = None
    globs = [{} for _ in range(LAYERS)]
    blocks = [None] * LAYERS
    for k in reversed(range(LAYERS)):
        layer = layers[k]
        is_head = k == LAYERS - 1
        gate = gate_back(
            is_head, row_count, owners, exchange(pay), upper,
            None if is_head else crosses[k], stream, layer,
        )
        stream = gate["stream"]
        globs[k]["three"] = gate["glob3"]
        blocks[k] = gate["grads"]
        if is_head:
            head_glob, bias_loss = gate["glob"], gate["glob3"][2:6].reshape(LOGITS)
            grad_head = jnp.concatenate([gate["grad_w"], top["grad_fc"]], axis=1)
            shard_head = to_owner(grad_head.reshape(owners, -1, HEADPAD))
        else:
            globs[k + 1]["one"] = gate["glob"]
        tap = tap_back(
            k == 0, row_count, exchange(gate["pay"]), gate["dz2"], layer, stream, layers[max(k - 1, 0)]
        )
        globs[k]["two"] = tap["glob"]
        pay = tap["pay"]
        upper = dict(
            xb_far=layer["xb_far"], weights=layer["mats"], dz=tap["dz"], norm=layer["norm1"], taps=tap["taps"]
        )
    late_taps = jnp.moveaxis(tap["taps"][:9].astype(BF16).reshape(9, owners, side_width), 1, 0)
    late_taps = jnp.broadcast_to(late_taps[None], (replicas, *late_taps.shape))
    late_taps = exchange(late_taps.reshape(devices, 9, side_width))
    final = last_back(row_count, replicas, owners, exchange(pay), layers[0], tap["dz"])
    globs[0]["one"] = final["glob"]
    late_taps = jnp.sum(late_taps.astype(F32), axis=0)

    shards = [None] * LAYERS
    room = blocks[0].shape[1]
    pair = replica_sum(to_owner(jnp.concatenate([blocks[2], blocks[1]], axis=1)))
    shards[2], shards[1] = pair[:room], pair[room:]
    shards[0] = replica_sum(to_owner(blocks[0]))
    shard_head = replica_sum(shard_head)

    part = slice_rows(devices)
    chunks = EXPAND // CHUNK
    late = jnp.sum(exchange(final["grads"]).astype(F32), axis=0).astype(BF16)
    other = lax.ppermute(late, "fsdp", [(half + k, k) for k in range(half)])
    late = spread_over(jnp.stack([late, other]), "dp")[:, :, : chunks * part]
    late = jnp.moveaxis(late.reshape(replicas, 2, chunks, part, CHUNK), 2, 3)
    late = late.reshape(rows_dev, EXPAND).astype(F32)

    def mats_of(shard):
        rows = shard[: chunks * rows_dev].reshape(chunks, rows_dev, CHUNK)
        return jnp.moveaxis(rows, 0, 1).reshape(rows_dev, EXPAND)

    from_mats = [late] + [mats_of(shard) for shard in shards]
    owns_expand = mine < half
    grad_mats = jnp.stack(
        [jnp.where(owns_expand, from_mats[k], from_mats[k + 1]) for k in range(LAYERS)]
    )

    def own_columns(vector, width):
        return lax.dynamic_slice_in_dim(vector, mine * width, width, axis=-1)

    first_row = chunks * rows_dev
    last_row = first_row + 2 * SQUEEZE
    vec_ids = mine * vec_width + jnp.arange(vec_width)
    side_list, vec_list = [], []
    for k in range(LAYERS):
        shard = shards[k][:, :side_width]
        taps = late_taps if k == 0 else shards[k - 1][last_row + 2 : last_row + 11, :side_width]
        norms_part = own_columns(
            jnp.concatenate([globs[k]["one"][0:2], globs[k]["two"][0:2]], axis=0), side_width
        )
        side_list.append(
            jnp.concatenate([taps, shard[first_row : last_row + 1], norms_part], axis=0)
        )
        outer = globs[k]["three"]
        outer = own_columns(
            jnp.concatenate([jnp.zeros((SQUEEZE,), F32), outer[0], outer[1]]), vec_width
        )
        vec_list.append(jnp.where(vec_ids < SQUEEZE, shard[last_row + 1, :vec_width], outer))
    grad_side = jnp.stack(side_list)
    grad_vecs = jnp.stack(vec_list)
    head_tail = own_columns(head_glob[0:2], head_mat.shape[0]).T
    grad_head = jnp.concatenate([shard_head[:, : WIDTH + CLASSES], head_tail], axis=1)
    grad_bias = bias_loss[:CLASSES]
    loss_value = (bias_loss[CLASSES] + bias_loss[CLASSES + 1]) / image_count

    step_float = step[0].astype(F32)
    side_decay = (jnp.arange(SIDE) < 9 + 2 * SQUEEZE).astype(F32)[None, :, None]
    head_decay = (jnp.arange(HEADCOLS) < WIDTH + CLASSES).astype(F32)[None, :]
    mats_moment, mats_square, mats_dir = lamb_moments(
        layer_mats, mats_first, mats_second, grad_mats, 1.0, step_float
    )
    side_moment, side_square, side_dir = lamb_moments(
        layer_side, side_first, side_second, grad_side, side_decay, step_float
    )
    vecs_moment, vecs_square, vecs_dir = lamb_moments(
        layer_vecs, vecs_first, vecs_second, grad_vecs, 0.0, step_float
    )
    head_moment, head_square, head_dir = lamb_moments(
        head_mat, head_first, head_second, grad_head, head_decay, step_float
    )
    bias_moment, bias_square, bias_dir = lamb_moments(
        fc_bias, bias_first, bias_second, grad_bias, 0.0, step_float
    )
    row_ids = mine * rows_dev + jnp.arange(rows_dev)
    squares = jnp.stack(
        [
            group_sums(layer_mats, layer_side, head_mat, row_ids),
            group_sums(mats_dir, side_dir, head_dir, row_ids),
        ]
    )
    norms = jnp.sqrt(jnp.sum(spread_over(squares, "fsdp"), axis=0))
    mats_rate, side_rate, head_rate = rate_maps(norms[0] / norms[1], row_ids)
    mats_new = layer_mats - mats_rate[:, :, None] * mats_dir
    side_new = layer_side - side_rate[:, :, None] * side_dir
    vecs_new = layer_vecs - RATE_VECTOR * vecs_dir
    head_new = head_mat - head_rate[None, :] * head_dir
    bias_new = fc_bias - RATE_VECTOR * bias_dir
    return (
        loss_value,
        mats_new, mats_moment, mats_square,
        side_new, side_moment, side_square,
        vecs_new, vecs_moment, vecs_square,
        head_new, head_moment, head_square,
        bias_new, bias_moment, bias_square,
        norms,
    )


def solution(mesh):
    rows, columns = P(None, "fsdp", None), P(None, None, "fsdp")
    vecs, heads = P(None, "fsdp"), P("fsdp", None)
    return jax.shard_map(
        body,
        mesh=mesh,
        in_specs=(
            P(BOTH, None, None), P(BOTH), P(BOTH, None), P(BOTH), P(),
            rows, columns, vecs, heads, P(),
            rows, rows, columns, columns, vecs, vecs, heads, heads, P(), P(),
        ),
        out_specs=(
            P(),
            rows, rows, rows,
            columns, columns, columns,
            vecs, vecs, vecs,
            heads, heads, heads,
            P(), P(), P(), P(),
        ),
        check_vma=False,
    )
```

time: 958 us -> 703 us (0.73)
  waiting for transfers between devices: 478 us -> 188 us
  local copies, waits for them, and re-layouts: 186 us -> 111 us
  blocking collectives: 54.3 us -> 122 us
  Pallas kernels: 120 us -> 156 us
    psum x2 -> x0, waiting for transfers between devices: 191 us -> none  [the longest x1 137 us: body(): crosses.append(lax.psum(cross, BOTH))]
    reduce_scatter x4 -> x3, waiting for transfers between devices: 138 us -> 0.02 us  [to_owner(): lax.psum_scatter(blocks.reshape(rows, blocks.shape[2]), 'fsdp', scatter_d...]
    unnamed x399 -> x283, local copies, waits for them, and re-layouts: 136 us -> 54.1 us
    all_to_all x14 -> x17, waiting for transfers between devices: 87.2 us -> 162 us  [the longest x12 111 us: exchange(): return lax.all_to_all(payload, BOTH, 0, 0)]
    all_gather x1, waiting for transfers between devices: 37.3 us -> 0.02 us  [body(): lax.all_gather(jnp.pad(side_low[1:], ((0, 0), (0, 0), (0, side_room - sid...]
    pallas_call x18 -> x19, Pallas kernels: 120 us -> 156 us  [call(): pl.pallas_call(flat, out_shape=out_shapes, in_specs=in_specs, out_specs=o...]
    all_to_all x4 -> x7, blocking collectives: 54.3 us -> 89.1 us  [exchange(): return lax.all_to_all(payload, BOTH, 0, 0)]
    all_gather x0 -> x1, blocking collectives: none -> 33 us  [body(): side_zero = lax.all_gather(side_low[0], 'fsdp', axis=1, tiled=True)]
  transfers between devices with their start and end apart: 28 -> 26, of which waited for: 19 -> 17; matrix products, arithmetic and copies ran while one was open for 9% -> 10% of each run, Pallas kernels for 9% -> 9%
where the time goes in v2:
time: 703 us; the launch traced here: 691 us
  waiting for transfers between devices  188 us (27%)
  Pallas kernels  156 us (22%)
  blocking collectives  122 us (17%)
  local copies, waits for them, and re-layouts  111 us (16%)
  starting transfers between devices  57.3 us (8%)
  other arithmetic  35.6 us (5%)
  between operations  20.7 us (3%)
    pallas_call x19, Pallas kernels, call(): pl.pallas_call(flat, out_shape=out_shapes, in_specs=in_specs, out_specs=o...  156 us
    all_to_all x12, waiting for transfers between devices, exchange(): return lax.all_to_all(payload, BOTH, 0, 0)  111 us
    all_to_all x7, blocking collectives, exchange(): return lax.all_to_all(payload, BOTH, 0, 0)  89.1 us
    unnamed x283, local copies, waits for them, and re-layouts  54.1 us
    all_to_all x5, waiting for transfers between devices, spread_over(): return lax.all_to_all(copies, axis, 0, 0)  50.4 us
    all_to_all x12, starting transfers between devices, exchange(): return lax.all_to_all(payload, BOTH, 0, 0)  37.6 us
    all_gather x1, blocking collectives, body(): side_zero = lax.all_gather(side_low[0], 'fsdp', axis=1, tiled=True)  33 us
    slice x2, local copies, waits for them, and re-layouts, vec_rows(): side[SIDE].reshape(owners, side_width)[:, :vec_width].reshape(VECS)  23.8 us
  transfers between devices with their start and end apart: 26, of which 17 were waited for; matrix products, arithmetic and copies ran while one was open for 10% of the time, Pallas kernels for 9%

profile of v2, /device:TPU:0, one launch (start us, length us, event | category | flops | bytes accessed | tf_op | source)
XLA Modules:
  0.0 691.4 jit_solution(5053713011307740678)
XLA Ops:
  19.7 18.6 %all-gather.13.cloned.1.call-done = bf16[1,512,1536]{2,1,0:T(8,128)(2,1)} async-done(((bf16[1,64,1536]{2,1,0:T(8,128)(2,1)}), bf16[1,512,1536]{2,1,0:T(8,128)(2,1)}) %all-gather.13.cloned.1.call-update) | async-done | bytes 1572880 | tf_op jit(solution)/shard_map/all_gather | solution.py:1248
  46.7 33.0 %all-gather.1 = bf16[1,144,1536]{1,0,2:T(2,128)(2,1)} all-gather(bf16[1,144,192]{1,0,2:T(2,128)(2,1)S(1)} %slice.350), channel_id=3, replica_groups=mesh['dp'=4,'fsdp'=8] {'fsdp'}, dimensions={2}, use_global_device_ids=true | all-gather | bytes 497664 | tf_op jit(solution)/shard_map/all_gather | solution.py:1250
  95.3 22.9 %slice_reduce_fusion = bf16[1536]{0:T(1024)(128)(2,1)S(1)} fusion(bf16[1,144,1536]{1,0,2:T(2,128)(2,1)} %all-gather.1), kind=kLoop, calls=%fused_computation.22 | loop fusion | bytes 6144 | tf_op jit(solution)/shard_map/slice | solution.py:1262
  159.4 11.8 %all-to-all-done.3.refs_0_ = bf16[32,32,128]{2,1,0:T(8,128)(2,1)S(1)} async-done(((bf16[32,32,128]{2,1,0:T(8,128)(2,1)}), bf16[32,32,128]{2,1,0:T(8,128)(2,1)S(1)}, u32[]{:S(2)}, u32[]{:S(2)}) %all-to-all-start.3) | async-done | bytes 262176 | tf_op jit(solution)/shard_map/all_to_all | solution.py:1206
  182.5 11.9 %all-to-all-done.4.refs_0_ = bf16[32,40,128]{2,1,0:T(8,128)(2,1)S(1)} async-done(((bf16[32,40,128]{2,1,0:T(8,128)(2,1)}), bf16[32,40,128]{2,1,0:T(8,128)(2,1)S(1)}, u32[]{:S(2)}, u32[]{:S(2)}) %all-to-all-start.4) | async-done | bytes 327712 | tf_op jit(solution)/shard_map/all_to_all | solution.py:1206
  249.9 12.1 %all-to-all-done.7.refs_0_ = bf16[32,40,128]{2,1,0:T(8,128)(2,1)S(1)} async-done(((bf16[32,40,128]{2,1,0:T(8,128)(2,1)}), bf16[32,40,128]{2,1,0:T(8,128)(2,1)S(1)}, u32[]{:S(2)}, u32[]{:S(2)}) %all-to-all-start.7) | async-done | bytes 327712 | tf_op jit(solution)/shard_map/all_to_all | solution.py:1206
  306.9 11.5 %shard_map.334 = (bf16[640,1280]{1,0:T(8,128)(2,1)S(1)}, bf16[32,48,128]{2,1,0:T(8,128)(2,1)S(1)}, f32[8,1280]{1,0:T(8,128)S(1)}, bf16[1280,1024]{1,0:T(8,128)(2,1)S(1)}) custom-call(bf16[32,32,128]{2,1,0:T(8,128)(2,1)} %all-to-all-done.9.refs_0_, bf16[640,256]{1,0:T(8,128)(2,1)S(1)} %copy-done.47, f32[1,1024]{1,0:T(1,128)S(1)} %bitcast.145, ...), custom_call_target="tpu_custom_call" | custom-call | tf_op jit(solution)/shard_map/pallas_call | solution.py:129
  321.1 15.8 %all_to_all.120.refs_0_ = bf16[32,48,128]{2,1,0:T(8,128)(2,1)S(1)} all-to-all(bf16[32,48,128]{2,1,0:T(8,128)(2,1)S(1)} %get-tuple-element.132), channel_id=1, replica_groups=mesh['dp'=4,'fsdp'=8] {'dp','fsdp'}, dimensions={0} | all-to-all | bytes 786432 | tf_op jit(solution)/shard_map/all_to_all | solution.py:1206
  336.9 16.6 %shard_map.335 = (bf16[640,1536]{1,0:T(8,128)(2,1)}, bf16[32,24,128]{2,1,0:T(8,128)(2,1)S(1)}, f32[640,256]{1,0:T(8,128)S(1)}, bf16[8,528,256]{2,1,0:T(8,128)(2,...) custom-call(bf16[32,48,128]{2,1,0:T(8,128)(2,1)S(1)} %all_to_all.120.refs_0_, ...), custom_call_target="tpu_custom_call" | custom-call | tf_op jit(solution)/shard_map/pallas_call | solution.py:129
  354.1 10.8 %all_to_all.121.refs_0_ = bf16[32,24,128]{2,1,0:T(8,128)(2,1)S(1)} all-to-all(bf16[32,24,128]{2,1,0:T(8,128)(2,1)S(1)} %get-tuple-element.143), channel_id=1, replica_groups=mesh['dp'=4,'fsdp'=8] {'dp','fsdp'}, dimensions={0} | all-to-all | bytes 393216 | tf_op jit(solution)/shard_map/all_to_all | solution.py:1206
  364.9 14.1 %shard_map.336 = (bf16[640,1536]{1,0:T(8,128)(2,1)}, bf16[32,32,128]{2,1,0:T(8,128)(2,1)S(1)}, f32[16,1536]{1,0:T(8,128)S(1)}, f32[8,1536]{1,0:T(8,128)S(1)}) custom-call(bf16[32,24,128]{2,1,0:T(8,128)(2,1)S(1)} %all_to_all.121.refs_0_, bf16[640,1536]{1,0:T(8,128)(2,1)} %get-tuple-element.144.refs_1_, ...), custom_call_target="tpu_custom_call" | custom-call | tf_op jit(solution)/shard_map/pallas_call | solution.py:129
  379.1 12.9 %all_to_all.122.refs_0_ = bf16[32,32,128]{2,1,0:T(8,128)(2,1)S(1)} all-to-all(bf16[32,32,128]{2,1,0:T(8,128)(2,1)S(1)} %get-tuple-element.149), channel_id=1, replica_groups=mesh['dp'=4,'fsdp'=8] {'dp','fsdp'}, dimensions={0} | all-to-all | bytes 524288 | tf_op jit(solution)/shard_map/all_to_all | solution.py:1206
  392.1 17.1 %shard_map.337 = (bf16[640,1536]{1,0:T(8,128)(2,1)}, bf16[32,24,128]{2,1,0:T(8,128)(2,1)S(1)}, f32[640,256]{1,0:T(8,128)S(1)}, bf16[8,528,256]{2,1,0:T(8,128)(2,...) custom-call(bf16[32,32,128]{2,1,0:T(8,128)(2,1)S(1)} %all_to_all.122.refs_0_, ...), custom_call_target="tpu_custom_call" | custom-call | tf_op jit(solution)/shard_map/pallas_call | solution.py:129
  409.2 11.3 %all_to_all.123.refs_0_ = bf16[32,24,128]{2,1,0:T(8,128)(2,1)S(1)} all-to-all(bf16[32,24,128]{2,1,0:T(8,128)(2,1)S(1)} %get-tuple-element.159), channel_id=1, replica_groups=mesh['dp'=4,'fsdp'=8] {'dp','fsdp'}, dimensions={0} | all-to-all | bytes 393216 | tf_op jit(solution)/shard_map/all_to_all | solution.py:1206
  420.5 14.1 %shard_map.338 = (bf16[640,1536]{1,0:T(8,128)(2,1)}, bf16[32,32,128]{2,1,0:T(8,128)(2,1)S(1)}, f32[16,1536]{1,0:T(8,128)S(1)}, f32[8,1536]{1,0:T(8,128)S(1)}) custom-call(bf16[32,24,128]{2,1,0:T(8,128)(2,1)S(1)} %all_to_all.123.refs_0_, bf16[640,1536]{1,0:T(8,128)(2,1)} %get-tuple-element.160.refs_1_, bf16[144,1536]{1,0:T(8,128)(2,1)S(1)} %copy-done.11, ...), custom_call_target="tpu_custom_call" | custom-call | tf_op jit(solution)/shard_map/pallas_call | solution.py:129
  435.3 12.9 %all_to_all.124.refs_0_ = bf16[32,32,128]{2,1,0:T(8,128)(2,1)S(1)} all-to-all(bf16[32,32,128]{2,1,0:T(8,128)(2,1)S(1)} %get-tuple-element.165), channel_id=1, replica_groups=mesh['dp'=4,'fsdp'=8] {'dp','fsdp'}, dimensions={0} | all-to-all | bytes 524288 | tf_op jit(solution)/shard_map/all_to_all | solution.py:1206
  449.3 17.3 %shard_map.339 = (bf16[640,1536]{1,0:T(8,128)(2,1)}, bf16[32,24,128]{2,1,0:T(8,128)(2,1)S(1)}, f32[640,256]{1,0:T(8,128)}, bf16[8,528,256]{2,1,0:T(8,128)(2,1)},...) custom-call(bf16[32,32,128]{2,1,0:T(8,128)(2,1)S(1)} %all_to_all.124.refs_0_, bf16[640,1536]{1,0:T(8,128)(2,1)} %get-tuple-element.166.refs_1_, ...), custom_call_target="tpu_custom_call" | custom-call | tf_op jit(solution)/shard_map/pallas_call | solution.py:129
  475.5 13.2 %all_to_all.125.refs_0_ = bf16[32,24,128]{2,1,0:T(8,128)(2,1)S(1)} all-to-all(bf16[32,24,128]{2,1,0:T(8,128)(2,1)S(1)} %get-tuple-element.175), channel_id=1, replica_groups=mesh['dp'=4,'fsdp'=8] {'dp','fsdp'}, dimensions={0} | all-to-all | bytes 393216 | tf_op jit(solution)/shard_map/all_to_all | solution.py:1206
  488.8 11.7 %shard_map.340 = (bf16[640,1536]{1,0:T(8,128)(2,1)S(1)}, bf16[32,24,128]{2,1,0:T(8,128)(2,1)S(1)}, f32[16,1536]{1,0:T(8,128)S(1)}, f32[8,1536]{1,0:T(8,128)S(1)}) custom-call(bf16[32,24,128]{2,1,0:T(8,128)(2,1)S(1)} %all_to_all.125.refs_0_, bf16[640,1536]{1,0:T(8,128)(2,1)} %get-tuple-element.176.refs_1_, bf16[144,1536]{1,0:T(8,128)(2,1)S(1)} %bitcast.143, ...), custom_call_target="tpu_custom_call" | custom-call | tf_op jit(solution)/shard_map/pallas_call | solution.py:129
  500.5 12.2 %all_to_all.126.refs_0_ = bf16[32,24,128]{2,1,0:T(8,128)(2,1)S(1)} all-to-all(bf16[32,24,128]{2,1,0:T(8,128)(2,1)S(1)} %get-tuple-element.179), channel_id=1, replica_groups=mesh['dp'=4,'fsdp'=8] {'dp','fsdp'}, dimensions={0} | all-to-all | bytes 393216 | tf_op jit(solution)/shard_map/all_to_all | solution.py:1206
  521.3 34.4 %all-to-all-done.17 = bf16[32,48,256]{2,1,0:T(8,128)(2,1)S(1)} async-done(((bf16[32,48,256]{2,1,0:T(8,128)(2,1)}), bf16[32,48,256]{2,1,0:T(8,128)(2,1)S(1)}, u32[]{:S(2)}, u32[]{:S(2)}) %all-to-all-start.17) | async-done | bytes 786464 | tf_op jit(solution)/shard_map/all_to_all | solution.py:1206
  584.6 10.5 %all-to-all-done.19 = bf16[4,528,256]{2,1,0:T(8,128)(2,1)S(1)} async-done(((bf16[4,528,256]{2,1,0:T(8,128)(2,1)}), bf16[4,528,256]{2,1,0:T(8,128)(2,1)S(1)}, u32[]{:S(2)}, u32[]{:S(2)}) %all-to-all-start.19) | async-done | bytes 1081376 | tf_op jit(solution)/shard_map/all_to_all | solution.py:1211
  605.4 15.5 %all-to-all-done.22 = bf16[4,160,1280]{2,1,0:T(8,128)(2,1)S(1)} async-done(((bf16[4,160,1280]{2,1,0:T(8,128)(2,1)}), bf16[4,160,1280]{2,1,0:T(8,128)(2,1)S(1)}, u32[]{:S(2)}, u32[]{:S(2)}) %all-to-all-start.22) | async-done | bytes 1638432 | tf_op jit(solution)/shard_map/all_to_all | solution.py:1211
  637.3 15.4 %all-to-all-done.20 = bf16[4,1056,256]{2,1,0:T(8,128)(2,1)S(1)} async-done(((bf16[4,1056,256]{2,1,0:T(8,128)(2,1)}), bf16[4,1056,256]{2,1,0:T(8,128)(2,1)S(1)}, u32[]{:S(2)}, u32[]{:S(2)}) %all-to-all-start.20) | async-done | bytes 2162720 | tf_op jit(solution)/shard_map/all_to_all | solution.py:1211
  (480 shorter events, 293.1 us)
Async XLA Ops:
  7.2 31.1 %all-gather.13.cloned.1.call-start = ((), (), s32[]{:S(2)}) async-start(), calls=%async_computation.31 | async-start | bytes 1769472 | tf_op jit(solution)/shard_map/all_gather | solution.py:1248
  10.5 123.8 %all-gather.15.cloned.1.call-start = ((), (), s32[]{:S(2)}) async-start(), calls=%async_computation.32 | async-start | bytes 1769472 | tf_op jit(solution)/shard_map/all_gather | solution.py:1248
  11.2 142.1 %all-gather.17.cloned.1.call-start = ((), (), s32[]{:S(2)}) async-start(), calls=%async_computation.33 | async-start | bytes 1327104 | tf_op jit(solution)/shard_map/all_gather | solution.py:1252
  14.6 191.7 %all-gather.19.cloned.1.call-start = ((), (), s32[]{:S(2)}) async-start(), calls=%async_computation.34 | async-start | bytes 1769472 | tf_op jit(solution)/shard_map/all_gather | solution.py:1248
  15.3 258.7 %all-gather.11.cloned.1.call-start = ((), (), s32[]{:S(2)}) async-start(), calls=%async_computation.27 | async-start | bytes 3686400 | tf_op jit(solution)/shard_map/all_gather | solution.py:1257
  42.3 40.9 %all-to-all-start = ((bf16[32,16,128]{2,1,0:T(8,128)(2,1)}), bf16[32,16,128]{2,1,0:T(8,128)(2,1)S(1)}, u32[]{:S(2)}, u32[]{:S(2)}) async-start(bf16[32,16,128]{2,1,0:T(8,128)(2,1)} %shard_map.324), calls=%async_computation | async-start | bytes 262144 | tf_op jit(solution)/shard_map/all_to_all | solution.py:1206
  92.3 26.2 %all-to-all-start.1 = ((bf16[32,40,128]{2,1,0:T(8,128)(2,1)}), bf16[32,40,128]{2,1,0:T(8,128)(2,1)S(1)}, u32[]{:S(2)}, u32[]{:S(2)}) async-start(bf16[32,40,128]{2,1,0:T(8,128)(2,1)} %get-tuple-element.108), calls=%async_computation.1 | async-start | bytes 655360 | tf_op jit(solution)/shard_map/all_to_all | solution.py:1206
  127.9 13.7 %all-to-all-start.2 = ((bf16[32,8,128]{2,1,0:T(8,128)(2,1)}), bf16[32,8,128]{2,1,0:T(8,128)(2,1)S(1)}, u32[]{:S(2)}, u32[]{:S(2)}) async-start(bf16[32,8,128]{2,1,0:T(8,128)(2,1)} %get-tuple-element.110), calls=%async_computation.2 | async-start | bytes 131072 | tf_op jit(solution)/shard_map/all_to_all | solution.py:1206
  150.7 20.5 %all-to-all-start.3 = ((bf16[32,32,128]{2,1,0:T(8,128)(2,1)}), bf16[32,32,128]{2,1,0:T(8,128)(2,1)S(1)}, u32[]{:S(2)}, u32[]{:S(2)}) async-start(bf16[32,32,128]{2,1,0:T(8,128)(2,1)} %get-tuple-element.113), calls=%async_computation.3 | async-start | bytes 524288 | tf_op jit(solution)/shard_map/all_to_all | solution.py:1206
  179.7 14.7 %all-to-all-start.4 = ((bf16[32,40,128]{2,1,0:T(8,128)(2,1)}), bf16[32,40,128]{2,1,0:T(8,128)(2,1)S(1)}, u32[]{:S(2)}, u32[]{:S(2)}) async-start(bf16[32,40,128]{2,1,0:T(8,128)(2,1)} %copy-done.49), calls=%async_computation.4 | async-start | bytes 655360 | tf_op jit(solution)/shard_map/all_to_all | solution.py:1206
  203.8 11.3 %all-to-all-start.5 = ((bf16[32,24,128]{2,1,0:T(8,128)(2,1)}), bf16[32,24,128]{2,1,0:T(8,128)(2,1)S(1)}, u32[]{:S(2)}, u32[]{:S(2)}) async-start(bf16[32,24,128]{2,1,0:T(8,128)(2,1)} %get-tuple-element.118), calls=%async_computation.5 | async-start | bytes 393216 | tf_op jit(solution)/shard_map/all_to_all | solution.py:1206
  225.9 13.0 %all-to-all-start.6 = ((bf16[32,32,128]{2,1,0:T(8,128)(2,1)}), bf16[32,32,128]{2,1,0:T(8,128)(2,1)S(1)}, u32[]{:S(2)}, u32[]{:S(2)}) async-start(bf16[32,32,128]{2,1,0:T(8,128)(2,1)} %get-tuple-element.121), calls=%async_computation.6 | async-start | bytes 524288 | tf_op jit(solution)/shard_map/all_to_all | solution.py:1206
  247.3 14.7 %all-to-all-start.7 = ((bf16[32,40,128]{2,1,0:T(8,128)(2,1)}), bf16[32,40,128]{2,1,0:T(8,128)(2,1)S(1)}, u32[]{:S(2)}, u32[]{:S(2)}) async-start(bf16[32,40,128]{2,1,0:T(8,128)(2,1)} %copy-done.50), calls=%async_computation.7 | async-start | bytes 655360 | tf_op jit(solution)/shard_map/all_to_all | solution.py:1206
  271.4 11.3 %all-to-all-start.8 = ((bf16[32,24,128]{2,1,0:T(8,128)(2,1)}), bf16[32,24,128]{2,1,0:T(8,128)(2,1)S(1)}, u32[]{:S(2)}, u32[]{:S(2)}) async-start(bf16[32,24,128]{2,1,0:T(8,128)(2,1)} %copy-done.80), calls=%async_computation.8 | async-start | bytes 393216 | tf_op jit(solution)/shard_map/all_to_all | solution.py:1206
  291.4 13.7 %all-to-all-start.9 = ((bf16[32,32,128]{2,1,0:T(8,128)(2,1)}), bf16[32,32,128]{2,1,0:T(8,128)(2,1)}, u32[]{:S(2)}, u32[]{:S(2)}) async-start(bf16[32,32,128]{2,1,0:T(8,128)(2,1)} %copy-done.55), calls=%async_computation.9 | async-start | bytes 524288 | tf_op jit(solution)/shard_map/all_to_all | solution.py:1206
  294.8 281.2 %reduce-scatter.4.cloned.1.call-start = ((), (), s32[]{:S(2)}) async-start(), calls=%async_computation.28 | async-start | bytes 2433024 | tf_op jit(solution)/shard_map/reduce_scatter | solution.py:1300
  466.6 117.9 %reduce-scatter.8.cloned.1.call-start = ((), (), s32[]{:S(2)}) async-start(), calls=%async_computation.30 | async-start | bytes 3686400 | tf_op jit(solution)/shard_map/reduce_scatter | solution.py:1300
  469.8 151.1 %reduce-scatter.6.cloned.1.call-start = ((), (), s32[]{:S(2)}) async-start(), calls=%async_computation.29 | async-start | bytes 4866048 | tf_op jit(solution)/shard_map/reduce_scatter | solution.py:1300
  517.4 38.3 %all-to-all-start.17 = ((bf16[32,48,256]{2,1,0:T(8,128)(2,1)}), bf16[32,48,256]{2,1,0:T(8,128)(2,1)S(1)}, u32[]{:S(2)}, u32[]{:S(2)}) async-start(bf16[32,48,256]{2,1,0:T(8,128)(2,1)} %get-tuple-element.181), calls=%async_computation.17 | async-start | bytes 1572864 | tf_op jit(solution)/shard_map/all_to_all | solution.py:1206
  555.7 10.6 %all-to-all-start.21 = ((bf16[32,2,864]{2,1,0:T(2,128)(2,1)}), bf16[32,2,864]{2,1,0:T(2,128)(2,1)S(1)}, u32[]{:S(2)}, u32[]{:S(2)}) async-start(bf16[32,2,864]{2,1,0:T(2,128)(2,1)} %reshape.408), calls=%async_computation.23 | async-start | bytes 229376 | tf_op jit(solution)/shard_map/all_to_all | solution.py:1206
  567.0 9.0 %all-to-all-start.18 = ((bf16[4,2,48,256]{3,2,1,0:T(8,128)(2,1)}), bf16[4,2,48,256]{3,2,1,0:T(8,128)(2,1)S(1)}, u32[]{:S(2)}, u32[]{:S(2)}) async-start(bf16[4,2,48,256]{3,2,1,0:T(8,128)(2,1)} %broadcast_in_dim.180), calls=%async_computation.18 | async-start | bytes 393216 | tf_op jit(solution)/shard_map/all_to_all | solution.py:1211
  578.0 17.1 %all-to-all-start.19 = ((bf16[4,528,256]{2,1,0:T(8,128)(2,1)}), bf16[4,528,256]{2,1,0:T(8,128)(2,1)S(1)}, u32[]{:S(2)}, u32[]{:S(2)}) async-start(bf16[4,528,256]{2,1,0:T(8,128)(2,1)} %broadcast_in_dim.181), calls=%async_computation.20 | async-start | bytes 2162688 | tf_op jit(solution)/shard_map/all_to_all | solution.py:1211
  597.7 23.2 %all-to-all-start.22 = ((bf16[4,160,1280]{2,1,0:T(8,128)(2,1)}), bf16[4,160,1280]{2,1,0:T(8,128)(2,1)S(1)}, u32[]{:S(2)}, u32[]{:S(2)}) async-start(bf16[4,160,1280]{2,1,0:T(8,128)(2,1)} %broadcast_in_dim.184), calls=%async_computation.25 | async-start | bytes 3276800 | tf_op jit(solution)/shard_map/all_to_all | solution.py:1211
  623.8 29.0 %all-to-all-start.20 = ((bf16[4,1056,256]{2,1,0:T(8,128)(2,1)}), bf16[4,1056,256]{2,1,0:T(8,128)(2,1)S(1)}, u32[]{:S(2)}, u32[]{:S(2)}) async-start(bf16[4,1056,256]{2,1,0:T(8,128)(2,1)} %broadcast_in_dim.182), calls=%async_computation.22 | async-start | bytes 4325376 | tf_op jit(solution)/shard_map/all_to_all | solution.py:1211
  (138 other events, 1593.0 us)
Sparse Core Ops, SparseCore 0:
  10.6 27.6 all-gather.12
  40.5 38.7 all-gather.14
  81.5 23.4 all-gather.16
  106.5 25.1 all-gather.18
  133.7 44.4 all-gather.10
  466.8 35.9 reduce-scatter.3
  505.0 53.1 reduce-scatter.7
  560.7 57.0 reduce-scatter.5

commit v3 on v2

--- a/solution.py
+++ b/solution.py
@@ -1,4 +1,5 @@
 import functools
+import types
 
 import jax
 import jax.numpy as jnp
@@ -30,7 +31,7 @@
 RATE_MATRIX = 0.5
 RATE_VECTOR = 0.25
 
-BOTH = ("dp", "fsdp")
+REPLICAS, OWNERS = BOTH = ("dp", "fsdp")
 F32 = jnp.float32
 BF16 = jnp.bfloat16
 LANE = 128
@@ -38,10 +39,13 @@
 ROWS = MAP * TILE
 CHUNK = 256
 PARTS = CHUNK // LANE
-VMEM_BYTES = 48 * 1024 * 1024
+VMEM_BYTES = 60 * 1024 * 1024
 
 NT = (((1,), (1,)), ((), ()))
 TN = (((0,), (0,)), ((), ()))
+
+
+NEAR, FAR, RAW = range(3)
 
 
 class Refs:
@@ -49,92 +53,93 @@
         for name, ref in zip(names, refs):
             setattr(self, name, ref)
         self.loads = loads
-        self.stores = stores
+        self.stores = {id(getattr(self, name)): (k, self.far(name)) for k, name in enumerate(stores)}
         self.pending = {}
+
+    def far(self, name):
+        return getattr(self, name + "_far")
 
     def start(self):
         for index, (name, where) in enumerate(self.loads):
-            source = getattr(self, name + "_far")
-            if where is not None:
-                source = source.at[where]
-            copy = pltpu.make_async_copy(source, getattr(self, name), self.load_sem.at[index])
+            source = self.far(name) if where is None else self.far(name).at[where]
+            near = getattr(self, name)
+            copy = pltpu.make_async_copy(source, near, self.load_sem.at[index])
             copy.start()
-            self.pending[name] = copy
-
-    def wait(self, *names):
-        for name in names:
-            self.pending.pop(name).wait()
-
-    def send(self, *names):
-        for name in names:
-            copy = pltpu.make_async_copy(
-                getattr(self, name), getattr(self, name + "_far"), self.store_sem.at[self.stores.index(name)]
-            )
+            self.pending[id(near)] = copy
+
+    def wait(self, *refs):
+        for ref in refs:
+            self.pending.pop(id(ref)).wait()
+
+    def send(self, *refs):
+        for ref in refs:
+            index, far = self.stores[id(ref)]
+            copy = pltpu.make_async_copy(ref, far, self.store_sem.at[index])
             copy.start()
-            self.pending["out " + name] = copy
-
-    def finish(self):
-        for name in list(self.pending):
-            self.pending.pop(name).wait()
+            self.pending[id(far)] = copy
+
+    def part(self, ref, index, at):
+        far = self.stores[id(ref)][1]
+        return pltpu.make_async_copy(ref.at[:, at], far.at[:, at], self.part_sem.at[index])
+
+    def finish(self, ref=None):
+        for key in list(self.pending):
+            self.pending.pop(key).wait()
+        if ref is not None:
+            for index in range(ref.shape[1] // CHUNK):
+                self.part(ref, index, pl.ds(index * CHUNK, CHUNK)).wait()
 
 
 def shape(dims, dtype=F32):
     return jax.ShapeDtypeStruct(dims, dtype)
 
 
-def call(kernel, ins, outs, scratch):
+def vmem(dims, dtype=F32):
+    return pltpu.VMEM(dims, dtype)
+
+
+def call(kernel, ins, outs, scratch, alias=()):
     near, far = pl.BlockSpec(memory_space=pltpu.VMEM), pl.BlockSpec(memory_space=pltpu.HBM)
     names, arrays, in_specs, loads, stores, extra = [], [], [], [], [], {}
     for name, (array, place) in ins.items():
         arrays.append(array)
-        if isinstance(place, str) and place == "near":
+        in_specs.append(near if place == NEAR else far)
+        if place == NEAR or place == RAW:
             names.append(name)
-            in_specs.append(near)
             continue
         names.append(name + "_far")
-        in_specs.append(far)
-        where = None if isinstance(place, str) else place
-        dims = array.shape
-        if where is not None:
-            dims = tuple(
-                len(range(*part.indices(size))) for part, size in zip(where, array.shape)
-            )
-            where = tuple(
-                pl.ds(part.indices(size)[0], dim) for part, size, dim in zip(where, array.shape, dims)
-            )
+        dims, where = array.shape, None
+        if place != FAR:
+            starts = [part.indices(size)[:2] for part, size in zip(place, dims)]
+            dims = tuple(stop - start for start, stop in starts)
+            where = tuple(pl.ds(start, stop - start) for start, stop in starts)
         loads.append((name, where))
-        extra[name] = pltpu.VMEM(dims, array.dtype)
-    out_shapes, out_specs, out_names = [], [], []
+        extra[name] = vmem(dims, array.dtype)
     for name, (struct, place) in outs.items():
-        if place in ("near", "both"):
-            names.append(name)
-            out_names.append(name)
-            out_shapes.append(struct)
-            out_specs.append(near)
-        if place in ("far", "both"):
-            names.append(name + "_far")
-            out_names.append(name + "_far" if place == "both" else name)
-            out_shapes.append(struct)
-            out_specs.append(far)
+        names.append(name + "_far" if place == FAR else name)
+        if place == FAR:
             stores.append(name)
-            if place == "far":
-                extra[name] = pltpu.VMEM(struct.shape, struct.dtype)
+            extra[name] = vmem(struct.shape, struct.dtype)
     extra.update(scratch)
-    extra["load_sem"] = pltpu.SemaphoreType.DMA((max(len(loads), 1),))
-    extra["store_sem"] = pltpu.SemaphoreType.DMA((max(len(stores), 1),))
+    extra.update(
+        load_sem=pltpu.SemaphoreType.DMA((max(len(loads), 1),)),
+        store_sem=pltpu.SemaphoreType.DMA((max(len(stores), 1),)),
+        part_sem=pltpu.SemaphoreType.DMA((EXPAND // CHUNK,)),
+    )
 
     def flat(*refs):
         kernel(Refs(names + list(extra), refs, loads, stores))
 
     results = pl.pallas_call(
         flat,
-        out_shape=out_shapes,
+        out_shape=[struct for struct, _ in outs.values()],
         in_specs=in_specs,
-        out_specs=out_specs,
+        out_specs=[near if place == NEAR else far for _, place in outs.values()],
         scratch_shapes=list(extra.values()),
+        input_output_aliases={list(ins).index(a): list(outs).index(b) for a, b in alias},
         compiler_params=pltpu.CompilerParams(vmem_limit_bytes=VMEM_BYTES),
     )(*arrays)
-    return dict(zip(out_names, results))
+    return types.SimpleNamespace(**dict(zip(outs, results)))
 
 
 def dot(left, right):
@@ -336,7 +341,7 @@
         mixed = weight * dot(own_hot, pixels) + (1.0 - weight) * dot(other_hot, pixels)
         r.x[tile_rows(tile), :] = mixed
     r.xb[...] = r.x[...].astype(BF16)
-    r.send("x", "xb")
+    r.send(r.x, r.xb)
     r.finish()
 
 
@@ -344,8 +349,8 @@
     dims = images.shape
     return call(
         mix_kernel,
-        dict(images=(images, "near"), partner=(partner, "near"), mix=(mix_pair, "near")),
-        dict(x=(shape(dims), "far"), xb=(shape(dims, BF16), "both")),
+        dict(images=(images, NEAR), partner=(partner, NEAR), mix=(mix_pair, NEAR)),
+        dict(x=(shape(dims), FAR), xb=(shape(dims, BF16), FAR)),
         {},
     )
 
@@ -353,7 +358,7 @@
 def first_kernel(r):
     count = r.xb.shape[0]
     r.start()
-    r.wait("w")
+    r.wait(r.xb, r.w)
     product_sums(r.xb, r.w, False, r.h, r.stat)
     write_alike(r.pay, pack_product_moments(r.xb, r.stat[0:1, :], r.stat[1:2, :], count))
 
@@ -362,9 +367,9 @@
     count = xb.shape[0]
     return call(
         first_kernel,
-        dict(xb=(xb, "near"), w=(mats, (slice(0, WIDTH), slice(None)))),
-        dict(pay=(shape((devices, 16, LANE), BF16), "near")),
-        dict(h=pltpu.VMEM((count, CHUNK), F32), stat=pltpu.VMEM((8, EXPAND), F32)),
+        dict(xb=(xb, FAR), w=(mats, (slice(0, WIDTH), slice(None)))),
+        dict(pay=(shape((devices, 16, LANE), BF16), NEAR)),
+        dict(h=vmem((count, CHUNK), F32), stat=vmem((8, EXPAND), F32)),
     )
 
 
@@ -384,12 +389,12 @@
 def spatial_kernel(r):
     count = r.xb.shape[0]
     r.start()
-    r.wait("side", "w")
+    r.wait(r.side, r.w, r.xb)
     rows = r.side[...].astype(F32)
     r.taps[0:9, :] = rows[0:9, :]
     mean, inverse = read_product_moments(r.recv, r.w[...], False, EXPAND, count)
     keep_norm(r.norm, mean, inverse, rows[10:11, :], rows[11:12, :])
-    r.send("norm")
+    r.send(r.norm)
     if r.recv.shape[1] > 16:
         r.cross[...] = jnp.sum(r.recv[...].astype(F32)[:, 16:32], axis=0)
 
@@ -421,54 +426,58 @@
             total, squares = lax.fori_loop(0, count // ROWS, tile_step, (zero, zero))
             r.stat[0:1, lanes] = column_sum(total)
             r.stat[1:2, lanes] = column_sum(squares)
-        pltpu.make_async_copy(r.d.at[:, at_chunk], r.d_far.at[:, at_chunk], r.part_sem.at[index]).start()
+        r.part(r.d, index, at_chunk).start()
         return carry
 
     lax.fori_loop(0, EXPAND // CHUNK, step, 0)
     write_alike(r.pay, pack_moments(r.stat[0:1, :], r.stat[1:2, :], count))
-    for index in range(EXPAND // CHUNK):
-        at_chunk = pl.ds(index * CHUNK, CHUNK)
-        pltpu.make_async_copy(r.d.at[:, at_chunk], r.d_far.at[:, at_chunk], r.part_sem.at[index]).wait()
-    r.finish()
+    r.finish(r.d)
 
 
 def spatial(xb, mats, side, recv):
     count = xb.shape[0]
     devices = recv.shape[0]
     outs = dict(
-        d=(shape((count, EXPAND), BF16), "both"),
-        pay=(shape((devices, moment_rows(EXPAND), LANE), BF16), "near"),
-        norm=(shape((8, EXPAND)), "far"),
+        d=(shape((count, EXPAND), BF16), FAR),
+        pay=(shape((devices, moment_rows(EXPAND), LANE), BF16), NEAR),
+        norm=(shape((8, EXPAND)), FAR),
     )
     if recv.shape[1] > 16:
-        outs["cross"] = (shape((16, LANE)), "near")
+        outs["cross"] = (shape((16, LANE)), NEAR)
     return call(
         spatial_kernel,
         dict(
-            recv=(recv, "near"),
-            xb=(xb, "near"),
+            recv=(recv, NEAR),
             side=(side, (slice(2 * SQUEEZE, SIDE_PAD), slice(None))),
+            xb=(xb, FAR),
             w=(mats, (slice(0, WIDTH), slice(None))),
         ),
         outs,
         dict(
-            h=pltpu.VMEM((count, CHUNK), F32),
-            taps=pltpu.VMEM((16, EXPAND), F32),
-            stat=pltpu.VMEM((8, EXPAND), F32),
-            part_sem=pltpu.SemaphoreType.DMA((EXPAND // CHUNK,)),
+            h=vmem((count, CHUNK), F32),
+            taps=vmem((16, EXPAND), F32),
+            stat=vmem((8, EXPAND), F32),
         ),
     )
 
 
-def project_kernel(with_cross, r):
+def project_kernel(with_cross, owners, r):
     count = r.d.shape[0]
     tiles = count // ROWS
     r.start()
     mean, inverse = read_moments(r.recv, EXPAND, count)
-    r.wait("side")
+    r.wait(r.side)
     rows = r.side[2 * SQUEEZE : SIDE_PAD, :].astype(F32)
     keep_norm(r.norm, mean, inverse, rows[12:13, :], rows[13:14, :])
-    r.send("norm")
+    r.send(r.norm)
+    width, vec_width = EXPAND // owners, VECS // owners
+    vec = jnp.concatenate(
+        [rows[14:15, k * width : k * width + vec_width] for k in range(owners)], axis=1
+    )
+    r.vec[...] = jnp.concatenate(
+        [vec[:, SQUEEZE : SQUEEZE + WIDTH], vec[:, SQUEEZE + WIDTH :], jnp.zeros((6, WIDTH), F32)], axis=0
+    )
+    r.wait(r.d)
 
     def activate(index, carry):
         lanes = chunk_at(index, LANE)
@@ -483,13 +492,13 @@
         return carry
 
     lax.fori_loop(0, EXPAND // LANE, activate, 0)
-    r.send("pooled")
-    before = folded(dot_nt(stacked(r.pooled[...]), r.side[0:SQUEEZE, :])) + r.vec[2:3, :SQUEEZE]
+    r.send(r.pooled)
+    before = folded(dot_nt(stacked(r.pooled[...]), r.side[0:SQUEEZE, :])) + vec[:, :SQUEEZE]
     r.squeeze[...] = before
-    r.send("squeeze")
+    r.send(r.squeeze)
     opened = folded(dot(stacked(before * sigmoid(before)), r.side[SQUEEZE : 2 * SQUEEZE, :]))
     r.excite[...] = sigmoid(opened + rows[9:10, :])
-    r.send("excite")
+    r.send(r.excite)
 
     def gate(index, carry):
         lanes = chunk_at(index, LANE)
@@ -500,9 +509,10 @@
         return carry
 
     lax.fori_loop(0, EXPAND // LANE, gate, 0)
-    r.wait("w")
+    r.wait(r.w)
     projected = dot_nt(r.y[...], r.w[...])
     r.p[...] = projected
+    r.send(r.p)
     moments = pack_moments(column_sum(projected), column_sum(projected * projected), count)
     if with_cross:
         moments = jnp.concatenate([moments, r.cross[...]], axis=0)
@@ -510,33 +520,33 @@
     r.finish()
 
 
-def project(d, mats, side, vec, recv, cross):
+def project(d, mats, side, recv, cross, owners):
     count = d.shape[0]
     images = count // MAP
     devices = recv.shape[0]
     ins = dict(
-        recv=(recv, "near"),
-        d=(d, "near"),
-        vec=(vec, "near"),
-        side=(side, "far"),
+        recv=(recv, NEAR),
+        side=(side, FAR),
+        d=(d, FAR),
         w=(mats, (slice(WIDTH, 2 * WIDTH), slice(None))),
     )
     rows = moment_rows(WIDTH)
     if cross is not None:
-        ins["cross"] = (cross, "near")
+        ins["cross"] = (cross, NEAR)
         rows += 16
     return call(
-        functools.partial(project_kernel, cross is not None),
+        functools.partial(project_kernel, cross is not None, owners),
         ins,
         dict(
-            p=(shape((count, WIDTH)), "near"),
-            pay=(shape((devices, rows, LANE), BF16), "near"),
-            norm=(shape((8, EXPAND)), "far"),
-            pooled=(shape((images, EXPAND)), "far"),
-            excite=(shape((images, EXPAND)), "far"),
-            squeeze=(shape((images, SQUEEZE)), "far"),
+            p=(shape((count, WIDTH)), FAR),
+            vec=(shape((8, WIDTH)), NEAR),
+            pay=(shape((devices, rows, LANE), BF16), NEAR),
+            norm=(shape((8, EXPAND)), FAR),
+            pooled=(shape((images, EXPAND)), FAR),
+            excite=(shape((images, EXPAND)), FAR),
+            squeeze=(shape((images, SQUEEZE)), FAR),
         ),
-        dict(a=pltpu.VMEM((count, EXPAND), F32), y=pltpu.VMEM((count, EXPAND), BF16)),
+        dict(a=vmem((count, EXPAND), F32), y=vmem((count, EXPAND), BF16)),
     )
 
 
@@ -547,16 +557,17 @@
     keep_norm(r.norm, mean, inverse, r.vec[0:1, :], r.vec[1:2, :])
     if with_cross:
         r.cross[...] = read_matrix(r.recv, moment_rows(WIDTH))
-        r.send("cross")
+        r.send(r.cross)
+    r.wait(r.p)
     normed = (r.p[...] - mean) * inverse
     r.normed[...] = normed
-    r.wait("before")
+    r.wait(r.before)
     result = r.before[...] + (normed * r.vec[0:1, :] + r.vec[1:2, :])
     r.x[...] = result
     r.xb[...] = result.astype(BF16)
-    r.send("norm", "normed", "x", "xb")
+    r.send(r.norm, r.normed, r.x, r.xb)
     cross = dot_tn(normed.astype(BF16), r.xb[...])
-    r.wait("w")
+    r.wait(r.w)
     product_sums(r.xb, r.w, transposed, r.h, r.stat)
     moments = pack_product_moments(r.xb, r.stat[0:1, :], r.stat[1:2, :], count)
     write_with_slices(r.pay, moments, cross)
@@ -570,21 +581,21 @@
     columns = HEAD if transposed else EXPAND
     where = (slice(0, HEAD), slice(0, WIDTH)) if transposed else (slice(0, WIDTH), slice(None))
     outs = dict(
-        x=(shape((count, WIDTH)), "far"),
-        xb=(shape((count, WIDTH), BF16), "both"),
-        normed=(shape((count, WIDTH)), "far"),
-        pay=(shape((devices, 32, LANE), BF16), "near"),
-        norm=(shape((8, WIDTH)), "far"),
+        x=(shape((count, WIDTH)), FAR),
+        xb=(shape((count, WIDTH), BF16), FAR),
+        normed=(shape((count, WIDTH)), FAR),
+        pay=(shape((devices, 32, LANE), BF16), NEAR),
+        norm=(shape((8, WIDTH)), FAR),
     )
     if with_cross:
-        outs["cross"] = (shape((WIDTH, WIDTH)), "far")
+        outs["cross"] = (shape((WIDTH, WIDTH)), FAR)
     return call(
         functools.partial(residual_kernel, transposed, with_cross),
         dict(
-            recv=(recv, "near"), p=(p, "near"), vec=(vec, "near"), before=(x, "far"), w=(weights, where)
+            recv=(recv, NEAR), vec=(vec, NEAR), p=(p, FAR), before=(x, FAR), w=(weights, where)
         ),
         outs,
-        dict(h=pltpu.VMEM((count, CHUNK), F32), stat=pltpu.VMEM((8, columns), F32)),
+        dict(h=vmem((count, CHUNK), F32), stat=vmem((8, columns), F32)),
     )
 
 
@@ -601,13 +612,13 @@
     tiles = count // ROWS
     images = count // MAP
     r.start()
-    r.wait("w")
+    r.wait(r.xb, r.w)
     mean, inverse = read_product_moments(r.recv, r.w[...], True, HEAD, count)
     cross = jnp.sum(r.recv[...].astype(F32)[:, 16:32], axis=0)
-    r.wait("classifier")
+    r.wait(r.classifier)
     gain_bias = head_rows(r.classifier[:, LOGITS - LANE :])
     keep_norm(r.norm, mean, inverse, gain_bias[0:1, :], gain_bias[1:2, :])
-    r.send("norm")
+    r.send(r.norm)
 
     def features(index, carry):
         at_chunk = chunk_at(index)
@@ -647,7 +658,8 @@
     ) / image_count
     grad_low = grad_logits.astype(BF16)
     r.grad_fc[...] = dot_tn(features_low, grad_low).astype(BF16)
-    r.send("grad_fc")
+    fc_copy = pltpu.make_async_copy(r.grad_fc, r.grad_head.at[:, pl.ds(WIDTH, LOGITS)], r.part_sem.at[0])
+    fc_copy.start()
     r.f[...] = dot_nt(grad_low, classifier) / MAP
     bias_sum = column_sum(grad_logits)
     bias_ids = lax.broadcasted_iota(jnp.int32, (1, LOGITS), 1)
@@ -679,8 +691,9 @@
         return carry
 
     lax.fori_loop(0, HEAD // LANE, back, 0)
+    r.send(r.dz)
     below = dot(r.q[...], r.w[...])
-    r.wait("normed")
+    r.wait(r.normed)
     rows = fold(
         [
             r.stat[0:1, :], r.stat[1:2, :] * inverse,
@@ -689,6 +702,7 @@
         32,
     )
     write_alike(r.pay, jnp.concatenate([rows, cross], axis=0))
+    fc_copy.wait()
     r.finish()
 
 
@@ -699,28 +713,29 @@
     return call(
         functools.partial(head_kernel, image_count),
         dict(
-            recv=(recv, "near"),
-            xb=(xb, "near"),
-            bias=(bias, "near"),
-            label_col=(label_col, "near"),
-            label_row=(label_row, "near"),
-            partner=(partner, "near"),
-            mix=(mix_pair, "near"),
+            recv=(recv, NEAR),
+            xb=(xb, FAR),
+            bias=(bias, NEAR),
+            label_col=(label_col, NEAR),
+            label_row=(label_row, NEAR),
+            partner=(partner, NEAR),
+            mix=(mix_pair, NEAR),
             w=(head_full, (slice(0, HEAD), slice(0, WIDTH))),
             classifier=(head_full, (slice(0, HEAD), slice(WIDTH, HEADPAD))),
-            normed=(normed, "far"),
+            normed=(normed, FAR),
         ),
         dict(
-            dz=(shape((count, HEAD), BF16), "near"),
-            pay=(shape((devices, 48, LANE), BF16), "near"),
-            norm=(shape((8, HEAD)), "far"),
-            grad_fc=(shape((HEAD, LOGITS), BF16), "far"),
+            dz=(shape((count, HEAD), BF16), FAR),
+            pay=(shape((devices, 48, LANE), BF16), NEAR),
+            norm=(shape((8, HEAD)), FAR),
+            grad_head=(shape((HEAD, HEADPAD), BF16), RAW),
         ),
         dict(
-            h=pltpu.VMEM((count, HEAD), F32),
-            f=pltpu.VMEM((images, HEAD), F32),
-            q=pltpu.VMEM((count, HEAD), BF16),
-            stat=pltpu.VMEM((8, HEAD), F32),
+            h=vmem((count, HEAD), F32),
+            grad_fc=vmem((HEAD, LOGITS), BF16),
+            f=vmem((images, HEAD), F32),
+            q=vmem((count, HEAD), BF16),
+            stat=vmem((8, HEAD), F32),
         ),
     )
 
@@ -732,8 +747,8 @@
     r.glob[0:1, :] = sum_gain
     r.glob[1:2, :] = sum_bias
     r.glob[2:8, :] = jnp.zeros((6, columns), F32)
-    r.send("glob")
-    r.wait("unorm", "xb", "w")
+    r.send(r.glob)
+    r.wait(r.unorm, r.xb, r.w, r.dz)
     mean = r.unorm[0:1, :]
     scale = r.unorm[2:3, :]
     slant = scale * r.unorm[1:2, :] * (sum_gain / row_count)
@@ -790,7 +805,8 @@
     sums = read_sums(r.recv)
     bias_pull, slant = product_back(is_head, row_count, sums, columns, r)
     if is_head:
-        r.send("grad_w")
+        head_copy = pltpu.make_async_copy(r.grad_w, r.grad_head.at[:, pl.ds(0, WIDTH)], r.part_sem.at[0])
+        head_copy.start()
         weights = r.w[...].astype(F32)
         column = lax.broadcasted_iota(jnp.int32, (1, WIDTH), 1)
         high, low = halves(jnp.broadcast_to(bias_pull, (TILE, columns)))
@@ -810,7 +826,7 @@
         square = product[count : count + WIDTH]
         pull = column_sum(product[count + WIDTH : count + WIDTH + 2])
         stream = r.stream_in[...] + product[0:count]
-        r.wait("cross")
+        r.wait(r.cross)
         cross = r.cross[...]
     r.stream[...] = stream
     sum_bias = spread(sums, 2 * groups, WIDTH // LANE) - pull
@@ -826,14 +842,14 @@
     else:
         r.glob3[2:6, :] = jnp.zeros((4, WIDTH), F32)
     r.glob3[6:8, :] = jnp.zeros((2, WIDTH), F32)
-    r.send("glob3")
-    r.wait("norm3", "normed")
+    r.send(r.glob3)
+    r.wait(r.norm3, r.normed)
     grad_p = r.norm3[2:3, :] * (
         stream - sum_bias / row_count - r.normed[...] * (sum_gain / row_count)
     )
     r.gp[...] = grad_p.astype(BF16)
     r.gt[...] = r.gp[...].T
-    r.wait("wp", "d", "norm2", "excite")
+    r.wait(r.wp, r.d, r.norm2, r.excite)
     half = owners // 2
 
     def first(index, carry):
@@ -868,7 +884,7 @@
         return carry
 
     lax.fori_loop(0, EXPAND // CHUNK, first, 0)
-    r.wait("pooled", "squeeze", "side")
+    r.wait(r.pooled, r.squeeze, r.side)
     excite = r.excite[...]
     grad_gate = r.ge[...] * excite * (1.0 - excite)
     before = r.squeeze[...]
@@ -900,6 +916,7 @@
         return carry
 
     lax.fori_loop(0, EXPAND // LANE, second, 0)
+    r.send(r.dz2)
     write_alike(r.pay, fold([r.stat[0:1, :], r.stat[1:2, :] * r.norm2[1:2, :]], 24))
     squeezed_high, squeezed_low = halves(squeezed)
     pre_high, pre_low = halves(grad_pre)
@@ -918,69 +935,84 @@
     )
     taps = None
     if not is_head:
-        r.wait("taps")
+        r.wait(r.taps)
         taps = r.taps[...]
     owner_blocks(r, owners, half, taps)
-    r.send("grads")
+    room = r.grads.shape[1]
+    place = pl.ds((r.blocks.shape[1] - room) * (not is_head), room)
+    blocks_copy = pltpu.make_async_copy(r.grads, r.blocks.at[:, place, :], r.part_sem.at[1])
+    blocks_copy.start()
+    blocks_copy.wait()
+    if is_head:
+        head_copy.wait()
     r.finish()
 
 
-def gate_back(is_head, row_count, owners, recv, upper, cross, stream, lower):
-    count = upper["xb_far"].shape[0]
+def gate_back(is_head, row_count, owners, recv, upper, cross, stream, lower, blocks, extra_room):
+    count = upper.xb.shape[0]
     images = count // MAP
     devices = recv.shape[0]
     columns = HEAD if is_head else EXPAND
     block = EXPAND // CHUNK * (2 * WIDTH // owners) + 2 * SQUEEZE + 16
     where = (slice(0, HEAD), slice(0, WIDTH)) if is_head else (slice(0, WIDTH), slice(None))
     ins = dict(
-        recv=(recv, "near"),
-        dz=(upper["dz"], "near"),
-        unorm=(upper["norm"], "far"),
-        xb=(upper["xb_far"], "far"),
-        w=(upper["weights"], where),
-        norm3=(lower["norm3"], "far"),
-        normed=(lower["normed"], "far"),
-        norm2=(lower["norm2"], "far"),
-        wp=(lower["mats"], (slice(WIDTH, 2 * WIDTH), slice(None))),
-        d=(lower["d_far"], "far"),
-        excite=(lower["excite"], "far"),
-        pooled=(lower["pooled"], "far"),
-        squeeze=(lower["squeeze"], "far"),
-        side=(lower["side"], (slice(0, 2 * SQUEEZE), slice(None))),
+        recv=(recv, NEAR),
+        unorm=(upper.norm, FAR),
+        xb=(upper.xb, FAR),
+        w=(upper.weights, where),
+        dz=(upper.dz, FAR),
+        norm3=(lower.norm3, FAR),
+        normed=(lower.normed, FAR),
+        norm2=(lower.norm2, FAR),
+        wp=(lower.mats, (slice(WIDTH, 2 * WIDTH), slice(None))),
+        d=(lower.d, FAR),
+        excite=(lower.excite, FAR),
+        pooled=(lower.pooled, FAR),
+        squeeze=(lower.squeeze, FAR),
+        side=(lower.side, (slice(0, 2 * SQUEEZE), slice(None))),
     )
     outs = dict(
-        dz2=(shape((count, EXPAND), BF16), "near"),
-        pay=(shape((devices, 24, LANE), BF16), "near"),
-        stream=(shape((count, WIDTH)), "near"),
-        grads=(shape((owners, block, CHUNK), BF16), "far"),
-        glob=(shape((8, columns)), "far"),
-        glob3=(shape((8, WIDTH)), "far"),
+        dz2=(shape((count, EXPAND), BF16), FAR),
+        pay=(shape((devices, 24, LANE), BF16), NEAR),
+        stream=(shape((count, WIDTH)), NEAR),
+        blocks=(shape((owners, block * (1 + extra_room), CHUNK), BF16), RAW),
+        glob=(shape((8, columns)), FAR),
+        glob3=(shape((8, WIDTH)), FAR),
     )
     scratch = dict(
-        xt=pltpu.VMEM((WIDTH, count), BF16),
-        h=pltpu.VMEM((count, CHUNK), F32),
-        coef=pltpu.VMEM((8, EXPAND), F32),
-        dh=pltpu.VMEM((count + WIDTH + 16, columns), BF16),
-        u=pltpu.VMEM((count, EXPAND), F32),
-        slope=pltpu.VMEM((count, EXPAND), F32),
-        y=pltpu.VMEM((count, EXPAND), BF16),
-        gp=pltpu.VMEM((count, WIDTH), BF16),
-        gt=pltpu.VMEM((WIDTH, count), BF16),
-        ge=pltpu.VMEM((images, EXPAND), F32),
-        pool=pltpu.VMEM((images, EXPAND), F32),
-        rx=pltpu.VMEM((2 * SQUEEZE, EXPAND), F32),
-        excite_sum=pltpu.VMEM((1, EXPAND), F32),
-        squeeze_sum=pltpu.VMEM((1, LANE), F32),
-        stat=pltpu.VMEM((8, EXPAND), F32),
-    )
+        grads=vmem((owners, block, CHUNK), BF16),
+        xt=vmem((WIDTH, count), BF16),
+        h=vmem((count, CHUNK), F32),
+        coef=vmem((8, EXPAND), F32),
+        dh=vmem((count + WIDTH + 16, columns), BF16),
+        u=vmem((count, EXPAND), F32),
+        slope=vmem((count, EXPAND), F32),
+        y=vmem((count, EXPAND), BF16),
+        gp=vmem((count, WIDTH), BF16),
+        gt=vmem((WIDTH, count), BF16),
+        ge=vmem((images, EXPAND), F32),
+        pool=vmem((images, EXPAND), F32),
+        rx=vmem((2 * SQUEEZE, EXPAND), F32),
+        excite_sum=vmem((1, EXPAND), F32),
+        squeeze_sum=vmem((1, LANE), F32),
+        stat=vmem((8, EXPAND), F32),
+    )
+    alias = []
     if is_head:
-        outs["grad_w"] = (shape((HEAD, WIDTH), BF16), "far")
+        ins["grad_head_in"] = (upper.grad_head, RAW)
+        outs["grad_head"] = (shape((HEAD, HEADPAD), BF16), RAW)
+        scratch["grad_w"] = vmem((HEAD, WIDTH), BF16)
+        alias.append(("grad_head_in", "grad_head"))
     else:
-        ins["cross"] = (cross, "far")
-        ins["stream_in"] = (stream, "near")
-        ins["taps"] = (upper["taps"], "far")
-        scratch["grad_w"] = pltpu.VMEM((WIDTH, EXPAND), BF16)
-    return call(functools.partial(gate_kernel, is_head, row_count, owners), ins, outs, scratch)
+        ins["cross"] = (cross, FAR)
+        ins["stream_in"] = (stream, NEAR)
+        ins["taps"] = (upper.taps, FAR)
+        scratch["grad_w"] = vmem((WIDTH, EXPAND), BF16)
+        if blocks is not None:
+            ins["blocks_in"] = (blocks, RAW)
+            outs["blocks"] = (shape(blocks.shape, BF16), RAW)
+            alias.append(("blocks_in", "blocks"))
+    return call(functools.partial(gate_kernel, is_head, row_count, owners), ins, outs, scratch, alias)
 
 
 def tap_kernel(is_first, row_count, r):
@@ -993,14 +1025,14 @@
     r.glob[0:1, :] = sum_gain
     r.glob[1:2, :] = sum_bias
     r.glob[2:8, :] = jnp.zeros((6, EXPAND), F32)
-    r.send("glob")
-    r.wait("side", "norm2")
+    r.send(r.glob)
+    r.wait(r.side, r.norm2)
     scale2 = r.norm2[2:3, :]
     slant2 = scale2 * r.norm2[1:2, :] * (sum_gain / row_count)
     r.coef[0:9, :] = r.side[...].astype(F32)[0:9, :]
     r.coef[9:10, :] = slant2
     r.coef[10:11, :] = r.norm2[0:1, :] * slant2 - scale2 * (sum_bias / row_count)
-    r.wait("norm1", "xb", "w", "d")
+    r.wait(r.norm1, r.xb, r.w, r.d, r.dz2)
 
     def step(index, carry):
         at_chunk = chunk_at(index)
@@ -1050,51 +1082,52 @@
                 r.taps[k : k + 1, lanes] = column_sum(result[k])
             r.stat[0:1, lanes] = column_sum(result[9])
             r.stat[1:2, lanes] = column_sum(result[10])
+        r.part(r.dz, index, at_chunk).start()
         return carry
 
     lax.fori_loop(0, EXPAND // CHUNK, step, 0)
     r.taps[9:16, :] = jnp.zeros((7, EXPAND), F32)
-    r.send("taps")
+    r.send(r.taps)
     vectors = [r.stat[0:1, :], r.stat[1:2, :] * r.norm1[1:2, :]]
     if not is_first:
         below = r.stream[...] + dot_nt(r.q[...], r.w[...])
-        r.wait("normed")
+        r.wait(r.normed)
         vectors.append(column_sum(below))
         vectors.append(column_sum(below * r.normed[...]))
     write_alike(r.pay, fold(vectors, r.pay.shape[1]))
-    r.finish()
+    r.finish(r.dz)
 
 
 def tap_back(is_first, row_count, recv, dz2, layer, stream, below):
     count = dz2.shape[0]
     devices = recv.shape[0]
     ins = dict(
-        recv=(recv, "near"),
-        dz2=(dz2, "near"),
-        side=(layer["side"], (slice(2 * SQUEEZE, SIDE_PAD), slice(None))),
-        norm2=(layer["norm2"], "far"),
-        norm1=(layer["norm1"], "far"),
-        xb=(layer["xb_far"], "far"),
-        w=(layer["mats"], (slice(0, WIDTH), slice(None))),
-        d=(layer["d_far"], "far"),
+        recv=(recv, NEAR),
+        side=(layer.side, (slice(2 * SQUEEZE, SIDE_PAD), slice(None))),
+        norm2=(layer.norm2, FAR),
+        norm1=(layer.norm1, FAR),
+        xb=(layer.xb, FAR),
+        w=(layer.mats, (slice(0, WIDTH), slice(None))),
+        dz2=(dz2, FAR),
+        d=(layer.d, FAR),
     )
     scratch = dict(
-        h=pltpu.VMEM((count, CHUNK), F32),
-        coef=pltpu.VMEM((16, EXPAND), F32),
-        stat=pltpu.VMEM((8, EXPAND), F32),
+        h=vmem((count, CHUNK), F32),
+        coef=vmem((16, EXPAND), F32),
+        stat=vmem((8, EXPAND), F32),
     )
     if not is_first:
-        ins["stream"] = (stream, "near")
-        ins["normed"] = (below["normed"], "far")
-        scratch["q"] = pltpu.VMEM((count, EXPAND), BF16)
+        ins["stream"] = (stream, NEAR)
+        ins["normed"] = (below.normed, FAR)
+        scratch["q"] = vmem((count, EXPAND), BF16)
     return call(
         functools.partial(tap_kernel, is_first, row_count),
         ins,
         dict(
-            dz=(shape((count, EXPAND), BF16), "near"),
-            pay=(shape((devices, 24 if is_first else 32, LANE), BF16), "near"),
-            taps=(shape((16, EXPAND)), "far"),
-            glob=(shape((8, EXPAND)), "far"),
+            dz=(shape((count, EXPAND), BF16), FAR),
+            pay=(shape((devices, 24 if is_first else 32, LANE), BF16), NEAR),
+            taps=(shape((16, EXPAND)), FAR),
+            glob=(shape((8, EXPAND)), FAR),
         ),
         scratch,
     )
@@ -1128,22 +1161,22 @@
     return call(
         functools.partial(last_kernel, row_count, replicas, owners),
         dict(
-            recv=(recv, "near"),
-            dz=(dz, "near"),
-            unorm=(layer["norm1"], "far"),
-            xb=(layer["xb_far"], "far"),
-            w=(layer["mats"], (slice(0, WIDTH), slice(None))),
+            recv=(recv, NEAR),
+            dz=(dz, FAR),
+            unorm=(layer.norm1, FAR),
+            xb=(layer.xb, FAR),
+            w=(layer.mats, (slice(0, WIDTH), slice(None))),
         ),
         dict(
-            grads=(shape((devices, block, CHUNK), BF16), "near"),
-            glob=(shape((8, EXPAND)), "far"),
+            grads=(shape((devices, block, CHUNK), BF16), NEAR),
+            glob=(shape((8, EXPAND)), FAR),
         ),
         dict(
-            xt=pltpu.VMEM((WIDTH, count), BF16),
-            h=pltpu.VMEM((count, CHUNK), F32),
-            coef=pltpu.VMEM((8, EXPAND), F32),
-            dh=pltpu.VMEM((count, EXPAND), BF16),
-            grad_w=pltpu.VMEM((WIDTH, EXPAND), F32),
+            xt=vmem((WIDTH, count), BF16),
+            h=vmem((count, CHUNK), F32),
+            coef=vmem((8, EXPAND), F32),
+            dh=vmem((count, EXPAND), BF16),
+            grad_w=vmem((WIDTH, EXPAND), F32),
         ),
     )
 
@@ -1206,13 +1239,22 @@
     return lax.all_to_all(payload, BOTH, 0, 0)
 
 
+def before(value, *others):
+    return lax.optimization_barrier((value, *others))[0]
+
+
 def spread_over(array, axis):
     copies = jnp.broadcast_to(array[None], (lax.axis_size(axis), *array.shape))
     return lax.all_to_all(copies, axis, 0, 0)
 
 
 def replica_sum(array):
-    return jnp.sum(spread_over(array, "dp").astype(F32), axis=0)
+    count = lax.axis_size(REPLICAS)
+    total = array.astype(F32)
+    for turn in range(1, count):
+        pairs = [(k, (k + turn) % count) for k in range(count)]
+        total = total + lax.ppermute(array, REPLICAS, pairs).astype(F32)
+    return total
 
 
 def body(
@@ -1222,13 +1264,13 @@
     head_first, head_second, bias_first, bias_second,
 ):
     local_images = images.shape[0]
-    owners = lax.axis_size("fsdp")
-    replicas = lax.axis_size("dp")
+    owners = lax.axis_size(OWNERS)
+    replicas = lax.axis_size(REPLICAS)
     devices = owners * replicas
     image_count = float(local_images * devices)
     count = local_images * MAP
     row_count = float(count * devices)
-    mine = lax.axis_index("fsdp")
+    mine = lax.axis_index(OWNERS)
     side_width = layer_side.shape[2]
     vec_width = layer_vecs.shape[1]
     rows_dev = layer_mats.shape[1]
@@ -1245,110 +1287,108 @@
         axis=1,
     ).astype(BF16)
     mats_all = [
-        lax.all_gather(layer_mats[k].astype(BF16), "fsdp", axis=0, tiled=True) for k in range(LAYERS)
+        lax.all_gather(layer_mats[k].astype(BF16), OWNERS, axis=0, tiled=True) for k in range(LAYERS)
     ]
-    side_zero = lax.all_gather(side_low[0], "fsdp", axis=1, tiled=True)
+    side_zero = lax.all_gather(side_low[0], OWNERS, axis=1, tiled=True)
     side_room = -(-side_width // CHUNK) * CHUNK
     side_rest = lax.all_gather(
-        jnp.pad(side_low[1:], ((0, 0), (0, 0), (0, side_room - side_width))), "fsdp", axis=0
+        jnp.pad(side_low[1:], ((0, 0), (0, 0), (0, side_room - side_width))), OWNERS, axis=0
     )
     side_rest = jnp.moveaxis(side_rest[..., :side_width], 0, 2).reshape(LAYERS - 1, SIDE_PAD, EXPAND)
     side_all = [side_zero, side_rest[0], side_rest[1]]
     head_full = lax.all_gather(
-        jnp.pad(head_mat, ((0, 0), (0, HEADPAD - HEADCOLS))).astype(BF16), "fsdp", axis=0, tiled=True
-    )
-
-    def vec_rows(side):
-        vec = side[SIDE].reshape(owners, side_width)[:, :vec_width].reshape(VECS).astype(F32)
-        squeeze_bias = jnp.pad(vec[:SQUEEZE], (0, WIDTH - SQUEEZE))
-        rows = jnp.stack([vec[SQUEEZE : SQUEEZE + WIDTH], vec[SQUEEZE + WIDTH :], squeeze_bias])
-        return jnp.pad(rows, ((0, 5), (0, 0)))
-
-    vecs_all = [vec_rows(side) for side in side_all]
+        jnp.pad(head_mat, ((0, 0), (0, HEADPAD - HEADCOLS))).astype(BF16), OWNERS, axis=0, tiled=True
+    )
 
     partner_col = partner[:, None]
     layers = []
     crosses = []
-    entry = mix(images.reshape(count, WIDTH), partner_col, mix_pair)
-    x, xb, xb_far = entry["x"], entry["xb"], entry["xb_far"]
-    pay = first(xb, mats_all[0], devices)["pay"]
+    entry = mix(before(images, side_zero).reshape(count, WIDTH), partner_col, mix_pair)
+    x, xb = entry.x, entry.xb
+    pay = first(xb, mats_all[0], devices).pay
     for k in range(LAYERS):
-        mats, side, vec = mats_all[k], side_all[k], vecs_all[k]
+        mats, side = mats_all[k], side_all[k]
         one = spatial(xb, mats, side, exchange(pay))
-        two = project(one["d"], mats, side, vec, exchange(one["pay"]), one.get("cross"))
+        two = project(one.d, mats, side, exchange(one.pay), getattr(one, "cross", None), owners)
         last = k == LAYERS - 1
         three = residual(
-            x, two["p"], vec, exchange(two["pay"]), head_full if last else mats_all[k + 1], last
+            x, two.p, two.vec, exchange(two.pay), head_full if last else mats_all[k + 1], last
         )
-        if "cross" in three:
-            crosses.append(three["cross"])
+        if k:
+            crosses.append(three.cross)
         layers.append(
-            dict(
-                xb_far=xb_far, d_far=one["d_far"], norm1=one["norm"], norm2=two["norm"],
-                pooled=two["pooled"], excite=two["excite"], squeeze=two["squeeze"],
-                norm3=three["norm"], normed=three["normed"], mats=mats, weights=mats, side=side,
+            types.SimpleNamespace(
+                xb=xb, d=one.d, norm1=one.norm, norm2=two.norm,
+                pooled=two.pooled, excite=two.excite, squeeze=two.squeeze,
+                norm3=three.norm, normed=three.normed, mats=mats, weights=mats, side=side,
             )
         )
-        x, xb, xb_far, pay = three["x"], three["xb"], three["xb_far"], three["pay"]
+        x, xb, pay = three.x, three.xb, three.pay
     top = head(
         xb, head_full, jnp.pad(fc_bias, (0, LOGITS - CLASSES))[None], labels[:, None], labels[None, :],
-        partner_col, mix_pair, layers[-1]["normed"], exchange(pay), image_count,
+        partner_col, mix_pair, layers[-1].normed, exchange(pay), image_count,
     )
 
     def to_owner(blocks):
-        rows = blocks.shape[0] * blocks.shape[1]
         return lax.psum_scatter(
-            blocks.reshape(rows, blocks.shape[2]), "fsdp", scatter_dimension=0, tiled=True
+            blocks.reshape(-1, blocks.shape[-1]), OWNERS, scatter_dimension=0, tiled=True
         )
 
-    upper = dict(xb_far=xb_far, weights=head_full, dz=top["dz"], norm=top["norm"])
-    pay = top["pay"]
+    upper = types.SimpleNamespace(
+        xb=xb, weights=head_full, dz=top.dz, norm=top.norm, grad_head=top.grad_head
+    )
+    pay = top.pay
     stream = None
-    globs = [{} for _ in range(LAYERS)]
-    blocks = [None] * LAYERS
+    blocks = None
+    waiting = []
+    globs_one, globs_two, globs_three = [None] * LAYERS, [None] * LAYERS, [None] * LAYERS
     for k in reversed(range(LAYERS)):
         layer = layers[k]
         is_head = k == LAYERS - 1
         gate = gate_back(
             is_head, row_count, owners, exchange(pay), upper,
-            None if is_head else crosses[k], stream, layer,
+            None if is_head else crosses[k], stream, layer, blocks, is_head,
         )
-        stream = gate["stream"]
-        globs[k]["three"] = gate["glob3"]
-        blocks[k] = gate["grads"]
+        stream = gate.stream
+        globs_three[k] = gate.glob3
         if is_head:
-            head_glob, bias_loss = gate["glob"], gate["glob3"][2:6].reshape(LOGITS)
-            grad_head = jnp.concatenate([gate["grad_w"], top["grad_fc"]], axis=1)
-            shard_head = to_owner(grad_head.reshape(owners, -1, HEADPAD))
+            head_glob, bias_loss = gate.glob, gate.glob3[2:6].reshape(LOGITS)
+            shard_head = to_owner(gate.grad_head)
+            blocks = gate.blocks
         else:
-            globs[k + 1]["one"] = gate["glob"]
+            globs_one[k + 1] = gate.glob
+            if k:
+                pair = to_owner(gate.blocks)
+                blocks = None
+            else:
+                shard_zero = to_owner(gate.blocks)
         tap = tap_back(
-            k == 0, row_count, exchange(gate["pay"]), gate["dz2"], layer, stream, layers[max(k - 1, 0)]
+            k == 0, row_count, exchange(gate.pay), gate.dz2, layer, stream, layers[max(k - 1, 0)]
         )
-        globs[k]["two"] = tap["glob"]
-        pay = tap["pay"]
-        upper = dict(
-            xb_far=layer["xb_far"], weights=layer["mats"], dz=tap["dz"], norm=layer["norm1"], taps=tap["taps"]
+        globs_two[k] = tap.glob
+        pay = tap.pay
+        if k == 1:
+            shard_head = replica_sum(shard_head)
+            pay = before(pay, shard_head)
+        upper = types.SimpleNamespace(
+            xb=layer.xb, weights=layer.mats, dz=tap.dz, norm=layer.norm1, taps=tap.taps
         )
-    late_taps = jnp.moveaxis(tap["taps"][:9].astype(BF16).reshape(9, owners, side_width), 1, 0)
+    pair = replica_sum(pair)
+    pay = before(pay, pair)
+    late_taps = jnp.moveaxis(tap.taps[:9].astype(BF16).reshape(9, owners, side_width), 1, 0)
     late_taps = jnp.broadcast_to(late_taps[None], (replicas, *late_taps.shape))
     late_taps = exchange(late_taps.reshape(devices, 9, side_width))
-    final = last_back(row_count, replicas, owners, exchange(pay), layers[0], tap["dz"])
-    globs[0]["one"] = final["glob"]
+    final = last_back(row_count, replicas, owners, exchange(pay), layers[0], tap.dz)
+    globs_one[0] = final.glob
     late_taps = jnp.sum(late_taps.astype(F32), axis=0)
-
-    shards = [None] * LAYERS
-    room = blocks[0].shape[1]
-    pair = replica_sum(to_owner(jnp.concatenate([blocks[2], blocks[1]], axis=1)))
-    shards[2], shards[1] = pair[:room], pair[room:]
-    shards[0] = replica_sum(to_owner(blocks[0]))
-    shard_head = replica_sum(shard_head)
+    room = pair.shape[0] // 2
+    shards = [replica_sum(shard_zero), pair[room:], pair[:room]]
 
     part = slice_rows(devices)
     chunks = EXPAND // CHUNK
-    late = jnp.sum(exchange(final["grads"]).astype(F32), axis=0).astype(BF16)
-    other = lax.ppermute(late, "fsdp", [(half + k, k) for k in range(half)])
-    late = spread_over(jnp.stack([late, other]), "dp")[:, :, : chunks * part]
+    late = jnp.sum(exchange(final.grads).astype(F32), axis=0).astype(BF16)
+    other = lax.ppermute(late, OWNERS, [(half + k, k) for k in range(half)])
+    late = spread_over(jnp.stack([late, other]), REPLICAS)[:, :, : chunks * part]
     late = jnp.moveaxis(late.reshape(replicas, 2, chunks, part, CHUNK), 2, 3)
     late = late.reshape(rows_dev, EXPAND).astype(F32)
 
@@ -1373,12 +1413,12 @@
         shard = shards[k][:, :side_width]
         taps = late_taps if k == 0 else shards[k - 1][last_row + 2 : last_row + 11, :side_width]
         norms_part = own_columns(
-            jnp.concatenate([globs[k]["one"][0:2], globs[k]["two"][0:2]], axis=0), side_width
+            jnp.concatenate([globs_one[k][0:2], globs_two[k][0:2]], axis=0), side_width
         )
         side_list.append(
             jnp.concatenate([taps, shard[first_row : last_row + 1], norms_part], axis=0)
         )
-        outer = globs[k]["three"]
+        outer = globs_three[k]
         outer = own_columns(
             jnp.concatenate([jnp.zeros((SQUEEZE,), F32), outer[0], outer[1]]), vec_width
         )
@@ -1415,7 +1455,7 @@
             group_sums(mats_dir, side_dir, head_dir, row_ids),
         ]
     )
-    norms = jnp.sqrt(jnp.sum(spread_over(squares, "fsdp"), axis=0))
+    norms = jnp.sqrt(jnp.sum(spread_over(squares, OWNERS), axis=0))
     mats_rate, side_rate, head_rate = rate_maps(norms[0] / norms[1], row_ids)
     mats_new = layer_mats - mats_rate[:, :, None] * mats_dir
     side_new = layer_side - side_rate[:, :, None] * side_dir
@@ -1434,8 +1474,8 @@
 
 
 def solution(mesh):
-    rows, columns = P(None, "fsdp", None), P(None, None, "fsdp")
-    vecs, heads = P(None, "fsdp"), P("fsdp", None)
+    rows, columns = P(None, OWNERS, None), P(None, None, OWNERS)
+    vecs, heads = P(None, OWNERS), P(OWNERS, None)
     return jax.shard_map(
         body,
         mesh=mesh,

time: 703 us -> 632 us (0.90)
  waiting for transfers between devices: 188 us -> 88.1 us
  blocking collectives: 122 us -> 201 us
  local copies, waits for them, and re-layouts: 111 us -> 43.1 us
  Pallas kernels: 156 us -> 182 us
    all_to_all x7 -> x9, blocking collectives: 89.1 us -> 170 us  [exchange(): return lax.all_to_all(payload, BOTH, 0, 0)]
    all_to_all x5 -> x2, waiting for transfers between devices: 50.4 us -> 4.86 us  [spread_over(): return lax.all_to_all(copies, axis, 0, 0)]
    unnamed x283 -> x129, local copies, waits for them, and re-layouts: 54.1 us -> 14.1 us
    all_to_all x12 -> x10, waiting for transfers between devices: 111 us -> 76.6 us  [exchange(): return lax.all_to_all(payload, BOTH, 0, 0)]
    pallas_call x19, Pallas kernels: 156 us -> 182 us  [call(): pl.pallas_call(flat, out_shape=[struct for struct, _ in outs.values()], i...]
    all_gather x3, waiting for transfers between devices: 18.7 us -> 0.06 us  [body(): lax.all_gather(layer_mats[k].astype(BF16), OWNERS, axis=0, tiled=True)]
    slice x10 -> x8, local copies, waits for them, and re-layouts: 24.7 us -> 6.79 us  [the longest x3 3.59 us: body(): globs_two[k][0:2]]
    ppermute x1 -> x10, starting transfers between devices: 1.29 us -> 13 us  [the longest x9 11.7 us: replica_sum(): total = total + lax.ppermute(array, REPLICAS, pairs).astype(F32)]
  transfers between devices with their start and end apart: 26 -> 30, of which waited for: 17 -> 11; matrix products, arithmetic and copies ran while one was open for 10% -> 9% of each run, Pallas kernels for 9% -> 24%
where the time goes in v3:
time: 632 us; the launch traced here: 620 us
  blocking collectives  201 us (32%)
  Pallas kernels  182 us (29%)
  waiting for transfers between devices  88.1 us (14%)
  starting transfers between devices  51.3 us (8%)
  local copies, waits for them, and re-layouts  43.1 us (7%)
  other arithmetic  35.3 us (6%)
  between operations  20.2 us (3%)
    pallas_call x19, Pallas kernels, call(): pl.pallas_call(flat, out_shape=[struct for struct, _ in outs.values()], i...  182 us
    all_to_all x9, blocking collectives, exchange(): return lax.all_to_all(payload, BOTH, 0, 0)  170 us
    all_to_all x10, waiting for transfers between devices, exchange(): return lax.all_to_all(payload, BOTH, 0, 0)  76.6 us
    all_to_all x10, starting transfers between devices, exchange(): return lax.all_to_all(payload, BOTH, 0, 0)  31.2 us
    all_gather x1, blocking collectives, body(): side_zero = lax.all_gather(side_low[0], OWNERS, axis=1, tiled=True)  31 us
    unnamed x129, local copies, waits for them, and re-layouts  14.1 us
  transfers between devices with their start and end apart: 30, of which 11 were waited for; matrix products, arithmetic and copies ran while one was open for 9% of the time, Pallas kernels for 24%

profile of v3, /device:TPU:0, one launch (start us, length us, event | category | flops | bytes accessed | tf_op | source)
XLA Modules:
  0.0 620.3 jit_solution(16269524334953227916)
XLA Ops:
  16.4 31.0 %all-gather = bf16[1,144,1536]{1,0,2:T(2,128)(2,1)S(1)} all-gather(bf16[1,144,192]{1,0,2:T(2,128)(2,1)S(1)} %slice.281), channel_id=2, replica_groups=mesh['dp'=4,'fsdp'=8] {'fsdp'}, dimensions={2}, use_global_device_ids=true | all-gather | bytes 497664 | tf_op jit(solution)/shard_map/all_gather | solution.py:1292
  57.9 18.8 %all_to_all.105.refs_0_ = bf16[32,16,128]{2,1,0:T(8,128)(2,1)} all-to-all(bf16[32,16,128]{2,1,0:T(8,128)(2,1)} %shard_map.324), channel_id=1, replica_groups=mesh['dp'=4,'fsdp'=8] {'dp','fsdp'}, dimensions={0} | all-to-all | bytes 262144 | tf_op jit(solution)/shard_map/all_to_all | solution.py:1239
  76.7 9.1 %shard_map.325 = (bf16[640,1536]{1,0:T(8,128)(2,1)}, bf16[32,40,128]{2,1,0:T(8,128)(2,1)}, f32[8,1536]{1,0:T(8,128)}) custom-call(bf16[32,16,128]{2,1,0:T(8,128)(2,1)} %all_to_all.105.refs_0_, bf16[144,1536]{1,0:T(8,128)(2,1)} %bitcast.127, bf16[640,256]{1,0:T(8,128)(2,1)} %get-tuple-element.107.refs_0_.refs_2_.refs_4_.refs_3_, bf16[512,1536]{1,0:T(8,128)(2,1)} %bitcast.109), custom_call_target="tpu_custom_call" | custom-call | tf_op jit(solution)/shard_map/pallas_call | solution.py:133
  85.8 22.9 %all_to_all.106.refs_0_ = bf16[32,40,128]{2,1,0:T(8,128)(2,1)} all-to-all(bf16[32,40,128]{2,1,0:T(8,128)(2,1)} %get-tuple-element.108), channel_id=1, replica_groups=mesh['dp'=4,'fsdp'=8] {'dp','fsdp'}, dimensions={0} | all-to-all | bytes 655360 | tf_op jit(solution)/shard_map/all_to_all | solution.py:1239
  146.4 9.1 %shard_map.328 = (bf16[640,1536]{1,0:T(8,128)(2,1)}, bf16[32,40,128]{2,1,0:T(8,128)(2,1)}, f32[8,1536]{1,0:T(8,128)}, f32[16,128]{1,0:T(8,128)}) custom-call(bf16[32,32,128]{2,1,0:T(8,128)(2,1)} %copy-done.7, bf16[144,1536]{1,0:T(8,128)(2,1)} %squeeze.47.refs_1_.refs_13_, bf16[640,256]{1,0:T(8,128)(2,1)} %get-tuple-element.115.refs_2_.refs_4_, ...), custom_call_target="tpu_custom_call" | custom-call | tf_op jit(solution)/shard_map/pallas_call | solution.py:133
  155.6 24.8 %all_to_all.107.refs_0_ = bf16[32,40,128]{2,1,0:T(8,128)(2,1)} all-to-all(bf16[32,40,128]{2,1,0:T(8,128)(2,1)} %get-tuple-element.116), channel_id=1, replica_groups=mesh['dp'=4,'fsdp'=8] {'dp','fsdp'}, dimensions={0} | all-to-all | bytes 655360 | tf_op jit(solution)/shard_map/all_to_all | solution.py:1239
  190.4 8.7 %all-to-all-done.5.refs_0_ = bf16[32,24,128]{2,1,0:T(8,128)(2,1)S(1)} async-done(((bf16[32,24,128]{2,1,0:T(8,128)(2,1)}), bf16[32,24,128]{2,1,0:T(8,128)(2,1)S(1)}, u32[]{:S(2)}, u32[]{:S(2)}) %all-to-all-start.5) | async-done | bytes 196640 | tf_op jit(solution)/shard_map/all_to_all | solution.py:1239
  209.2 9.2 %all-to-all-done.6.refs_0_ = bf16[32,32,128]{2,1,0:T(8,128)(2,1)S(1)} async-done(((bf16[32,32,128]{2,1,0:T(8,128)(2,1)}), bf16[32,32,128]{2,1,0:T(8,128)(2,1)S(1)}, u32[]{:S(2)}, u32[]{:S(2)}) %all-to-all-start.6) | async-done | bytes 262176 | tf_op jit(solution)/shard_map/all_to_all | solution.py:1239
  219.1 9.1 %shard_map.331 = (bf16[640,1536]{1,0:T(8,128)(2,1)}, bf16[32,40,128]{2,1,0:T(8,128)(2,1)}, f32[8,1536]{1,0:T(8,128)}, f32[16,128]{1,0:T(8,128)}) custom-call(bf16[32,32,128]{2,1,0:T(8,128)(2,1)} %copy-done.9, bf16[144,1536]{1,0:T(8,128)(2,1)} %squeeze.48.refs_1_.refs_13_, bf16[640,256]{1,0:T(8,128)(2,1)} %get-tuple-element.124.refs_2_.refs_4_, ...), custom_call_target="tpu_custom_call" | custom-call | tf_op jit(solution)/shard_map/pallas_call | solution.py:133
  228.2 15.4 %all_to_all.108.refs_0_ = bf16[32,40,128]{2,1,0:T(8,128)(2,1)} all-to-all(bf16[32,40,128]{2,1,0:T(8,128)(2,1)} %get-tuple-element.125), channel_id=1, replica_groups=mesh['dp'=4,'fsdp'=8] {'dp','fsdp'}, dimensions={0} | all-to-all | bytes 655360 | tf_op jit(solution)/shard_map/all_to_all | solution.py:1239
  272.4 9.0 %all-to-all-done.9.refs_0_ = bf16[32,32,128]{2,1,0:T(8,128)(2,1)S(1)} async-done(((bf16[32,32,128]{2,1,0:T(8,128)(2,1)}), bf16[32,32,128]{2,1,0:T(8,128)(2,1)S(1)}, u32[]{:S(2)}, u32[]{:S(2)}) %all-to-all-start.9) | async-done | bytes 262176 | tf_op jit(solution)/shard_map/all_to_all | solution.py:1239
  282.1 12.0 %shard_map.334 = (bf16[640,1280]{1,0:T(8,128)(2,1)}, bf16[32,48,128]{2,1,0:T(8,128)(2,1)}, f32[8,1280]{1,0:T(8,128)}, bf16[1280,1280]{1,0:T(8,128)(2,1)}) custom-call(bf16[32,32,128]{2,1,0:T(8,128)(2,1)} %copy-done.8, bf16[640,256]{1,0:T(8,128)(2,1)} %get-tuple-element.133.refs_1_.refs_2_, f32[1,1024]{1,0:T(1,128)} %bitcast.150, s32[40,1]{1,0:T(8,128)} %copy.127.refs_3_, ...), custom_call_target="tpu_custom_call" | custom-call | tf_op jit(solution)/shard_map/pallas_call | solution.py:133
  294.1 16.9 %all_to_all.109.refs_0_ = bf16[32,48,128]{2,1,0:T(8,128)(2,1)} all-to-all(bf16[32,48,128]{2,1,0:T(8,128)(2,1)} %get-tuple-element.135), channel_id=1, replica_groups=mesh['dp'=4,'fsdp'=8] {'dp','fsdp'}, dimensions={0} | all-to-all | bytes 786432 | tf_op jit(solution)/shard_map/all_to_all | solution.py:1239
  310.9 16.2 %shard_map.335 = (bf16[640,1536]{1,0:T(8,128)(2,1)}, bf16[32,24,128]{2,1,0:T(8,128)(2,1)}, f32[640,256]{1,0:T(8,128)}, bf16[8,1056,256]{2,1,0:T(8,128)(2,1)}, f3...) custom-call(bf16[32,48,128]{2,1,0:T(8,128)(2,1)} %all_to_all.109.refs_0_, ...), custom_call_target="tpu_custom_call", output_to_operand_aliasing={{6}: (14, {})} | custom-call | tf_op jit(solution)/shard_map/pallas_call | solution.py:133
  328.1 14.4 %all_to_all.110.refs_0_ = bf16[32,24,128]{2,1,0:T(8,128)(2,1)} all-to-all(bf16[32,24,128]{2,1,0:T(8,128)(2,1)S(1)} %copy-done.23), channel_id=1, replica_groups=mesh['dp'=4,'fsdp'=8] {'dp','fsdp'}, dimensions={0} | all-to-all | bytes 393216 | tf_op jit(solution)/shard_map/all_to_all | solution.py:1239
  342.4 13.8 %shard_map.336 = (bf16[640,1536]{1,0:T(8,128)(2,1)}, bf16[32,32,128]{2,1,0:T(8,128)(2,1)}, f32[16,1536]{1,0:T(8,128)}, f32[8,1536]{1,0:T(8,128)}) custom-call(bf16[32,24,128]{2,1,0:T(8,128)(2,1)} %all_to_all.110.refs_0_, bf16[144,1536]{1,0:T(8,128)(2,1)} %squeeze.48.refs_1_.refs_13_, f32[8,1536]{1,0:T(8,128)} %get-tuple-element.139.refs_7_.refs_2_, ...), custom_call_target="tpu_custom_call" | custom-call | tf_op jit(solution)/shard_map/pallas_call | solution.py:133
  356.2 18.6 %all_to_all.111.refs_0_ = bf16[32,32,128]{2,1,0:T(8,128)(2,1)} all-to-all(bf16[32,32,128]{2,1,0:T(8,128)(2,1)} %get-tuple-element.150), channel_id=1, replica_groups=mesh['dp'=4,'fsdp'=8] {'dp','fsdp'}, dimensions={0} | all-to-all | bytes 524288 | tf_op jit(solution)/shard_map/all_to_all | solution.py:1239
  374.8 16.6 %shard_map.337 = (bf16[640,1536]{1,0:T(8,128)(2,1)}, bf16[32,24,128]{2,1,0:T(8,128)(2,1)}, f32[640,256]{1,0:T(8,128)}, bf16[8,1056,256]{2,1,0:T(8,128)(2,1)}, f32[8,1536]{1,0:T(8,128)}, /*index=5*/f32[8,256]{1,0:T(8,128)}) custom-call(bf16[32,32,128]{2,1,0:T(8,128)(2,1)} %all_to_all.111.refs_0_, ...), custom_call_target="tpu_custom_call", output_to_operand_aliasing={{3}: (17, {})} | custom-call | tf_op jit(solution)/shard_map/pallas_call | solution.py:133
  395.1 19.7 %all_to_all.112.refs_0_ = bf16[32,24,128]{2,1,0:T(8,128)(2,1)} all-to-all(bf16[32,24,128]{2,1,0:T(8,128)(2,1)S(1)} %copy-done.22), channel_id=1, replica_groups=mesh['dp'=4,'fsdp'=8] {'dp','fsdp'}, dimensions={0} | all-to-all | bytes 393216 | tf_op jit(solution)/shard_map/all_to_all | solution.py:1239
  414.9 13.8 %shard_map.338 = (bf16[640,1536]{1,0:T(8,128)(2,1)}, bf16[32,32,128]{2,1,0:T(8,128)(2,1)}, f32[16,1536]{1,0:T(8,128)}, f32[8,1536]{1,0:T(8,128)}) custom-call(bf16[32,24,128]{2,1,0:T(8,128)(2,1)} %all_to_all.112.refs_0_, bf16[144,1536]{1,0:T(8,128)(2,1)} %squeeze.47.refs_1_.refs_13_, f32[8,1536]{1,0:T(8,128)} %get-tuple-element.153.refs_7_.refs_2_, ...), custom_call_target="tpu_custom_call" | custom-call | tf_op jit(solution)/shard_map/pallas_call | solution.py:133
  429.7 18.2 %all_to_all.113.refs_0_ = bf16[32,32,128]{2,1,0:T(8,128)(2,1)} all-to-all(bf16[32,32,128]{2,1,0:T(8,128)(2,1)S(1)} %copy-done.21), channel_id=1, replica_groups=mesh['dp'=4,'fsdp'=8] {'dp','fsdp'}, dimensions={0} | all-to-all | bytes 524288 | tf_op jit(solution)/shard_map/all_to_all | solution.py:1239
  447.8 16.7 %shard_map.339 = (bf16[640,1536]{1,0:T(8,128)(2,1)}, bf16[32,24,128]{2,1,0:T(8,128)(2,1)}, f32[640,256]{1,0:T(8,128)}, bf16[8,528,256]{2,1,0:T(8,128)(2,1)}, f32[8,1536]{1,0:T(8,128)}, /*index=5*/f32[8,256]{1,0:T(8,128)}) custom-call(bf16[32,32,128]{2,1,0:T(8,128)(2,1)} %all_to_all.113.refs_0_, f32[8,1536]{1,0:T(8,128)} %get-tuple-element.161.refs_3_.refs_1_, ...), custom_call_target="tpu_custom_call" | custom-call | tf_op jit(solution)/shard_map/pallas_call | solution.py:133
  479.6 18.7 %all-to-all-done.15.refs_0_ = bf16[32,24,128]{2,1,0:T(8,128)(2,1)S(1)} async-done(((bf16[32,24,128]{2,1,0:T(8,128)(2,1)}), bf16[32,24,128]{2,1,0:T(8,128)(2,1)S(1)}, u32[]{:S(2)}, u32[]{:S(2)}) %all-to-all-start.15) | async-done | bytes 196640 | tf_op jit(solution)/shard_map/all_to_all | solution.py:1239
  499.0 13.2 %shard_map.340 = (bf16[640,1536]{1,0:T(8,128)(2,1)}, bf16[32,24,128]{2,1,0:T(8,128)(2,1)}, f32[16,1536]{1,0:T(8,128)}, f32[8,1536]{1,0:T(8,128)}) custom-call(bf16[32,24,128]{2,1,0:T(8,128)(2,1)} %copy-done.10, bf16[144,1536]{1,0:T(8,128)(2,1)} %bitcast.130, f32[8,1536]{1,0:T(8,128)} %get-tuple-element.170.refs_7_.refs_2_, ...), custom_call_target="tpu_custom_call" | custom-call | tf_op jit(solution)/shard_map/pallas_call | solution.py:133
  (312 shorter events, 224.2 us)
Async XLA Ops:
  7.2 46.9 %all-gather.13.cloned.1.call-start = ((), (), s32[]{:S(2)}) async-start(), calls=%async_computation.28 | async-start | bytes 1769472 | tf_op jit(solution)/shard_map/all_gather | solution.py:1290
  10.5 108.2 %all-gather.15.cloned.1.call-start = ((), (), s32[]{:S(2)}) async-start(), calls=%async_computation.29 | async-start | bytes 1769472 | tf_op jit(solution)/shard_map/all_gather | solution.py:1290
  11.2 124.1 %all-gather.17.cloned.1.call-start = ((), (), s32[]{:S(2)}) async-start(), calls=%async_computation.30 | async-start | bytes 1327104 | tf_op jit(solution)/shard_map/all_gather | solution.py:1294
  14.7 175.8 %all-gather.19.cloned.1.call-start = ((), (), s32[]{:S(2)}) async-start(), calls=%async_computation.31 | async-start | bytes 1769472 | tf_op jit(solution)/shard_map/all_gather | solution.py:1290
  15.2 238.4 %all-gather.11.cloned.1.call-start = ((), (), s32[]{:S(2)}) async-start(), calls=%async_computation.24 | async-start | bytes 3686400 | tf_op jit(solution)/shard_map/all_gather | solution.py:1299
  132.7 13.0 %all-to-all-start.3 = ((bf16[32,32,128]{2,1,0:T(8,128)(2,1)}), bf16[32,32,128]{2,1,0:T(8,128)(2,1)S(1)}, u32[]{:S(2)}, u32[]{:S(2)}) async-start(bf16[32,32,128]{2,1,0:T(8,128)(2,1)} %get-tuple-element.114), calls=%async_computation.3 | async-start | bytes 524288 | tf_op jit(solution)/shard_map/all_to_all | solution.py:1239
  205.2 13.2 %all-to-all-start.6 = ((bf16[32,32,128]{2,1,0:T(8,128)(2,1)}), bf16[32,32,128]{2,1,0:T(8,128)(2,1)S(1)}, u32[]{:S(2)}, u32[]{:S(2)}) async-start(bf16[32,32,128]{2,1,0:T(8,128)(2,1)} %get-tuple-element.123), calls=%async_computation.6 | async-start | bytes 524288 | tf_op jit(solution)/shard_map/all_to_all | solution.py:1239
  268.4 13.0 %all-to-all-start.9 = ((bf16[32,32,128]{2,1,0:T(8,128)(2,1)}), bf16[32,32,128]{2,1,0:T(8,128)(2,1)S(1)}, u32[]{:S(2)}, u32[]{:S(2)}) async-start(bf16[32,32,128]{2,1,0:T(8,128)(2,1)} %get-tuple-element.132), calls=%async_computation.9 | async-start | bytes 524288 | tf_op jit(solution)/shard_map/all_to_all | solution.py:1239
  271.0 120.5 %reduce-scatter.4.cloned.1.call-start = ((), (), s32[]{:S(2)}) async-start(), calls=%async_computation.25 | async-start | bytes 3686400 | tf_op jit(solution)/shard_map/reduce_scatter | solution.py:1333
  327.2 142.2 %reduce-scatter.6.cloned.1.call-start = ((), (), s32[]{:S(2)}) async-start(), calls=%async_computation.26 | async-start | bytes 4866048 | tf_op jit(solution)/shard_map/reduce_scatter | solution.py:1333
  391.5 163.5 %reduce-scatter.8.cloned.1.call-start = ((), (), s32[]{:S(2)}) async-start(), calls=%async_computation.27 | async-start | bytes 2433024 | tf_op jit(solution)/shard_map/reduce_scatter | solution.py:1333
  391.6 37.1 %collective-permute-start = (bf16[160,1280]{1,0:T(8,128)(2,1)}, bf16[160,1280]{1,0:T(8,128)(2,1)S(1)}, u32[]{:S(2)}, u32[]{:S(2)}) collective-permute-start(bf16[160,1280]{1,0:T(8,128)(2,1)} %reduce-scatter.4.cloned.1.call-done), channel_id=1, source_target_pairs={{0,8},{8,16},{16,24},{24,0},{1,9},{9,17},{17,25},{25,1},{2,10},{10... | collective-permute-start | bytes 1228808 | tf_op jit(solution)/shard_map/ppermute | solution.py:1256
  391.6 37.1 %collective-permute-start.1 = (bf16[160,1280]{1,0:T(8,128)(2,1)}, bf16[160,1280]{1,0:T(8,128)(2,1)S(1)}, u32[]{:S(2)}, u32[]{:S(2)}) collective-permute-start(bf16[160,1280]{1,0:T(8,128)(2,1)} %reduce-scatter.4.cloned.1.call-done), channel_id=1, source_target_pairs={{0,16},{8,24},{16,0},{24,8},{1,17},{9,25},{17,1},{25,9},{2,18},{10... | collective-permute-start | bytes 1228808 | tf_op jit(solution)/shard_map/ppermute | solution.py:1256
  392.7 36.0 %collective-permute-start.2 = (bf16[160,1280]{1,0:T(8,128)(2,1)}, bf16[160,1280]{1,0:T(8,128)(2,1)S(1)}, u32[]{:S(2)}, u32[]{:S(2)}) collective-permute-start(bf16[160,1280]{1,0:T(8,128)(2,1)} %reduce-scatter.4.cloned.1.call-done), channel_id=1, source_target_pairs={{0,24},{8,0},{16,8},{24,16},{1,25},{9,1},{17,9},{25,17},{2,26},{10... | collective-permute-start | bytes 1228808 | tf_op jit(solution)/shard_map/ppermute | solution.py:1256
  469.4 42.8 %collective-permute-start.3 = (bf16[1056,256]{1,0:T(8,128)(2,1)}, bf16[1056,256]{1,0:T(8,128)(2,1)S(1)}, u32[]{:S(2)}, u32[]{:S(2)}) collective-permute-start(bf16[1056,256]{1,0:T(8,128)(2,1)} %reduce-scatter.6.cloned.1.call-done), channel_id=1, source_target_pairs={{0,8},{8,16},{16,24},{24,0},{1,9},{9,17},{17,25},{25,1},{2,10},{10... | collective-permute-start | bytes 1622024 | tf_op jit(solution)/shard_map/ppermute | solution.py:1256
  469.4 42.9 %collective-permute-start.4 = (bf16[1056,256]{1,0:T(8,128)(2,1)}, bf16[1056,256]{1,0:T(8,128)(2,1)}, u32[]{:S(2)}, u32[]{:S(2)}) collective-permute-start(bf16[1056,256]{1,0:T(8,128)(2,1)} %reduce-scatter.6.cloned.1.call-done), channel_id=1, source_target_pairs={{0,16},{8,24},{16,0},{24,8},{1,17},{9,25},{17,1},{25,9},{2,18},{10... | collective-permute-start | bytes 1622024 | tf_op jit(solution)/shard_map/ppermute | solution.py:1256
  470.5 42.5 %collective-permute-start.5 = (bf16[1056,256]{1,0:T(8,128)(2,1)}, bf16[1056,256]{1,0:T(8,128)(2,1)}, u32[]{:S(2)}, u32[]{:S(2)}) collective-permute-start(bf16[1056,256]{1,0:T(8,128)(2,1)} %reduce-scatter.6.cloned.1.call-done), channel_id=1, source_target_pairs={{0,24},{8,0},{16,8},{24,16},{1,25},{9,1},{17,9},{25,17},{2,26},{10... | collective-permute-start | bytes 1622024 | tf_op jit(solution)/shard_map/ppermute | solution.py:1256
  473.6 24.7 %all-to-all-start.15 = ((bf16[32,24,128]{2,1,0:T(8,128)(2,1)}), bf16[32,24,128]{2,1,0:T(8,128)(2,1)S(1)}, u32[]{:S(2)}, u32[]{:S(2)}) async-start(bf16[32,24,128]{2,1,0:T(8,128)(2,1)} %get-tuple-element.176), calls=%async_computation.16 | async-start | bytes 393216 | tf_op jit(solution)/shard_map/all_to_all | solution.py:1239
  514.7 12.0 %all-to-all-start.16 = ((bf16[32,24,128]{2,1,0:T(8,128)(2,1)}), bf16[32,24,128]{2,1,0:T(8,128)(2,1)}, u32[]{:S(2)}, u32[]{:S(2)}) async-start(bf16[32,24,128]{2,1,0:T(8,128)(2,1)} %get-tuple-element.181), calls=%async_computation.18 | async-start | bytes 393216 | tf_op jit(solution)/shard_map/all_to_all | solution.py:1239
  526.7 14.2 %all-to-all-start.19 = ((bf16[32,2,864]{2,1,0:T(2,128)(2,1)}), bf16[32,2,864]{2,1,0:T(2,128)(2,1)S(1)}, u32[]{:S(2)}, u32[]{:S(2)}) async-start(bf16[32,2,864]{2,1,0:T(2,128)(2,1)} %reshape.386), calls=%async_computation.22 | async-start | bytes 229376 | tf_op jit(solution)/shard_map/all_to_all | solution.py:1239
  541.0 27.8 %all-to-all-start.17 = ((bf16[32,48,256]{2,1,0:T(8,128)(2,1)}), bf16[32,48,256]{2,1,0:T(8,128)(2,1)S(1)}, u32[]{:S(2)}, u32[]{:S(2)}) async-start(bf16[32,48,256]{2,1,0:T(8,128)(2,1)} %get-tuple-element.183), calls=%async_computation.19 | async-start | bytes 1572864 | tf_op jit(solution)/shard_map/all_to_all | solution.py:1239
  555.0 24.8 %collective-permute-start.7 = (bf16[528,256]{1,0:T(8,128)(2,1)}, bf16[528,256]{1,0:T(8,128)(2,1)}, u32[]{:S(2)}, u32[]{:S(2)}) collective-permute-start(bf16[528,256]{1,0:T(8,128)(2,1)} %reduce-scatter.8.cloned.1.call-done), channel_id=1, source_target_pairs={{0,8},{8,16},{16,24},{24,0},{1,9},{9,17},{17,25},{25,1},{2,10},{10... | collective-permute-start | bytes 811016 | tf_op jit(solution)/shard_map/ppermute | solution.py:1256
  556.7 23.1 %collective-permute-start.8 = (bf16[528,256]{1,0:T(8,128)(2,1)}, bf16[528,256]{1,0:T(8,128)(2,1)}, u32[]{:S(2)}, u32[]{:S(2)}) collective-permute-start(bf16[528,256]{1,0:T(8,128)(2,1)} %reduce-scatter.8.cloned.1.call-done), channel_id=1, source_target_pairs={{0,16},{8,24},{16,0},{24,8},{1,17},{9,25},{17,1},{25,9},{2,18},{10... | collective-permute-start | bytes 811016 | tf_op jit(solution)/shard_map/ppermute | solution.py:1256
  558.2 21.6 %collective-permute-start.9 = (bf16[528,256]{1,0:T(8,128)(2,1)}, bf16[528,256]{1,0:T(8,128)(2,1)}, u32[]{:S(2)}, u32[]{:S(2)}) collective-permute-start(bf16[528,256]{1,0:T(8,128)(2,1)} %reduce-scatter.8.cloned.1.call-done), channel_id=1, source_target_pairs={{0,24},{8,0},{16,8},{24,16},{1,25},{9,1},{17,9},{25,17},{2,26},{10... | collective-permute-start | bytes 811016 | tf_op jit(solution)/shard_map/ppermute | solution.py:1256
  (65 other events, 369.8 us)
Sparse Core Ops, SparseCore 0:
  10.6 39.1 all-gather.12
  52.1 26.9 all-gather.14
  80.6 27.9 all-gather.16
  110.8 25.5 all-gather.18
  138.4 45.4 all-gather.10
  327.3 45.7 reduce-scatter.3
  391.6 56.2 reduce-scatter.5
  464.7 35.1 reduce-scatter.7

commit v4 on v3

--- a/solution.py
+++ b/solution.py
@@ -45,7 +45,7 @@
 TN = (((0,), (0,)), ((), ()))
 
 
-NEAR, FAR, RAW = range(3)
+NEAR, FAR, RAW, CHUNKS = range(4)
 
 
 class Refs:
@@ -55,17 +55,28 @@
         self.loads = loads
         self.stores = {id(getattr(self, name)): (k, self.far(name)) for k, name in enumerate(stores)}
         self.pending = {}
+        self.chunks = {}
 
     def far(self, name):
         return getattr(self, name + "_far")
 
     def start(self):
         for index, (name, where) in enumerate(self.loads):
-            source = self.far(name) if where is None else self.far(name).at[where]
+            source = self.far(name) if where is None or where == CHUNKS else self.far(name).at[where]
             near = getattr(self, name)
+            if where == CHUNKS:
+                self.chunks[id(near)] = (self.far(name), index)
+                for turn in range(near.shape[1] // CHUNK):
+                    self.chunk(near, turn, pl.ds(turn * CHUNK, CHUNK)).start()
+                continue
             copy = pltpu.make_async_copy(source, near, self.load_sem.at[index])
             copy.start()
             self.pending[id(near)] = copy
+
+    def chunk(self, near, turn, at):
+        far, index = self.chunks[id(near)]
+        semaphore = self.load_sem.at[len(self.loads) + index * (EXPAND // CHUNK) + turn]
+        return pltpu.make_async_copy(far.at[:, at], near.at[:, at], semaphore)
 
     def wait(self, *refs):
         for ref in refs:
@@ -109,7 +120,9 @@
             continue
         names.append(name + "_far")
         dims, where = array.shape, None
-        if place != FAR:
+        if place == CHUNKS:
+            where = CHUNKS
+        elif place != FAR:
             starts = [part.indices(size)[:2] for part, size in zip(place, dims)]
             dims = tuple(stop - start for start, stop in starts)
             where = tuple(pl.ds(start, stop - start) for start, stop in starts)
@@ -122,7 +135,7 @@
             extra[name] = vmem(struct.shape, struct.dtype)
     extra.update(scratch)
     extra.update(
-        load_sem=pltpu.SemaphoreType.DMA((max(len(loads), 1),)),
+        load_sem=pltpu.SemaphoreType.DMA((max(len(loads), 1) * (1 + EXPAND // CHUNK),)),
         store_sem=pltpu.SemaphoreType.DMA((max(len(stores), 1),)),
         part_sem=pltpu.SemaphoreType.DMA((EXPAND // CHUNK,)),
     )
@@ -272,12 +285,6 @@
     return spread(mean, 0, groups), lax.rsqrt(spread(variance, 0, groups) + EPS_BN)
 
 
-def pack_product_moments(x_ref, total, squares, count):
-    sums = column_sum(x_ref[...].astype(F32))
-    high = sums.astype(BF16).astype(F32)
-    return fold([high, sums - high, centred(total, squares, count)], 16)
-
-
 def read_product_moments(recv_ref, weights, transposed, columns, count):
     devices, rows = recv_ref.shape[:2]
     values = recv_ref[...]
@@ -308,19 +315,32 @@
     norm_ref[4:8, :] = jnp.zeros((4, norm_ref.shape[1]), F32)
 
 
-def product_sums(x_ref, w_ref, transposed, h_ref, stat_ref):
+def product_moments(x_ref, w_ref, transposed, columns, left_ref, stat_ref, beside=None):
+    count = x_ref.shape[0]
+    values = x_ref[...]
+    if beside is None:
+        square = dot_tn(values, values)
+    else:
+        product = dot_tn(jnp.concatenate([values, beside], axis=1), values)
+        square, cross = product[:WIDTH], product[WIDTH:]
+    sums = column_sum(values.astype(F32))
+    left_ref[0 : 2 * WIDTH, :] = stacked(square)
+    tail = jnp.concatenate([half.astype(F32) for half in halves(sums)] + [jnp.zeros((14, WIDTH), F32)], axis=0)
+    left_ref[2 * WIDTH :, :] = tail.astype(BF16)
+
     def step(index, carry):
         at = chunk_at(index)
-        if transposed:
-            h_ref[...] = dot_nt(x_ref[...], w_ref[at, :])
-        else:
-            h_ref[...] = dot(x_ref[...], w_ref[:, at])
-        hidden = h_ref[...]
-        stat_ref[0:1, at] = column_sum(hidden)
-        stat_ref[1:2, at] = column_sum(hidden * hidden)
+        weights = w_ref[at, :].T if transposed else w_ref[:, at]
+        product = dot(left_ref[...], weights)
+        total = column_sum(product[2 * WIDTH : 2 * WIDTH + 2])
+        squares = column_sum(folded(product[: 2 * WIDTH]) * weights.astype(F32))
+        stat_ref[0:1, at] = jnp.maximum(squares - total * total / count, 0.0)
         return carry
 
-    lax.fori_loop(0, stat_ref.shape[1] // CHUNK, step, 0)
+    lax.fori_loop(0, columns // CHUNK, step, 0, unroll=True)
+    high = sums.astype(BF16).astype(F32)
+    rows = fold([high, sums - high, stat_ref[0:1, :]], 16)
+    return rows if beside is None else (rows, cross)
 
 
 def mix_kernel(r):
@@ -356,20 +376,19 @@
 
 
 def first_kernel(r):
-    count = r.xb.shape[0]
     r.start()
     r.wait(r.xb, r.w)
-    product_sums(r.xb, r.w, False, r.h, r.stat)
-    write_alike(r.pay, pack_product_moments(r.xb, r.stat[0:1, :], r.stat[1:2, :], count))
+    write_alike(r.pay, product_moments(r.xb, r.w, False, EXPAND, r.left, r.stat))
+    r.send(r.pay)
+    r.finish()
 
 
 def first(xb, mats, devices):
-    count = xb.shape[0]
     return call(
         first_kernel,
         dict(xb=(xb, FAR), w=(mats, (slice(0, WIDTH), slice(None)))),
-        dict(pay=(shape((devices, 16, LANE), BF16), NEAR)),
-        dict(h=vmem((count, CHUNK), F32), stat=vmem((8, EXPAND), F32)),
+        dict(pay=(shape((devices, 16, LANE), BF16), FAR)),
+        dict(left=vmem((2 * WIDTH + 16, WIDTH), BF16), stat=vmem((8, EXPAND))),
     )
 
 
@@ -389,7 +408,7 @@
 def spatial_kernel(r):
     count = r.xb.shape[0]
     r.start()
-    r.wait(r.side, r.w, r.xb)
+    r.wait(r.recv, r.side, r.w, r.xb)
     rows = r.side[...].astype(F32)
     r.taps[0:9, :] = rows[0:9, :]
     mean, inverse = read_product_moments(r.recv, r.w[...], False, EXPAND, count)
@@ -397,6 +416,7 @@
     r.send(r.norm)
     if r.recv.shape[1] > 16:
         r.cross[...] = jnp.sum(r.recv[...].astype(F32)[:, 16:32], axis=0)
+        r.send(r.cross)
 
     def step(index, carry):
         at_chunk = chunk_at(index)
@@ -423,7 +443,7 @@
                 return total, squares
 
             zero = jnp.zeros((TILE, LANE), F32)
-            total, squares = lax.fori_loop(0, count // ROWS, tile_step, (zero, zero))
+            total, squares = lax.fori_loop(0, count // ROWS, tile_step, (zero, zero), unroll=True)
             r.stat[0:1, lanes] = column_sum(total)
             r.stat[1:2, lanes] = column_sum(squares)
         r.part(r.d, index, at_chunk).start()
@@ -431,6 +451,7 @@
 
     lax.fori_loop(0, EXPAND // CHUNK, step, 0)
     write_alike(r.pay, pack_moments(r.stat[0:1, :], r.stat[1:2, :], count))
+    r.send(r.pay)
     r.finish(r.d)
 
 
@@ -439,15 +460,15 @@
     devices = recv.shape[0]
     outs = dict(
         d=(shape((count, EXPAND), BF16), FAR),
-        pay=(shape((devices, moment_rows(EXPAND), LANE), BF16), NEAR),
+        pay=(shape((devices, moment_rows(EXPAND), LANE), BF16), FAR),
         norm=(shape((8, EXPAND)), FAR),
     )
     if recv.shape[1] > 16:
-        outs["cross"] = (shape((16, LANE)), NEAR)
+        outs["cross"] = (shape((16, LANE)), FAR)
     return call(
         spatial_kernel,
         dict(
-            recv=(recv, NEAR),
+            recv=(recv, FAR),
             side=(side, (slice(2 * SQUEEZE, SIDE_PAD), slice(None))),
             xb=(xb, FAR),
             w=(mats, (slice(0, WIDTH), slice(None))),
@@ -465,6 +486,7 @@
     count = r.d.shape[0]
     tiles = count // ROWS
     r.start()
+    r.wait(r.recv)
     mean, inverse = read_moments(r.recv, EXPAND, count)
     r.wait(r.side)
     rows = r.side[2 * SQUEEZE : SIDE_PAD, :].astype(F32)
@@ -477,21 +499,23 @@
     r.vec[...] = jnp.concatenate(
         [vec[:, SQUEEZE : SQUEEZE + WIDTH], vec[:, SQUEEZE + WIDTH :], jnp.zeros((6, WIDTH), F32)], axis=0
     )
-    r.wait(r.d)
+    r.send(r.vec)
 
     def activate(index, carry):
-        lanes = chunk_at(index, LANE)
-        scale_row = r.norm[2:3, lanes]
-        shift_row = r.norm[3:4, lanes]
-        for tile in range(tiles):
-            at = tile_rows(tile)
-            pre = r.d[at, lanes].astype(F32) * scale_row + shift_row
-            active = pre * sigmoid(pre)
-            r.a[at, lanes] = active
-            r.pooled[tile_images(tile), lanes] = jnp.sum(as_tile(active), axis=0) / MAP
+        r.chunk(r.d, index, chunk_at(index)).wait()
+        for part in range(PARTS):
+            lanes = chunk_at(index * PARTS + part, LANE)
+            scale_row = r.norm[2:3, lanes]
+            shift_row = r.norm[3:4, lanes]
+            for tile in range(tiles):
+                at = tile_rows(tile)
+                pre = r.d[at, lanes].astype(F32) * scale_row + shift_row
+                active = pre * sigmoid(pre)
+                r.a[at, lanes] = active
+                r.pooled[tile_images(tile), lanes] = jnp.sum(as_tile(active), axis=0) / MAP
         return carry
 
-    lax.fori_loop(0, EXPAND // LANE, activate, 0)
+    lax.fori_loop(0, EXPAND // CHUNK, activate, 0)
     r.send(r.pooled)
     before = folded(dot_nt(stacked(r.pooled[...]), r.side[0:SQUEEZE, :])) + vec[:, :SQUEEZE]
     r.squeeze[...] = before
@@ -515,8 +539,10 @@
     r.send(r.p)
     moments = pack_moments(column_sum(projected), column_sum(projected * projected), count)
     if with_cross:
+        r.wait(r.cross)
         moments = jnp.concatenate([moments, r.cross[...]], axis=0)
     write_alike(r.pay, moments)
+    r.send(r.pay)
     r.finish()
 
 
@@ -525,22 +551,22 @@
     images = count // MAP
     devices = recv.shape[0]
     ins = dict(
-        recv=(recv, NEAR),
+        recv=(recv, FAR),
         side=(side, FAR),
-        d=(d, FAR),
+        d=(d, CHUNKS),
         w=(mats, (slice(WIDTH, 2 * WIDTH), slice(None))),
     )
     rows = moment_rows(WIDTH)
     if cross is not None:
-        ins["cross"] = (cross, NEAR)
+        ins["cross"] = (cross, FAR)
         rows += 16
     return call(
         functools.partial(project_kernel, cross is not None, owners),
         ins,
         dict(
             p=(shape((count, WIDTH)), FAR),
-            vec=(shape((8, WIDTH)), NEAR),
-            pay=(shape((devices, rows, LANE), BF16), NEAR),
+            vec=(shape((8, WIDTH)), FAR),
+            pay=(shape((devices, rows, LANE), BF16), FAR),
             norm=(shape((8, EXPAND)), FAR),
             pooled=(shape((images, EXPAND)), FAR),
             excite=(shape((images, EXPAND)), FAR),
@@ -553,6 +579,7 @@
 def residual_kernel(transposed, with_cross, r):
     count = r.p.shape[0]
     r.start()
+    r.wait(r.recv, r.vec)
     mean, inverse = read_moments(r.recv, WIDTH, count)
     keep_norm(r.norm, mean, inverse, r.vec[0:1, :], r.vec[1:2, :])
     if with_cross:
@@ -566,11 +593,12 @@
     r.x[...] = result
     r.xb[...] = result.astype(BF16)
     r.send(r.norm, r.normed, r.x, r.xb)
-    cross = dot_tn(normed.astype(BF16), r.xb[...])
     r.wait(r.w)
-    product_sums(r.xb, r.w, transposed, r.h, r.stat)
-    moments = pack_product_moments(r.xb, r.stat[0:1, :], r.stat[1:2, :], count)
+    moments, cross = product_moments(
+        r.xb, r.w, transposed, r.stat.shape[1], r.left, r.stat, normed.astype(BF16)
+    )
     write_with_slices(r.pay, moments, cross)
+    r.send(r.pay)
     r.finish()
 
 
@@ -584,7 +612,7 @@
         x=(shape((count, WIDTH)), FAR),
         xb=(shape((count, WIDTH), BF16), FAR),
         normed=(shape((count, WIDTH)), FAR),
-        pay=(shape((devices, 32, LANE), BF16), NEAR),
+        pay=(shape((devices, 32, LANE), BF16), FAR),
         norm=(shape((8, WIDTH)), FAR),
     )
     if with_cross:
@@ -592,10 +620,10 @@
     return call(
         functools.partial(residual_kernel, transposed, with_cross),
         dict(
-            recv=(recv, NEAR), vec=(vec, NEAR), p=(p, FAR), before=(x, FAR), w=(weights, where)
+            recv=(recv, FAR), vec=(vec, FAR), p=(p, FAR), before=(x, FAR), w=(weights, where)
         ),
         outs,
-        dict(h=vmem((count, CHUNK), F32), stat=vmem((8, columns), F32)),
+        dict(left=vmem((2 * WIDTH + 16, WIDTH), BF16), stat=vmem((8, columns))),
     )
 
 
@@ -612,7 +640,7 @@
     tiles = count // ROWS
     images = count // MAP
     r.start()
-    r.wait(r.xb, r.w)
+    r.wait(r.recv, r.xb, r.w)
     mean, inverse = read_product_moments(r.recv, r.w[...], True, HEAD, count)
     cross = jnp.sum(r.recv[...].astype(F32)[:, 16:32], axis=0)
     r.wait(r.classifier)
@@ -702,6 +730,7 @@
         32,
     )
     write_alike(r.pay, jnp.concatenate([rows, cross], axis=0))
+    r.send(r.pay)
     fc_copy.wait()
     r.finish()
 
@@ -713,7 +742,7 @@
     return call(
         functools.partial(head_kernel, image_count),
         dict(
-            recv=(recv, NEAR),
+            recv=(recv, FAR),
             xb=(xb, FAR),
             bias=(bias, NEAR),
             label_col=(label_col, NEAR),
@@ -726,7 +755,7 @@
         ),
         dict(
             dz=(shape((count, HEAD), BF16), FAR),
-            pay=(shape((devices, 48, LANE), BF16), NEAR),
+            pay=(shape((devices, 48, LANE), BF16), FAR),
             norm=(shape((8, HEAD)), FAR),
             grad_head=(shape((HEAD, HEADPAD), BF16), RAW),
         ),
@@ -748,7 +777,7 @@
     r.glob[1:2, :] = sum_bias
     r.glob[2:8, :] = jnp.zeros((6, columns), F32)
     r.send(r.glob)
-    r.wait(r.unorm, r.xb, r.w, r.dz)
+    r.wait(r.unorm, r.xb, r.w)
     mean = r.unorm[0:1, :]
     scale = r.unorm[2:3, :]
     slant = scale * r.unorm[1:2, :] * (sum_gain / row_count)
@@ -759,6 +788,7 @@
 
     def step(index, carry):
         at = chunk_at(index)
+        r.chunk(r.dz, index, at).wait()
         if is_head:
             r.h[...] = dot_nt(r.xb[...], r.w[at, :])
         else:
@@ -772,7 +802,7 @@
             r.grad_w[:, at] = dot(r.xt[...], low).astype(r.grad_w.dtype)
         return carry
 
-    lax.fori_loop(0, columns // CHUNK, step, 0)
+    lax.fori_loop(0, columns // CHUNK, step, 0, unroll=True)
     return scale * sum_bias, slant
 
 
@@ -802,10 +832,11 @@
     tiles = count // ROWS
     rows_dev = 2 * WIDTH // owners
     r.start()
+    r.wait(r.recv)
     sums = read_sums(r.recv)
     bias_pull, slant = product_back(is_head, row_count, sums, columns, r)
     if is_head:
-        head_copy = pltpu.make_async_copy(r.grad_w, r.grad_head.at[:, pl.ds(0, WIDTH)], r.part_sem.at[0])
+        head_copy = pltpu.make_async_copy(r.grad_w, r.grad_head.at[:, pl.ds(0, WIDTH)], r.own_sem.at[0])
         head_copy.start()
         weights = r.w[...].astype(F32)
         column = lax.broadcasted_iota(jnp.int32, (1, WIDTH), 1)
@@ -825,10 +856,11 @@
         product = dot_nt(r.dh[...], r.w[...])
         square = product[count : count + WIDTH]
         pull = column_sum(product[count + WIDTH : count + WIDTH + 2])
+        r.wait(r.cross, r.stream_in)
         stream = r.stream_in[...] + product[0:count]
-        r.wait(r.cross)
         cross = r.cross[...]
     r.stream[...] = stream
+    r.send(r.stream)
     sum_bias = spread(sums, 2 * groups, WIDTH // LANE) - pull
     corrected = column_sum(cross.T * square)
     sum_gain = spread(sums, 2 * groups + WIDTH // LANE, WIDTH // LANE) - corrected
@@ -849,11 +881,12 @@
     )
     r.gp[...] = grad_p.astype(BF16)
     r.gt[...] = r.gp[...].T
-    r.wait(r.wp, r.d, r.norm2, r.excite)
+    r.wait(r.wp, r.norm2, r.excite)
     half = owners // 2
 
     def first(index, carry):
         at_chunk = chunk_at(index)
+        r.chunk(r.d, index, at_chunk).wait()
         r.h[...] = dot(r.gp[...], r.wp[:, at_chunk])
         for part in range(PARTS):
             lanes = chunk_at(index * PARTS + part, LANE)
@@ -870,8 +903,10 @@
                 factor = r.excite[near, lanes]
                 r.ge[near, lanes] = jnp.sum(as_tile(grad * active), axis=0)
                 r.y[at, lanes] = (as_tile(active) * factor[None]).reshape(ROWS, LANE).astype(BF16)
-                r.slope[at, lanes] = slope
-                r.u[at, lanes] = (as_tile(grad * slope) * factor[None]).reshape(ROWS, LANE)
+                r.slope[at, lanes] = slope.astype(r.slope.dtype)
+                r.u[at, lanes] = (
+                    (as_tile(grad * slope) * factor[None]).reshape(ROWS, LANE).astype(r.u.dtype)
+                )
         grad_p_chunk = dot(r.gt[...], r.y[:, at_chunk])
         place = pl.ds(pl.multiple_of(index * rows_dev, rows_dev), rows_dev)
         for owner in range(half):
@@ -897,27 +932,6 @@
     grad_pre = grad_squeezed * (opened * (1.0 + before * (1.0 - opened)))
     r.pool[...] = folded(dot(stacked(grad_pre), reduce_mat)) / MAP
 
-    def second(index, carry):
-        lanes = chunk_at(index, LANE)
-        mean_row = r.norm2[0:1, lanes]
-        total = jnp.zeros((TILE, LANE), F32)
-        weighted = jnp.zeros((TILE, LANE), F32)
-        for tile in range(tiles):
-            at = tile_rows(tile)
-            pool = r.pool[tile_images(tile), lanes]
-            grad = as_tile(r.u[at, lanes]) + as_tile(r.slope[at, lanes]) * pool[None]
-            total = total + jnp.sum(grad, axis=0)
-            weighted = weighted + jnp.sum(
-                grad * as_tile(r.d[at, lanes].astype(F32) - mean_row), axis=0
-            )
-            r.dz2[at, lanes] = grad.reshape(ROWS, LANE).astype(BF16)
-        r.stat[0:1, lanes] = column_sum(total)
-        r.stat[1:2, lanes] = column_sum(weighted)
-        return carry
-
-    lax.fori_loop(0, EXPAND // LANE, second, 0)
-    r.send(r.dz2)
-    write_alike(r.pay, fold([r.stat[0:1, :], r.stat[1:2, :] * r.norm2[1:2, :]], 24))
     squeezed_high, squeezed_low = halves(squeezed)
     pre_high, pre_low = halves(grad_pre)
     pooled_high, pooled_low = halves(r.pooled[...])
@@ -940,12 +954,36 @@
     owner_blocks(r, owners, half, taps)
     room = r.grads.shape[1]
     place = pl.ds((r.blocks.shape[1] - room) * (not is_head), room)
-    blocks_copy = pltpu.make_async_copy(r.grads, r.blocks.at[:, place, :], r.part_sem.at[1])
+    blocks_copy = pltpu.make_async_copy(r.grads, r.blocks.at[:, place, :], r.own_sem.at[1])
     blocks_copy.start()
+
+    def second(index, carry):
+        for part in range(PARTS):
+            lanes = chunk_at(index * PARTS + part, LANE)
+            mean_row = r.norm2[0:1, lanes]
+            total = jnp.zeros((TILE, LANE), F32)
+            weighted = jnp.zeros((TILE, LANE), F32)
+            for tile in range(tiles):
+                at = tile_rows(tile)
+                pool = r.pool[tile_images(tile), lanes]
+                grad = as_tile(r.u[at, lanes].astype(F32)) + as_tile(r.slope[at, lanes].astype(F32)) * pool[None]
+                total = total + jnp.sum(grad, axis=0)
+                weighted = weighted + jnp.sum(
+                    grad * as_tile(r.d[at, lanes].astype(F32) - mean_row), axis=0
+                )
+                r.dz2[at, lanes] = grad.reshape(ROWS, LANE).astype(BF16)
+            r.stat[0:1, lanes] = column_sum(total)
+            r.stat[1:2, lanes] = column_sum(weighted)
+        r.part(r.dz2, index, chunk_at(index)).start()
+        return carry
+
+    lax.fori_loop(0, EXPAND // CHUNK, second, 0)
+    write_alike(r.pay, fold([r.stat[0:1, :], r.stat[1:2, :] * r.norm2[1:2, :]], 24))
+    r.send(r.pay)
     blocks_copy.wait()
     if is_head:
         head_copy.wait()
-    r.finish()
+    r.finish(r.dz2)
 
 
 def gate_back(is_head, row_count, owners, recv, upper, cross, stream, lower, blocks, extra_room):
@@ -956,16 +994,16 @@
     block = EXPAND // CHUNK * (2 * WIDTH // owners) + 2 * SQUEEZE + 16
     where = (slice(0, HEAD), slice(0, WIDTH)) if is_head else (slice(0, WIDTH), slice(None))
     ins = dict(
-        recv=(recv, NEAR),
+        recv=(recv, FAR),
         unorm=(upper.norm, FAR),
         xb=(upper.xb, FAR),
         w=(upper.weights, where),
-        dz=(upper.dz, FAR),
+        dz=(upper.dz, CHUNKS),
         norm3=(lower.norm3, FAR),
         normed=(lower.normed, FAR),
         norm2=(lower.norm2, FAR),
         wp=(lower.mats, (slice(WIDTH, 2 * WIDTH), slice(None))),
-        d=(lower.d, FAR),
+        d=(lower.d, CHUNKS),
         excite=(lower.excite, FAR),
         pooled=(lower.pooled, FAR),
         squeeze=(lower.squeeze, FAR),
@@ -973,8 +1011,8 @@
     )
     outs = dict(
         dz2=(shape((count, EXPAND), BF16), FAR),
-        pay=(shape((devices, 24, LANE), BF16), NEAR),
-        stream=(shape((count, WIDTH)), NEAR),
+        pay=(shape((devices, 24, LANE), BF16), FAR),
+        stream=(shape((count, WIDTH)), FAR),
         blocks=(shape((owners, block * (1 + extra_room), CHUNK), BF16), RAW),
         glob=(shape((8, columns)), FAR),
         glob3=(shape((8, WIDTH)), FAR),
@@ -985,8 +1023,8 @@
         h=vmem((count, CHUNK), F32),
         coef=vmem((8, EXPAND), F32),
         dh=vmem((count + WIDTH + 16, columns), BF16),
-        u=vmem((count, EXPAND), F32),
-        slope=vmem((count, EXPAND), F32),
+        u=vmem((count, EXPAND), BF16),
+        slope=vmem((count, EXPAND), BF16),
         y=vmem((count, EXPAND), BF16),
         gp=vmem((count, WIDTH), BF16),
         gt=vmem((WIDTH, count), BF16),
@@ -996,6 +1034,7 @@
         excite_sum=vmem((1, EXPAND), F32),
         squeeze_sum=vmem((1, LANE), F32),
         stat=vmem((8, EXPAND), F32),
+        own_sem=pltpu.SemaphoreType.DMA((2,)),
     )
     alias = []
     if is_head:
@@ -1005,7 +1044,7 @@
         alias.append(("grad_head_in", "grad_head"))
     else:
         ins["cross"] = (cross, FAR)
-        ins["stream_in"] = (stream, NEAR)
+        ins["stream_in"] = (stream, FAR)
         ins["taps"] = (upper.taps, FAR)
         scratch["grad_w"] = vmem((WIDTH, EXPAND), BF16)
         if blocks is not None:
@@ -1019,6 +1058,7 @@
     count = r.dz2.shape[0]
     groups = EXPAND // LANE
     r.start()
+    r.wait(r.recv)
     sums = read_sums(r.recv)
     sum_bias = spread(sums, 0, groups)
     sum_gain = spread(sums, groups, groups)
@@ -1032,10 +1072,12 @@
     r.coef[0:9, :] = r.side[...].astype(F32)[0:9, :]
     r.coef[9:10, :] = slant2
     r.coef[10:11, :] = r.norm2[0:1, :] * slant2 - scale2 * (sum_bias / row_count)
-    r.wait(r.norm1, r.xb, r.w, r.d, r.dz2)
+    r.wait(r.norm1, r.xb, r.w)
 
     def step(index, carry):
         at_chunk = chunk_at(index)
+        r.chunk(r.dz2, index, at_chunk).wait()
+        r.chunk(r.d, index, at_chunk).wait()
         r.h[...] = dot(r.xb[...], r.w[:, at_chunk])
         for part in range(PARTS):
             lanes = chunk_at(index * PARTS + part, LANE)
@@ -1077,7 +1119,7 @@
                 return (*[sums_in[k] + tap_sums[k] for k in range(9)], total, weighted)
 
             zero = jnp.zeros((TILE, LANE), F32)
-            result = lax.fori_loop(0, count // ROWS, tile_step, (zero,) * 11)
+            result = lax.fori_loop(0, count // ROWS, tile_step, (zero,) * 11, unroll=True)
             for k in range(9):
                 r.taps[k : k + 1, lanes] = column_sum(result[k])
             r.stat[0:1, lanes] = column_sum(result[9])
@@ -1090,11 +1132,12 @@
     r.send(r.taps)
     vectors = [r.stat[0:1, :], r.stat[1:2, :] * r.norm1[1:2, :]]
     if not is_first:
+        r.wait(r.normed, r.stream)
         below = r.stream[...] + dot_nt(r.q[...], r.w[...])
-        r.wait(r.normed)
         vectors.append(column_sum(below))
         vectors.append(column_sum(below * r.normed[...]))
     write_alike(r.pay, fold(vectors, r.pay.shape[1]))
+    r.send(r.pay)
     r.finish(r.dz)
 
 
@@ -1102,14 +1145,14 @@
     count = dz2.shape[0]
     devices = recv.shape[0]
     ins = dict(
-        recv=(recv, NEAR),
+        recv=(recv, FAR),
         side=(layer.side, (slice(2 * SQUEEZE, SIDE_PAD), slice(None))),
         norm2=(layer.norm2, FAR),
         norm1=(layer.norm1, FAR),
         xb=(layer.xb, FAR),
         w=(layer.mats, (slice(0, WIDTH), slice(None))),
-        dz2=(dz2, FAR),
-        d=(layer.d, FAR),
+        dz2=(dz2, CHUNKS),
+        d=(layer.d, CHUNKS),
     )
     scratch = dict(
         h=vmem((count, CHUNK), F32),
@@ -1117,7 +1160,7 @@
         stat=vmem((8, EXPAND), F32),
     )
     if not is_first:
-        ins["stream"] = (stream, NEAR)
+        ins["stream"] = (stream, FAR)
         ins["normed"] = (below.normed, FAR)
         scratch["q"] = vmem((count, EXPAND), BF16)
     return call(
@@ -1125,7 +1168,7 @@
         ins,
         dict(
             dz=(shape((count, EXPAND), BF16), FAR),
-            pay=(shape((devices, 24 if is_first else 32, LANE), BF16), NEAR),
+            pay=(shape((devices, 24 if is_first else 32, LANE), BF16), FAR),
             taps=(shape((16, EXPAND)), FAR),
             glob=(shape((8, EXPAND)), FAR),
         ),
@@ -1135,22 +1178,25 @@
 
 def last_kernel(row_count, replicas, owners, r):
     r.start()
+    r.wait(r.recv)
     product_back(False, row_count, read_sums(r.recv), EXPAND, r)
     half = owners // 2
     part = slice_rows(replicas * owners)
     rows_dev = 2 * WIDTH // owners
     chunks = EXPAND // CHUNK
-    pad = r.grads.shape[1] - chunks * part
-    for replica in range(replicas):
-        for owner in range(owners):
-            first_row = rows_dev * (owner % half) + (2 * replica + owner // half) * part
-            own = r.grad_w[first_row : first_row + part, :]
-            block = jnp.concatenate(
-                [own[:, k * CHUNK : (k + 1) * CHUNK] for k in range(chunks)]
-                + ([jnp.zeros((pad, CHUNK), F32)] if pad else []),
-                axis=0,
-            )
-            r.grads[replica * owners + owner, :, :] = block.astype(BF16)
+    for device in range(replicas * owners):
+        replica, owner = device // owners, device % owners
+        first_row = rows_dev * (owner % half) + (2 * replica + owner // half) * part
+        for k in range(chunks):
+            r.shares[device, k * part : (k + 1) * part, :] = r.grad_w[
+                first_row : first_row + part, k * CHUNK : (k + 1) * CHUNK
+            ]
+    if r.shares.shape[1] > chunks * part:
+        r.shares[:, chunks * part :, :] = jnp.zeros(
+            (replicas * owners, r.shares.shape[1] - chunks * part, CHUNK), F32
+        )
+    r.grads[...] = r.shares[...].astype(BF16)
+    r.send(r.grads)
     r.finish()
 
 
@@ -1161,14 +1207,14 @@
     return call(
         functools.partial(last_kernel, row_count, replicas, owners),
         dict(
-            recv=(recv, NEAR),
-            dz=(dz, FAR),
+            recv=(recv, FAR),
+            dz=(dz, CHUNKS),
             unorm=(layer.norm1, FAR),
             xb=(layer.xb, FAR),
             w=(layer.mats, (slice(0, WIDTH), slice(None))),
         ),
         dict(
-            grads=(shape((devices, block, CHUNK), BF16), NEAR),
+            grads=(shape((devices, block, CHUNK), BF16), FAR),
             glob=(shape((8, EXPAND)), FAR),
         ),
         dict(
@@ -1177,6 +1223,7 @@
             coef=vmem((8, EXPAND), F32),
             dh=vmem((count, EXPAND), BF16),
             grad_w=vmem((WIDTH, EXPAND), F32),
+            shares=vmem((devices, block, CHUNK), F32),
         ),
     )
 

time: 632 us -> 601 us (0.951)
  Pallas kernels: 182 us -> 149 us
    pallas_call x19, Pallas kernels: 182 us -> 149 us  [call(): pl.pallas_call(flat, out_shape=[struct for struct, _ in outs.values()], i...]
  transfers between devices with their start and end apart: 30 -> 30, of which waited for: 11 -> 11; matrix products, arithmetic and copies ran while one was open for 9% -> 9% of each run, Pallas kernels for 24% -> 20%
where the time goes in v4:
time: 601 us; the launch traced here: 590 us
  blocking collectives  197 us (33%)
  Pallas kernels  149 us (25%)
  waiting for transfers between devices  91.8 us (15%)
  starting transfers between devices  53.5 us (9%)
  local copies, waits for them, and re-layouts  43.1 us (7%)
  other arithmetic  35.3 us (6%)
  between operations  20.2 us (3%)
    all_to_all x9, blocking collectives, exchange(): return lax.all_to_all(payload, BOTH, 0, 0)  166 us
    pallas_call x19, Pallas kernels, call(): pl.pallas_call(flat, out_shape=[struct for struct, _ in outs.values()], i...  149 us
    all_to_all x10, waiting for transfers between devices, exchange(): return lax.all_to_all(payload, BOTH, 0, 0)  80.2 us
    all_to_all x10, starting transfers between devices, exchange(): return lax.all_to_all(payload, BOTH, 0, 0)  33.3 us
    all_gather x1, blocking collectives, body(): side_zero = lax.all_gather(side_low[0], OWNERS, axis=1, tiled=True)  31 us
    unnamed x129, local copies, waits for them, and re-layouts  14.1 us
  transfers between devices with their start and end apart: 30, of which 11 were waited for; matrix products, arithmetic and copies ran while one was open for 9% of the time, Pallas kernels for 20%

profile of v4, /device:TPU:0, one launch (start us, length us, event | category | flops | bytes accessed | tf_op | source)
XLA Modules:
  0.0 590.4 jit_solution(3404493064963401142)
XLA Ops:
  16.4 31.0 %all-gather = bf16[1,144,1536]{1,0,2:T(2,128)(2,1)S(1)} all-gather(bf16[1,144,192]{1,0,2:T(2,128)(2,1)S(1)} %slice.281), channel_id=2, replica_groups=mesh['dp'=4,'fsdp'=8] {'fsdp'}, dimensions={2}, use_global_device_ids=true | all-gather | bytes 497664 | tf_op jit(solution)/shard_map/all_gather | solution.py:1339
  57.2 18.4 %all_to_all.105.refs_0_ = bf16[32,16,128]{2,1,0:T(8,128)(2,1)} all-to-all(bf16[32,16,128]{2,1,0:T(8,128)(2,1)} %shard_map.324), channel_id=1, replica_groups=mesh['dp'=4,'fsdp'=8] {'dp','fsdp'}, dimensions={0} | all-to-all | bytes 262144 | tf_op jit(solution)/shard_map/all_to_all | solution.py:1286
  82.6 19.8 %all_to_all.106.refs_0_ = bf16[32,40,128]{2,1,0:T(8,128)(2,1)} all-to-all(bf16[32,40,128]{2,1,0:T(8,128)(2,1)} %get-tuple-element.108), channel_id=1, replica_groups=mesh['dp'=4,'fsdp'=8] {'dp','fsdp'}, dimensions={0} | all-to-all | bytes 655360 | tf_op jit(solution)/shard_map/all_to_all | solution.py:1286
  112.2 7.4 %all-to-all-done.2.refs_0_ = bf16[32,8,128]{2,1,0:T(8,128)(2,1)S(1)} async-done(((bf16[32,8,128]{2,1,0:T(8,128)(2,1)}), bf16[32,8,128]{2,1,0:T(8,128)(2,1)S(1)}, u32[]{:S(2)}, u32[]{:S(2)}) %all-to-all-start.2) | async-done | bytes 65568 | tf_op jit(solution)/shard_map/all_to_all | solution.py:1286
  130.0 10.9 %all-to-all-done.3.refs_0_ = bf16[32,32,128]{2,1,0:T(8,128)(2,1)S(1)} async-done(((bf16[32,32,128]{2,1,0:T(8,128)(2,1)}), bf16[32,32,128]{2,1,0:T(8,128)(2,1)S(1)}, u32[]{:S(2)}, u32[]{:S(2)}) %all-to-all-start.3) | async-done | bytes 262176 | tf_op jit(solution)/shard_map/all_to_all | solution.py:1286
  148.7 24.2 %all_to_all.107.refs_0_ = bf16[32,40,128]{2,1,0:T(8,128)(2,1)} all-to-all(bf16[32,40,128]{2,1,0:T(8,128)(2,1)} %get-tuple-element.116), channel_id=1, replica_groups=mesh['dp'=4,'fsdp'=8] {'dp','fsdp'}, dimensions={0} | all-to-all | bytes 655360 | tf_op jit(solution)/shard_map/all_to_all | solution.py:1286
  181.5 9.4 %all-to-all-done.5.refs_0_ = bf16[32,24,128]{2,1,0:T(8,128)(2,1)S(1)} async-done(((bf16[32,24,128]{2,1,0:T(8,128)(2,1)}), bf16[32,24,128]{2,1,0:T(8,128)(2,1)S(1)}, u32[]{:S(2)}, u32[]{:S(2)}) %all-to-all-start.5) | async-done | bytes 196640 | tf_op jit(solution)/shard_map/all_to_all | solution.py:1286
  199.3 9.2 %all-to-all-done.6.refs_0_ = bf16[32,32,128]{2,1,0:T(8,128)(2,1)S(1)} async-done(((bf16[32,32,128]{2,1,0:T(8,128)(2,1)}), bf16[32,32,128]{2,1,0:T(8,128)(2,1)S(1)}, u32[]{:S(2)}, u32[]{:S(2)}) %all-to-all-start.6) | async-done | bytes 262176 | tf_op jit(solution)/shard_map/all_to_all | solution.py:1286
  216.3 15.4 %all_to_all.108.refs_0_ = bf16[32,40,128]{2,1,0:T(8,128)(2,1)} all-to-all(bf16[32,40,128]{2,1,0:T(8,128)(2,1)} %get-tuple-element.125), channel_id=1, replica_groups=mesh['dp'=4,'fsdp'=8] {'dp','fsdp'}, dimensions={0} | all-to-all | bytes 655360 | tf_op jit(solution)/shard_map/all_to_all | solution.py:1286
  240.0 8.7 %all-to-all-done.8.refs_0_ = bf16[32,24,128]{2,1,0:T(8,128)(2,1)S(1)} async-done(((bf16[32,24,128]{2,1,0:T(8,128)(2,1)}), bf16[32,24,128]{2,1,0:T(8,128)(2,1)S(1)}, u32[]{:S(2)}, u32[]{:S(2)}) %all-to-all-start.8) | async-done | bytes 196640 | tf_op jit(solution)/shard_map/all_to_all | solution.py:1286
  257.3 9.0 %all-to-all-done.9.refs_0_ = bf16[32,32,128]{2,1,0:T(8,128)(2,1)S(1)} async-done(((bf16[32,32,128]{2,1,0:T(8,128)(2,1)}), bf16[32,32,128]{2,1,0:T(8,128)(2,1)S(1)}, u32[]{:S(2)}, u32[]{:S(2)}) %all-to-all-start.9) | async-done | bytes 262176 | tf_op jit(solution)/shard_map/all_to_all | solution.py:1286
  267.0 12.1 %shard_map.334 = (bf16[640,1280]{1,0:T(8,128)(2,1)}, bf16[32,48,128]{2,1,0:T(8,128)(2,1)}, f32[8,1280]{1,0:T(8,128)}, bf16[1280,1280]{1,0:T(8,128)(2,1)}) custom-call(bf16[32,32,128]{2,1,0:T(8,128)(2,1)} %copy-done.8, bf16[640,256]{1,0:T(8,128)(2,1)} %get-tuple-element.133.refs_1_.refs_2_, f32[1,1024]{1,0:T(1,128)} %bitcast.150, s32[40,1]{1,0:T(8,128)} %copy.127.refs_3_, ...), custom_call_target="tpu_custom_call" | custom-call | tf_op jit(solution)/shard_map/pallas_call | solution.py:146
  279.1 17.0 %all_to_all.109.refs_0_ = bf16[32,48,128]{2,1,0:T(8,128)(2,1)} all-to-all(bf16[32,48,128]{2,1,0:T(8,128)(2,1)} %get-tuple-element.135), channel_id=1, replica_groups=mesh['dp'=4,'fsdp'=8] {'dp','fsdp'}, dimensions={0} | all-to-all | bytes 786432 | tf_op jit(solution)/shard_map/all_to_all | solution.py:1286
  296.1 13.2 %shard_map.335 = (bf16[640,1536]{1,0:T(8,128)(2,1)}, bf16[32,24,128]{2,1,0:T(8,128)(2,1)}, f32[640,256]{1,0:T(8,128)}, bf16[8,1056,256]{2,1,0:T(8,128)(2,1)}, f3...) custom-call(bf16[32,48,128]{2,1,0:T(8,128)(2,1)} %all_to_all.109.refs_0_, ...), custom_call_target="tpu_custom_call", output_to_operand_aliasing={{6}: (14, {})} | custom-call | tf_op jit(solution)/shard_map/pallas_call | solution.py:146
  310.2 14.4 %all_to_all.110.refs_0_ = bf16[32,24,128]{2,1,0:T(8,128)(2,1)} all-to-all(bf16[32,24,128]{2,1,0:T(8,128)(2,1)S(1)} %copy-done.23), channel_id=1, replica_groups=mesh['dp'=4,'fsdp'=8] {'dp','fsdp'}, dimensions={0} | all-to-all | bytes 393216 | tf_op jit(solution)/shard_map/all_to_all | solution.py:1286
  324.7 11.9 %shard_map.336 = (bf16[640,1536]{1,0:T(8,128)(2,1)}, bf16[32,32,128]{2,1,0:T(8,128)(2,1)}, f32[16,1536]{1,0:T(8,128)}, f32[8,1536]{1,0:T(8,128)}) custom-call(bf16[32,24,128]{2,1,0:T(8,128)(2,1)} %all_to_all.110.refs_0_, bf16[144,1536]{1,0:T(8,128)(2,1)} %squeeze.48.refs_1_.refs_13_, f32[8,1536]{1,0:T(8,128)} %get-tuple-element.139.refs_7_.refs_2_, ...), custom_call_target="tpu_custom_call" | custom-call | tf_op jit(solution)/shard_map/pallas_call | solution.py:146
  336.6 18.7 %all_to_all.111.refs_0_ = bf16[32,32,128]{2,1,0:T(8,128)(2,1)} all-to-all(bf16[32,32,128]{2,1,0:T(8,128)(2,1)} %get-tuple-element.150), channel_id=1, replica_groups=mesh['dp'=4,'fsdp'=8] {'dp','fsdp'}, dimensions={0} | all-to-all | bytes 524288 | tf_op jit(solution)/shard_map/all_to_all | solution.py:1286
  355.3 13.6 %shard_map.337 = (bf16[640,1536]{1,0:T(8,128)(2,1)}, bf16[32,24,128]{2,1,0:T(8,128)(2,1)}, f32[640,256]{1,0:T(8,128)}, bf16[8,1056,256]{2,1,0:T(8,128)(2,1)}, f32[8,1536]{1,0:T(8,128)}, /*index=5*/f32[8,256]{1,0:T(8,128)}) custom-call(bf16[32,32,128]{2,1,0:T(8,128)(2,1)} %all_to_all.111.refs_0_, ...), custom_call_target="tpu_custom_call", output_to_operand_aliasing={{3}: (17, {})} | custom-call | tf_op jit(solution)/shard_map/pallas_call | solution.py:146
  372.7 19.7 %all_to_all.112.refs_0_ = bf16[32,24,128]{2,1,0:T(8,128)(2,1)} all-to-all(bf16[32,24,128]{2,1,0:T(8,128)(2,1)S(1)} %copy-done.22), channel_id=1, replica_groups=mesh['dp'=4,'fsdp'=8] {'dp','fsdp'}, dimensions={0} | all-to-all | bytes 393216 | tf_op jit(solution)/shard_map/all_to_all | solution.py:1286
  392.4 12.0 %shard_map.338 = (bf16[640,1536]{1,0:T(8,128)(2,1)}, bf16[32,32,128]{2,1,0:T(8,128)(2,1)}, f32[16,1536]{1,0:T(8,128)}, f32[8,1536]{1,0:T(8,128)}) custom-call(bf16[32,24,128]{2,1,0:T(8,128)(2,1)} %all_to_all.112.refs_0_, bf16[144,1536]{1,0:T(8,128)(2,1)} %squeeze.47.refs_1_.refs_13_, f32[8,1536]{1,0:T(8,128)} %get-tuple-element.153.refs_7_.refs_2_, ...), custom_call_target="tpu_custom_call" | custom-call | tf_op jit(solution)/shard_map/pallas_call | solution.py:146
  405.4 18.3 %all_to_all.113.refs_0_ = bf16[32,32,128]{2,1,0:T(8,128)(2,1)} all-to-all(bf16[32,32,128]{2,1,0:T(8,128)(2,1)S(1)} %copy-done.21), channel_id=1, replica_groups=mesh['dp'=4,'fsdp'=8] {'dp','fsdp'}, dimensions={0} | all-to-all | bytes 524288 | tf_op jit(solution)/shard_map/all_to_all | solution.py:1286
  423.7 13.6 %shard_map.339 = (bf16[640,1536]{1,0:T(8,128)(2,1)}, bf16[32,24,128]{2,1,0:T(8,128)(2,1)}, f32[640,256]{1,0:T(8,128)}, bf16[8,528,256]{2,1,0:T(8,128)(2,1)}, f32[8,1536]{1,0:T(8,128)}, /*index=5*/f32[8,256]{1,0:T(8,128)}) custom-call(bf16[32,32,128]{2,1,0:T(8,128)(2,1)} %all_to_all.113.refs_0_, f32[8,1536]{1,0:T(8,128)} %get-tuple-element.161.refs_3_.refs_1_, ...), custom_call_target="tpu_custom_call" | custom-call | tf_op jit(solution)/shard_map/pallas_call | solution.py:146
  452.4 18.7 %all-to-all-done.15.refs_0_ = bf16[32,24,128]{2,1,0:T(8,128)(2,1)S(1)} async-done(((bf16[32,24,128]{2,1,0:T(8,128)(2,1)}), bf16[32,24,128]{2,1,0:T(8,128)(2,1)S(1)}, u32[]{:S(2)}, u32[]{:S(2)}) %all-to-all-start.15) | async-done | bytes 196640 | tf_op jit(solution)/shard_map/all_to_all | solution.py:1286
  471.8 10.8 %shard_map.340 = (bf16[640,1536]{1,0:T(8,128)(2,1)}, bf16[32,24,128]{2,1,0:T(8,128)(2,1)}, f32[16,1536]{1,0:T(8,128)}, f32[8,1536]{1,0:T(8,128)}) custom-call(bf16[32,24,128]{2,1,0:T(8,128)(2,1)} %copy-done.10, bf16[144,1536]{1,0:T(8,128)(2,1)} %bitcast.130, f32[8,1536]{1,0:T(8,128)} %get-tuple-element.170.refs_7_.refs_2_, ...), custom_call_target="tpu_custom_call" | custom-call | tf_op jit(solution)/shard_map/pallas_call | solution.py:146
  (312 shorter events, 212.8 us)
Async XLA Ops:
  7.2 46.9 %all-gather.13.cloned.1.call-start = ((), (), s32[]{:S(2)}) async-start(), calls=%async_computation.28 | async-start | bytes 1769472 | tf_op jit(solution)/shard_map/all_gather | solution.py:1337
  10.5 101.7 %all-gather.15.cloned.1.call-start = ((), (), s32[]{:S(2)}) async-start(), calls=%async_computation.29 | async-start | bytes 1769472 | tf_op jit(solution)/shard_map/all_gather | solution.py:1337
  11.2 115.5 %all-gather.17.cloned.1.call-start = ((), (), s32[]{:S(2)}) async-start(), calls=%async_computation.30 | async-start | bytes 1327104 | tf_op jit(solution)/shard_map/all_gather | solution.py:1341
  14.7 166.8 %all-gather.19.cloned.1.call-start = ((), (), s32[]{:S(2)}) async-start(), calls=%async_computation.31 | async-start | bytes 1769472 | tf_op jit(solution)/shard_map/all_gather | solution.py:1337
  15.2 224.7 %all-gather.11.cloned.1.call-start = ((), (), s32[]{:S(2)}) async-start(), calls=%async_computation.24 | async-start | bytes 3686400 | tf_op jit(solution)/shard_map/all_gather | solution.py:1346
  124.1 16.8 %all-to-all-start.3 = ((bf16[32,32,128]{2,1,0:T(8,128)(2,1)}), bf16[32,32,128]{2,1,0:T(8,128)(2,1)S(1)}, u32[]{:S(2)}, u32[]{:S(2)}) async-start(bf16[32,32,128]{2,1,0:T(8,128)(2,1)} %get-tuple-element.114), calls=%async_computation.3 | async-start | bytes 524288 | tf_op jit(solution)/shard_map/all_to_all | solution.py:1286
  178.6 12.3 %all-to-all-start.5 = ((bf16[32,24,128]{2,1,0:T(8,128)(2,1)}), bf16[32,24,128]{2,1,0:T(8,128)(2,1)S(1)}, u32[]{:S(2)}, u32[]{:S(2)}) async-start(bf16[32,24,128]{2,1,0:T(8,128)(2,1)} %get-tuple-element.119), calls=%async_computation.5 | async-start | bytes 393216 | tf_op jit(solution)/shard_map/all_to_all | solution.py:1286
  195.5 13.0 %all-to-all-start.6 = ((bf16[32,32,128]{2,1,0:T(8,128)(2,1)}), bf16[32,32,128]{2,1,0:T(8,128)(2,1)S(1)}, u32[]{:S(2)}, u32[]{:S(2)}) async-start(bf16[32,32,128]{2,1,0:T(8,128)(2,1)} %get-tuple-element.123), calls=%async_computation.6 | async-start | bytes 524288 | tf_op jit(solution)/shard_map/all_to_all | solution.py:1286
  253.3 13.0 %all-to-all-start.9 = ((bf16[32,32,128]{2,1,0:T(8,128)(2,1)}), bf16[32,32,128]{2,1,0:T(8,128)(2,1)S(1)}, u32[]{:S(2)}, u32[]{:S(2)}) async-start(bf16[32,32,128]{2,1,0:T(8,128)(2,1)} %get-tuple-element.132), calls=%async_computation.9 | async-start | bytes 524288 | tf_op jit(solution)/shard_map/all_to_all | solution.py:1286
  255.9 113.1 %reduce-scatter.4.cloned.1.call-start = ((), (), s32[]{:S(2)}) async-start(), calls=%async_computation.25 | async-start | bytes 3686400 | tf_op jit(solution)/shard_map/reduce_scatter | solution.py:1380
  309.3 132.9 %reduce-scatter.6.cloned.1.call-start = ((), (), s32[]{:S(2)}) async-start(), calls=%async_computation.26 | async-start | bytes 4866048 | tf_op jit(solution)/shard_map/reduce_scatter | solution.py:1380
  368.9 156.1 %reduce-scatter.8.cloned.1.call-start = ((), (), s32[]{:S(2)}) async-start(), calls=%async_computation.27 | async-start | bytes 2433024 | tf_op jit(solution)/shard_map/reduce_scatter | solution.py:1380
  369.0 35.4 %collective-permute-start = (bf16[160,1280]{1,0:T(8,128)(2,1)}, bf16[160,1280]{1,0:T(8,128)(2,1)S(1)}, u32[]{:S(2)}, u32[]{:S(2)}) collective-permute-start(bf16[160,1280]{1,0:T(8,128)(2,1)} %reduce-scatter.4.cloned.1.call-done), channel_id=1, source_target_pairs={{0,8},{8,16},{16,24},{24,0},{1,9},{9,17},{17,25},{25,1},{2,10},{10... | collective-permute-start | bytes 1228808 | tf_op jit(solution)/shard_map/ppermute | solution.py:1303
  369.1 35.4 %collective-permute-start.1 = (bf16[160,1280]{1,0:T(8,128)(2,1)}, bf16[160,1280]{1,0:T(8,128)(2,1)S(1)}, u32[]{:S(2)}, u32[]{:S(2)}) collective-permute-start(bf16[160,1280]{1,0:T(8,128)(2,1)} %reduce-scatter.4.cloned.1.call-done), channel_id=1, source_target_pairs={{0,16},{8,24},{16,0},{24,8},{1,17},{9,25},{17,1},{25,9},{2,18},{10... | collective-permute-start | bytes 1228808 | tf_op jit(solution)/shard_map/ppermute | solution.py:1303
  370.2 34.3 %collective-permute-start.2 = (bf16[160,1280]{1,0:T(8,128)(2,1)}, bf16[160,1280]{1,0:T(8,128)(2,1)S(1)}, u32[]{:S(2)}, u32[]{:S(2)}) collective-permute-start(bf16[160,1280]{1,0:T(8,128)(2,1)} %reduce-scatter.4.cloned.1.call-done), channel_id=1, source_target_pairs={{0,24},{8,0},{16,8},{24,16},{1,25},{9,1},{17,9},{25,17},{2,26},{10... | collective-permute-start | bytes 1228808 | tf_op jit(solution)/shard_map/ppermute | solution.py:1303
  442.2 40.4 %collective-permute-start.3 = (bf16[1056,256]{1,0:T(8,128)(2,1)}, bf16[1056,256]{1,0:T(8,128)(2,1)S(1)}, u32[]{:S(2)}, u32[]{:S(2)}) collective-permute-start(bf16[1056,256]{1,0:T(8,128)(2,1)} %reduce-scatter.6.cloned.1.call-done), channel_id=1, source_target_pairs={{0,8},{8,16},{16,24},{24,0},{1,9},{9,17},{17,25},{25,1},{2,10},{10... | collective-permute-start | bytes 1622024 | tf_op jit(solution)/shard_map/ppermute | solution.py:1303
  442.2 40.4 %collective-permute-start.4 = (bf16[1056,256]{1,0:T(8,128)(2,1)}, bf16[1056,256]{1,0:T(8,128)(2,1)}, u32[]{:S(2)}, u32[]{:S(2)}) collective-permute-start(bf16[1056,256]{1,0:T(8,128)(2,1)} %reduce-scatter.6.cloned.1.call-done), channel_id=1, source_target_pairs={{0,16},{8,24},{16,0},{24,8},{1,17},{9,25},{17,1},{25,9},{2,18},{10... | collective-permute-start | bytes 1622024 | tf_op jit(solution)/shard_map/ppermute | solution.py:1303
  443.3 40.1 %collective-permute-start.5 = (bf16[1056,256]{1,0:T(8,128)(2,1)}, bf16[1056,256]{1,0:T(8,128)(2,1)}, u32[]{:S(2)}, u32[]{:S(2)}) collective-permute-start(bf16[1056,256]{1,0:T(8,128)(2,1)} %reduce-scatter.6.cloned.1.call-done), channel_id=1, source_target_pairs={{0,24},{8,0},{16,8},{24,16},{1,25},{9,1},{17,9},{25,17},{2,26},{10... | collective-permute-start | bytes 1622024 | tf_op jit(solution)/shard_map/ppermute | solution.py:1303
  446.5 24.7 %all-to-all-start.15 = ((bf16[32,24,128]{2,1,0:T(8,128)(2,1)}), bf16[32,24,128]{2,1,0:T(8,128)(2,1)S(1)}, u32[]{:S(2)}, u32[]{:S(2)}) async-start(bf16[32,24,128]{2,1,0:T(8,128)(2,1)} %get-tuple-element.176), calls=%async_computation.16 | async-start | bytes 393216 | tf_op jit(solution)/shard_map/all_to_all | solution.py:1286
  497.1 13.9 %all-to-all-start.19 = ((bf16[32,2,864]{2,1,0:T(2,128)(2,1)}), bf16[32,2,864]{2,1,0:T(2,128)(2,1)S(1)}, u32[]{:S(2)}, u32[]{:S(2)}) async-start(bf16[32,2,864]{2,1,0:T(2,128)(2,1)} %reshape.386), calls=%async_computation.22 | async-start | bytes 229376 | tf_op jit(solution)/shard_map/all_to_all | solution.py:1286
  511.0 27.9 %all-to-all-start.17 = ((bf16[32,48,256]{2,1,0:T(8,128)(2,1)}), bf16[32,48,256]{2,1,0:T(8,128)(2,1)S(1)}, u32[]{:S(2)}, u32[]{:S(2)}) async-start(bf16[32,48,256]{2,1,0:T(8,128)(2,1)} %get-tuple-element.183), calls=%async_computation.19 | async-start | bytes 1572864 | tf_op jit(solution)/shard_map/all_to_all | solution.py:1286
  525.1 24.8 %collective-permute-start.7 = (bf16[528,256]{1,0:T(8,128)(2,1)}, bf16[528,256]{1,0:T(8,128)(2,1)}, u32[]{:S(2)}, u32[]{:S(2)}) collective-permute-start(bf16[528,256]{1,0:T(8,128)(2,1)} %reduce-scatter.8.cloned.1.call-done), channel_id=1, source_target_pairs={{0,8},{8,16},{16,24},{24,0},{1,9},{9,17},{17,25},{25,1},{2,10},{10... | collective-permute-start | bytes 811016 | tf_op jit(solution)/shard_map/ppermute | solution.py:1303
  526.8 23.1 %collective-permute-start.8 = (bf16[528,256]{1,0:T(8,128)(2,1)}, bf16[528,256]{1,0:T(8,128)(2,1)}, u32[]{:S(2)}, u32[]{:S(2)}) collective-permute-start(bf16[528,256]{1,0:T(8,128)(2,1)} %reduce-scatter.8.cloned.1.call-done), channel_id=1, source_target_pairs={{0,16},{8,24},{16,0},{24,8},{1,17},{9,25},{17,1},{25,9},{2,18},{10... | collective-permute-start | bytes 811016 | tf_op jit(solution)/shard_map/ppermute | solution.py:1303
  528.3 21.6 %collective-permute-start.9 = (bf16[528,256]{1,0:T(8,128)(2,1)}, bf16[528,256]{1,0:T(8,128)(2,1)}, u32[]{:S(2)}, u32[]{:S(2)}) collective-permute-start(bf16[528,256]{1,0:T(8,128)(2,1)} %reduce-scatter.8.cloned.1.call-done), channel_id=1, source_target_pairs={{0,24},{8,0},{16,8},{24,16},{1,25},{9,1},{17,9},{25,17},{2,26},{10... | collective-permute-start | bytes 811016 | tf_op jit(solution)/shard_map/ppermute | solution.py:1303
  (65 other events, 364.8 us)
Sparse Core Ops, SparseCore 0:
  10.6 39.1 all-gather.12
  52.1 26.9 all-gather.14
  80.6 26.9 all-gather.16
  109.7 28.5 all-gather.18
  140.3 46.8 all-gather.10
  309.5 46.2 reduce-scatter.3
  369.1 56.9 reduce-scatter.5
  437.5 34.7 reduce-scatter.7

commit v5 on v4

--- a/solution.py
+++ b/solution.py
@@ -45,7 +45,7 @@
 TN = (((0,), (0,)), ((), ()))
 
 
-NEAR, FAR, RAW, CHUNKS = range(4)
+NEAR, FAR, RAW, CHUNKS, LOOSE = range(5)
 
 
 class Refs:
@@ -110,11 +110,13 @@
 
 
 def call(kernel, ins, outs, scratch, alias=()):
-    near, far = pl.BlockSpec(memory_space=pltpu.VMEM), pl.BlockSpec(memory_space=pltpu.HBM)
+    near, far, loose = (
+        pl.BlockSpec(memory_space=space) for space in (pltpu.VMEM, pltpu.HBM, pl.ANY)
+    )
     names, arrays, in_specs, loads, stores, extra = [], [], [], [], [], {}
     for name, (array, place) in ins.items():
         arrays.append(array)
-        in_specs.append(near if place == NEAR else far)
+        in_specs.append(near if place == NEAR else loose if place == LOOSE else far)
         if place == NEAR or place == RAW:
             names.append(name)
             continue
@@ -122,7 +124,7 @@
         dims, where = array.shape, None
         if place == CHUNKS:
             where = CHUNKS
-        elif place != FAR:
+        elif place != FAR and place != LOOSE:
             starts = [part.indices(size)[:2] for part, size in zip(place, dims)]
             dims = tuple(stop - start for start, stop in starts)
             where = tuple(pl.ds(start, stop - start) for start, stop in starts)
@@ -259,8 +261,12 @@
     return jnp.concatenate([left, right], axis=1)
 
 
+def mean_parts(columns):
+    return 1 if columns == EXPAND else 2
+
+
 def moment_rows(columns):
-    return -(-3 * columns // LANE // 8) * 8
+    return -(-(mean_parts(columns) + 1) * columns // LANE // 8) * 8
 
 
 def centred(total, squares, count):
@@ -270,17 +276,21 @@
 def pack_moments(total, squares, count):
     mean = total / count
     high = mean.astype(BF16).astype(F32)
-    return fold([high, mean - high, centred(total, squares, count)], moment_rows(total.shape[1]))
+    parts = [high, mean - high][: mean_parts(total.shape[1])]
+    return fold(parts + [centred(total, squares, count)], moment_rows(total.shape[1]))
 
 
 def read_moments(recv_ref, columns, count):
     groups = columns // LANE
     devices = recv_ref.shape[0]
     parts = recv_ref[...].astype(F32)
-    means = parts[:, :groups] + parts[:, groups : 2 * groups]
+    given = mean_parts(columns)
+    means = parts[:, :groups]
+    if given > 1:
+        means = means + parts[:, groups : 2 * groups]
     mean = jnp.sum(means, axis=0) / devices
     apart = means - mean[None]
-    spread_sum = jnp.sum(parts[:, 2 * groups : 3 * groups], axis=0) / count
+    spread_sum = jnp.sum(parts[:, given * groups : (given + 1) * groups], axis=0) / count
     variance = (spread_sum + jnp.sum(apart * apart, axis=0)) / devices
     return spread(mean, 0, groups), lax.rsqrt(spread(variance, 0, groups) + EPS_BN)
 
@@ -468,7 +478,7 @@
     return call(
         spatial_kernel,
         dict(
-            recv=(recv, FAR),
+            recv=(recv, LOOSE),
             side=(side, (slice(2 * SQUEEZE, SIDE_PAD), slice(None))),
             xb=(xb, FAR),
             w=(mats, (slice(0, WIDTH), slice(None))),
@@ -551,7 +561,7 @@
     images = count // MAP
     devices = recv.shape[0]
     ins = dict(
-        recv=(recv, FAR),
+        recv=(recv, LOOSE),
         side=(side, FAR),
         d=(d, CHUNKS),
         w=(mats, (slice(WIDTH, 2 * WIDTH), slice(None))),
@@ -620,7 +630,7 @@
     return call(
         functools.partial(residual_kernel, transposed, with_cross),
         dict(
-            recv=(recv, FAR), vec=(vec, FAR), p=(p, FAR), before=(x, FAR), w=(weights, where)
+            recv=(recv, LOOSE), vec=(vec, FAR), p=(p, FAR), before=(x, FAR), w=(weights, where)
         ),
         outs,
         dict(left=vmem((2 * WIDTH + 16, WIDTH), BF16), stat=vmem((8, columns))),
@@ -710,12 +720,12 @@
             slope = as_tile(gate * (1.0 + pre * (1.0 - gate)))
             grad = slope * r.f[tile_images(tile), lanes][None]
             total = total + jnp.sum(grad, axis=0)
-            weighted = weighted + jnp.sum(grad * as_tile(hidden - mean_row), axis=0)
+            weighted = weighted + jnp.sum(grad * as_tile(hidden), axis=0)
             flat = grad.reshape(ROWS, LANE)
             r.dz[at, lanes] = flat.astype(BF16)
             r.q[at, lanes] = (flat * scale_row).astype(BF16)
         r.stat[0:1, lanes] = column_sum(total)
-        r.stat[1:2, lanes] = column_sum(weighted)
+        r.stat[1:2, lanes] = column_sum(weighted) - mean_row * column_sum(total)
         return carry
 
     lax.fori_loop(0, HEAD // LANE, back, 0)
@@ -742,7 +752,7 @@
     return call(
         functools.partial(head_kernel, image_count),
         dict(
-            recv=(recv, FAR),
+            recv=(recv, LOOSE),
             xb=(xb, FAR),
             bias=(bias, NEAR),
             label_col=(label_col, NEAR),
@@ -968,12 +978,10 @@
                 pool = r.pool[tile_images(tile), lanes]
                 grad = as_tile(r.u[at, lanes].astype(F32)) + as_tile(r.slope[at, lanes].astype(F32)) * pool[None]
                 total = total + jnp.sum(grad, axis=0)
-                weighted = weighted + jnp.sum(
-                    grad * as_tile(r.d[at, lanes].astype(F32) - mean_row), axis=0
-                )
+                weighted = weighted + jnp.sum(grad * as_tile(r.d[at, lanes].astype(F32)), axis=0)
                 r.dz2[at, lanes] = grad.reshape(ROWS, LANE).astype(BF16)
             r.stat[0:1, lanes] = column_sum(total)
-            r.stat[1:2, lanes] = column_sum(weighted)
+            r.stat[1:2, lanes] = column_sum(weighted) - mean_row * column_sum(total)
         r.part(r.dz2, index, chunk_at(index)).start()
         return carry
 
@@ -994,7 +1002,7 @@
     block = EXPAND // CHUNK * (2 * WIDTH // owners) + 2 * SQUEEZE + 16
     where = (slice(0, HEAD), slice(0, WIDTH)) if is_head else (slice(0, WIDTH), slice(None))
     ins = dict(
-        recv=(recv, FAR),
+        recv=(recv, LOOSE),
         unorm=(upper.norm, FAR),
         xb=(upper.xb, FAR),
         w=(upper.weights, where),
@@ -1097,7 +1105,7 @@
                 flat = pre * gate
                 active = as_tile(flat)
                 slope = as_tile(gate + flat - flat * gate)
-                apart = as_tile(hidden - r.norm1[0:1, lanes])
+                hidden = as_tile(hidden)
                 grad_a = [None] * MAP
                 tap_sums = [None] * 9
                 for target, tap, source in TERMS:
@@ -1110,7 +1118,7 @@
                 for place in range(MAP):
                     grad = grad_a[place] * slope[place]
                     total = total + grad
-                    weighted = weighted + grad * apart[place]
+                    weighted = weighted + grad * hidden[place]
                     grads.append(grad)
                 grad = jnp.concatenate(grads, axis=0)
                 r.dz[at, lanes] = grad.astype(BF16)
@@ -1122,8 +1130,9 @@
             result = lax.fori_loop(0, count // ROWS, tile_step, (zero,) * 11, unroll=True)
             for k in range(9):
                 r.taps[k : k + 1, lanes] = column_sum(result[k])
-            r.stat[0:1, lanes] = column_sum(result[9])
-            r.stat[1:2, lanes] = column_sum(result[10])
+            total = column_sum(result[9])
+            r.stat[0:1, lanes] = total
+            r.stat[1:2, lanes] = column_sum(result[10]) - r.norm1[0:1, lanes] * total
         r.part(r.dz, index, at_chunk).start()
         return carry
 
@@ -1145,7 +1154,7 @@
     count = dz2.shape[0]
     devices = recv.shape[0]
     ins = dict(
-        recv=(recv, FAR),
+        recv=(recv, LOOSE),
         side=(layer.side, (slice(2 * SQUEEZE, SIDE_PAD), slice(None))),
         norm2=(layer.norm2, FAR),
         norm1=(layer.norm1, FAR),
@@ -1207,7 +1216,7 @@
     return call(
         functools.partial(last_kernel, row_count, replicas, owners),
         dict(
-            recv=(recv, FAR),
+            recv=(recv, LOOSE),
             dz=(dz, CHUNKS),
             unorm=(layer.norm1, FAR),
             xb=(layer.xb, FAR),
@@ -1295,13 +1304,14 @@
     return lax.all_to_all(copies, axis, 0, 0)
 
 
-def replica_sum(array):
+def replica_sum(array, turned=False):
     count = lax.axis_size(REPLICAS)
-    total = array.astype(F32)
-    for turn in range(1, count):
-        pairs = [(k, (k + turn) % count) for k in range(count)]
-        total = total + lax.ppermute(array, REPLICAS, pairs).astype(F32)
-    return total
+    steps = [1 << k for k in range(count.bit_length() - 1)]
+    total = array
+    for step in reversed(steps) if turned else steps:
+        other = lax.ppermute(total, REPLICAS, [(k, k ^ step) for k in range(count)])
+        total = (total.astype(F32) + other.astype(F32)).astype(BF16)
+    return total.astype(F32)
 
 
 def body(
@@ -1333,16 +1343,20 @@
         ],
         axis=1,
     ).astype(BF16)
-    mats_all = [
-        lax.all_gather(layer_mats[k].astype(BF16), OWNERS, axis=0, tiled=True) for k in range(LAYERS)
+    side_rows = -(-SIDE_PAD * side_width // EXPAND)
+    side_flat = jnp.pad(side_low[0].reshape(-1), (0, side_rows * EXPAND - SIDE_PAD * side_width))
+    packed = lax.all_gather(
+        jnp.concatenate([layer_mats[0].astype(BF16), side_flat.reshape(side_rows, EXPAND)], axis=0),
+        OWNERS, axis=0,
+    )
+    mats_all = [packed[:, :rows_dev].reshape(2 * WIDTH, EXPAND)] + [
+        lax.all_gather(layer_mats[k].astype(BF16), OWNERS, axis=0, tiled=True) for k in range(1, LAYERS)
     ]
-    side_zero = lax.all_gather(side_low[0], OWNERS, axis=1, tiled=True)
     side_room = -(-side_width // CHUNK) * CHUNK
     side_rest = lax.all_gather(
         jnp.pad(side_low[1:], ((0, 0), (0, 0), (0, side_room - side_width))), OWNERS, axis=0
     )
     side_rest = jnp.moveaxis(side_rest[..., :side_width], 0, 2).reshape(LAYERS - 1, SIDE_PAD, EXPAND)
-    side_all = [side_zero, side_rest[0], side_rest[1]]
     head_full = lax.all_gather(
         jnp.pad(head_mat, ((0, 0), (0, HEADPAD - HEADCOLS))).astype(BF16), OWNERS, axis=0, tiled=True
     )
@@ -1350,9 +1364,12 @@
     partner_col = partner[:, None]
     layers = []
     crosses = []
-    entry = mix(before(images, side_zero).reshape(count, WIDTH), partner_col, mix_pair)
+    entry = mix(images.reshape(count, WIDTH), partner_col, mix_pair)
     x, xb = entry.x, entry.xb
     pay = first(xb, mats_all[0], devices).pay
+    side_flat = before(packed, pay)[:, rows_dev:].reshape(owners, -1)[:, : SIDE_PAD * side_width]
+    side_zero = jnp.moveaxis(side_flat.reshape(owners, SIDE_PAD, side_width), 0, 1).reshape(SIDE_PAD, EXPAND)
+    side_all = [side_zero, side_rest[0], side_rest[1]]
     for k in range(LAYERS):
         mats, side = mats_all[k], side_all[k]
         one = spatial(xb, mats, side, exchange(pay))
@@ -1415,19 +1432,18 @@
         globs_two[k] = tap.glob
         pay = tap.pay
         if k == 1:
-            shard_head = replica_sum(shard_head)
             pay = before(pay, shard_head)
         upper = types.SimpleNamespace(
             xb=layer.xb, weights=layer.mats, dz=tap.dz, norm=layer.norm1, taps=tap.taps
         )
-    pair = replica_sum(pair)
     pay = before(pay, pair)
     late_taps = jnp.moveaxis(tap.taps[:9].astype(BF16).reshape(9, owners, side_width), 1, 0)
     late_taps = jnp.broadcast_to(late_taps[None], (replicas, *late_taps.shape))
-    late_taps = exchange(late_taps.reshape(devices, 9, side_width))
-    final = last_back(row_count, replicas, owners, exchange(pay), layers[0], tap.dz)
+    received = exchange(pay)
+    final = last_back(row_count, replicas, owners, received, layers[0], tap.dz)
     globs_one[0] = final.glob
-    late_taps = jnp.sum(late_taps.astype(F32), axis=0)
+    shard_head = replica_sum(before(shard_head, received))
+    pair = replica_sum(before(pair, received), True)
     room = pair.shape[0] // 2
     shards = [replica_sum(shard_zero), pair[room:], pair[:room]]
 
@@ -1435,6 +1451,8 @@
     chunks = EXPAND // CHUNK
     late = jnp.sum(exchange(final.grads).astype(F32), axis=0).astype(BF16)
     other = lax.ppermute(late, OWNERS, [(half + k, k) for k in range(half)])
+    late_taps = exchange(before(late_taps.reshape(devices, 9, side_width), received))
+    late_taps = jnp.sum(late_taps.astype(F32), axis=0)
     late = spread_over(jnp.stack([late, other]), REPLICAS)[:, :, : chunks * part]
     late = jnp.moveaxis(late.reshape(replicas, 2, chunks, part, CHUNK), 2, 3)
     late = late.reshape(rows_dev, EXPAND).astype(F32)

time: 601 us -> 567 us (0.943)
  blocking collectives: 197 us -> 87.5 us
  waiting for transfers between devices: 91.8 us -> 161 us
    all_to_all x9 -> x6, blocking collectives: 166 us -> 87.5 us  [exchange(): return lax.all_to_all(payload, BOTH, 0, 0)]
    all_gather x1 -> x0, blocking collectives: 31 us -> none  [body(): side_zero = lax.all_gather(side_low[0], OWNERS, axis=1, tiled=True)]
    all_to_all x10 -> x13, waiting for transfers between devices: 80.2 us -> 109 us  [exchange(): return lax.all_to_all(payload, BOTH, 0, 0)]
    all_gather x0 -> x1, waiting for transfers between devices: none -> 25.2 us  [body(): lax.all_gather(jnp.concatenate([layer_mats[0].astype(BF16), side_flat.res...]
    ppermute x9 -> x6, waiting for transfers between devices: 0.02 us -> 16.6 us  [replica_sum(): other = lax.ppermute(total, REPLICAS, [(k, k ^ step) for k in range(count)])]
    all_to_all x10 -> x13, starting transfers between devices: 33.3 us -> 42.2 us  [exchange(): return lax.all_to_all(payload, BOTH, 0, 0)]
    unnamed x129 -> x119, local copies, waits for them, and re-layouts: 14.1 us -> 15.2 us
  transfers between devices with their start and end apart: 30 -> 30, of which waited for: 11 -> 17; matrix products, arithmetic and copies ran while one was open for 9% -> 9% of each run, Pallas kernels for 20% -> 21%
where the time goes in v5:
time: 567 us; the launch traced here: 557 us
  waiting for transfers between devices  161 us (28%)
  Pallas kernels  148 us (26%)
  blocking collectives  87.5 us (15%)
  starting transfers between devices  59 us (10%)
  local copies, waits for them, and re-layouts  41.7 us (7%)
  other arithmetic  39.5 us (7%)
  between operations  20.2 us (4%)
    pallas_call x19, Pallas kernels, call(): pl.pallas_call(flat, out_shape=[struct for struct, _ in outs.values()], i...  148 us
    all_to_all x13, waiting for transfers between devices, exchange(): return lax.all_to_all(payload, BOTH, 0, 0)  109 us
    all_to_all x6, blocking collectives, exchange(): return lax.all_to_all(payload, BOTH, 0, 0)  87.5 us
    all_to_all x13, starting transfers between devices, exchange(): return lax.all_to_all(payload, BOTH, 0, 0)  42.2 us
    all_gather x1, waiting for transfers between devices, body(): lax.all_gather(jnp.concatenate([layer_mats[0].astype(BF16), side_flat.res...  25.2 us
    ppermute x6, waiting for transfers between devices, replica_sum(): other = lax.ppermute(total, REPLICAS, [(k, k ^ step) for k in range(count)])  16.6 us
    unnamed x119, local copies, waits for them, and re-layouts  15.2 us
  transfers between devices with their start and end apart: 30, of which 17 were waited for; matrix products, arithmetic and copies ran while one was open for 9% of the time, Pallas kernels for 21%

profile of v5, /device:TPU:0, one launch (start us, length us, event | category | flops | bytes accessed | tf_op | source)
XLA Modules:
  0.0 556.9 jit_solution(7000880549462564529)
XLA Ops:
  19.4 25.2 %all-gather.19.cloned.1.call-done = bf16[8,82,1536]{2,1,0:T(8,128)(2,1)} async-done(((bf16[1,82,1536]{2,1,0:T(8,128)(2,1)}), bf16[8,82,1536]{2,1,0:T(8,128)(2,1)}) %all-gather.19.cloned.1.call-update) | async-done | bytes 2015248 | tf_op jit(solution)/shard_map/all_gather | solution.py:1348
  56.4 9.4 %all-to-all-done.refs_0_ = bf16[32,16,128]{2,1,0:T(8,128)(2,1)S(1)} async-done(((bf16[32,16,128]{2,1,0:T(8,128)(2,1)}), bf16[32,16,128]{2,1,0:T(8,128)(2,1)S(1)}, u32[]{:S(2)}, u32[]{:S(2)}) %all-to-all-start) | async-done | bytes 131104 | tf_op jit(solution)/shard_map/all_to_all | solution.py:1295
  73.5 12.0 %all_to_all.105.refs_0_ = bf16[32,24,128]{2,1,0:T(8,128)(2,1)} all-to-all(bf16[32,24,128]{2,1,0:T(8,128)(2,1)} %get-tuple-element.111), channel_id=1, replica_groups=mesh['dp'=4,'fsdp'=8] {'dp','fsdp'}, dimensions={0} | all-to-all | bytes 393216 | tf_op jit(solution)/shard_map/all_to_all | solution.py:1295
  111.5 14.2 %all-to-all-done.3.refs_0_ = bf16[32,32,128]{2,1,0:T(8,128)(2,1)S(1)} async-done(((bf16[32,32,128]{2,1,0:T(8,128)(2,1)}), bf16[32,32,128]{2,1,0:T(8,128)(2,1)S(1)}, u32[]{:S(2)}, u32[]{:S(2)}) %all-to-all-start.3) | async-done | bytes 262176 | tf_op jit(solution)/shard_map/all_to_all | solution.py:1295
  133.4 13.2 %all_to_all.106.refs_0_ = bf16[32,24,128]{2,1,0:T(8,128)(2,1)} all-to-all(bf16[32,24,128]{2,1,0:T(8,128)(2,1)} %get-tuple-element.119), channel_id=1, replica_groups=mesh['dp'=4,'fsdp'=8] {'dp','fsdp'}, dimensions={0} | all-to-all | bytes 393216 | tf_op jit(solution)/shard_map/all_to_all | solution.py:1295
  158.5 15.0 %all-to-all-done.5.refs_0_ = bf16[32,24,128]{2,1,0:T(8,128)(2,1)S(1)} async-done(((bf16[32,24,128]{2,1,0:T(8,128)(2,1)}), bf16[32,24,128]{2,1,0:T(8,128)(2,1)S(1)}, u32[]{:S(2)}, u32[]{:S(2)}) %all-to-all-start.5) | async-done | bytes 196640 | tf_op jit(solution)/shard_map/all_to_all | solution.py:1295
  181.9 9.2 %all-to-all-done.6.refs_0_ = bf16[32,32,128]{2,1,0:T(8,128)(2,1)S(1)} async-done(((bf16[32,32,128]{2,1,0:T(8,128)(2,1)}), bf16[32,32,128]{2,1,0:T(8,128)(2,1)S(1)}, u32[]{:S(2)}, u32[]{:S(2)}) %all-to-all-start.6) | async-done | bytes 262176 | tf_op jit(solution)/shard_map/all_to_all | solution.py:1295
  198.8 12.0 %all_to_all.107.refs_0_ = bf16[32,24,128]{2,1,0:T(8,128)(2,1)} all-to-all(bf16[32,24,128]{2,1,0:T(8,128)(2,1)} %get-tuple-element.128), channel_id=1, replica_groups=mesh['dp'=4,'fsdp'=8] {'dp','fsdp'}, dimensions={0} | all-to-all | bytes 393216 | tf_op jit(solution)/shard_map/all_to_all | solution.py:1295
  219.2 8.7 %all-to-all-done.8.refs_0_ = bf16[32,24,128]{2,1,0:T(8,128)(2,1)S(1)} async-done(((bf16[32,24,128]{2,1,0:T(8,128)(2,1)}), bf16[32,24,128]{2,1,0:T(8,128)(2,1)S(1)}, u32[]{:S(2)}, u32[]{:S(2)}) %all-to-all-start.8) | async-done | bytes 196640 | tf_op jit(solution)/shard_map/all_to_all | solution.py:1295
  236.5 9.0 %all-to-all-done.9.refs_0_ = bf16[32,32,128]{2,1,0:T(8,128)(2,1)S(1)} async-done(((bf16[32,32,128]{2,1,0:T(8,128)(2,1)}), bf16[32,32,128]{2,1,0:T(8,128)(2,1)S(1)}, u32[]{:S(2)}, u32[]{:S(2)}) %all-to-all-start.9) | async-done | bytes 262176 | tf_op jit(solution)/shard_map/all_to_all | solution.py:1295
  246.3 12.0 %shard_map.334 = (bf16[640,1280]{1,0:T(8,128)(2,1)}, bf16[32,48,128]{2,1,0:T(8,128)(2,1)}, f32[8,1280]{1,0:T(8,128)}, bf16[1280,1280]{1,0:T(8,128)(2,1)}) custom-call(bf16[32,32,128]{2,1,0:T(8,128)(2,1)} %copy-done.11, bf16[640,256]{1,0:T(8,128)(2,1)} %get-tuple-element.136.refs_1_.refs_2_, f32[1,1024]{1,0:T(1,128)} %bitcast.149, s32[40,1]{1,0:T(8,128)} %copy.134.refs_3_, ...), custom_call_target="tpu_custom_call" | custom-call | tf_op jit(solution)/shard_map/pallas_call | solution.py:148
  258.3 17.0 %all_to_all.108.refs_0_ = bf16[32,48,128]{2,1,0:T(8,128)(2,1)} all-to-all(bf16[32,48,128]{2,1,0:T(8,128)(2,1)} %get-tuple-element.138), channel_id=1, replica_groups=mesh['dp'=4,'fsdp'=8] {'dp','fsdp'}, dimensions={0} | all-to-all | bytes 786432 | tf_op jit(solution)/shard_map/all_to_all | solution.py:1295
  275.3 13.1 %shard_map.335 = (bf16[640,1536]{1,0:T(8,128)(2,1)}, bf16[32,24,128]{2,1,0:T(8,128)(2,1)}, f32[640,256]{1,0:T(8,128)}, bf16[8,1056,256]{2,1,0:T(8,128)(2,1)}, f3...) custom-call(bf16[32,48,128]{2,1,0:T(8,128)(2,1)} %all_to_all.108.refs_0_, ...), custom_call_target="tpu_custom_call", output_to_operand_aliasing={{6}: (14, {})} | custom-call | tf_op jit(solution)/shard_map/pallas_call | solution.py:148
  289.3 14.5 %all_to_all.109.refs_0_ = bf16[32,24,128]{2,1,0:T(8,128)(2,1)} all-to-all(bf16[32,24,128]{2,1,0:T(8,128)(2,1)S(1)} %copy-done.30), channel_id=1, replica_groups=mesh['dp'=4,'fsdp'=8] {'dp','fsdp'}, dimensions={0} | all-to-all | bytes 393216 | tf_op jit(solution)/shard_map/all_to_all | solution.py:1295
  303.8 11.7 %shard_map.336 = (bf16[640,1536]{1,0:T(8,128)(2,1)}, bf16[32,32,128]{2,1,0:T(8,128)(2,1)}, f32[16,1536]{1,0:T(8,128)}, f32[8,1536]{1,0:T(8,128)}) custom-call(bf16[32,24,128]{2,1,0:T(8,128)(2,1)} %all_to_all.109.refs_0_, bf16[144,1536]{1,0:T(8,128)(2,1)} %squeeze.44.refs_1_.refs_13_, f32[8,1536]{1,0:T(8,128)} %get-tuple-element.142.refs_7_.refs_2_, ...), custom_call_target="tpu_custom_call" | custom-call | tf_op jit(solution)/shard_map/pallas_call | solution.py:148
  315.5 18.7 %all_to_all.110.refs_0_ = bf16[32,32,128]{2,1,0:T(8,128)(2,1)} all-to-all(bf16[32,32,128]{2,1,0:T(8,128)(2,1)} %get-tuple-element.153), channel_id=1, replica_groups=mesh['dp'=4,'fsdp'=8] {'dp','fsdp'}, dimensions={0} | all-to-all | bytes 524288 | tf_op jit(solution)/shard_map/all_to_all | solution.py:1295
  334.2 13.5 %shard_map.337 = (bf16[640,1536]{1,0:T(8,128)(2,1)}, bf16[32,24,128]{2,1,0:T(8,128)(2,1)}, f32[640,256]{1,0:T(8,128)}, bf16[8,1056,256]{2,1,0:T(8,128)(2,1)}, f32[8,1536]{1,0:T(8,128)}, /*index=5*/f32[8,256]{1,0:T(8,128)}) custom-call(bf16[32,32,128]{2,1,0:T(8,128)(2,1)} %all_to_all.110.refs_0_, ...), custom_call_target="tpu_custom_call", output_to_operand_aliasing={{3}: (17, {})} | custom-call | tf_op jit(solution)/shard_map/pallas_call | solution.py:148
  356.7 9.1 %all-to-all-done.13.refs_0_ = bf16[32,24,128]{2,1,0:T(8,128)(2,1)S(1)} async-done(((bf16[32,24,128]{2,1,0:T(8,128)(2,1)}), bf16[32,24,128]{2,1,0:T(8,128)(2,1)S(1)}, u32[]{:S(2)}, u32[]{:S(2)}) %all-to-all-start.13) | async-done | bytes 196640 | tf_op jit(solution)/shard_map/all_to_all | solution.py:1295
  366.5 11.7 %shard_map.338 = (bf16[640,1536]{1,0:T(8,128)(2,1)}, bf16[32,32,128]{2,1,0:T(8,128)(2,1)}, f32[16,1536]{1,0:T(8,128)}, f32[8,1536]{1,0:T(8,128)}) custom-call(bf16[32,24,128]{2,1,0:T(8,128)(2,1)} %copy-done.19, bf16[144,1536]{1,0:T(8,128)(2,1)} %squeeze.43.refs_1_.refs_13_, f32[8,1536]{1,0:T(8,128)} %get-tuple-element.156.refs_7_.refs_2_, ...), custom_call_target="tpu_custom_call" | custom-call | tf_op jit(solution)/shard_map/pallas_call | solution.py:148
  385.0 11.4 %all-to-all-done.14.refs_0_ = bf16[32,32,128]{2,1,0:T(8,128)(2,1)S(1)} async-done(((bf16[32,32,128]{2,1,0:T(8,128)(2,1)}), bf16[32,32,128]{2,1,0:T(8,128)(2,1)S(1)}, u32[]{:S(2)}, u32[]{:S(2)}) %all-to-all-start.14) | async-done | bytes 262176 | tf_op jit(solution)/shard_map/all_to_all | solution.py:1295
  397.0 13.6 %shard_map.339 = (bf16[640,1536]{1,0:T(8,128)(2,1)}, bf16[32,24,128]{2,1,0:T(8,128)(2,1)}, f32[640,256]{1,0:T(8,128)}, bf16[8,528,256]{2,1,0:T(8,128)(2,1)}, f32[8,1536]{1,0:T(8,128)}, /*index=5*/f32[8,256]{1,0:T(8,128)}) custom-call(bf16[32,32,128]{2,1,0:T(8,128)(2,1)} %copy-done.9, f32[8,1536]{1,0:T(8,128)} %get-tuple-element.164.refs_3_.refs_1_, ...), custom_call_target="tpu_custom_call" | custom-call | tf_op jit(solution)/shard_map/pallas_call | solution.py:148
  422.6 10.7 %shard_map.340 = (bf16[640,1536]{1,0:T(8,128)(2,1)}, bf16[32,24,128]{2,1,0:T(8,128)(2,1)}, f32[16,1536]{1,0:T(8,128)}, f32[8,1536]{1,0:T(8,128)}) custom-call(bf16[32,24,128]{2,1,0:T(8,128)(2,1)} %copy-done.16, bf16[144,1536]{1,0:T(8,128)(2,1)} %reshape.365.refs_1_.refs_13_, f32[8,1536]{1,0:T(8,128)} %get-tuple-element.173.refs_7_.refs_2_, ...), custom_call_target="tpu_custom_call" | custom-call | tf_op jit(solution)/shard_map/pallas_call | solution.py:148
  439.3 9.3 %all-to-all-done.16.refs_0_ = bf16[32,24,128]{2,1,0:T(8,128)(2,1)S(1)} async-done(((bf16[32,24,128]{2,1,0:T(8,128)(2,1)}), bf16[32,24,128]{2,1,0:T(8,128)(2,1)S(1)}, u32[]{:S(2)}, u32[]{:S(2)}) %all-to-all-start.16) | async-done | bytes 196640 | tf_op jit(solution)/shard_map/all_to_all | solution.py:1295
  476.9 13.6 %collective-permute-done.6 = bf16[160,1280]{1,0:T(8,128)(2,1)S(1)} collective-permute-done((bf16[160,1280]{1,0:T(8,128)(2,1)S(1)}, bf16[160,1280]{1,0:T(8,128)(2,1)S(1)}, u32[]{:S(2)}, u32[]{:S(2)}) %collective-permute-start.6) | collective-permute-done | bytes 409632 | tf_op jit(solution)/shard_map/ppermute | solution.py:1312
  (309 shorter events, 229.0 us)
Async XLA Ops:
  7.2 37.3 %all-gather.19.cloned.1.call-start = ((), (), s32[]{:S(2)}) async-start(), calls=%async_computation.31 | async-start | bytes 2433024 | tf_op jit(solution)/shard_map/all_gather | solution.py:1348
  12.1 81.6 %all-gather.13.cloned.1.call-start = ((), (), s32[]{:S(2)}) async-start(), calls=%async_computation.28 | async-start | bytes 1769472 | tf_op jit(solution)/shard_map/all_gather | solution.py:1353
  12.8 95.4 %all-gather.15.cloned.1.call-start = ((), (), s32[]{:S(2)}) async-start(), calls=%async_computation.29 | async-start | bytes 1327104 | tf_op jit(solution)/shard_map/all_gather | solution.py:1356
  13.6 144.9 %all-gather.17.cloned.1.call-start = ((), (), s32[]{:S(2)}) async-start(), calls=%async_computation.30 | async-start | bytes 1769472 | tf_op jit(solution)/shard_map/all_gather | solution.py:1353
  14.2 205.0 %all-gather.11.cloned.1.call-start = ((), (), s32[]{:S(2)}) async-start(), calls=%async_computation.24 | async-start | bytes 3686400 | tf_op jit(solution)/shard_map/all_gather | solution.py:1360
  50.4 15.4 %all-to-all-start = ((bf16[32,16,128]{2,1,0:T(8,128)(2,1)}), bf16[32,16,128]{2,1,0:T(8,128)(2,1)S(1)}, u32[]{:S(2)}, u32[]{:S(2)}) async-start(bf16[32,16,128]{2,1,0:T(8,128)(2,1)} %shard_map.324), calls=%async_computation | async-start | bytes 262144 | tf_op jit(solution)/shard_map/all_to_all | solution.py:1295
  105.6 20.1 %all-to-all-start.3 = ((bf16[32,32,128]{2,1,0:T(8,128)(2,1)}), bf16[32,32,128]{2,1,0:T(8,128)(2,1)S(1)}, u32[]{:S(2)}, u32[]{:S(2)}) async-start(bf16[32,32,128]{2,1,0:T(8,128)(2,1)} %get-tuple-element.117), calls=%async_computation.3 | async-start | bytes 524288 | tf_op jit(solution)/shard_map/all_to_all | solution.py:1295
  152.3 21.2 %all-to-all-start.5 = ((bf16[32,24,128]{2,1,0:T(8,128)(2,1)}), bf16[32,24,128]{2,1,0:T(8,128)(2,1)S(1)}, u32[]{:S(2)}, u32[]{:S(2)}) async-start(bf16[32,24,128]{2,1,0:T(8,128)(2,1)} %get-tuple-element.122), calls=%async_computation.5 | async-start | bytes 393216 | tf_op jit(solution)/shard_map/all_to_all | solution.py:1295
  178.1 13.0 %all-to-all-start.6 = ((bf16[32,32,128]{2,1,0:T(8,128)(2,1)}), bf16[32,32,128]{2,1,0:T(8,128)(2,1)S(1)}, u32[]{:S(2)}, u32[]{:S(2)}) async-start(bf16[32,32,128]{2,1,0:T(8,128)(2,1)} %get-tuple-element.126), calls=%async_computation.6 | async-start | bytes 524288 | tf_op jit(solution)/shard_map/all_to_all | solution.py:1295
  216.5 11.4 %all-to-all-start.8 = ((bf16[32,24,128]{2,1,0:T(8,128)(2,1)}), bf16[32,24,128]{2,1,0:T(8,128)(2,1)S(1)}, u32[]{:S(2)}, u32[]{:S(2)}) async-start(bf16[32,24,128]{2,1,0:T(8,128)(2,1)} %get-tuple-element.131), calls=%async_computation.8 | async-start | bytes 393216 | tf_op jit(solution)/shard_map/all_to_all | solution.py:1295
  232.5 13.1 %all-to-all-start.9 = ((bf16[32,32,128]{2,1,0:T(8,128)(2,1)}), bf16[32,32,128]{2,1,0:T(8,128)(2,1)S(1)}, u32[]{:S(2)}, u32[]{:S(2)}) async-start(bf16[32,32,128]{2,1,0:T(8,128)(2,1)} %get-tuple-element.135), calls=%async_computation.9 | async-start | bytes 524288 | tf_op jit(solution)/shard_map/all_to_all | solution.py:1295
  235.2 143.1 %reduce-scatter.4.cloned.1.call-start = ((), (), s32[]{:S(2)}) async-start(), calls=%async_computation.25 | async-start | bytes 3686400 | tf_op jit(solution)/shard_map/reduce_scatter | solution.py:1397
  288.4 144.9 %reduce-scatter.6.cloned.1.call-start = ((), (), s32[]{:S(2)}) async-start(), calls=%async_computation.26 | async-start | bytes 4866048 | tf_op jit(solution)/shard_map/reduce_scatter | solution.py:1397
  350.3 15.5 %all-to-all-start.13 = ((bf16[32,24,128]{2,1,0:T(8,128)(2,1)}), bf16[32,24,128]{2,1,0:T(8,128)(2,1)S(1)}, u32[]{:S(2)}, u32[]{:S(2)}) async-start(bf16[32,24,128]{2,1,0:T(8,128)(2,1)} %get-tuple-element.163), calls=%async_computation.13 | async-start | bytes 393216 | tf_op jit(solution)/shard_map/all_to_all | solution.py:1295
  378.3 18.0 %all-to-all-start.14 = ((bf16[32,32,128]{2,1,0:T(8,128)(2,1)}), bf16[32,32,128]{2,1,0:T(8,128)(2,1)S(1)}, u32[]{:S(2)}, u32[]{:S(2)}) async-start(bf16[32,32,128]{2,1,0:T(8,128)(2,1)} %get-tuple-element.170), calls=%async_computation.15 | async-start | bytes 524288 | tf_op jit(solution)/shard_map/all_to_all | solution.py:1295
  413.2 82.9 %reduce-scatter.8.cloned.1.call-start = ((), (), s32[]{:S(2)}) async-start(), calls=%async_computation.27 | async-start | bytes 2433024 | tf_op jit(solution)/shard_map/reduce_scatter | solution.py:1397
  433.4 15.1 %all-to-all-start.16 = ((bf16[32,24,128]{2,1,0:T(8,128)(2,1)}), bf16[32,24,128]{2,1,0:T(8,128)(2,1)S(1)}, u32[]{:S(2)}, u32[]{:S(2)}) async-start(bf16[32,24,128]{2,1,0:T(8,128)(2,1)} %get-tuple-element.184), calls=%async_computation.18 | async-start | bytes 393216 | tf_op jit(solution)/shard_map/all_to_all | solution.py:1295
  448.5 23.7 %collective-permute-start.5 = (bf16[160,1280]{1,0:T(8,128)(2,1)}, bf16[160,1280]{1,0:T(8,128)(2,1)}, u32[]{:S(2)}, u32[]{:S(2)}) collective-permute-start(bf16[160,1280]{1,0:T(8,128)(2,1)} %reduce-scatter.4.cloned.1.call-done), channel_id=1, source_target_pairs={{0,8},{8,0},{16,24},{24,16},{1,9},{9,1},{17,25},{25,17},{2,10},{10... | collective-permute-start | bytes 1228808 | tf_op jit(solution)/shard_map/ppermute | solution.py:1312
  451.2 14.4 %all-to-all-start.19 = ((bf16[32,2,864]{2,1,0:T(2,128)(2,1)}), bf16[32,2,864]{2,1,0:T(2,128)(2,1)S(1)}, u32[]{:S(2)}, u32[]{:S(2)}) async-start(bf16[32,2,864]{2,1,0:T(2,128)(2,1)} %reshape.401), calls=%async_computation.22 | async-start | bytes 229376 | tf_op jit(solution)/shard_map/all_to_all | solution.py:1295
  455.6 19.7 %collective-permute-start.3 = (bf16[1056,256]{1,0:T(8,128)(2,1)S(1)}, bf16[1056,256]{1,0:T(8,128)(2,1)S(1)}, u32[]{:S(2)}, u32[]{:S(2)}) collective-permute-start(bf16[1056,256]{1,0:T(8,128)(2,1)S(1)} %copy-done.23), channel_id=1, source_target_pairs={{0,16},{8,24},{16,0},{24,8},{1,17},{9,25},{17,1},{25,9},{2,18},{10... | collective-permute-start | bytes 1622024 | tf_op jit(solution)/shard_map/ppermute | solution.py:1312
  466.2 30.6 %all-to-all-start.17 = ((bf16[32,48,256]{2,1,0:T(8,128)(2,1)}), bf16[32,48,256]{2,1,0:T(8,128)(2,1)}, u32[]{:S(2)}, u32[]{:S(2)}) async-start(bf16[32,48,256]{2,1,0:T(8,128)(2,1)} %get-tuple-element.186), calls=%async_computation.19 | async-start | bytes 1572864 | tf_op jit(solution)/shard_map/all_to_all | solution.py:1295
  473.5 17.1 %collective-permute-start.6 = (bf16[160,1280]{1,0:T(8,128)(2,1)S(1)}, bf16[160,1280]{1,0:T(8,128)(2,1)S(1)}, u32[]{:S(2)}, u32[]{:S(2)}) collective-permute-start(bf16[160,1280]{1,0:T(8,128)(2,1)S(1)} %add_convert_fusion.3), channel_id=1, source_target_pairs={{0,16},{8,24},{16,0},{24,8},{1,17},{9,25},{17,1},{25,9},{2,18},{10... | collective-permute-start | bytes 1228808 | tf_op jit(solution)/shard_map/ppermute | solution.py:1312
  475.4 19.1 %collective-permute-start.4 = (bf16[1056,256]{1,0:T(8,128)(2,1)S(1)}, bf16[1056,256]{1,0:T(8,128)(2,1)S(1)}, u32[]{:S(2)}, u32[]{:S(2)}) collective-permute-start(bf16[1056,256]{1,0:T(8,128)(2,1)S(1)} %add_convert_fusion.1), channel_id=1, source_target_pairs={{0,8},{8,0},{16,24},{24,16},{1,9},{9,1},{17,25},{25,17},{2,10},{10... | collective-permute-start | bytes 1622024 | tf_op jit(solution)/shard_map/ppermute | solution.py:1312
  496.1 13.6 %collective-permute-start.1 = (bf16[528,256]{1,0:T(8,128)(2,1)}, bf16[528,256]{1,0:T(8,128)(2,1)}, u32[]{:S(2)}, u32[]{:S(2)}) collective-permute-start(bf16[528,256]{1,0:T(8,128)(2,1)} %reduce-scatter.8.cloned.1.call-done), channel_id=1, source_target_pairs={{0,8},{8,0},{16,24},{24,16},{1,9},{9,1},{17,25},{25,17},{2,10},{10... | collective-permute-start | bytes 811016 | tf_op jit(solution)/shard_map/ppermute | solution.py:1312
  (63 other events, 376.0 us)
Sparse Core Ops, SparseCore 0:
  12.2 32.3 all-gather.18
  46.8 27.6 all-gather.12
  76.1 21.2 all-gather.14
  99.5 30.4 all-gather.16
  132.1 45.2 all-gather.10
  288.5 46.2 reduce-scatter.3
  347.9 57.0 reduce-scatter.5
  416.4 39.1 reduce-scatter.7

commit v6 on v5

--- a/solution.py
+++ b/solution.py
@@ -295,7 +295,7 @@
     return spread(mean, 0, groups), lax.rsqrt(spread(variance, 0, groups) + EPS_BN)
 
 
-def read_product_moments(recv_ref, weights, transposed, columns, count):
+def product_means(recv_ref, weights, transposed, count):
     devices, rows = recv_ref.shape[:2]
     values = recv_ref[...]
     flat = values.reshape(devices * rows, LANE)
@@ -304,7 +304,34 @@
     left = dot(jnp.where((column == 0) | (column == 2), 1.0, 0.0).astype(BF16), flat)
     right = dot(jnp.where((column == 1) | (column == 3), 1.0, 0.0).astype(BF16), flat)
     sums = stacked(jnp.concatenate([left, right], axis=1) / count)
-    means = folded(dot_nt(sums, weights) if transposed else dot(sums, weights))
+    return folded(dot_nt(sums, weights) if transposed else dot(sums, weights))
+
+
+def read_square_moments(recv_ref, square_ref, w_ref, left_ref, stat_ref, count):
+    devices = recv_ref.shape[0]
+    means = product_means(recv_ref, w_ref[...], False, count)
+    mean = column_sum(means) / devices
+    apart = means - mean
+    left_ref[...] = jnp.concatenate(
+        [read_matrix(square_ref, 0), read_matrix(square_ref, 16)], axis=0
+    ).astype(BF16)
+
+    def step(index, carry):
+        at = chunk_at(index)
+        weights = w_ref[:, at]
+        squares = column_sum(folded(dot(left_ref[...], weights)) * weights.astype(F32))
+        stat_ref[0:1, at] = jnp.maximum(squares, 0.0)
+        return carry
+
+    lax.fori_loop(0, w_ref.shape[1] // CHUNK, step, 0, unroll=True)
+    variance = (stat_ref[0:1, :] / count + column_sum(apart * apart)) / devices
+    return mean, lax.rsqrt(variance + EPS_BN)
+
+
+def read_product_moments(recv_ref, weights, transposed, columns, count):
+    devices = recv_ref.shape[0]
+    values = recv_ref[...]
+    means = product_means(recv_ref, weights, transposed, count)
     mean = column_sum(means) / devices
     apart = means - mean
     squares = jnp.sum(values.astype(F32), axis=0)
@@ -325,14 +352,11 @@
     norm_ref[4:8, :] = jnp.zeros((4, norm_ref.shape[1]), F32)
 
 
-def product_moments(x_ref, w_ref, transposed, columns, left_ref, stat_ref, beside=None):
+def product_moments(x_ref, w_ref, transposed, columns, left_ref, stat_ref, beside):
     count = x_ref.shape[0]
     values = x_ref[...]
-    if beside is None:
-        square = dot_tn(values, values)
-    else:
-        product = dot_tn(jnp.concatenate([values, beside], axis=1), values)
-        square, cross = product[:WIDTH], product[WIDTH:]
+    product = dot_tn(jnp.concatenate([values, beside], axis=1), values)
+    square, cross = product[:WIDTH], product[WIDTH:]
     sums = column_sum(values.astype(F32))
     left_ref[0 : 2 * WIDTH, :] = stacked(square)
     tail = jnp.concatenate([half.astype(F32) for half in halves(sums)] + [jnp.zeros((14, WIDTH), F32)], axis=0)
@@ -349,8 +373,7 @@
 
     lax.fori_loop(0, columns // CHUNK, step, 0, unroll=True)
     high = sums.astype(BF16).astype(F32)
-    rows = fold([high, sums - high, stat_ref[0:1, :]], 16)
-    return rows if beside is None else (rows, cross)
+    return fold([high, sums - high, stat_ref[0:1, :]], 16), cross
 
 
 def mix_kernel(r):
@@ -372,33 +395,56 @@
         r.x[tile_rows(tile), :] = mixed
     r.xb[...] = r.x[...].astype(BF16)
     r.send(r.x, r.xb)
+    low = r.xb[...]
+    sums = column_sum(low.astype(F32))
+    padded = jnp.concatenate([sums, jnp.zeros((TILE - 1, WIDTH), F32)], axis=0)
+    outer = lax.dot_general(
+        padded, padded, TN, preferred_element_type=F32, precision=lax.Precision.HIGHEST
+    )
+    square = dot_tn(low, low) - outer / count
+    high = sums.astype(BF16).astype(F32)
+    rows = fold([high, sums - high], 8)
+    devices = r.pay.shape[0]
+    part = slice_rows(devices)
+    for device in range(devices):
+        own = square[device * part : (device + 1) * part, :]
+        block = [rows, own[:, :LANE], own[:, LANE:]]
+        if 2 * part < 16:
+            block.append(jnp.zeros((16 - 2 * part, LANE), F32))
+        r.pay[device, :, :] = jnp.concatenate(block, axis=0).astype(BF16)
+    r.send(r.pay)
     r.finish()
 
 
-def mix(images, partner, mix_pair):
+def mix(images, partner, mix_pair, devices):
     dims = images.shape
     return call(
         mix_kernel,
         dict(images=(images, NEAR), partner=(partner, NEAR), mix=(mix_pair, NEAR)),
-        dict(x=(shape(dims), FAR), xb=(shape(dims, BF16), FAR)),
+        dict(
+            x=(shape(dims), FAR),
+            xb=(shape(dims, BF16), FAR),
+            pay=(shape((devices, 24, LANE), BF16), FAR),
+        ),
         {},
     )
 
 
-def first_kernel(r):
+def share_kernel(r):
     r.start()
-    r.wait(r.xb, r.w)
-    write_alike(r.pay, product_moments(r.xb, r.w, False, EXPAND, r.left, r.stat))
+    r.wait(r.recv)
+    high, low = halves(jnp.sum(r.recv[...].astype(F32), axis=0)[8:24])
+    write_alike(r.pay, jnp.concatenate([high.astype(F32), low.astype(F32)], axis=0))
     r.send(r.pay)
     r.finish()
 
 
-def first(xb, mats, devices):
+def share(recv):
     return call(
-        first_kernel,
-        dict(xb=(xb, FAR), w=(mats, (slice(0, WIDTH), slice(None)))),
-        dict(pay=(shape((devices, 16, LANE), BF16), FAR)),
-        dict(left=vmem((2 * WIDTH + 16, WIDTH), BF16), stat=vmem((8, EXPAND))),
+        share_kernel,
+        dict(recv=(recv, LOOSE)),
+        dict(pay=(shape((recv.shape[0], 32, LANE), BF16), FAR)),
+        {},
     )
 
 
@@ -415,16 +461,20 @@
 TERMS = list(tap_terms())
 
 
-def spatial_kernel(r):
+def spatial_kernel(from_square, r):
     count = r.xb.shape[0]
     r.start()
     r.wait(r.recv, r.side, r.w, r.xb)
     rows = r.side[...].astype(F32)
     r.taps[0:9, :] = rows[0:9, :]
-    mean, inverse = read_product_moments(r.recv, r.w[...], False, EXPAND, count)
+    if from_square:
+        r.wait(r.square)
+        mean, inverse = read_square_moments(r.recv, r.square, r.w, r.left, r.stat, count)
+    else:
+        mean, inverse = read_product_moments(r.recv, r.w[...], False, EXPAND, count)
     keep_norm(r.norm, mean, inverse, rows[10:11, :], rows[11:12, :])
     r.send(r.norm)
-    if r.recv.shape[1] > 16:
+    if not from_square:
         r.cross[...] = jnp.sum(r.recv[...].astype(F32)[:, 16:32], axis=0)
         r.send(r.cross)
 
@@ -465,7 +515,7 @@
     r.finish(r.d)
 
 
-def spatial(xb, mats, side, recv):
+def spatial(xb, mats, side, recv, square):
     count = xb.shape[0]
     devices = recv.shape[0]
     outs = dict(
@@ -473,18 +523,22 @@
         pay=(shape((devices, moment_rows(EXPAND), LANE), BF16), FAR),
         norm=(shape((8, EXPAND)), FAR),
     )
-    if recv.shape[1] > 16:
+    ins = dict(
+        recv=(recv, LOOSE),
+        side=(side, (slice(2 * SQUEEZE, SIDE_PAD), slice(None))),
+        xb=(xb, FAR),
+        w=(mats, (slice(0, WIDTH), slice(None))),
+    )
+    if square is None:
         outs["cross"] = (shape((16, LANE)), FAR)
+    else:
+        ins["square"] = (square, LOOSE)
     return call(
-        spatial_kernel,
-        dict(
-            recv=(recv, LOOSE),
-            side=(side, (slice(2 * SQUEEZE, SIDE_PAD), slice(None))),
-            xb=(xb, FAR),
-            w=(mats, (slice(0, WIDTH), slice(None))),
-        ),
+        functools.partial(spatial_kernel, square is not None),
+        ins,
         outs,
         dict(
+            left=vmem((2 * WIDTH, WIDTH), BF16),
             h=vmem((count, CHUNK), F32),
             taps=vmem((16, EXPAND), F32),
             stat=vmem((8, EXPAND), F32),
@@ -671,7 +725,7 @@
                 r.f[tile_images(tile), lanes] = jnp.sum(active, axis=0) / MAP
         return carry
 
-    lax.fori_loop(0, HEAD // CHUNK, features, 0)
+    lax.fori_loop(0, HEAD // CHUNK, features, 0, unroll=True)
     features_low = r.f[...].astype(BF16)
     classifier = r.classifier[...]
     ids = lax.broadcasted_iota(jnp.int32, (images, LOGITS), 1)
@@ -1333,46 +1387,51 @@
     rows_dev = layer_mats.shape[1]
     half = owners // 2
 
-    side_low = jnp.concatenate(
-        [
-            layer_side[:, 9 : 9 + 2 * SQUEEZE],
-            layer_side[:, :9],
-            layer_side[:, 9 + 2 * SQUEEZE :],
-            jnp.pad(layer_vecs, ((0, 0), (0, side_width - vec_width)))[:, None, :],
-            jnp.zeros((LAYERS, 1, side_width), F32),
-        ],
-        axis=1,
-    ).astype(BF16)
+    def side_as_sent(side, vecs):
+        blank = jnp.zeros((side.shape[0], 1, side_width), F32)
+        vecs = jnp.pad(vecs, ((0, 0), (0, side_width - vec_width)))[:, None, :]
+        pieces = [side[:, 9 : 9 + 2 * SQUEEZE], side[:, :9], side[:, 9 + 2 * SQUEEZE :], vecs, blank]
+        return jnp.concatenate(pieces, axis=1).astype(BF16)
+
     side_rows = -(-SIDE_PAD * side_width // EXPAND)
-    side_flat = jnp.pad(side_low[0].reshape(-1), (0, side_rows * EXPAND - SIDE_PAD * side_width))
+    side_flat = jnp.pad(side_as_sent(layer_side[:1], layer_vecs[:1]).reshape(-1), (0, side_rows * EXPAND - SIDE_PAD * side_width))
     packed = lax.all_gather(
         jnp.concatenate([layer_mats[0].astype(BF16), side_flat.reshape(side_rows, EXPAND)], axis=0),
         OWNERS, axis=0,
     )
-    mats_all = [packed[:, :rows_dev].reshape(2 * WIDTH, EXPAND)] + [
-        lax.all_gather(layer_mats[k].astype(BF16), OWNERS, axis=0, tiled=True) for k in range(1, LAYERS)
+    partner_col = partner[:, None]
+    layers = []
+    crosses = []
+    entry = mix(images.reshape(count, WIDTH), partner_col, mix_pair, devices)
+    x, xb = entry.x, entry.xb
+    received = exchange(entry.pay)
+    shared = share(received).pay
+    later_mats, later_side, later_vecs, later_head, _ = lax.optimization_barrier(
+        (layer_mats, layer_side, layer_vecs, head_mat, shared)
+    )
+    mats_all = [None] + [
+        lax.all_gather(later_mats[k].astype(BF16), OWNERS, axis=0, tiled=True) for k in range(1, LAYERS)
     ]
     side_room = -(-side_width // CHUNK) * CHUNK
     side_rest = lax.all_gather(
-        jnp.pad(side_low[1:], ((0, 0), (0, 0), (0, side_room - side_width))), OWNERS, axis=0
+        jnp.pad(side_as_sent(later_side[1:], later_vecs[1:]), ((0, 0), (0, 0), (0, side_room - side_width))), OWNERS, axis=0
     )
     side_rest = jnp.moveaxis(side_rest[..., :side_width], 0, 2).reshape(LAYERS - 1, SIDE_PAD, EXPAND)
     head_full = lax.all_gather(
-        jnp.pad(head_mat, ((0, 0), (0, HEADPAD - HEADCOLS))).astype(BF16), OWNERS, axis=0, tiled=True
-    )
-
-    partner_col = partner[:, None]
-    layers = []
-    crosses = []
-    entry = mix(images.reshape(count, WIDTH), partner_col, mix_pair)
-    x, xb = entry.x, entry.xb
-    pay = first(xb, mats_all[0], devices).pay
-    side_flat = before(packed, pay)[:, rows_dev:].reshape(owners, -1)[:, : SIDE_PAD * side_width]
+        jnp.pad(later_head, ((0, 0), (0, HEADPAD - HEADCOLS))).astype(BF16), OWNERS, axis=0, tiled=True
+    )
+
+    square = exchange(shared)
+    packed = before(packed, shared)
+    mats_all[0] = packed[:, :rows_dev].reshape(2 * WIDTH, EXPAND)
+    side_flat = packed[:, rows_dev:].reshape(owners, -1)[:, : SIDE_PAD * side_width]
     side_zero = jnp.moveaxis(side_flat.reshape(owners, SIDE_PAD, side_width), 0, 1).reshape(SIDE_PAD, EXPAND)
     side_all = [side_zero, side_rest[0], side_rest[1]]
     for k in range(LAYERS):
         mats, side = mats_all[k], side_all[k]
-        one = spatial(xb, mats, side, exchange(pay))
+        if k:
+            received, square = exchange(pay), None
+        one = spatial(xb, mats, side, received, square)
         two = project(one.d, mats, side, exchange(one.pay), getattr(one, "cross", None), owners)
         last = k == LAYERS - 1
         three = residual(

time: 567 us -> 556 us (0.981)
  waiting for transfers between devices: 161 us -> 120 us
  blocking collectives: 87.5 us -> 113 us
  local copies, waits for them, and re-layouts: 41.7 us -> 51.2 us
    all_to_all x6 -> x7, blocking collectives: 87.5 us -> 113 us  [exchange(): return lax.all_to_all(payload, BOTH, 0, 0)]
    all_gather x1, waiting for transfers between devices: 25.2 us -> 2.95 us  [body(): lax.all_gather(jnp.concatenate([layer_mats[0].astype(BF16), side_flat.res...]
    all_to_all x13, waiting for transfers between devices: 109 us -> 93.2 us  [exchange(): return lax.all_to_all(payload, BOTH, 0, 0)]
    unnamed x119 -> x127, local copies, waits for them, and re-layouts: 15.2 us -> 14.2 us
  transfers between devices with their start and end apart: 30 -> 30, of which waited for: 17 -> 17; matrix products, arithmetic and copies ran while one was open for 9% -> 11% of each run, Pallas kernels for 21% -> 22%
where the time goes in v6:
time: 556 us; the launch traced here: 545 us
  Pallas kernels  147 us (26%)
  waiting for transfers between devices  120 us (22%)
  blocking collectives  113 us (20%)
  starting transfers between devices  55 us (10%)
  local copies, waits for them, and re-layouts  51.2 us (9%)
  other arithmetic  38.2 us (7%)
  between operations  20.1 us (4%)
    pallas_call x19, Pallas kernels, call(): pl.pallas_call(flat, out_shape=[struct for struct, _ in outs.values()], i...  147 us
    all_to_all x7, blocking collectives, exchange(): return lax.all_to_all(payload, BOTH, 0, 0)  113 us
    all_to_all x13, waiting for transfers between devices, exchange(): return lax.all_to_all(payload, BOTH, 0, 0)  93.2 us
    all_to_all x13, starting transfers between devices, exchange(): return lax.all_to_all(payload, BOTH, 0, 0)  37.5 us
    ppermute x6, waiting for transfers between devices, replica_sum(): other = lax.ppermute(total, REPLICAS, [(k, k ^ step) for k in range(count)])  14.7 us
    unnamed x127, local copies, waits for them, and re-layouts  14.2 us
  transfers between devices with their start and end apart: 30, of which 17 were waited for; matrix products, arithmetic and copies ran while one was open for 11% of the time, Pallas kernels for 22%

profile of v6, /device:TPU:0, one launch (start us, length us, event | category | flops | bytes accessed | tf_op | source)
XLA Modules:
  0.0 544.7 jit_solution(3800494898863804677)
XLA Ops:
  16.1 21.8 %all_to_all.110.refs_0_ = bf16[32,24,128]{2,1,0:T(8,128)(2,1)} all-to-all(bf16[32,24,128]{2,1,0:T(8,128)(2,1)} %get-tuple-element.114), channel_id=1, replica_groups=mesh['dp'=4,'fsdp'=8] {'dp','fsdp'}, dimensions={0} | all-to-all | bytes 393216 | tf_op jit(solution)/shard_map/all_to_all | solution.py:1349
  56.9 7.7 %shard_map.325 = (bf16[640,1536]{1,0:T(8,128)(2,1)}, bf16[32,24,128]{2,1,0:T(8,128)(2,1)}, f32[8,1536]{1,0:T(8,128)}) custom-call(bf16[32,24,128]{2,1,0:T(8,128)(2,1)} %all_to_all.110.refs_0_, bf16[144,1536]{1,0:T(8,128)(2,1)} %reshape.381.refs_1_.refs_13_, bf16[640,256]{1,0:T(8,128)(2,1)} %get-tuple-element.116.refs_2_.refs_4_.refs_3_, ...), custom_call_target="tpu_custom_call" | custom-call | tf_op jit(solution)/shard_map/pallas_call | solution.py:148
  64.6 15.1 %all_to_all.111.refs_0_ = bf16[32,24,128]{2,1,0:T(8,128)(2,1)} all-to-all(bf16[32,24,128]{2,1,0:T(8,128)(2,1)} %get-tuple-element.117), channel_id=1, replica_groups=mesh['dp'=4,'fsdp'=8] {'dp','fsdp'}, dimensions={0} | all-to-all | bytes 393216 | tf_op jit(solution)/shard_map/all_to_all | solution.py:1349
  87.9 8.0 %all-to-all-done.3.refs_0_ = bf16[32,8,128]{2,1,0:T(8,128)(2,1)S(1)} async-done(((bf16[32,8,128]{2,1,0:T(8,128)(2,1)}), bf16[32,8,128]{2,1,0:T(8,128)(2,1)S(1)}, u32[]{:S(2)}, u32[]{:S(2)}) %all-to-all-start.3) | async-done | bytes 65568 | tf_op jit(solution)/shard_map/all_to_all | solution.py:1349
  121.2 14.1 %all_to_all.112.refs_0_ = bf16[32,24,128]{2,1,0:T(8,128)(2,1)} all-to-all(bf16[32,24,128]{2,1,0:T(8,128)(2,1)} %get-tuple-element.128), channel_id=1, replica_groups=mesh['dp'=4,'fsdp'=8] {'dp','fsdp'}, dimensions={0} | all-to-all | bytes 393216 | tf_op jit(solution)/shard_map/all_to_all | solution.py:1349
  143.5 14.2 %all-to-all-done.6.refs_0_ = bf16[32,24,128]{2,1,0:T(8,128)(2,1)S(1)} async-done(((bf16[32,24,128]{2,1,0:T(8,128)(2,1)}), bf16[32,24,128]{2,1,0:T(8,128)(2,1)S(1)}, u32[]{:S(2)}, u32[]{:S(2)}) %all-to-all-start.6) | async-done | bytes 196640 | tf_op jit(solution)/shard_map/all_to_all | solution.py:1349
  166.3 15.9 %all-to-all-done.7.refs_0_ = bf16[32,32,128]{2,1,0:T(8,128)(2,1)S(1)} async-done(((bf16[32,32,128]{2,1,0:T(8,128)(2,1)}), bf16[32,32,128]{2,1,0:T(8,128)(2,1)S(1)}, u32[]{:S(2)}, u32[]{:S(2)}) %all-to-all-start.7) | async-done | bytes 262176 | tf_op jit(solution)/shard_map/all_to_all | solution.py:1349
  190.0 12.0 %all_to_all.113.refs_0_ = bf16[32,24,128]{2,1,0:T(8,128)(2,1)} all-to-all(bf16[32,24,128]{2,1,0:T(8,128)(2,1)} %get-tuple-element.137), channel_id=1, replica_groups=mesh['dp'=4,'fsdp'=8] {'dp','fsdp'}, dimensions={0} | all-to-all | bytes 393216 | tf_op jit(solution)/shard_map/all_to_all | solution.py:1349
  210.3 8.7 %all-to-all-done.9.refs_0_ = bf16[32,24,128]{2,1,0:T(8,128)(2,1)S(1)} async-done(((bf16[32,24,128]{2,1,0:T(8,128)(2,1)}), bf16[32,24,128]{2,1,0:T(8,128)(2,1)S(1)}, u32[]{:S(2)}, u32[]{:S(2)}) %all-to-all-start.9) | async-done | bytes 196640 | tf_op jit(solution)/shard_map/all_to_all | solution.py:1349
  228.1 8.6 %all-to-all-done.10.refs_0_ = bf16[32,32,128]{2,1,0:T(8,128)(2,1)S(1)} async-done(((bf16[32,32,128]{2,1,0:T(8,128)(2,1)}), bf16[32,32,128]{2,1,0:T(8,128)(2,1)S(1)}, u32[]{:S(2)}, u32[]{:S(2)}) %all-to-all-start.10) | async-done | bytes 262176 | tf_op jit(solution)/shard_map/all_to_all | solution.py:1349
  237.4 10.9 %shard_map.334 = (bf16[640,1280]{1,0:T(8,128)(2,1)}, bf16[32,48,128]{2,1,0:T(8,128)(2,1)}, f32[8,1280]{1,0:T(8,128)}, bf16[1280,1280]{1,0:T(8,128)(2,1)}) custom-call(bf16[32,32,128]{2,1,0:T(8,128)(2,1)} %copy-done.14, bf16[640,256]{1,0:T(8,128)(2,1)} %get-tuple-element.146.refs_1_.refs_2_, f32[1,1024]{1,0:T(1,128)} %bitcast.150, s32[40,1]{1,0:T(8,128)} %copy.134.refs_3_, ...), custom_call_target="tpu_custom_call" | custom-call | tf_op jit(solution)/shard_map/pallas_call | solution.py:148
  248.3 16.9 %all_to_all.114.refs_0_ = bf16[32,48,128]{2,1,0:T(8,128)(2,1)} all-to-all(bf16[32,48,128]{2,1,0:T(8,128)(2,1)} %get-tuple-element.148), channel_id=1, replica_groups=mesh['dp'=4,'fsdp'=8] {'dp','fsdp'}, dimensions={0} | all-to-all | bytes 786432 | tf_op jit(solution)/shard_map/all_to_all | solution.py:1349
  265.2 13.1 %shard_map.335 = (bf16[640,1536]{1,0:T(8,128)(2,1)}, bf16[32,24,128]{2,1,0:T(8,128)(2,1)}, f32[640,256]{1,0:T(8,128)}, bf16[8,1056,256]{2,1,0:T(8,128)(2,1)}, f3...) custom-call(bf16[32,48,128]{2,1,0:T(8,128)(2,1)} %all_to_all.114.refs_0_, ...), custom_call_target="tpu_custom_call", output_to_operand_aliasing={{6}: (14, {})} | custom-call | tf_op jit(solution)/shard_map/pallas_call | solution.py:148
  279.2 14.5 %all_to_all.115.refs_0_ = bf16[32,24,128]{2,1,0:T(8,128)(2,1)} all-to-all(bf16[32,24,128]{2,1,0:T(8,128)(2,1)S(1)} %copy-done.32), channel_id=1, replica_groups=mesh['dp'=4,'fsdp'=8] {'dp','fsdp'}, dimensions={0} | all-to-all | bytes 393216 | tf_op jit(solution)/shard_map/all_to_all | solution.py:1349
  293.6 11.7 %shard_map.336 = (bf16[640,1536]{1,0:T(8,128)(2,1)}, bf16[32,32,128]{2,1,0:T(8,128)(2,1)}, f32[16,1536]{1,0:T(8,128)}, f32[8,1536]{1,0:T(8,128)}) custom-call(bf16[32,24,128]{2,1,0:T(8,128)(2,1)} %all_to_all.115.refs_0_, bf16[144,1536]{1,0:T(8,128)(2,1)} %squeeze.44.refs_1_.refs_13_, f32[8,1536]{1,0:T(8,128)} %get-tuple-element.152.refs_7_.refs_2_, ...), custom_call_target="tpu_custom_call" | custom-call | tf_op jit(solution)/shard_map/pallas_call | solution.py:148
  305.3 18.9 %all_to_all.116.refs_0_ = bf16[32,32,128]{2,1,0:T(8,128)(2,1)} all-to-all(bf16[32,32,128]{2,1,0:T(8,128)(2,1)} %get-tuple-element.163), channel_id=1, replica_groups=mesh['dp'=4,'fsdp'=8] {'dp','fsdp'}, dimensions={0} | all-to-all | bytes 524288 | tf_op jit(solution)/shard_map/all_to_all | solution.py:1349
  324.2 13.5 %shard_map.337 = (bf16[640,1536]{1,0:T(8,128)(2,1)}, bf16[32,24,128]{2,1,0:T(8,128)(2,1)}, f32[640,256]{1,0:T(8,128)}, bf16[8,1056,256]{2,1,0:T(8,128)(2,1)}, f32[8,1536]{1,0:T(8,128)}, /*index=5*/f32[8,256]{1,0:T(8,128)}) custom-call(bf16[32,32,128]{2,1,0:T(8,128)(2,1)} %all_to_all.116.refs_0_, ...), custom_call_target="tpu_custom_call", output_to_operand_aliasing={{3}: (17, {})} | custom-call | tf_op jit(solution)/shard_map/pallas_call | solution.py:148
  345.0 8.8 %all-to-all-done.14.refs_0_ = bf16[32,24,128]{2,1,0:T(8,128)(2,1)S(1)} async-done(((bf16[32,24,128]{2,1,0:T(8,128)(2,1)}), bf16[32,24,128]{2,1,0:T(8,128)(2,1)S(1)}, u32[]{:S(2)}, u32[]{:S(2)}) %all-to-all-start.14) | async-done | bytes 196640 | tf_op jit(solution)/shard_map/all_to_all | solution.py:1349
  354.5 11.7 %shard_map.338 = (bf16[640,1536]{1,0:T(8,128)(2,1)}, bf16[32,32,128]{2,1,0:T(8,128)(2,1)}, f32[16,1536]{1,0:T(8,128)}, f32[8,1536]{1,0:T(8,128)}) custom-call(bf16[32,24,128]{2,1,0:T(8,128)(2,1)} %copy-done.23, bf16[144,1536]{1,0:T(8,128)(2,1)} %squeeze.43.refs_1_.refs_13_, f32[8,1536]{1,0:T(8,128)} %get-tuple-element.166.refs_7_.refs_2_, ...), custom_call_target="tpu_custom_call" | custom-call | tf_op jit(solution)/shard_map/pallas_call | solution.py:148
  373.1 11.3 %all-to-all-done.15.refs_0_ = bf16[32,32,128]{2,1,0:T(8,128)(2,1)S(1)} async-done(((bf16[32,32,128]{2,1,0:T(8,128)(2,1)}), bf16[32,32,128]{2,1,0:T(8,128)(2,1)S(1)}, u32[]{:S(2)}, u32[]{:S(2)}) %all-to-all-start.15) | async-done | bytes 262176 | tf_op jit(solution)/shard_map/all_to_all | solution.py:1349
  385.2 13.5 %shard_map.339 = (bf16[640,1536]{1,0:T(8,128)(2,1)}, bf16[32,24,128]{2,1,0:T(8,128)(2,1)}, f32[640,256]{1,0:T(8,128)}, bf16[8,528,256]{2,1,0:T(8,128)(2,1)}, f32[8,1536]{1,0:T(8,128)}, /*index=5*/f32[8,256]{1,0:T(8,128)}) custom-call(bf16[32,32,128]{2,1,0:T(8,128)(2,1)} %copy-done.12, f32[8,1536]{1,0:T(8,128)} %get-tuple-element.174.refs_3_.refs_1_, ...), custom_call_target="tpu_custom_call" | custom-call | tf_op jit(solution)/shard_map/pallas_call | solution.py:148
  410.8 10.7 %shard_map.340 = (bf16[640,1536]{1,0:T(8,128)(2,1)}, bf16[32,24,128]{2,1,0:T(8,128)(2,1)}, f32[16,1536]{1,0:T(8,128)}, f32[8,1536]{1,0:T(8,128)}) custom-call(bf16[32,24,128]{2,1,0:T(8,128)(2,1)} %copy-done.20, bf16[144,1536]{1,0:T(8,128)(2,1)} %reshape.381.refs_1_.refs_13_, f32[8,1536]{1,0:T(8,128)} %get-tuple-element.183.refs_7_.refs_2_, ...), custom_call_target="tpu_custom_call" | custom-call | tf_op jit(solution)/shard_map/pallas_call | solution.py:148
  428.6 7.5 %all-to-all-done.17.refs_0_ = bf16[32,24,128]{2,1,0:T(8,128)(2,1)S(1)} async-done(((bf16[32,24,128]{2,1,0:T(8,128)(2,1)}), bf16[32,24,128]{2,1,0:T(8,128)(2,1)S(1)}, u32[]{:S(2)}, u32[]{:S(2)}) %all-to-all-start.17) | async-done | bytes 196640 | tf_op jit(solution)/shard_map/all_to_all | solution.py:1349
  465.9 12.6 %collective-permute-done.6 = bf16[160,1280]{1,0:T(8,128)(2,1)S(1)} collective-permute-done((bf16[160,1280]{1,0:T(8,128)(2,1)S(1)}, bf16[160,1280]{1,0:T(8,128)(2,1)S(1)}, u32[]{:S(2)}, u32[]{:S(2)}) %collective-permute-start.6) | collective-permute-done | bytes 409632 | tf_op jit(solution)/shard_map/ppermute | solution.py:1366
  (325 shorter events, 222.7 us)
Async XLA Ops:
  7.2 41.5 %all-gather.19.cloned.1.call-start = ((), (), s32[]{:S(2)}) async-start(), calls=%async_computation.32 | async-start | bytes 2433024 | tf_op jit(solution)/shard_map/all_gather | solution.py:1398
  11.4 76.5 %all-gather.13.cloned.1.call-start = ((), (), s32[]{:S(2)}) async-start(), calls=%async_computation.29 | async-start | bytes 1769472 | tf_op jit(solution)/shard_map/all_gather | solution.py:1413
  40.6 62.9 %all-gather.15.cloned.1.call-start = ((), (), s32[]{:S(2)}) async-start(), calls=%async_computation.30 | async-start | bytes 1327104 | tf_op jit(solution)/shard_map/all_gather | solution.py:1416
  41.6 101.9 %all-gather.17.cloned.1.call-start = ((), (), s32[]{:S(2)}) async-start(), calls=%async_computation.31 | async-start | bytes 1769472 | tf_op jit(solution)/shard_map/all_gather | solution.py:1413
  42.2 168.1 %all-gather.11.cloned.1.call-start = ((), (), s32[]{:S(2)}) async-start(), calls=%async_computation.25 | async-start | bytes 3686400 | tf_op jit(solution)/shard_map/all_gather | solution.py:1420
  43.1 13.1 %all-to-all-start.1 = ((bf16[32,32,128]{2,1,0:T(8,128)(2,1)}), bf16[32,32,128]{2,1,0:T(8,128)(2,1)S(1)}, u32[]{:S(2)}, u32[]{:S(2)}) async-start(bf16[32,32,128]{2,1,0:T(8,128)(2,1)} %shard_map.324), calls=%async_computation.1 | async-start | bytes 524288 | tf_op jit(solution)/shard_map/all_to_all | solution.py:1349
  100.5 13.0 %all-to-all-start.4 = ((bf16[32,32,128]{2,1,0:T(8,128)(2,1)}), bf16[32,32,128]{2,1,0:T(8,128)(2,1)S(1)}, u32[]{:S(2)}, u32[]{:S(2)}) async-start(bf16[32,32,128]{2,1,0:T(8,128)(2,1)} %get-tuple-element.124), calls=%async_computation.4 | async-start | bytes 524288 | tf_op jit(solution)/shard_map/all_to_all | solution.py:1349
  140.9 16.9 %all-to-all-start.6 = ((bf16[32,24,128]{2,1,0:T(8,128)(2,1)}), bf16[32,24,128]{2,1,0:T(8,128)(2,1)S(1)}, u32[]{:S(2)}, u32[]{:S(2)}) async-start(bf16[32,24,128]{2,1,0:T(8,128)(2,1)} %get-tuple-element.131), calls=%async_computation.6 | async-start | bytes 393216 | tf_op jit(solution)/shard_map/all_to_all | solution.py:1349
  162.5 19.8 %all-to-all-start.7 = ((bf16[32,32,128]{2,1,0:T(8,128)(2,1)}), bf16[32,32,128]{2,1,0:T(8,128)(2,1)S(1)}, u32[]{:S(2)}, u32[]{:S(2)}) async-start(bf16[32,32,128]{2,1,0:T(8,128)(2,1)} %get-tuple-element.135), calls=%async_computation.7 | async-start | bytes 524288 | tf_op jit(solution)/shard_map/all_to_all | solution.py:1349
  207.7 11.4 %all-to-all-start.9 = ((bf16[32,24,128]{2,1,0:T(8,128)(2,1)}), bf16[32,24,128]{2,1,0:T(8,128)(2,1)S(1)}, u32[]{:S(2)}, u32[]{:S(2)}) async-start(bf16[32,24,128]{2,1,0:T(8,128)(2,1)} %get-tuple-element.140), calls=%async_computation.9 | async-start | bytes 393216 | tf_op jit(solution)/shard_map/all_to_all | solution.py:1349
  223.6 13.1 %all-to-all-start.10 = ((bf16[32,32,128]{2,1,0:T(8,128)(2,1)}), bf16[32,32,128]{2,1,0:T(8,128)(2,1)S(1)}, u32[]{:S(2)}, u32[]{:S(2)}) async-start(bf16[32,32,128]{2,1,0:T(8,128)(2,1)} %get-tuple-element.145), calls=%async_computation.10 | async-start | bytes 524288 | tf_op jit(solution)/shard_map/all_to_all | solution.py:1349
  226.3 139.9 %reduce-scatter.4.cloned.1.call-start = ((), (), s32[]{:S(2)}) async-start(), calls=%async_computation.26 | async-start | bytes 3686400 | tf_op jit(solution)/shard_map/reduce_scatter | solution.py:1456
  278.3 143.2 %reduce-scatter.6.cloned.1.call-start = ((), (), s32[]{:S(2)}) async-start(), calls=%async_computation.27 | async-start | bytes 4866048 | tf_op jit(solution)/shard_map/reduce_scatter | solution.py:1456
  338.9 15.0 %all-to-all-start.14 = ((bf16[32,24,128]{2,1,0:T(8,128)(2,1)}), bf16[32,24,128]{2,1,0:T(8,128)(2,1)S(1)}, u32[]{:S(2)}, u32[]{:S(2)}) async-start(bf16[32,24,128]{2,1,0:T(8,128)(2,1)} %get-tuple-element.173), calls=%async_computation.14 | async-start | bytes 393216 | tf_op jit(solution)/shard_map/all_to_all | solution.py:1349
  366.3 18.2 %all-to-all-start.15 = ((bf16[32,32,128]{2,1,0:T(8,128)(2,1)}), bf16[32,32,128]{2,1,0:T(8,128)(2,1)S(1)}, u32[]{:S(2)}, u32[]{:S(2)}) async-start(bf16[32,32,128]{2,1,0:T(8,128)(2,1)} %get-tuple-element.180), calls=%async_computation.16 | async-start | bytes 524288 | tf_op jit(solution)/shard_map/all_to_all | solution.py:1349
  401.3 83.2 %reduce-scatter.8.cloned.1.call-start = ((), (), s32[]{:S(2)}) async-start(), calls=%async_computation.28 | async-start | bytes 2433024 | tf_op jit(solution)/shard_map/reduce_scatter | solution.py:1456
  421.5 14.6 %all-to-all-start.17 = ((bf16[32,24,128]{2,1,0:T(8,128)(2,1)}), bf16[32,24,128]{2,1,0:T(8,128)(2,1)S(1)}, u32[]{:S(2)}, u32[]{:S(2)}) async-start(bf16[32,24,128]{2,1,0:T(8,128)(2,1)} %get-tuple-element.194), calls=%async_computation.19 | async-start | bytes 393216 | tf_op jit(solution)/shard_map/all_to_all | solution.py:1349
  436.2 23.8 %collective-permute-start.5 = (bf16[160,1280]{1,0:T(8,128)(2,1)}, bf16[160,1280]{1,0:T(8,128)(2,1)}, u32[]{:S(2)}, u32[]{:S(2)}) collective-permute-start(bf16[160,1280]{1,0:T(8,128)(2,1)} %reduce-scatter.4.cloned.1.call-done), channel_id=1, source_target_pairs={{0,8},{8,0},{16,24},{24,16},{1,9},{9,1},{17,25},{25,17},{2,10},{10... | collective-permute-start | bytes 1228808 | tf_op jit(solution)/shard_map/ppermute | solution.py:1366
  438.8 15.2 %all-to-all-start.20 = ((bf16[32,2,864]{2,1,0:T(2,128)(2,1)}), bf16[32,2,864]{2,1,0:T(2,128)(2,1)S(1)}, u32[]{:S(2)}, u32[]{:S(2)}) async-start(bf16[32,2,864]{2,1,0:T(2,128)(2,1)} %reshape.418), calls=%async_computation.23 | async-start | bytes 229376 | tf_op jit(solution)/shard_map/all_to_all | solution.py:1349
  444.1 19.0 %collective-permute-start.3 = (bf16[1056,256]{1,0:T(8,128)(2,1)S(1)}, bf16[1056,256]{1,0:T(8,128)(2,1)}, u32[]{:S(2)}, u32[]{:S(2)}) collective-permute-start(bf16[1056,256]{1,0:T(8,128)(2,1)S(1)} %copy-done.27), channel_id=1, source_target_pairs={{0,16},{8,24},{16,0},{24,8},{1,17},{9,25},{17,1},{25,9},{2,18},{10... | collective-permute-start | bytes 1622024 | tf_op jit(solution)/shard_map/ppermute | solution.py:1366
  454.0 31.6 %all-to-all-start.18 = ((bf16[32,48,256]{2,1,0:T(8,128)(2,1)}), bf16[32,48,256]{2,1,0:T(8,128)(2,1)}, u32[]{:S(2)}, u32[]{:S(2)}) async-start(bf16[32,48,256]{2,1,0:T(8,128)(2,1)} %get-tuple-element.196), calls=%async_computation.20 | async-start | bytes 1572864 | tf_op jit(solution)/shard_map/all_to_all | solution.py:1349
  461.2 17.4 %collective-permute-start.6 = (bf16[160,1280]{1,0:T(8,128)(2,1)S(1)}, bf16[160,1280]{1,0:T(8,128)(2,1)S(1)}, u32[]{:S(2)}, u32[]{:S(2)}) collective-permute-start(bf16[160,1280]{1,0:T(8,128)(2,1)S(1)} %add_convert_fusion.3), channel_id=1, source_target_pairs={{0,16},{8,24},{16,0},{24,8},{1,17},{9,25},{17,1},{25,9},{2,18},{10... | collective-permute-start | bytes 1228808 | tf_op jit(solution)/shard_map/ppermute | solution.py:1366
  464.4 18.3 %collective-permute-start.4 = (bf16[1056,256]{1,0:T(8,128)(2,1)S(1)}, bf16[1056,256]{1,0:T(8,128)(2,1)S(1)}, u32[]{:S(2)}, u32[]{:S(2)}) collective-permute-start(bf16[1056,256]{1,0:T(8,128)(2,1)S(1)} %add_convert_fusion.1), channel_id=1, source_target_pairs={{0,8},{8,0},{16,24},{24,16},{1,9},{9,1},{17,25},{25,17},{2,10},{10... | collective-permute-start | bytes 1622024 | tf_op jit(solution)/shard_map/ppermute | solution.py:1366
  484.5 13.3 %collective-permute-start.1 = (bf16[528,256]{1,0:T(8,128)(2,1)}, bf16[528,256]{1,0:T(8,128)(2,1)}, u32[]{:S(2)}, u32[]{:S(2)}) collective-permute-start(bf16[528,256]{1,0:T(8,128)(2,1)} %reduce-scatter.8.cloned.1.call-done), channel_id=1, source_target_pairs={{0,8},{8,0},{16,24},{24,16},{1,9},{9,1},{17,25},{25,17},{2,10},{10... | collective-permute-start | bytes 811016 | tf_op jit(solution)/shard_map/ppermute | solution.py:1366
  (67 other events, 424.4 us)
Sparse Core Ops, SparseCore 0:
  11.5 37.1 all-gather.18
  50.9 26.4 all-gather.12
  79.0 24.4 all-gather.14
  105.6 25.6 all-gather.16
  133.3 50.1 all-gather.10
  278.4 46.2 reduce-scatter.3
  337.9 56.9 reduce-scatter.5
  404.5 39.1 reduce-scatter.7

commit v7 on v6

--- a/solution.py
+++ b/solution.py
@@ -48,6 +48,26 @@
 NEAR, FAR, RAW, CHUNKS, LOOSE = range(5)
 
 
+class Blocks:
+    def __init__(self, first, count, rows):
+        self.first, self.count, self.rows = first, count, rows
+
+
+def expand_rows(mats):
+    return (mats, half_of(mats, 0))
+
+
+def project_rows(mats):
+    return (mats, half_of(mats, 1))
+
+
+def half_of(mats, part):
+    if mats.ndim == 2:
+        return (slice(part * WIDTH, (part + 1) * WIDTH), slice(None))
+    count = mats.shape[0] // 2
+    return Blocks(part * count, count, WIDTH // count)
+
+
 class Refs:
     def __init__(self, names, refs, loads, stores):
         for name, ref in zip(names, refs):
@@ -61,9 +81,20 @@
         return getattr(self, name + "_far")
 
     def start(self):
+        later = len(self.loads) * (1 + EXPAND // CHUNK)
         for index, (name, where) in enumerate(self.loads):
+            near = getattr(self, name)
+            if isinstance(where, Blocks):
+                copies = []
+                for k in range(where.count):
+                    source = self.far(name).at[where.first + k, pl.ds(0, where.rows), :]
+                    target = near.at[pl.ds(k * where.rows, where.rows), :]
+                    copies.append(pltpu.make_async_copy(source, target, self.load_sem.at[later + k]))
+                    copies[-1].start()
+                later += where.count
+                self.pending[id(near)] = copies
+                continue
             source = self.far(name) if where is None or where == CHUNKS else self.far(name).at[where]
-            near = getattr(self, name)
             if where == CHUNKS:
                 self.chunks[id(near)] = (self.far(name), index)
                 for turn in range(near.shape[1] // CHUNK):
@@ -71,7 +102,7 @@
                 continue
             copy = pltpu.make_async_copy(source, near, self.load_sem.at[index])
             copy.start()
-            self.pending[id(near)] = copy
+            self.pending[id(near)] = [copy]
 
     def chunk(self, near, turn, at):
         far, index = self.chunks[id(near)]
@@ -80,14 +111,15 @@
 
     def wait(self, *refs):
         for ref in refs:
-            self.pending.pop(id(ref)).wait()
+            for copy in self.pending.pop(id(ref)):
+                copy.wait()
 
     def send(self, *refs):
         for ref in refs:
             index, far = self.stores[id(ref)]
             copy = pltpu.make_async_copy(ref, far, self.store_sem.at[index])
             copy.start()
-            self.pending[id(far)] = copy
+            self.pending[id(far)] = [copy]
 
     def part(self, ref, index, at):
         far = self.stores[id(ref)][1]
@@ -95,7 +127,8 @@
 
     def finish(self, ref=None):
         for key in list(self.pending):
-            self.pending.pop(key).wait()
+            for copy in self.pending.pop(key):
+                copy.wait()
         if ref is not None:
             for index in range(ref.shape[1] // CHUNK):
                 self.part(ref, index, pl.ds(index * CHUNK, CHUNK)).wait()
@@ -122,7 +155,9 @@
             continue
         names.append(name + "_far")
         dims, where = array.shape, None
-        if place == CHUNKS:
+        if isinstance(place, Blocks):
+            dims, where = (place.count * place.rows, dims[2]), place
+        elif place == CHUNKS:
             where = CHUNKS
         elif place != FAR and place != LOOSE:
             starts = [part.indices(size)[:2] for part, size in zip(place, dims)]
@@ -137,7 +172,10 @@
             extra[name] = vmem(struct.shape, struct.dtype)
     extra.update(scratch)
     extra.update(
-        load_sem=pltpu.SemaphoreType.DMA((max(len(loads), 1) * (1 + EXPAND // CHUNK),)),
+        load_sem=pltpu.SemaphoreType.DMA((
+            max(len(loads), 1) * (1 + EXPAND // CHUNK)
+            + sum(where.count for _, where in loads if isinstance(where, Blocks)),
+        )),
         store_sem=pltpu.SemaphoreType.DMA((max(len(stores), 1),)),
         part_sem=pltpu.SemaphoreType.DMA((EXPAND // CHUNK,)),
     )
@@ -527,7 +565,7 @@
         recv=(recv, LOOSE),
         side=(side, (slice(2 * SQUEEZE, SIDE_PAD), slice(None))),
         xb=(xb, FAR),
-        w=(mats, (slice(0, WIDTH), slice(None))),
+        w=expand_rows(mats),
     )
     if square is None:
         outs["cross"] = (shape((16, LANE)), FAR)
@@ -618,7 +656,7 @@
         recv=(recv, LOOSE),
         side=(side, FAR),
         d=(d, CHUNKS),
-        w=(mats, (slice(WIDTH, 2 * WIDTH), slice(None))),
+        w=project_rows(mats),
     )
     rows = moment_rows(WIDTH)
     if cross is not None:
@@ -1054,17 +1092,17 @@
     devices = recv.shape[0]
     columns = HEAD if is_head else EXPAND
     block = EXPAND // CHUNK * (2 * WIDTH // owners) + 2 * SQUEEZE + 16
-    where = (slice(0, HEAD), slice(0, WIDTH)) if is_head else (slice(0, WIDTH), slice(None))
+    head_part = (slice(0, HEAD), slice(0, WIDTH))
     ins = dict(
         recv=(recv, LOOSE),
         unorm=(upper.norm, FAR),
         xb=(upper.xb, FAR),
-        w=(upper.weights, where),
+        w=(upper.weights, head_part) if is_head else expand_rows(upper.weights),
         dz=(upper.dz, CHUNKS),
         norm3=(lower.norm3, FAR),
         normed=(lower.normed, FAR),
         norm2=(lower.norm2, FAR),
-        wp=(lower.mats, (slice(WIDTH, 2 * WIDTH), slice(None))),
+        wp=project_rows(lower.mats),
         d=(lower.d, CHUNKS),
         excite=(lower.excite, FAR),
         pooled=(lower.pooled, FAR),
@@ -1213,7 +1251,7 @@
         norm2=(layer.norm2, FAR),
         norm1=(layer.norm1, FAR),
         xb=(layer.xb, FAR),
-        w=(layer.mats, (slice(0, WIDTH), slice(None))),
+        w=expand_rows(layer.mats),
         dz2=(dz2, CHUNKS),
         d=(layer.d, CHUNKS),
     )
@@ -1247,6 +1285,8 @@
     part = slice_rows(replicas * owners)
     rows_dev = 2 * WIDTH // owners
     chunks = EXPAND // CHUNK
+    if chunks * part % 8:
+        r.shares[...] = jnp.zeros(r.shares.shape, F32)
     for device in range(replicas * owners):
         replica, owner = device // owners, device % owners
         first_row = rows_dev * (owner % half) + (2 * replica + owner // half) * part
@@ -1254,19 +1294,30 @@
             r.shares[device, k * part : (k + 1) * part, :] = r.grad_w[
                 first_row : first_row + part, k * CHUNK : (k + 1) * CHUNK
             ]
-    if r.shares.shape[1] > chunks * part:
-        r.shares[:, chunks * part :, :] = jnp.zeros(
-            (replicas * owners, r.shares.shape[1] - chunks * part, CHUNK), F32
-        )
+    r.wait(r.taps)
+    width = EXPAND // owners
+    tap_rows = -(-9 * width // CHUNK)
+    first_tap = -(-chunks * part // 8) * 8
+    for owner in range(owners):
+        pieces = [r.taps[k : k + 1, owner * width : (owner + 1) * width] for k in range(9)]
+        pieces.append(jnp.zeros((1, tap_rows * CHUNK - 9 * width), F32))
+        flat = jnp.concatenate(pieces, axis=1)
+        lines = [flat[:, k * CHUNK : (k + 1) * CHUNK] for k in range(tap_rows)]
+        lines.append(jnp.zeros((r.shares.shape[1] - first_tap - tap_rows, CHUNK), F32))
+        lines = jnp.concatenate(lines, axis=0)
+        for replica in range(replicas):
+            r.shares[replica * owners + owner, first_tap:, :] = lines
     r.grads[...] = r.shares[...].astype(BF16)
     r.send(r.grads)
     r.finish()
 
 
-def last_back(row_count, replicas, owners, recv, layer, dz):
+def last_back(row_count, replicas, owners, recv, layer, dz, taps):
     count = dz.shape[0]
     devices = recv.shape[0]
-    block = -(-EXPAND // CHUNK * slice_rows(devices) // 16) * 16
+    tap_rows = -(-9 * EXPAND // owners // CHUNK)
+    block = -(-EXPAND // CHUNK * slice_rows(devices) // 8) * 8 + 8
+    assert tap_rows <= 8
     return call(
         functools.partial(last_kernel, row_count, replicas, owners),
         dict(
@@ -1274,7 +1325,8 @@
             dz=(dz, CHUNKS),
             unorm=(layer.norm1, FAR),
             xb=(layer.xb, FAR),
-            w=(layer.mats, (slice(0, WIDTH), slice(None))),
+            w=expand_rows(layer.mats),
+            taps=(taps, FAR),
         ),
         dict(
             grads=(shape((devices, block, CHUNK), BF16), FAR),
@@ -1423,7 +1475,7 @@
 
     square = exchange(shared)
     packed = before(packed, shared)
-    mats_all[0] = packed[:, :rows_dev].reshape(2 * WIDTH, EXPAND)
+    mats_all[0] = packed
     side_flat = packed[:, rows_dev:].reshape(owners, -1)[:, : SIDE_PAD * side_width]
     side_zero = jnp.moveaxis(side_flat.reshape(owners, SIDE_PAD, side_width), 0, 1).reshape(SIDE_PAD, EXPAND)
     side_all = [side_zero, side_rest[0], side_rest[1]]
@@ -1496,10 +1548,8 @@
             xb=layer.xb, weights=layer.mats, dz=tap.dz, norm=layer.norm1, taps=tap.taps
         )
     pay = before(pay, pair)
-    late_taps = jnp.moveaxis(tap.taps[:9].astype(BF16).reshape(9, owners, side_width), 1, 0)
-    late_taps = jnp.broadcast_to(late_taps[None], (replicas, *late_taps.shape))
     received = exchange(pay)
-    final = last_back(row_count, replicas, owners, received, layers[0], tap.dz)
+    final = last_back(row_count, replicas, owners, received, layers[0], tap.dz, tap.taps)
     globs_one[0] = final.glob
     shard_head = replica_sum(before(shard_head, received))
     pair = replica_sum(before(pair, received), True)
@@ -1508,11 +1558,12 @@
 
     part = slice_rows(devices)
     chunks = EXPAND // CHUNK
-    late = jnp.sum(exchange(final.grads).astype(F32), axis=0).astype(BF16)
+    summed = jnp.sum(exchange(final.grads).astype(F32), axis=0)
+    first_tap = -(-chunks * part // 8) * 8
+    late_taps = summed[first_tap:].reshape(-1)[: 9 * side_width].reshape(9, side_width)
+    late = summed[: chunks * part].astype(BF16)
     other = lax.ppermute(late, OWNERS, [(half + k, k) for k in range(half)])
-    late_taps = exchange(before(late_taps.reshape(devices, 9, side_width), received))
-    late_taps = jnp.sum(late_taps.astype(F32), axis=0)
-    late = spread_over(jnp.stack([late, other]), REPLICAS)[:, :, : chunks * part]
+    late = spread_over(jnp.stack([late, other]), REPLICAS)
     late = jnp.moveaxis(late.reshape(replicas, 2, chunks, part, CHUNK), 2, 3)
     late = late.reshape(rows_dev, EXPAND).astype(F32)
 

time: 556 us -> 552 us (level)
  waiting for transfers between devices: 120 us -> 135 us
  local copies, waits for them, and re-layouts: 51.2 us -> 43.2 us
  starting transfers between devices: 55 us -> 47.7 us
    all_to_all x13 -> x12, waiting for transfers between devices: 93.2 us -> 99.2 us  [exchange(): return lax.all_to_all(payload, BOTH, 0, 0)]
    all_to_all x13 -> x12, starting transfers between devices: 37.5 us -> 33.6 us  [exchange(): return lax.all_to_all(payload, BOTH, 0, 0)]
    unnamed x127 -> x105, local copies, waits for them, and re-layouts: 14.2 us -> 11.9 us
  transfers between devices with their start and end apart: 30 -> 29, of which waited for: 17 -> 20; matrix products, arithmetic and copies ran while one was open for 11% -> 8% of each run, Pallas kernels for 22% -> 22%
where the time goes in v7:
time: 552 us; the launch traced here: 541 us
  Pallas kernels  148 us (27%)
  waiting for transfers between devices  135 us (24%)
  blocking collectives  113 us (20%)
  starting transfers between devices  47.7 us (9%)
  local copies, waits for them, and re-layouts  43.2 us (8%)
  other arithmetic  34.2 us (6%)
  between operations  19.8 us (4%)
    pallas_call x19, Pallas kernels, call(): pl.pallas_call(flat, out_shape=[struct for struct, _ in outs.values()], i...  148 us
    all_to_all x7, blocking collectives, exchange(): return lax.all_to_all(payload, BOTH, 0, 0)  113 us
    all_to_all x12, waiting for transfers between devices, exchange(): return lax.all_to_all(payload, BOTH, 0, 0)  99.2 us
    all_to_all x12, starting transfers between devices, exchange(): return lax.all_to_all(payload, BOTH, 0, 0)  33.6 us
    ppermute x6, waiting for transfers between devices, replica_sum(): other = lax.ppermute(total, REPLICAS, [(k, k ^ step) for k in range(count)])  17.1 us
    unnamed x105, local copies, waits for them, and re-layouts  11.9 us
  transfers between devices with their start and end apart: 29, of which 20 were waited for; matrix products, arithmetic and copies ran while one was open for 8% of the time, Pallas kernels for 22%

profile of v7, /device:TPU:0, one launch (start us, length us, event | category | flops | bytes accessed | tf_op | source)
XLA Modules:
  0.0 541.0 jit_solution(533210404153415229)
XLA Ops:
  16.1 21.8 %all_to_all.105.refs_0_ = bf16[32,24,128]{2,1,0:T(8,128)(2,1)} all-to-all(bf16[32,24,128]{2,1,0:T(8,128)(2,1)} %get-tuple-element.113), channel_id=1, replica_groups=mesh['dp'=4,'fsdp'=8] {'dp','fsdp'}, dimensions={0} | all-to-all | bytes 393216 | tf_op jit(solution)/shard_map/all_to_all | solution.py:1401
  56.8 7.8 %shard_map.325 = (bf16[640,1536]{1,0:T(8,128)(2,1)}, bf16[32,24,128]{2,1,0:T(8,128)(2,1)}, f32[8,1536]{1,0:T(8,128)}) custom-call(bf16[32,24,128]{2,1,0:T(8,128)(2,1)} %all_to_all.105.refs_0_, bf16[144,1536]{1,0:T(8,128)(2,1)} %reshape.377.refs_1_.refs_13_, bf16[640,256]{1,0:T(8,128)(2,1)} %get-tuple-element.115.refs_2_.refs_4_.refs_3_, ...), custom_call_target="tpu_custom_call" | custom-call | tf_op jit(solution)/shard_map/pallas_call | solution.py:186
  64.6 15.2 %all_to_all.106.refs_0_ = bf16[32,24,128]{2,1,0:T(8,128)(2,1)} all-to-all(bf16[32,24,128]{2,1,0:T(8,128)(2,1)} %get-tuple-element.116), channel_id=1, replica_groups=mesh['dp'=4,'fsdp'=8] {'dp','fsdp'}, dimensions={0} | all-to-all | bytes 393216 | tf_op jit(solution)/shard_map/all_to_all | solution.py:1401
  88.0 8.0 %all-to-all-done.3.refs_0_ = bf16[32,8,128]{2,1,0:T(8,128)(2,1)S(1)} async-done(((bf16[32,8,128]{2,1,0:T(8,128)(2,1)}), bf16[32,8,128]{2,1,0:T(8,128)(2,1)S(1)}, u32[]{:S(2)}, u32[]{:S(2)}) %all-to-all-start.3) | async-done | bytes 65568 | tf_op jit(solution)/shard_map/all_to_all | solution.py:1401
  121.3 14.1 %all_to_all.107.refs_0_ = bf16[32,24,128]{2,1,0:T(8,128)(2,1)} all-to-all(bf16[32,24,128]{2,1,0:T(8,128)(2,1)} %get-tuple-element.127), channel_id=1, replica_groups=mesh['dp'=4,'fsdp'=8] {'dp','fsdp'}, dimensions={0} | all-to-all | bytes 393216 | tf_op jit(solution)/shard_map/all_to_all | solution.py:1401
  143.7 14.4 %all-to-all-done.6.refs_0_ = bf16[32,24,128]{2,1,0:T(8,128)(2,1)S(1)} async-done(((bf16[32,24,128]{2,1,0:T(8,128)(2,1)}), bf16[32,24,128]{2,1,0:T(8,128)(2,1)S(1)}, u32[]{:S(2)}, u32[]{:S(2)}) %all-to-all-start.6) | async-done | bytes 196640 | tf_op jit(solution)/shard_map/all_to_all | solution.py:1401
  166.6 15.9 %all-to-all-done.7.refs_0_ = bf16[32,32,128]{2,1,0:T(8,128)(2,1)S(1)} async-done(((bf16[32,32,128]{2,1,0:T(8,128)(2,1)}), bf16[32,32,128]{2,1,0:T(8,128)(2,1)S(1)}, u32[]{:S(2)}, u32[]{:S(2)}) %all-to-all-start.7) | async-done | bytes 262176 | tf_op jit(solution)/shard_map/all_to_all | solution.py:1401
  183.2 7.0 %shard_map.331 = (bf16[640,1536]{1,0:T(8,128)(2,1)}, bf16[32,24,128]{2,1,0:T(8,128)(2,1)}, f32[8,1536]{1,0:T(8,128)}, f32[16,128]{1,0:T(8,128)}) custom-call(bf16[32,32,128]{2,1,0:T(8,128)(2,1)} %copy-done.12, bf16[144,1536]{1,0:T(8,128)(2,1)} %squeeze.44.refs_1_.refs_13_, bf16[640,256]{1,0:T(8,128)(2,1)} %get-tuple-element.135.refs_2_.refs_4_, ...), custom_call_target="tpu_custom_call" | custom-call | tf_op jit(solution)/shard_map/pallas_call | solution.py:186
  190.2 12.0 %all_to_all.108.refs_0_ = bf16[32,24,128]{2,1,0:T(8,128)(2,1)} all-to-all(bf16[32,24,128]{2,1,0:T(8,128)(2,1)} %get-tuple-element.136), channel_id=1, replica_groups=mesh['dp'=4,'fsdp'=8] {'dp','fsdp'}, dimensions={0} | all-to-all | bytes 393216 | tf_op jit(solution)/shard_map/all_to_all | solution.py:1401
  210.6 8.7 %all-to-all-done.9.refs_0_ = bf16[32,24,128]{2,1,0:T(8,128)(2,1)S(1)} async-done(((bf16[32,24,128]{2,1,0:T(8,128)(2,1)}), bf16[32,24,128]{2,1,0:T(8,128)(2,1)S(1)}, u32[]{:S(2)}, u32[]{:S(2)}) %all-to-all-start.9) | async-done | bytes 196640 | tf_op jit(solution)/shard_map/all_to_all | solution.py:1401
  228.2 8.8 %all-to-all-done.10.refs_0_ = bf16[32,32,128]{2,1,0:T(8,128)(2,1)S(1)} async-done(((bf16[32,32,128]{2,1,0:T(8,128)(2,1)}), bf16[32,32,128]{2,1,0:T(8,128)(2,1)S(1)}, u32[]{:S(2)}, u32[]{:S(2)}) %all-to-all-start.10) | async-done | bytes 262176 | tf_op jit(solution)/shard_map/all_to_all | solution.py:1401
  237.7 10.9 %shard_map.334 = (bf16[640,1280]{1,0:T(8,128)(2,1)}, bf16[32,48,128]{2,1,0:T(8,128)(2,1)}, f32[8,1280]{1,0:T(8,128)}, bf16[1280,1280]{1,0:T(8,128)(2,1)}) custom-call(bf16[32,32,128]{2,1,0:T(8,128)(2,1)} %copy-done.11, bf16[640,256]{1,0:T(8,128)(2,1)} %get-tuple-element.145.refs_1_.refs_2_, f32[1,1024]{1,0:T(1,128)} %bitcast.145, s32[40,1]{1,0:T(8,128)} %copy.113.refs_3_, ...), custom_call_target="tpu_custom_call" | custom-call | tf_op jit(solution)/shard_map/pallas_call | solution.py:186
  248.6 16.9 %all_to_all.109.refs_0_ = bf16[32,48,128]{2,1,0:T(8,128)(2,1)} all-to-all(bf16[32,48,128]{2,1,0:T(8,128)(2,1)} %get-tuple-element.147), channel_id=1, replica_groups=mesh['dp'=4,'fsdp'=8] {'dp','fsdp'}, dimensions={0} | all-to-all | bytes 786432 | tf_op jit(solution)/shard_map/all_to_all | solution.py:1401
  265.4 13.1 %shard_map.335 = (bf16[640,1536]{1,0:T(8,128)(2,1)}, bf16[32,24,128]{2,1,0:T(8,128)(2,1)}, f32[640,256]{1,0:T(8,128)}, bf16[8,1056,256]{2,1,0:T(8,128)(2,1)}, f3...) custom-call(bf16[32,48,128]{2,1,0:T(8,128)(2,1)} %all_to_all.109.refs_0_, ...), custom_call_target="tpu_custom_call", output_to_operand_aliasing={{6}: (14, {})} | custom-call | tf_op jit(solution)/shard_map/pallas_call | solution.py:186
  279.4 14.4 %all_to_all.110.refs_0_ = bf16[32,24,128]{2,1,0:T(8,128)(2,1)} all-to-all(bf16[32,24,128]{2,1,0:T(8,128)(2,1)S(1)} %copy-done.27), channel_id=1, replica_groups=mesh['dp'=4,'fsdp'=8] {'dp','fsdp'}, dimensions={0} | all-to-all | bytes 393216 | tf_op jit(solution)/shard_map/all_to_all | solution.py:1401
  293.8 11.7 %shard_map.336 = (bf16[640,1536]{1,0:T(8,128)(2,1)}, bf16[32,32,128]{2,1,0:T(8,128)(2,1)}, f32[16,1536]{1,0:T(8,128)}, f32[8,1536]{1,0:T(8,128)}) custom-call(bf16[32,24,128]{2,1,0:T(8,128)(2,1)} %all_to_all.110.refs_0_, bf16[144,1536]{1,0:T(8,128)(2,1)} %squeeze.44.refs_1_.refs_13_, f32[8,1536]{1,0:T(8,128)} %get-tuple-element.151.refs_7_.refs_2_, ...), custom_call_target="tpu_custom_call" | custom-call | tf_op jit(solution)/shard_map/pallas_call | solution.py:186
  305.5 19.1 %all_to_all.111.refs_0_ = bf16[32,32,128]{2,1,0:T(8,128)(2,1)} all-to-all(bf16[32,32,128]{2,1,0:T(8,128)(2,1)} %get-tuple-element.162), channel_id=1, replica_groups=mesh['dp'=4,'fsdp'=8] {'dp','fsdp'}, dimensions={0} | all-to-all | bytes 524288 | tf_op jit(solution)/shard_map/all_to_all | solution.py:1401
  324.6 13.5 %shard_map.337 = (bf16[640,1536]{1,0:T(8,128)(2,1)}, bf16[32,24,128]{2,1,0:T(8,128)(2,1)}, f32[640,256]{1,0:T(8,128)}, bf16[8,1056,256]{2,1,0:T(8,128)(2,1)}, f32[8,1536]{1,0:T(8,128)}, /*index=5*/f32[8,256]{1,0:T(8,128)}) custom-call(bf16[32,32,128]{2,1,0:T(8,128)(2,1)} %all_to_all.111.refs_0_, ...), custom_call_target="tpu_custom_call", output_to_operand_aliasing={{3}: (17, {})} | custom-call | tf_op jit(solution)/shard_map/pallas_call | solution.py:186
  343.5 8.5 %all-to-all-done.14.refs_0_ = bf16[32,24,128]{2,1,0:T(8,128)(2,1)S(1)} async-done(((bf16[32,24,128]{2,1,0:T(8,128)(2,1)}), bf16[32,24,128]{2,1,0:T(8,128)(2,1)S(1)}, u32[]{:S(2)}, u32[]{:S(2)}) %all-to-all-start.14) | async-done | bytes 196640 | tf_op jit(solution)/shard_map/all_to_all | solution.py:1401
  352.6 11.7 %shard_map.338 = (bf16[640,1536]{1,0:T(8,128)(2,1)}, bf16[32,32,128]{2,1,0:T(8,128)(2,1)}, f32[16,1536]{1,0:T(8,128)}, f32[8,1536]{1,0:T(8,128)}) custom-call(bf16[32,24,128]{2,1,0:T(8,128)(2,1)} %copy-done.19, bf16[144,1536]{1,0:T(8,128)(2,1)} %squeeze.43.refs_1_.refs_13_, f32[8,1536]{1,0:T(8,128)} %get-tuple-element.165.refs_7_.refs_2_, ...), custom_call_target="tpu_custom_call" | custom-call | tf_op jit(solution)/shard_map/pallas_call | solution.py:186
  369.1 14.1 %all-to-all-done.15.refs_0_ = bf16[32,32,128]{2,1,0:T(8,128)(2,1)S(1)} async-done(((bf16[32,32,128]{2,1,0:T(8,128)(2,1)}), bf16[32,32,128]{2,1,0:T(8,128)(2,1)S(1)}, u32[]{:S(2)}, u32[]{:S(2)}) %all-to-all-start.15) | async-done | bytes 262176 | tf_op jit(solution)/shard_map/all_to_all | solution.py:1401
  383.9 13.6 %shard_map.339 = (bf16[640,1536]{1,0:T(8,128)(2,1)}, bf16[32,24,128]{2,1,0:T(8,128)(2,1)}, f32[640,256]{1,0:T(8,128)}, bf16[8,528,256]{2,1,0:T(8,128)(2,1)}, f32[8,1536]{1,0:T(8,128)}, /*index=5*/f32[8,256]{1,0:T(8,128)}) custom-call(bf16[32,32,128]{2,1,0:T(8,128)(2,1)} %copy-done.8, f32[8,1536]{1,0:T(8,128)} %get-tuple-element.173.refs_3_.refs_1_, ...), custom_call_target="tpu_custom_call" | custom-call | tf_op jit(solution)/shard_map/pallas_call | solution.py:186
  409.6 10.8 %shard_map.340 = (bf16[640,1536]{1,0:T(8,128)(2,1)}, bf16[32,24,128]{2,1,0:T(8,128)(2,1)}, f32[16,1536]{1,0:T(8,128)}, f32[8,1536]{1,0:T(8,128)}) custom-call(bf16[32,24,128]{2,1,0:T(8,128)(2,1)} %copy-done.15, bf16[144,1536]{1,0:T(8,128)(2,1)} %reshape.377.refs_1_.refs_13_, f32[8,1536]{1,0:T(8,128)} %get-tuple-element.182.refs_7_.refs_2_, ...), custom_call_target="tpu_custom_call" | custom-call | tf_op jit(solution)/shard_map/pallas_call | solution.py:186
  456.4 13.5 %collective-permute-done.6 = bf16[160,1280]{1,0:T(8,128)(2,1)S(1)} collective-permute-done((bf16[160,1280]{1,0:T(8,128)(2,1)S(1)}, bf16[160,1280]{1,0:T(8,128)(2,1)S(1)}, u32[]{:S(2)}, u32[]{:S(2)}) %collective-permute-start.6) | collective-permute-done | bytes 409632 | tf_op jit(solution)/shard_map/ppermute | solution.py:1418
  (298 shorter events, 215.7 us)
Async XLA Ops:
  7.2 41.5 %all-gather.19.cloned.1.call-start = ((), (), s32[]{:S(2)}) async-start(), calls=%async_computation.31 | async-start | bytes 2433024 | tf_op jit(solution)/shard_map/all_gather | solution.py:1450
  11.4 76.5 %all-gather.13.cloned.1.call-start = ((), (), s32[]{:S(2)}) async-start(), calls=%async_computation.28 | async-start | bytes 1769472 | tf_op jit(solution)/shard_map/all_gather | solution.py:1465
  40.6 63.0 %all-gather.15.cloned.1.call-start = ((), (), s32[]{:S(2)}) async-start(), calls=%async_computation.29 | async-start | bytes 1327104 | tf_op jit(solution)/shard_map/all_gather | solution.py:1468
  41.6 102.0 %all-gather.17.cloned.1.call-start = ((), (), s32[]{:S(2)}) async-start(), calls=%async_computation.30 | async-start | bytes 1769472 | tf_op jit(solution)/shard_map/all_gather | solution.py:1465
  42.2 168.4 %all-gather.11.cloned.1.call-start = ((), (), s32[]{:S(2)}) async-start(), calls=%async_computation.24 | async-start | bytes 3686400 | tf_op jit(solution)/shard_map/all_gather | solution.py:1472
  43.1 13.0 %all-to-all-start.1 = ((bf16[32,32,128]{2,1,0:T(8,128)(2,1)}), bf16[32,32,128]{2,1,0:T(8,128)(2,1)S(1)}, u32[]{:S(2)}, u32[]{:S(2)}) async-start(bf16[32,32,128]{2,1,0:T(8,128)(2,1)} %shard_map.324), calls=%async_computation.1 | async-start | bytes 524288 | tf_op jit(solution)/shard_map/all_to_all | solution.py:1401
  100.5 13.0 %all-to-all-start.4 = ((bf16[32,32,128]{2,1,0:T(8,128)(2,1)}), bf16[32,32,128]{2,1,0:T(8,128)(2,1)S(1)}, u32[]{:S(2)}, u32[]{:S(2)}) async-start(bf16[32,32,128]{2,1,0:T(8,128)(2,1)} %get-tuple-element.123), calls=%async_computation.4 | async-start | bytes 524288 | tf_op jit(solution)/shard_map/all_to_all | solution.py:1401
  141.0 17.0 %all-to-all-start.6 = ((bf16[32,24,128]{2,1,0:T(8,128)(2,1)}), bf16[32,24,128]{2,1,0:T(8,128)(2,1)S(1)}, u32[]{:S(2)}, u32[]{:S(2)}) async-start(bf16[32,24,128]{2,1,0:T(8,128)(2,1)} %get-tuple-element.130), calls=%async_computation.6 | async-start | bytes 393216 | tf_op jit(solution)/shard_map/all_to_all | solution.py:1401
  162.7 19.7 %all-to-all-start.7 = ((bf16[32,32,128]{2,1,0:T(8,128)(2,1)}), bf16[32,32,128]{2,1,0:T(8,128)(2,1)S(1)}, u32[]{:S(2)}, u32[]{:S(2)}) async-start(bf16[32,32,128]{2,1,0:T(8,128)(2,1)} %get-tuple-element.134), calls=%async_computation.7 | async-start | bytes 524288 | tf_op jit(solution)/shard_map/all_to_all | solution.py:1401
  207.9 11.4 %all-to-all-start.9 = ((bf16[32,24,128]{2,1,0:T(8,128)(2,1)}), bf16[32,24,128]{2,1,0:T(8,128)(2,1)S(1)}, u32[]{:S(2)}, u32[]{:S(2)}) async-start(bf16[32,24,128]{2,1,0:T(8,128)(2,1)} %get-tuple-element.139), calls=%async_computation.9 | async-start | bytes 393216 | tf_op jit(solution)/shard_map/all_to_all | solution.py:1401
  223.9 13.1 %all-to-all-start.10 = ((bf16[32,32,128]{2,1,0:T(8,128)(2,1)}), bf16[32,32,128]{2,1,0:T(8,128)(2,1)S(1)}, u32[]{:S(2)}, u32[]{:S(2)}) async-start(bf16[32,32,128]{2,1,0:T(8,128)(2,1)} %get-tuple-element.144), calls=%async_computation.10 | async-start | bytes 524288 | tf_op jit(solution)/shard_map/all_to_all | solution.py:1401
  226.6 137.8 %reduce-scatter.4.cloned.1.call-start = ((), (), s32[]{:S(2)}) async-start(), calls=%async_computation.25 | async-start | bytes 3686400 | tf_op jit(solution)/shard_map/reduce_scatter | solution.py:1508
  278.5 141.9 %reduce-scatter.6.cloned.1.call-start = ((), (), s32[]{:S(2)}) async-start(), calls=%async_computation.26 | async-start | bytes 4866048 | tf_op jit(solution)/shard_map/reduce_scatter | solution.py:1508
  338.1 13.8 %all-to-all-start.14 = ((bf16[32,24,128]{2,1,0:T(8,128)(2,1)}), bf16[32,24,128]{2,1,0:T(8,128)(2,1)S(1)}, u32[]{:S(2)}, u32[]{:S(2)}) async-start(bf16[32,24,128]{2,1,0:T(8,128)(2,1)} %get-tuple-element.172), calls=%async_computation.14 | async-start | bytes 393216 | tf_op jit(solution)/shard_map/all_to_all | solution.py:1401
  364.4 18.9 %all-to-all-start.15 = ((bf16[32,32,128]{2,1,0:T(8,128)(2,1)}), bf16[32,32,128]{2,1,0:T(8,128)(2,1)S(1)}, u32[]{:S(2)}, u32[]{:S(2)}) async-start(bf16[32,32,128]{2,1,0:T(8,128)(2,1)} %get-tuple-element.179), calls=%async_computation.16 | async-start | bytes 524288 | tf_op jit(solution)/shard_map/all_to_all | solution.py:1401
  397.5 11.4 %all-to-all-start.16 = ((bf16[32,24,128]{2,1,0:T(8,128)(2,1)}), bf16[32,24,128]{2,1,0:T(8,128)(2,1)S(1)}, u32[]{:S(2)}, u32[]{:S(2)}) async-start(bf16[32,24,128]{2,1,0:T(8,128)(2,1)} %get-tuple-element.188), calls=%async_computation.17 | async-start | bytes 393216 | tf_op jit(solution)/shard_map/all_to_all | solution.py:1401
  400.2 75.8 %reduce-scatter.8.cloned.1.call-start = ((), (), s32[]{:S(2)}) async-start(), calls=%async_computation.27 | async-start | bytes 2433024 | tf_op jit(solution)/shard_map/reduce_scatter | solution.py:1508
  420.4 15.0 %all-to-all-start.17 = ((bf16[32,24,128]{2,1,0:T(8,128)(2,1)}), bf16[32,24,128]{2,1,0:T(8,128)(2,1)S(1)}, u32[]{:S(2)}, u32[]{:S(2)}) async-start(bf16[32,24,128]{2,1,0:T(8,128)(2,1)} %get-tuple-element.193), calls=%async_computation.19 | async-start | bytes 393216 | tf_op jit(solution)/shard_map/all_to_all | solution.py:1401
  435.4 14.5 %collective-permute-start.5 = (bf16[160,1280]{1,0:T(8,128)(2,1)S(1)}, bf16[160,1280]{1,0:T(8,128)(2,1)}, u32[]{:S(2)}, u32[]{:S(2)}) collective-permute-start(bf16[160,1280]{1,0:T(8,128)(2,1)S(1)} %copy-done.25), channel_id=1, source_target_pairs={{0,8},{8,0},{16,24},{24,16},{1,9},{9,1},{17,25},{25,17},{2,10},{10... | collective-permute-start | bytes 1228808 | tf_op jit(solution)/shard_map/ppermute | solution.py:1418
  437.7 15.4 %collective-permute-start.3 = (bf16[1056,256]{1,0:T(8,128)(2,1)}, bf16[1056,256]{1,0:T(8,128)(2,1)}, u32[]{:S(2)}, u32[]{:S(2)}) collective-permute-start(bf16[1056,256]{1,0:T(8,128)(2,1)} %reduce-scatter.6.cloned.1.call-done), channel_id=1, source_target_pairs={{0,16},{8,24},{16,0},{24,8},{1,17},{9,25},{17,1},{25,9},{2,18},{10... | collective-permute-start | bytes 1622024 | tf_op jit(solution)/shard_map/ppermute | solution.py:1418
  445.3 40.4 %all-to-all-start.18 = ((bf16[32,56,256]{2,1,0:T(8,128)(2,1)}), bf16[32,56,256]{2,1,0:T(8,128)(2,1)}, u32[]{:S(2)}, u32[]{:S(2)}) async-start(bf16[32,56,256]{2,1,0:T(8,128)(2,1)} %get-tuple-element.196), calls=%async_computation.20 | async-start | bytes 1835008 | tf_op jit(solution)/shard_map/all_to_all | solution.py:1401
  451.0 18.9 %collective-permute-start.6 = (bf16[160,1280]{1,0:T(8,128)(2,1)S(1)}, bf16[160,1280]{1,0:T(8,128)(2,1)S(1)}, u32[]{:S(2)}, u32[]{:S(2)}) collective-permute-start(bf16[160,1280]{1,0:T(8,128)(2,1)S(1)} %add_convert_fusion.3), channel_id=1, source_target_pairs={{0,16},{8,24},{16,0},{24,8},{1,17},{9,25},{17,1},{25,9},{2,18},{10... | collective-permute-start | bytes 1228808 | tf_op jit(solution)/shard_map/ppermute | solution.py:1418
  454.3 19.7 %collective-permute-start.4 = (bf16[1056,256]{1,0:T(8,128)(2,1)S(1)}, bf16[1056,256]{1,0:T(8,128)(2,1)S(1)}, u32[]{:S(2)}, u32[]{:S(2)}) collective-permute-start(bf16[1056,256]{1,0:T(8,128)(2,1)S(1)} %add_convert_fusion.1), channel_id=1, source_target_pairs={{0,8},{8,0},{16,24},{24,16},{1,9},{9,1},{17,25},{25,17},{2,10},{10... | collective-permute-start | bytes 1622024 | tf_op jit(solution)/shard_map/ppermute | solution.py:1418
  485.7 18.2 %collective-permute-start.2 = (bf16[528,256]{1,0:T(8,128)(2,1)S(1)}, bf16[528,256]{1,0:T(8,128)(2,1)}, u32[]{:S(2)}, u32[]{:S(2)}) collective-permute-start(bf16[528,256]{1,0:T(8,128)(2,1)S(1)} %add_convert_fusion.5), channel_id=1, source_target_pairs={{0,16},{8,24},{16,0},{24,8},{1,17},{9,25},{17,1},{25,9},{2,18},{10... | collective-permute-start | bytes 811016 | tf_op jit(solution)/shard_map/ppermute | solution.py:1418
  (55 other events, 317.0 us)
Sparse Core Ops, SparseCore 0:
  11.5 37.1 all-gather.18
  50.9 26.9 all-gather.12
  79.5 24.0 all-gather.14
  105.7 25.7 all-gather.16
  133.6 50.1 all-gather.10
  278.7 46.2 reduce-scatter.3
  338.3 56.4 reduce-scatter.5
  403.3 39.2 reduce-scatter.7

commit v8 on v7

--- a/solution.py
+++ b/solution.py
@@ -1554,7 +1554,7 @@
     shard_head = replica_sum(before(shard_head, received))
     pair = replica_sum(before(pair, received), True)
     room = pair.shape[0] // 2
-    shards = [replica_sum(shard_zero), pair[room:], pair[:room]]
+    shards = [shard_zero, pair[room:], pair[:room]]
 
     part = slice_rows(devices)
     chunks = EXPAND // CHUNK
@@ -1562,6 +1562,7 @@
     first_tap = -(-chunks * part // 8) * 8
     late_taps = summed[first_tap:].reshape(-1)[: 9 * side_width].reshape(9, side_width)
     late = summed[: chunks * part].astype(BF16)
+    shards[0] = replica_sum(before(shards[0], late))
     other = lax.ppermute(late, OWNERS, [(half + k, k) for k in range(half)])
     late = spread_over(jnp.stack([late, other]), REPLICAS)
     late = jnp.moveaxis(late.reshape(replicas, 2, chunks, part, CHUNK), 2, 3)

time: 552 us -> 548 us (level)
    unnamed x105 -> x103, local copies, waits for them, and re-layouts: 11.9 us -> 12.2 us
where the time goes in v8:
time: 548 us; the launch traced here: 538 us
  Pallas kernels  147 us (27%)
  waiting for transfers between devices  131 us (24%)
  blocking collectives  114 us (21%)
  starting transfers between devices  49.6 us (9%)
  local copies, waits for them, and re-layouts  42.6 us (8%)
  other arithmetic  33.4 us (6%)
  between operations  19.8 us (4%)
    pallas_call x19, Pallas kernels, call(): pl.pallas_call(flat, out_shape=[struct for struct, _ in outs.values()], i...  147 us
    all_to_all x7, blocking collectives, exchange(): return lax.all_to_all(payload, BOTH, 0, 0)  114 us
    all_to_all x12, waiting for transfers between devices, exchange(): return lax.all_to_all(payload, BOTH, 0, 0)  98.7 us
    all_to_all x12, starting transfers between devices, exchange(): return lax.all_to_all(payload, BOTH, 0, 0)  33.6 us
    ppermute x6, waiting for transfers between devices, replica_sum(): other = lax.ppermute(total, REPLICAS, [(k, k ^ step) for k in range(count)])  16.6 us
    unnamed x103, local copies, waits for them, and re-layouts  12.2 us
  transfers between devices with their start and end apart: 29, of which 20 were waited for; matrix products, arithmetic and copies ran while one was open for 8% of the time, Pallas kernels for 22%

profile of v8, /device:TPU:0, one launch (start us, length us, event | category | flops | bytes accessed | tf_op | source)
XLA Modules:
  0.0 537.5 jit_solution(10799420683232014188)
XLA Ops:
  16.0 21.8 %all_to_all.105.refs_0_ = bf16[32,24,128]{2,1,0:T(8,128)(2,1)} all-to-all(bf16[32,24,128]{2,1,0:T(8,128)(2,1)} %get-tuple-element.114), channel_id=1, replica_groups=mesh['dp'=4,'fsdp'=8] {'dp','fsdp'}, dimensions={0} | all-to-all | bytes 393216 | tf_op jit(solution)/shard_map/all_to_all | solution.py:1401
  56.8 7.7 %shard_map.325 = (bf16[640,1536]{1,0:T(8,128)(2,1)}, bf16[32,24,128]{2,1,0:T(8,128)(2,1)}, f32[8,1536]{1,0:T(8,128)}) custom-call(bf16[32,24,128]{2,1,0:T(8,128)(2,1)} %all_to_all.105.refs_0_, bf16[144,1536]{1,0:T(8,128)(2,1)} %reshape.377.refs_1_.refs_13_, bf16[640,256]{1,0:T(8,128)(2,1)} %get-tuple-element.116.refs_2_.refs_4_.refs_3_, ...), custom_call_target="tpu_custom_call" | custom-call | tf_op jit(solution)/shard_map/pallas_call | solution.py:186
  64.6 15.2 %all_to_all.106.refs_0_ = bf16[32,24,128]{2,1,0:T(8,128)(2,1)} all-to-all(bf16[32,24,128]{2,1,0:T(8,128)(2,1)} %get-tuple-element.117), channel_id=1, replica_groups=mesh['dp'=4,'fsdp'=8] {'dp','fsdp'}, dimensions={0} | all-to-all | bytes 393216 | tf_op jit(solution)/shard_map/all_to_all | solution.py:1401
  88.0 8.0 %all-to-all-done.3.refs_0_ = bf16[32,8,128]{2,1,0:T(8,128)(2,1)S(1)} async-done(((bf16[32,8,128]{2,1,0:T(8,128)(2,1)}), bf16[32,8,128]{2,1,0:T(8,128)(2,1)S(1)}, u32[]{:S(2)}, u32[]{:S(2)}) %all-to-all-start.3) | async-done | bytes 65568 | tf_op jit(solution)/shard_map/all_to_all | solution.py:1401
  114.2 7.0 %shard_map.328 = (bf16[640,1536]{1,0:T(8,128)(2,1)}, bf16[32,24,128]{2,1,0:T(8,128)(2,1)}, f32[8,1536]{1,0:T(8,128)}, f32[16,128]{1,0:T(8,128)}) custom-call(bf16[32,32,128]{2,1,0:T(8,128)(2,1)} %copy-done.9, bf16[144,1536]{1,0:T(8,128)(2,1)} %squeeze.43.refs_1_.refs_13_, bf16[640,256]{1,0:T(8,128)(2,1)} %get-tuple-element.127.refs_2_.refs_4_, ...), custom_call_target="tpu_custom_call" | custom-call | tf_op jit(solution)/shard_map/pallas_call | solution.py:186
  121.3 14.1 %all_to_all.107.refs_0_ = bf16[32,24,128]{2,1,0:T(8,128)(2,1)} all-to-all(bf16[32,24,128]{2,1,0:T(8,128)(2,1)} %get-tuple-element.128), channel_id=1, replica_groups=mesh['dp'=4,'fsdp'=8] {'dp','fsdp'}, dimensions={0} | all-to-all | bytes 393216 | tf_op jit(solution)/shard_map/all_to_all | solution.py:1401
  143.6 14.3 %all-to-all-done.6.refs_0_ = bf16[32,24,128]{2,1,0:T(8,128)(2,1)S(1)} async-done(((bf16[32,24,128]{2,1,0:T(8,128)(2,1)}), bf16[32,24,128]{2,1,0:T(8,128)(2,1)S(1)}, u32[]{:S(2)}, u32[]{:S(2)}) %all-to-all-start.6) | async-done | bytes 196640 | tf_op jit(solution)/shard_map/all_to_all | solution.py:1401
  166.5 15.9 %all-to-all-done.7.refs_0_ = bf16[32,32,128]{2,1,0:T(8,128)(2,1)S(1)} async-done(((bf16[32,32,128]{2,1,0:T(8,128)(2,1)}), bf16[32,32,128]{2,1,0:T(8,128)(2,1)S(1)}, u32[]{:S(2)}, u32[]{:S(2)}) %all-to-all-start.7) | async-done | bytes 262176 | tf_op jit(solution)/shard_map/all_to_all | solution.py:1401
  190.1 12.0 %all_to_all.108.refs_0_ = bf16[32,24,128]{2,1,0:T(8,128)(2,1)} all-to-all(bf16[32,24,128]{2,1,0:T(8,128)(2,1)} %get-tuple-element.137), channel_id=1, replica_groups=mesh['dp'=4,'fsdp'=8] {'dp','fsdp'}, dimensions={0} | all-to-all | bytes 393216 | tf_op jit(solution)/shard_map/all_to_all | solution.py:1401
  210.5 8.7 %all-to-all-done.9.refs_0_ = bf16[32,24,128]{2,1,0:T(8,128)(2,1)S(1)} async-done(((bf16[32,24,128]{2,1,0:T(8,128)(2,1)}), bf16[32,24,128]{2,1,0:T(8,128)(2,1)S(1)}, u32[]{:S(2)}, u32[]{:S(2)}) %all-to-all-start.9) | async-done | bytes 196640 | tf_op jit(solution)/shard_map/all_to_all | solution.py:1401
  228.1 8.8 %all-to-all-done.10.refs_0_ = bf16[32,32,128]{2,1,0:T(8,128)(2,1)S(1)} async-done(((bf16[32,32,128]{2,1,0:T(8,128)(2,1)}), bf16[32,32,128]{2,1,0:T(8,128)(2,1)S(1)}, u32[]{:S(2)}, u32[]{:S(2)}) %all-to-all-start.10) | async-done | bytes 262176 | tf_op jit(solution)/shard_map/all_to_all | solution.py:1401
  237.6 10.9 %shard_map.334 = (bf16[640,1280]{1,0:T(8,128)(2,1)}, bf16[32,48,128]{2,1,0:T(8,128)(2,1)}, f32[8,1280]{1,0:T(8,128)}, bf16[1280,1280]{1,0:T(8,128)(2,1)}) custom-call(bf16[32,32,128]{2,1,0:T(8,128)(2,1)} %copy-done.11, bf16[640,256]{1,0:T(8,128)(2,1)} %get-tuple-element.146.refs_1_.refs_2_, f32[1,1024]{1,0:T(1,128)} %bitcast.145, s32[40,1]{1,0:T(8,128)} %copy.113.refs_3_, ...), custom_call_target="tpu_custom_call" | custom-call | tf_op jit(solution)/shard_map/pallas_call | solution.py:186
  248.5 16.9 %all_to_all.109.refs_0_ = bf16[32,48,128]{2,1,0:T(8,128)(2,1)} all-to-all(bf16[32,48,128]{2,1,0:T(8,128)(2,1)} %get-tuple-element.148), channel_id=1, replica_groups=mesh['dp'=4,'fsdp'=8] {'dp','fsdp'}, dimensions={0} | all-to-all | bytes 786432 | tf_op jit(solution)/shard_map/all_to_all | solution.py:1401
  265.3 13.1 %shard_map.335 = (bf16[640,1536]{1,0:T(8,128)(2,1)}, bf16[32,24,128]{2,1,0:T(8,128)(2,1)}, f32[640,256]{1,0:T(8,128)}, bf16[8,1056,256]{2,1,0:T(8,128)(2,1)}, f3...) custom-call(bf16[32,48,128]{2,1,0:T(8,128)(2,1)} %all_to_all.109.refs_0_, ...), custom_call_target="tpu_custom_call", output_to_operand_aliasing={{6}: (14, {})} | custom-call | tf_op jit(solution)/shard_map/pallas_call | solution.py:186
  279.3 14.5 %all_to_all.110.refs_0_ = bf16[32,24,128]{2,1,0:T(8,128)(2,1)} all-to-all(bf16[32,24,128]{2,1,0:T(8,128)(2,1)S(1)} %copy-done.26), channel_id=1, replica_groups=mesh['dp'=4,'fsdp'=8] {'dp','fsdp'}, dimensions={0} | all-to-all | bytes 393216 | tf_op jit(solution)/shard_map/all_to_all | solution.py:1401
  293.8 11.7 %shard_map.336 = (bf16[640,1536]{1,0:T(8,128)(2,1)}, bf16[32,32,128]{2,1,0:T(8,128)(2,1)}, f32[16,1536]{1,0:T(8,128)}, f32[8,1536]{1,0:T(8,128)}) custom-call(bf16[32,24,128]{2,1,0:T(8,128)(2,1)} %all_to_all.110.refs_0_, bf16[144,1536]{1,0:T(8,128)(2,1)} %squeeze.44.refs_1_.refs_13_, f32[8,1536]{1,0:T(8,128)} %get-tuple-element.152.refs_7_.refs_2_, ...), custom_call_target="tpu_custom_call" | custom-call | tf_op jit(solution)/shard_map/pallas_call | solution.py:186
  305.5 19.1 %all_to_all.111.refs_0_ = bf16[32,32,128]{2,1,0:T(8,128)(2,1)} all-to-all(bf16[32,32,128]{2,1,0:T(8,128)(2,1)} %get-tuple-element.163), channel_id=1, replica_groups=mesh['dp'=4,'fsdp'=8] {'dp','fsdp'}, dimensions={0} | all-to-all | bytes 524288 | tf_op jit(solution)/shard_map/all_to_all | solution.py:1401
  324.6 13.5 %shard_map.337 = (bf16[640,1536]{1,0:T(8,128)(2,1)}, bf16[32,24,128]{2,1,0:T(8,128)(2,1)}, f32[640,256]{1,0:T(8,128)}, bf16[8,1056,256]{2,1,0:T(8,128)(2,1)}, f32[8,1536]{1,0:T(8,128)}, /*index=5*/f32[8,256]{1,0:T(8,128)}) custom-call(bf16[32,32,128]{2,1,0:T(8,128)(2,1)} %all_to_all.111.refs_0_, ...), custom_call_target="tpu_custom_call", output_to_operand_aliasing={{3}: (17, {})} | custom-call | tf_op jit(solution)/shard_map/pallas_call | solution.py:186
  343.5 8.4 %all-to-all-done.14.refs_0_ = bf16[32,24,128]{2,1,0:T(8,128)(2,1)S(1)} async-done(((bf16[32,24,128]{2,1,0:T(8,128)(2,1)}), bf16[32,24,128]{2,1,0:T(8,128)(2,1)S(1)}, u32[]{:S(2)}, u32[]{:S(2)}) %all-to-all-start.14) | async-done | bytes 196640 | tf_op jit(solution)/shard_map/all_to_all | solution.py:1401
  352.6 11.7 %shard_map.338 = (bf16[640,1536]{1,0:T(8,128)(2,1)}, bf16[32,32,128]{2,1,0:T(8,128)(2,1)}, f32[16,1536]{1,0:T(8,128)}, f32[8,1536]{1,0:T(8,128)}) custom-call(bf16[32,24,128]{2,1,0:T(8,128)(2,1)} %copy-done.19, bf16[144,1536]{1,0:T(8,128)(2,1)} %squeeze.43.refs_1_.refs_13_, f32[8,1536]{1,0:T(8,128)} %get-tuple-element.166.refs_7_.refs_2_, ...), custom_call_target="tpu_custom_call" | custom-call | tf_op jit(solution)/shard_map/pallas_call | solution.py:186
  369.1 14.1 %all-to-all-done.15.refs_0_ = bf16[32,32,128]{2,1,0:T(8,128)(2,1)S(1)} async-done(((bf16[32,32,128]{2,1,0:T(8,128)(2,1)}), bf16[32,32,128]{2,1,0:T(8,128)(2,1)S(1)}, u32[]{:S(2)}, u32[]{:S(2)}) %all-to-all-start.15) | async-done | bytes 262176 | tf_op jit(solution)/shard_map/all_to_all | solution.py:1401
  383.9 13.6 %shard_map.339 = (bf16[640,1536]{1,0:T(8,128)(2,1)}, bf16[32,24,128]{2,1,0:T(8,128)(2,1)}, f32[640,256]{1,0:T(8,128)}, bf16[8,528,256]{2,1,0:T(8,128)(2,1)}, f32[8,1536]{1,0:T(8,128)}, /*index=5*/f32[8,256]{1,0:T(8,128)}) custom-call(bf16[32,32,128]{2,1,0:T(8,128)(2,1)} %copy-done.8, f32[8,1536]{1,0:T(8,128)} %get-tuple-element.174.refs_3_.refs_1_, ...), custom_call_target="tpu_custom_call" | custom-call | tf_op jit(solution)/shard_map/pallas_call | solution.py:186
  409.5 10.6 %shard_map.340 = (bf16[640,1536]{1,0:T(8,128)(2,1)}, bf16[32,24,128]{2,1,0:T(8,128)(2,1)}, f32[16,1536]{1,0:T(8,128)}, f32[8,1536]{1,0:T(8,128)}) custom-call(bf16[32,24,128]{2,1,0:T(8,128)(2,1)} %copy-done.15, bf16[144,1536]{1,0:T(8,128)(2,1)} %reshape.377.refs_1_.refs_13_, f32[8,1536]{1,0:T(8,128)} %get-tuple-element.183.refs_7_.refs_2_, ...), custom_call_target="tpu_custom_call" | custom-call | tf_op jit(solution)/shard_map/pallas_call | solution.py:186
  453.0 12.0 %collective-permute-done.6 = bf16[160,1280]{1,0:T(8,128)(2,1)S(1)} collective-permute-done((bf16[160,1280]{1,0:T(8,128)(2,1)S(1)}, bf16[160,1280]{1,0:T(8,128)(2,1)S(1)}, u32[]{:S(2)}, u32[]{:S(2)}) %collective-permute-start.6) | collective-permute-done | bytes 409632 | tf_op jit(solution)/shard_map/ppermute | solution.py:1418
  (296 shorter events, 214.1 us)
Async XLA Ops:
  7.2 41.5 %all-gather.19.cloned.1.call-start = ((), (), s32[]{:S(2)}) async-start(), calls=%async_computation.31 | async-start | bytes 2433024 | tf_op jit(solution)/shard_map/all_gather | solution.py:1450
  11.4 76.6 %all-gather.13.cloned.1.call-start = ((), (), s32[]{:S(2)}) async-start(), calls=%async_computation.28 | async-start | bytes 1769472 | tf_op jit(solution)/shard_map/all_gather | solution.py:1465
  40.6 63.2 %all-gather.15.cloned.1.call-start = ((), (), s32[]{:S(2)}) async-start(), calls=%async_computation.29 | async-start | bytes 1327104 | tf_op jit(solution)/shard_map/all_gather | solution.py:1468
  41.6 102.0 %all-gather.17.cloned.1.call-start = ((), (), s32[]{:S(2)}) async-start(), calls=%async_computation.30 | async-start | bytes 1769472 | tf_op jit(solution)/shard_map/all_gather | solution.py:1465
  42.2 168.3 %all-gather.11.cloned.1.call-start = ((), (), s32[]{:S(2)}) async-start(), calls=%async_computation.24 | async-start | bytes 3686400 | tf_op jit(solution)/shard_map/all_gather | solution.py:1472
  43.1 13.0 %all-to-all-start.1 = ((bf16[32,32,128]{2,1,0:T(8,128)(2,1)}), bf16[32,32,128]{2,1,0:T(8,128)(2,1)S(1)}, u32[]{:S(2)}, u32[]{:S(2)}) async-start(bf16[32,32,128]{2,1,0:T(8,128)(2,1)} %shard_map.324), calls=%async_computation.1 | async-start | bytes 524288 | tf_op jit(solution)/shard_map/all_to_all | solution.py:1401
  85.4 10.7 %all-to-all-start.3 = ((bf16[32,8,128]{2,1,0:T(8,128)(2,1)}), bf16[32,8,128]{2,1,0:T(8,128)(2,1)S(1)}, u32[]{:S(2)}, u32[]{:S(2)}) async-start(bf16[32,8,128]{2,1,0:T(8,128)(2,1)} %get-tuple-element.119), calls=%async_computation.3 | async-start | bytes 131072 | tf_op jit(solution)/shard_map/all_to_all | solution.py:1401
  100.6 13.0 %all-to-all-start.4 = ((bf16[32,32,128]{2,1,0:T(8,128)(2,1)}), bf16[32,32,128]{2,1,0:T(8,128)(2,1)S(1)}, u32[]{:S(2)}, u32[]{:S(2)}) async-start(bf16[32,32,128]{2,1,0:T(8,128)(2,1)} %get-tuple-element.124), calls=%async_computation.4 | async-start | bytes 524288 | tf_op jit(solution)/shard_map/all_to_all | solution.py:1401
  141.0 16.9 %all-to-all-start.6 = ((bf16[32,24,128]{2,1,0:T(8,128)(2,1)}), bf16[32,24,128]{2,1,0:T(8,128)(2,1)S(1)}, u32[]{:S(2)}, u32[]{:S(2)}) async-start(bf16[32,24,128]{2,1,0:T(8,128)(2,1)} %get-tuple-element.131), calls=%async_computation.6 | async-start | bytes 393216 | tf_op jit(solution)/shard_map/all_to_all | solution.py:1401
  162.6 19.7 %all-to-all-start.7 = ((bf16[32,32,128]{2,1,0:T(8,128)(2,1)}), bf16[32,32,128]{2,1,0:T(8,128)(2,1)S(1)}, u32[]{:S(2)}, u32[]{:S(2)}) async-start(bf16[32,32,128]{2,1,0:T(8,128)(2,1)} %get-tuple-element.135), calls=%async_computation.7 | async-start | bytes 524288 | tf_op jit(solution)/shard_map/all_to_all | solution.py:1401
  207.8 11.4 %all-to-all-start.9 = ((bf16[32,24,128]{2,1,0:T(8,128)(2,1)}), bf16[32,24,128]{2,1,0:T(8,128)(2,1)S(1)}, u32[]{:S(2)}, u32[]{:S(2)}) async-start(bf16[32,24,128]{2,1,0:T(8,128)(2,1)} %get-tuple-element.140), calls=%async_computation.9 | async-start | bytes 393216 | tf_op jit(solution)/shard_map/all_to_all | solution.py:1401
  223.8 13.1 %all-to-all-start.10 = ((bf16[32,32,128]{2,1,0:T(8,128)(2,1)}), bf16[32,32,128]{2,1,0:T(8,128)(2,1)S(1)}, u32[]{:S(2)}, u32[]{:S(2)}) async-start(bf16[32,32,128]{2,1,0:T(8,128)(2,1)} %get-tuple-element.145), calls=%async_computation.10 | async-start | bytes 524288 | tf_op jit(solution)/shard_map/all_to_all | solution.py:1401
  226.5 137.8 %reduce-scatter.4.cloned.1.call-start = ((), (), s32[]{:S(2)}) async-start(), calls=%async_computation.25 | async-start | bytes 3686400 | tf_op jit(solution)/shard_map/reduce_scatter | solution.py:1508
  278.4 141.7 %reduce-scatter.6.cloned.1.call-start = ((), (), s32[]{:S(2)}) async-start(), calls=%async_computation.26 | async-start | bytes 4866048 | tf_op jit(solution)/shard_map/reduce_scatter | solution.py:1508
  338.2 13.8 %all-to-all-start.14 = ((bf16[32,24,128]{2,1,0:T(8,128)(2,1)}), bf16[32,24,128]{2,1,0:T(8,128)(2,1)S(1)}, u32[]{:S(2)}, u32[]{:S(2)}) async-start(bf16[32,24,128]{2,1,0:T(8,128)(2,1)} %get-tuple-element.173), calls=%async_computation.14 | async-start | bytes 393216 | tf_op jit(solution)/shard_map/all_to_all | solution.py:1401
  364.3 18.9 %all-to-all-start.15 = ((bf16[32,32,128]{2,1,0:T(8,128)(2,1)}), bf16[32,32,128]{2,1,0:T(8,128)(2,1)S(1)}, u32[]{:S(2)}, u32[]{:S(2)}) async-start(bf16[32,32,128]{2,1,0:T(8,128)(2,1)} %get-tuple-element.180), calls=%async_computation.16 | async-start | bytes 524288 | tf_op jit(solution)/shard_map/all_to_all | solution.py:1401
  397.5 11.4 %all-to-all-start.16 = ((bf16[32,24,128]{2,1,0:T(8,128)(2,1)}), bf16[32,24,128]{2,1,0:T(8,128)(2,1)S(1)}, u32[]{:S(2)}, u32[]{:S(2)}) async-start(bf16[32,24,128]{2,1,0:T(8,128)(2,1)} %get-tuple-element.189), calls=%async_computation.17 | async-start | bytes 393216 | tf_op jit(solution)/shard_map/all_to_all | solution.py:1401
  420.1 11.4 %all-to-all-start.17 = ((bf16[32,24,128]{2,1,0:T(8,128)(2,1)}), bf16[32,24,128]{2,1,0:T(8,128)(2,1)S(1)}, u32[]{:S(2)}, u32[]{:S(2)}) async-start(bf16[32,24,128]{2,1,0:T(8,128)(2,1)} %get-tuple-element.194), calls=%async_computation.19 | async-start | bytes 393216 | tf_op jit(solution)/shard_map/all_to_all | solution.py:1401
  422.8 59.3 %reduce-scatter.8.cloned.1.call-start = ((), (), s32[]{:S(2)}) async-start(), calls=%async_computation.27 | async-start | bytes 2433024 | tf_op jit(solution)/shard_map/reduce_scatter | solution.py:1508
  431.5 15.7 %collective-permute-start.5 = (bf16[160,1280]{1,0:T(8,128)(2,1)S(1)}, bf16[160,1280]{1,0:T(8,128)(2,1)}, u32[]{:S(2)}, u32[]{:S(2)}) collective-permute-start(bf16[160,1280]{1,0:T(8,128)(2,1)S(1)} %copy-done.24), channel_id=1, source_target_pairs={{0,8},{8,0},{16,24},{24,16},{1,9},{9,1},{17,25},{25,17},{2,10},{10... | collective-permute-start | bytes 1228808 | tf_op jit(solution)/shard_map/ppermute | solution.py:1418
  435.0 15.2 %collective-permute-start.3 = (bf16[1056,256]{1,0:T(8,128)(2,1)}, bf16[1056,256]{1,0:T(8,128)(2,1)}, u32[]{:S(2)}, u32[]{:S(2)}) collective-permute-start(bf16[1056,256]{1,0:T(8,128)(2,1)} %reduce-scatter.6.cloned.1.call-done), channel_id=1, source_target_pairs={{0,16},{8,24},{16,0},{24,8},{1,17},{9,25},{17,1},{25,9},{2,18},{10... | collective-permute-start | bytes 1622024 | tf_op jit(solution)/shard_map/ppermute | solution.py:1418
  442.7 36.8 %all-to-all-start.18 = ((bf16[32,56,256]{2,1,0:T(8,128)(2,1)}), bf16[32,56,256]{2,1,0:T(8,128)(2,1)}, u32[]{:S(2)}, u32[]{:S(2)}) async-start(bf16[32,56,256]{2,1,0:T(8,128)(2,1)} %get-tuple-element.197), calls=%async_computation.20 | async-start | bytes 1835008 | tf_op jit(solution)/shard_map/all_to_all | solution.py:1401
  448.4 16.5 %collective-permute-start.6 = (bf16[160,1280]{1,0:T(8,128)(2,1)S(1)}, bf16[160,1280]{1,0:T(8,128)(2,1)S(1)}, u32[]{:S(2)}, u32[]{:S(2)}) collective-permute-start(bf16[160,1280]{1,0:T(8,128)(2,1)S(1)} %add_convert_fusion.3), channel_id=1, source_target_pairs={{0,16},{8,24},{16,0},{24,8},{1,17},{9,25},{17,1},{25,9},{2,18},{10... | collective-permute-start | bytes 1228808 | tf_op jit(solution)/shard_map/ppermute | solution.py:1418
  451.4 18.4 %collective-permute-start.4 = (bf16[1056,256]{1,0:T(8,128)(2,1)S(1)}, bf16[1056,256]{1,0:T(8,128)(2,1)S(1)}, u32[]{:S(2)}, u32[]{:S(2)}) collective-permute-start(bf16[1056,256]{1,0:T(8,128)(2,1)S(1)} %add_convert_fusion.1), channel_id=1, source_target_pairs={{0,8},{8,0},{16,24},{24,16},{1,9},{9,1},{17,25},{25,17},{2,10},{10... | collective-permute-start | bytes 1622024 | tf_op jit(solution)/shard_map/ppermute | solution.py:1418
  (54 other events, 304.5 us)
Sparse Core Ops, SparseCore 0:
  11.5 37.1 all-gather.18
  50.9 27.0 all-gather.12
  79.6 24.0 all-gather.14
  105.8 25.4 all-gather.16
  133.4 50.2 all-gather.10
  278.6 46.2 reduce-scatter.3
  338.3 56.4 reduce-scatter.5
  425.9 44.7 reduce-scatter.7
